TPU v7x, 32 devices: a whole 2x2x4 slice. The times are simulated.
32 devices in a mesh: expert: 8 (over z, y), head: 4 (over x, core).
Axes of the slice: x: 2, y: 2, z: 4, core: 2. Of those that a mesh axis runs over, the one named last changes fastest.
Arguments:
- hidden_in: bfloat16 [2048, 2048], P('expert'), may hold values from -6 to 6
- norm1_gain: float32 [2048], replicated, may hold values from 0.1 to 1.9
- w_query: bfloat16 [2048, 2048], P(None, 'head'), may hold values from -0.125 to 0.125
- w_key: bfloat16 [2048, 2048], P(None, 'head'), may hold values from -0.125 to 0.125
- w_value: bfloat16 [2048, 2048], P(None, 'head'), may hold values from -0.125 to 0.125
- w_out: bfloat16 [2048, 2048], P('head'), may hold values from -0.75 to 0.75
- query_gain: float32 [2048], P('head'), may hold values from 0.1 to 1.9
- key_gain: float32 [2048], P('head'), may hold values from 0.1 to 1.9
- norm2_gain: float32 [2048], replicated, may hold values from 0.1 to 1.9
- w_router: bfloat16 [2048, 16], replicated, may hold values from -0.0625 to 0.0625
- w_gate: bfloat16 [16, 2048, 1024], P('expert', None, 'head'), may hold values from -0.125 to 0.125
- w_up: bfloat16 [16, 2048, 1024], P('expert', None, 'head'), may hold values from -0.125 to 0.125
- w_down: bfloat16 [16, 1024, 2048], P('expert', 'head'), may hold values from -0.75 to 0.75
- routes: int32 [2048, 8], P('expert'), may hold values from 0 to 15, all different within a row; in each aligned block of 256 rows (0 to 255, 256 to 511, ...) at most 256 rows name the same one
- segments: int32 [2048], replicated, may hold values from 0 to 2, as said below
- cotangent: bfloat16 [2048, 2048], P('expert'), may hold values from -6 to 6
Outputs:
- output: bfloat16 [2048, 2048], P('expert')
- grad_input: float32 [2048, 2048], P('expert')
- grad_norm1: float32 [2048], replicated
- grad_query: float32 [2048, 2048], P('expert', 'head')
- grad_key: float32 [2048, 2048], P('expert', 'head')
- grad_value: float32 [2048, 2048], P('expert', 'head')
- grad_w_out: float32 [2048, 2048], P('head', 'expert')
- grad_query_gain: float32 [2048], P('head')
- grad_key_gain: float32 [2048], P('head')
- grad_norm2: float32 [2048], replicated
- grad_router: float32 [2048, 16], replicated
- grad_gate: float32 [16, 2048, 1024], P('expert', None, 'head')
- grad_up: float32 [16, 2048, 1024], P('expert', None, 'head')
- grad_down: float32 [16, 1024, 2048], P('expert', 'head')
Inputs may be any that keep to these rules, and one draw needn't show every extreme that they name: `routes`: each token names 8 different experts. Among the rows of one device, no expert is named more than 256 times, and in every draw some expert is named exactly 256 times by one device's rows. `segments`: never falling along the tokens; no document spans two sequences of 2048 tokens.
All inputs are finite; a program needn't handle non-finite values.
Results may differ from a plain program's by a relative error of at most 0.024.
Values may be sent and summed in bfloat16 or wider, within the bound.
A program may use at most 320 MiB of HBM per device.

v0:
```python
import jax
import jax.numpy as jnp
from jax import lax
from jax.sharding import PartitionSpec as P

HEAD_DIM = 128
TOP = 8
SEQ = 2048


EPSILON = 1e-05
ROPE_BASE = 10000.0
MASKED = -1000000000.0


def from_behind(shard, axis, by):
    size = lax.axis_size(axis)
    pairs = [(i, i + by) for i in range(size) if 0 <= i + by < size]
    return lax.ppermute(shard, axis, pairs)


def inverse_rms(values):
    return lax.rsqrt(jnp.mean(values * values, -1, keepdims=True) + EPSILON)


def norm_back(grad_normed, normed, inverse):
    return inverse * (grad_normed - normed * jnp.mean(grad_normed * normed, -1, keepdims=True))


def rope_tables(places, half_dim):
    inv_freq = ROPE_BASE ** (-lax.iota(jnp.int32, half_dim).astype(jnp.float32) / half_dim)
    angles = places[:, None] * inv_freq[None, :]
    return (jnp.cos(angles)[:, None, :], jnp.sin(angles)[:, None, :])


def rotate(values, cosine, sine_part, direction):
    half_dim = values.shape[-1] // 2
    first_half = values[..., :half_dim]
    second_half = values[..., half_dim:]
    turned = direction * sine_part
    return jnp.concatenate(
        [first_half * cosine - second_half * turned, second_half * cosine + first_half * turned], -1
    )


def on_device(
    hidden_in,
    norm1_gain,
    w_query,
    w_key,
    w_value,
    w_out,
    query_gain,
    key_gain,
    norm2_gain,
    w_router,
    w_gate,
    w_up,
    w_down,
    routes,
    segments,
    cotangent,
):
    seq_len, width = hidden_in.shape
    local_width = w_query.shape[1]
    head_count = local_width // HEAD_DIM
    expert_devs = lax.axis_size("expert")
    local_experts = w_gate.shape[0]
    expert_total = w_router.shape[1]
    capacity = 2 * seq_len * TOP // expert_total
    slab_rows = local_experts * capacity
    my_index = lax.axis_index("expert")
    group = SEQ // seq_len
    rank = my_index % group
    f32 = jnp.float32
    bf16 = jnp.bfloat16

    def split_heads(values):
        return values.reshape(seq_len, head_count, HEAD_DIM)

    inputs = hidden_in.astype(f32)
    inverse_attn = inverse_rms(inputs)
    normed_attn = inputs * inverse_attn
    attn_input = (normed_attn * norm1_gain).astype(bf16)
    q_raw = split_heads(jnp.dot(attn_input, w_query, preferred_element_type=f32))
    k_raw = split_heads(jnp.dot(attn_input, w_key, preferred_element_type=f32))
    v_heads = split_heads(jnp.dot(attn_input, w_value, preferred_element_type=f32).astype(bf16))
    q_gains = query_gain.reshape(head_count, HEAD_DIM)
    k_gains = key_gain.reshape(head_count, HEAD_DIM)
    q_inverse = inverse_rms(q_raw)
    q_normed = q_raw * q_inverse
    k_inverse = inverse_rms(k_raw)
    k_normed = k_raw * k_inverse
    local_places = lax.iota(jnp.int32, seq_len)
    query_places = rank * seq_len + local_places
    cosine, sine_part = rope_tables(query_places.astype(f32), HEAD_DIM // 2)
    queries = rotate(q_normed * q_gains, cosine, sine_part, 1.0).astype(bf16)
    key_rot = rotate(k_normed * k_gains, cosine, sine_part, 1.0).astype(bf16)
    score_scale = HEAD_DIM ** (-0.5)
    keys_values = jnp.stack([key_rot, v_heads])
    pieces = [keys_values]
    for offset in range(1, group):
        keys_values = from_behind(keys_values, "expert", 1)
        pieces.append(keys_values)
    stacked = jnp.stack(pieces, 1).reshape(2, group * seq_len, head_count, HEAD_DIM)
    keys_all = stacked[0]
    values_all = stacked[1]
    query_segs = lax.dynamic_slice_in_dim(segments, my_index * seq_len, seq_len, 0)
    key_segs = jnp.concatenate(
        [
            lax.dynamic_slice_in_dim(
                segments, jnp.maximum(my_index - offset, 0) * seq_len, seq_len, 0
            )
            for offset in range(group)
        ],
        0,
    )
    offsets = lax.iota(jnp.int32, group)
    key_places = ((rank - offsets)[:, None] * seq_len + local_places[None, :]).reshape(-1)
    key_valid = jnp.repeat(rank - offsets >= 0, seq_len)
    allowed = (
        key_valid[None, :]
        & (query_places[:, None] >= key_places[None, :])
        & (query_segs[:, None] == key_segs[None, :])
    )

    def scores_of():
        raw_scores = (
            jnp.einsum("thd,shd->hts", queries, keys_all, preferred_element_type=f32) * score_scale
        )
        return jnp.where(allowed[None], raw_scores, MASKED)

    scores = scores_of()
    row_max = jnp.max(scores, -1, keepdims=True)
    raised = jnp.exp(scores - row_max)
    exp_total = jnp.sum(raised, -1, keepdims=True)
    log_total = row_max + jnp.log(exp_total)
    attn_probs = (raised / exp_total).astype(bf16)
    context = (
        jnp.einsum("hts,shd->thd", attn_probs, values_all, preferred_element_type=f32)
        .reshape(seq_len, local_width)
        .astype(bf16)
    )
    attn_part = jnp.dot(context, w_out, preferred_element_type=f32)
    middle = inputs + lax.psum(attn_part, "head")
    inverse_moe = inverse_rms(middle)
    normed_moe = middle * inverse_moe
    moe_input = (normed_moe * norm2_gain).astype(bf16)
    logits = jnp.dot(moe_input, w_router, preferred_element_type=f32)
    chosen = jnp.take_along_axis(logits, routes, 1)
    raised_gate = jnp.exp(chosen - jnp.max(chosen, -1, keepdims=True))
    gate_weights = raised_gate / jnp.sum(raised_gate, -1, keepdims=True)
    catalog = lax.iota(jnp.int32, expert_total)
    route_hot = (routes[:, :, None] == catalog).astype(jnp.int32)
    token_hot = jnp.sum(route_hot, 1, dtype=jnp.int32)
    earlier = jnp.cumsum(token_hot, 0, dtype=jnp.int32) - token_hot
    position = routes * capacity + jnp.take_along_axis(earlier, routes, 1)
    flat_pos = position.reshape(-1)
    owners = (
        jnp.full((expert_total * capacity,), seq_len, jnp.int32)
        .at[flat_pos]
        .set(jnp.repeat(lax.iota(jnp.int32, seq_len), TOP))
    )
    padded = jnp.concatenate([moe_input, jnp.zeros((1, width), bf16)], 0)
    outgoing = padded[owners].reshape(expert_devs, slab_rows, width)
    arrived = lax.all_to_all(outgoing, "expert", split_axis=0, concat_axis=0, tiled=True)
    rows_in = arrived.reshape(expert_devs, local_experts, capacity, width)
    gate_act = jnp.einsum("sjcd,jdf->sjcf", rows_in, w_gate, preferred_element_type=f32)
    up_act = jnp.einsum("sjcd,jdf->sjcf", rows_in, w_up, preferred_element_type=f32)
    hidden = (jax.nn.silu(gate_act) * up_act).astype(bf16)
    partial_out = jnp.einsum("sjcf,jfd->sjcd", hidden, w_down, preferred_element_type=f32).reshape(
        expert_devs, slab_rows, width
    )
    rows_out = (
        lax.psum_scatter(partial_out.astype(jnp.bfloat16), "head", scatter_dimension=2, tiled=True)
        .astype(jnp.float32)
        .astype(bf16)
    )
    leaving = lax.all_gather(rows_out, "head", axis=2, tiled=True)
    returned = lax.all_to_all(leaving, "expert", split_axis=0, concat_axis=0, tiled=True)
    picked = returned.reshape(expert_total * capacity, width)[position]
    moe_out = jnp.einsum("tk,tkd->td", gate_weights, picked, preferred_element_type=f32)
    output = (middle + moe_out).astype(bf16)
    grad_final = cotangent.astype(f32)
    grad_gates = jnp.einsum("td,tkd->tk", grad_final, picked, preferred_element_type=f32)
    grad_chosen = gate_weights * (
        grad_gates - jnp.sum(grad_gates * gate_weights, -1, keepdims=True)
    )
    grad_logits = jnp.einsum("tk,tke->te", grad_chosen, route_hot.astype(f32)).astype(bf16)
    grad_router = jnp.dot(moe_input.T, grad_logits, preferred_element_type=f32)
    grad_moe_input = jnp.dot(grad_logits, w_router.T, preferred_element_type=f32)
    grad_expert_out = (gate_weights[:, :, None] * grad_final[:, None, :]).astype(bf16)
    grad_slab = (
        jnp.zeros((expert_total * capacity, width), bf16)
        .at[flat_pos]
        .set(grad_expert_out.reshape(seq_len * TOP, width))
    )
    grad_slab = grad_slab.reshape(expert_devs, slab_rows, width)
    grad_arrived = lax.all_to_all(grad_slab, "expert", split_axis=0, concat_axis=0, tiled=True)
    grad_rows_out = grad_arrived.reshape(expert_devs, local_experts, capacity, width)
    grad_hidden = jnp.einsum("sjcd,jfd->sjcf", grad_rows_out, w_down, preferred_element_type=f32)
    grad_down = jnp.einsum("sjcf,sjcd->jfd", hidden, grad_rows_out, preferred_element_type=f32)
    sigmoid = jax.nn.sigmoid(gate_act)
    grad_up_act = (grad_hidden * gate_act * sigmoid).astype(bf16)
    grad_gate_act = (grad_hidden * up_act * sigmoid * (1.0 + gate_act * (1.0 - sigmoid))).astype(
        bf16
    )
    grad_gate = jnp.einsum("sjcd,sjcf->jdf", rows_in, grad_gate_act, preferred_element_type=f32)
    grad_up = jnp.einsum("sjcd,sjcf->jdf", rows_in, grad_up_act, preferred_element_type=f32)
    grad_rows_in = jnp.einsum("sjcf,jdf->sjcd", grad_gate_act, w_gate, preferred_element_type=f32)
    grad_rows_in = grad_rows_in + jnp.einsum(
        "sjcf,jdf->sjcd", grad_up_act, w_up, preferred_element_type=f32
    )
    grad_back = (
        lax.psum_scatter(
            grad_rows_in.reshape(expert_devs, slab_rows, width).astype(jnp.bfloat16),
            "head",
            scatter_dimension=2,
            tiled=True,
        )
        .astype(jnp.float32)
        .astype(bf16)
    )
    leaving_grad = lax.all_gather(grad_back, "head", axis=2, tiled=True)
    grad_home = lax.all_to_all(leaving_grad, "expert", split_axis=0, concat_axis=0, tiled=True)
    grad_moe_input = grad_moe_input + jnp.sum(
        grad_home.reshape(expert_total * capacity, width)[position], 1, dtype=f32
    )
    grad_norm2 = jnp.sum(grad_moe_input * normed_moe, 0)
    grad_middle = grad_final + norm_back(grad_moe_input * norm2_gain, normed_moe, inverse_moe)
    grad_attn = grad_middle.astype(bf16)
    grad_out_turned = jnp.dot(grad_attn.T, context, preferred_element_type=f32)
    grad_context = split_heads(jnp.dot(grad_attn, w_out.T, preferred_element_type=f32).astype(bf16))
    attn_full = jnp.exp(scores_of() - log_total)
    attn_low = attn_full.astype(bf16)
    grad_values_all = jnp.einsum("hts,thd->shd", attn_low, grad_context, preferred_element_type=f32)
    grad_probs = jnp.einsum("thd,shd->hts", grad_context, values_all, preferred_element_type=f32)
    grad_scores = (
        attn_full * (grad_probs - jnp.sum(grad_probs * attn_full, -1, keepdims=True))
    ).astype(bf16)
    grad_queries = (
        jnp.einsum("hts,shd->thd", grad_scores, keys_all, preferred_element_type=f32) * score_scale
    )
    grad_keys_all = (
        jnp.einsum("hts,thd->shd", grad_scores, queries, preferred_element_type=f32) * score_scale
    )
    kv_terms = jnp.stack([grad_keys_all, grad_values_all]).reshape(
        2, group, seq_len, head_count, HEAD_DIM
    )
    kv_total = kv_terms[:, 0]
    for offset in range(1, group):
        kv_total = kv_total + from_behind(
            kv_terms[:, offset].astype(jnp.bfloat16), "expert", -offset
        ).astype(jnp.float32)
    grad_keys = kv_total[0]
    grad_values = kv_total[1]
    grad_q_normed = rotate(grad_queries, cosine, sine_part, -1.0)
    grad_k_normed = rotate(grad_keys, cosine, sine_part, -1.0)
    grad_query_gain = jnp.sum(grad_q_normed * q_normed, 0).reshape(local_width)
    grad_key_gain = jnp.sum(grad_k_normed * k_normed, 0).reshape(local_width)
    grad_q_raw = (
        norm_back(grad_q_normed * q_gains, q_normed, q_inverse)
        .reshape(seq_len, local_width)
        .astype(bf16)
    )
    grad_k_raw = (
        norm_back(grad_k_normed * k_gains, k_normed, k_inverse)
        .reshape(seq_len, local_width)
        .astype(bf16)
    )
    grad_v_raw = grad_values.reshape(seq_len, local_width).astype(bf16)
    grad_query = jnp.dot(attn_input.T, grad_q_raw, preferred_element_type=f32)
    grad_key = jnp.dot(attn_input.T, grad_k_raw, preferred_element_type=f32)
    grad_value = jnp.dot(attn_input.T, grad_v_raw, preferred_element_type=f32)
    input_part = jnp.dot(grad_q_raw, w_query.T, preferred_element_type=f32)
    input_part = input_part + jnp.dot(grad_k_raw, w_key.T, preferred_element_type=f32)
    input_part = input_part + jnp.dot(grad_v_raw, w_value.T, preferred_element_type=f32)
    grad_attn_input = lax.psum(input_part.astype(jnp.bfloat16), "head").astype(jnp.float32)
    grad_norm1 = jnp.sum(grad_attn_input * normed_attn, 0)
    grad_input = grad_middle + norm_back(grad_attn_input * norm1_gain, normed_attn, inverse_attn)
    grad_query, grad_key, grad_value, grad_out_turned = (
        lax.psum_scatter(
            grad_query.astype(jnp.bfloat16), "expert", scatter_dimension=0, tiled=True
        ).astype(jnp.float32),
        lax.psum_scatter(
            grad_key.astype(jnp.bfloat16), "expert", scatter_dimension=0, tiled=True
        ).astype(jnp.float32),
        lax.psum_scatter(
            grad_value.astype(jnp.bfloat16), "expert", scatter_dimension=0, tiled=True
        ).astype(jnp.float32),
        lax.psum_scatter(
            grad_out_turned.astype(jnp.bfloat16), "expert", scatter_dimension=0, tiled=True
        ).astype(jnp.float32),
    )
    grad_router, grad_norm1, grad_norm2, grad_query_gain, grad_key_gain = (
        lax.psum(grad_router.astype(jnp.bfloat16), "expert").astype(jnp.float32),
        lax.psum(grad_norm1.astype(jnp.bfloat16), "expert").astype(jnp.float32),
        lax.psum(grad_norm2.astype(jnp.bfloat16), "expert").astype(jnp.float32),
        lax.psum(grad_query_gain.astype(jnp.bfloat16), "expert").astype(jnp.float32),
        lax.psum(grad_key_gain.astype(jnp.bfloat16), "expert").astype(jnp.float32),
    )
    return (
        output,
        grad_input,
        grad_norm1,
        grad_query,
        grad_key,
        grad_value,
        grad_out_turned.T,
        grad_query_gain,
        grad_key_gain,
        grad_norm2,
        grad_router,
        grad_gate,
        grad_up,
        grad_down,
    )


def solution(mesh):
    return jax.shard_map(
        on_device,
        mesh=mesh,
        in_specs=(
            P("expert", None),
            P(),
            P(None, "head"),
            P(None, "head"),
            P(None, "head"),
            P("head", None),
            P("head"),
            P("head"),
            P(),
            P(),
            P("expert", None, "head"),
            P("expert", None, "head"),
            P("expert", "head", None),
            P("expert", None),
            P(),
            P("expert", None),
        ),
        out_specs=(
            P("expert", None),
            P("expert", None),
            P(),
            P("expert", "head"),
            P("expert", "head"),
            P("expert", "head"),
            P("head", "expert"),
            P("head"),
            P("head"),
            P(),
            P(),
            P("expert", None, "head"),
            P("expert", None, "head"),
            P("expert", "head", None),
        ),
        check_vma=False,
    )
```

profile of v0, /device:TPU:0, one launch (start us, length us, event | category | flops | bytes accessed | tf_op | source)
XLA Modules:
  0.0 2876.5 jit_solution(15280686987026685231)
XLA Ops:
  9.5 3.5 convolution_convert_fusion.6
  14.7 3.3 fusion.109
  31.9 5.7 collective-permute-start
  39.1 9.1 collective-permute-done
  48.2 5.2 collective-permute-start.1
  53.6 9.6 collective-permute-done.1
  63.2 5.2 collective-permute-start.2
  73.5 3.8 collective-permute-done.2
  77.3 5.2 collective-permute-start.3
  91.3 5.3 collective-permute-start.4
  99.3 4.7 collective-permute-done.4
  104.1 5.2 collective-permute-start.5
  116.1 5.8 collective-permute-start.6
  124.3 4.0 collective-permute-done.6
  144.7 13.6 gather_fusion.4
  159.5 8.1 scatter_custom_fusion
  167.6 31.7 %all-reduce.6.cloned.1.call-done = f32[256,2048]{1,0:T(8,128)} async-done(((f32[256,2048]{1,0:T(8,128)}), f32[256,2048]{1,0:T(8,128)}) %all-reduce.6.cloned.1.call-update) | async-done | bytes 2097168 | tf_op jit(solution)/shard_map/psum | solution.py:145
  204.0 21.0 gather_fusion
  224.9 370.7 %all_to_all.20 = bf16[8,512,2048]{2,1,0:T(8,128)(2,1)} all-to-all(bf16[8,512,2048]{2,1,0:T(8,128)(2,1)} %bitcast.313), channel_id=1, replica_groups=mesh['expert'=8,'head'=4] {'expert'}, dimensions={0} | all-to-all | bytes 33554432 | tf_op jit(solution)/shard_map/all_to_all | solution.py:166
  595.6 12.9 fusion.8
  608.5 11.8 fusion.28
  620.4 9.8 convert_bitcast_fusion
  630.2 14.1 copy.258
  644.3 124.5 %reduce-scatter.7.cloned.1.call-done = bf16[8,512,512]{2,1,0:T(8,128)(2,1)} async-done(((bf16[8,512,2048]{2,1,0:T(8,128)(2,1)}), bf16[8,512,512]{2,1,0:T(8,128)(2,1)}) %reduce-scatter.7.cloned.1.call-update) | async-done | bytes 4194320 | tf_op jit(solution)/shard_map/reduce_scatter | solution.py:175
  768.8 107.5 %all-gather.3.cloned.1.call-done = bf16[8,512,2048]{2,1,0:T(8,128)(2,1)} async-done(((bf16[8,512,512]{2,1,0:T(8,128)(2,1)}), bf16[8,512,2048]{2,1,0:T(8,128)(2,1)}) %all-gather.3.cloned.1.call-update) | async-done | bytes 16777232 | tf_op jit(solution)/shard_map/all_gather | solution.py:179
  876.3 5.7 all-to-all-start.1
  886.0 16.8 gather_fusion.3
  903.0 342.6 %all-to-all-done.1 = bf16[8,512,2048]{2,1,0:T(8,128)(2,1)} async-done(((bf16[8,512,2048]{2,1,0:T(8,128)(2,1)}), bf16[8,512,2048]{2,1,0:T(8,128)(2,1)}, u32[]{:S(2)}, u32[]{:S(2)}) %all-to-all-start.1) | async-done | bytes 16777248 | tf_op jit(solution)/shard_map/all_to_all | solution.py:180
  1245.6 24.3 gather_fusion.1
  1269.9 8.7 fusion.14
  1279.0 22.6 scatter_custom_fusion.1
  1301.6 370.4 %all_to_all.21 = bf16[8,512,2048]{2,1,0:T(8,128)(2,1)} all-to-all(bf16[8,512,2048]{2,1,0:T(8,128)(2,1)} %bitcast.316), channel_id=1, replica_groups=mesh['expert'=8,'head'=4] {'expert'}, dimensions={0} | all-to-all | bytes 33554432 | tf_op jit(solution)/shard_map/all_to_all | solution.py:199
  1672.0 12.3 fusion.27
  1684.3 13.2 fusion.55
  1697.5 17.6 fusion
  1715.1 14.1 copy.262
  1729.2 124.3 %reduce-scatter.9.cloned.1.call-done = bf16[8,512,512]{2,1,0:T(8,128)(2,1)} async-done(((bf16[8,512,2048]{2,1,0:T(8,128)(2,1)}), bf16[8,512,512]{2,1,0:T(8,128)(2,1)}) %reduce-scatter.9.cloned.1.call-update) | async-done | bytes 4194320 | tf_op jit(solution)/shard_map/reduce_scatter | solution.py:215
  1853.6 107.4 %all-gather.5.cloned.1.call-done = bf16[8,512,2048]{2,1,0:T(8,128)(2,1)} async-done(((bf16[8,512,512]{2,1,0:T(8,128)(2,1)}), bf16[8,512,2048]{2,1,0:T(8,128)(2,1)}) %all-gather.5.cloned.1.call-update) | async-done | bytes 16777232 | tf_op jit(solution)/shard_map/all_gather | solution.py:224
  1961.0 5.7 all-to-all-start.3
  1967.2 7.0 fusion.12
  1974.2 356.1 %all-to-all-done.3 = bf16[8,512,2048]{2,1,0:T(8,128)(2,1)} async-done(((bf16[8,512,2048]{2,1,0:T(8,128)(2,1)}), bf16[8,512,2048]{2,1,0:T(8,128)(2,1)}, u32[]{:S(2)}, u32[]{:S(2)}) %all-to-all-start.3) | async-done | bytes 16777248 | tf_op jit(solution)/shard_map/all_to_all | solution.py:225
  2330.3 24.7 gather_fusion.2
  2355.1 11.4 convert_reduce_fusion
  2366.5 3.1 multiply_reduce_fusion.1
  2373.3 7.2 fusion.38
  2380.5 6.7 multiply_reduce_fusion
  2387.2 5.3 copy.273
  2392.5 6.8 multiply_convert_fusion
  2404.3 5.3 copy.271
  2409.7 4.7 slice_bitcast_fusion.8
  2422.5 18.7 collective-permute-done.7
  2444.9 5.0 fusion.64
  2449.9 30.4 %collective-permute-done.11 = bf16[2,256,4,128]{3,1,2,0:T(8,128)(2,1)} collective-permute-done((bf16[2,256,4,128]{3,1,2,0:T(8,128)(2,1)}, bf16[2,256,4,128]{3,1,2,0:T(8,128)(2,1)}, u32[]{:S(2)}, u32[]{:S(2)}) %collective-permute-start.11) | collective-permute-done | bytes 524320 | tf_op jit(solution)/shard_map/ppermute | solution.py:19
  2480.3 7.4 collective-permute-done.10
  2516.0 31.0 %all-reduce.10.cloned.1.call-done = bf16[2048,16]{0,1:T(8,128)(2,1)} async-done(((bf16[2048,16]{0,1:T(8,128)(2,1)}), bf16[2048,16]{0,1:T(8,128)(2,1)}) %all-reduce.10.cloned.1.call-update) | async-done | bytes 65552 | tf_op jit(solution)/shard_map/psum | solution.py:296
  2550.9 12.5 convolution_bitcast_fusion
  2563.4 12.4 convolution_bitcast_fusion.1
  2575.8 12.5 fusion.35
  2590.3 36.2 %all-reduce.1 = (bf16[2048]{0:T(1024)(128)(2,1)S(1)}, bf16[512]{0:T(512)(128)(2,1)S(1)}, bf16[512]{0:T(512)(128)(2,1)S(1)}, bf16[2048]{0:T(1024)(128)(2,1)S(1)}) all-reduce(bf16[2048]{0:T(1024)(128)(2,1)S(1)} %get-tuple-element.100, bf16[512]{0:T(512)(128)(2,1)S(1)} %get-tuple-element.130, ...), channel_id=1, replica_groups=mesh['expert'=8,'head'=4] {'expert'}, use_global_device_ids=true, to_apply=%region_25.26 | all-reduce | flops 5120 | bytes 20480 | tf_op jit(solution)/shard_map/psum | solution.py:297
  2628.9 4.0 fusion.48
  2632.8 24.4 reduce-scatter.17.cloned.1.call-done
  2659.2 68.2 %reduce-scatter.11.cloned.1.call-done = bf16[256,512]{1,0:T(8,128)(2,1)} async-done(((bf16[2048,512]{1,0:T(8,128)(2,1)}), bf16[256,512]{1,0:T(8,128)(2,1)}) %reduce-scatter.11.cloned.1.call-update) | async-done | bytes 262160 | tf_op jit(solution)/shard_map/reduce_scatter | solution.py:282
  2729.2 68.5 %reduce-scatter.15.cloned.1.call-done = bf16[256,512]{1,0:T(8,128)(2,1)} async-done(((bf16[2048,512]{1,0:T(8,128)(2,1)}), bf16[256,512]{1,0:T(8,128)(2,1)}) %reduce-scatter.15.cloned.1.call-update) | async-done | bytes 262160 | tf_op jit(solution)/shard_map/reduce_scatter | solution.py:288
  2799.5 68.4 %reduce-scatter.13.cloned.1.call-done = bf16[256,512]{1,0:T(8,128)(2,1)} async-done(((bf16[2048,512]{1,0:T(8,128)(2,1)}), bf16[256,512]{1,0:T(8,128)(2,1)}) %reduce-scatter.13.cloned.1.call-update) | async-done | bytes 262160 | tf_op jit(solution)/shard_map/reduce_scatter | solution.py:285
  (331 shorter events, 136.3 us)
Async XLA Ops:
  7.2 613.2 %copy-start = (bf16[2,256,2048]{2,1,0:T(8,128)(2,1)S(1)}, bf16[2,256,2048]{2,1,0:T(8,128)(2,1)}, u32[]{:S(2)}) copy-start(bf16[2,256,2048]{2,1,0:T(8,128)(2,1)} %param.28) | copy-start | bytes 6291460
  7.2 192.1 %all-reduce.6.cloned.1.call-start = ((), (), s32[]{:S(2)}) async-start(), calls=%async_computation.10 | async-start | bytes 4194304 | tf_op jit(solution)/shard_map/psum | solution.py:145
  8.9 9.1 copy-start.71
  9.5 5.2 copy-start.9
  9.5 5.2 copy-start.56
  19.6 8.2 copy-start.67
  19.6 8.2 copy-start.69
  23.1 6.3 copy-start.62
  29.4 8.1 copy-start.54
  30.6 101.4 %copy-start.26 = (bf16[256,4,64]{2,0,1:T(8,128)(2,1)}, bf16[256,4,64]{2,0,1:T(8,128)(2,1)S(1)}, u32[]{:S(2)}) copy-start(bf16[256,4,64]{2,0,1:T(8,128)(2,1)S(1)} %get-tuple-element.140) | copy-start | bytes 393220
  31.9 16.4 collective-permute-start
  48.2 15.0 collective-permute-start.1
  63.2 14.1 collective-permute-start.2
  77.3 14.0 collective-permute-start.3
  91.3 12.8 collective-permute-start.4
  104.1 12.0 collective-permute-start.5
  116.1 12.3 collective-permute-start.6
  143.8 625.0 %reduce-scatter.7.cloned.1.call-start = ((), (), s32[]{:S(2)}) async-start(), calls=%async_computation.11 | async-start | bytes 20971520 | tf_op jit(solution)/shard_map/reduce_scatter | solution.py:175
  159.5 41.8 %copy-start.78 = (s32[2048,1]{0,1:T(1,128)}, s32[2048,1]{0,1:T(1,128)S(1)}, u32[]{:S(2)}) copy-start(s32[2048,1]{0,1:T(1,128)S(1)} %compare_select_fusion) | copy-start | bytes 24580
  167.6 35.0 %copy-start.58 = (f32[2048]{0:T(1024)S(1)}, f32[2048]{0:T(1024)}, u32[]{:S(2)}) copy-start(f32[2048]{0:T(1024)} %param.24) | copy-start | bytes 24580
  644.3 232.1 %all-gather.3.cloned.1.call-start = ((), (), s32[]{:S(2)}) async-start(), calls=%async_computation.12 | async-start | bytes 20971520 | tf_op jit(solution)/shard_map/all_gather | solution.py:179
  876.3 369.3 %all-to-all-start.1 = ((bf16[8,512,2048]{2,1,0:T(8,128)(2,1)}), bf16[8,512,2048]{2,1,0:T(8,128)(2,1)}, u32[]{:S(2)}, u32[]{:S(2)}) async-start(bf16[8,512,2048]{2,1,0:T(8,128)(2,1)} %all-gather.3.cloned.1.call-done), calls=%async_computation.2 | async-start | bytes 33554432 | tf_op jit(solution)/shard_map/all_to_all | solution.py:180
  882.1 971.4 %reduce-scatter.9.cloned.1.call-start = ((), (), s32[]{:S(2)}) async-start(), calls=%async_computation.13 | async-start | bytes 20971520 | tf_op jit(solution)/shard_map/reduce_scatter | solution.py:215
  886.0 17.0 copy-start.66
  1245.6 24.3 copy-start.25
  1672.0 12.3 copy-start.30
  1684.3 13.2 copy-start.23
  1684.3 13.2 copy-start.37
  1729.2 231.8 %all-gather.5.cloned.1.call-start = ((), (), s32[]{:S(2)}) async-start(), calls=%async_computation.14 | async-start | bytes 20971520 | tf_op jit(solution)/shard_map/all_gather | solution.py:224
  1853.6 113.2 %copy-start.65 = (f32[4,256]{1,0:T(4,128)S(1)}, f32[4,256]{1,0:T(4,128)}, u32[]{:S(2)}) copy-start(f32[4,256]{1,0:T(4,128)} %copy-done.64) | copy-start | bytes 12292
  1853.6 113.2 %copy-start.74 = (f32[4,256]{1,0:T(4,128)S(1)}, f32[4,256]{1,0:T(4,128)}, u32[]{:S(2)}) copy-start(f32[4,256]{1,0:T(4,128)} %copy-done.73) | copy-start | bytes 12292
  1853.6 113.3 %copy-start.55 = (s32[256,8]{0,1:T(8,128)S(1)}, s32[256,8]{0,1:T(8,128)}, u32[]{:S(2)}) copy-start(s32[256,8]{0,1:T(8,128)} %param.29) | copy-start | bytes 24580
  1961.0 369.3 %all-to-all-start.3 = ((bf16[8,512,2048]{2,1,0:T(8,128)(2,1)}), bf16[8,512,2048]{2,1,0:T(8,128)(2,1)}, u32[]{:S(2)}, u32[]{:S(2)}) async-start(bf16[8,512,2048]{2,1,0:T(8,128)(2,1)} %all-gather.5.cloned.1.call-done), calls=%async_computation.5 | async-start | bytes 33554432 | tf_op jit(solution)/shard_map/all_to_all | solution.py:225
  1966.8 580.3 %all-reduce.10.cloned.1.call-start = ((), (), s32[]{:S(2)}) async-start(), calls=%async_computation.20 | async-start | bytes 131072 | tf_op jit(solution)/shard_map/psum | solution.py:296
  2355.0 11.5 copy-start.7
  2355.0 11.5 copy-start.53
  2355.0 11.5 copy-start.59
  2355.0 11.4 copy-start.77
  2372.4 135.7 %copy-start.5 = (f32[256,2048]{1,0:T(8,128)}, f32[256,2048]{1,0:T(8,128)S(1)}, u32[]{:S(2)}) copy-start(f32[256,2048]{1,0:T(8,128)S(1)} %get-tuple-element.126) | copy-start | bytes 6291460
  2373.3 7.2 copy-start.16
  2392.5 8.8 copy-start.27
  2392.5 8.8 copy-start.29
  2409.7 7.4 copy-start.63
  2409.7 8.2 copy-start.61
  2409.7 34.2 %copy-start.14 = (bf16[256,2048]{1,0:T(8,128)(2,1)S(1)}, bf16[256,2048]{1,0:T(8,128)(2,1)}, u32[]{:S(2)}) copy-start(bf16[256,2048]{1,0:T(8,128)(2,1)} %copy-done.12) | copy-start | bytes 3145732
  2414.4 26.8 collective-permute-start.7
  2415.7 26.8 collective-permute-start.13
  2418.6 31.3 %collective-permute-start.12 = (bf16[2,256,4,128]{3,1,2,0:T(8,128)(2,1)}, bf16[2,256,4,128]{3,1,2,0:T(8,128)(2,1)}, u32[]{:S(2)}, u32[]{:S(2)}) collective-permute-start(bf16[2,256,4,128]{3,1,2,0:T(8,128)(2,1)} %get-tuple-element.119), channel_id=1, source_target_pairs={{24,0},{28,4},{25,1},{29,5},{26,2},{30,6},{27,3},{31,7}} | collective-permute-start | bytes 1572872 | tf_op jit(solution)/shard_map/ppermute | solution.py:19
  2419.9 60.4 %collective-permute-start.11 = (bf16[2,256,4,128]{3,1,2,0:T(8,128)(2,1)}, bf16[2,256,4,128]{3,1,2,0:T(8,128)(2,1)}, u32[]{:S(2)}, u32[]{:S(2)}) collective-permute-start(bf16[2,256,4,128]{3,1,2,0:T(8,128)(2,1)} %get-tuple-element.120), channel_id=1, source_target_pairs={{20,0},{24,4},{28,8},{21,1},{25,5},{29,9},{22,2},{26,6},{30,10},{2... | collective-permute-start | bytes 1572872 | tf_op jit(solution)/shard_map/ppermute | solution.py:19
  2421.2 66.4 %collective-permute-start.10 = (bf16[2,256,4,128]{3,1,2,0:T(8,128)(2,1)}, bf16[2,256,4,128]{3,1,2,0:T(8,128)(2,1)}, u32[]{:S(2)}, u32[]{:S(2)}) collective-permute-start(bf16[2,256,4,128]{3,1,2,0:T(8,128)(2,1)} %get-tuple-element.121), channel_id=1, source_target_pairs={{16,0},{20,4},{24,8},{28,12},{17,1},{21,5},{25,9},{29,13},{18,2},{... | collective-permute-start | bytes 1572872 | tf_op jit(solution)/shard_map/ppermute | solution.py:19
  2441.2 46.4 %collective-permute-start.9 = (bf16[2,256,4,128]{3,1,2,0:T(8,128)(2,1)}, bf16[2,256,4,128]{3,1,2,0:T(8,128)(2,1)}, u32[]{:S(2)}, u32[]{:S(2)}) collective-permute-start(bf16[2,256,4,128]{3,1,2,0:T(8,128)(2,1)} %get-tuple-element.122), channel_id=1, source_target_pairs={{12,0},{16,4},{20,8},{24,12},{28,16},{13,1},{17,5},{21,9},{25,13},... | collective-permute-start | bytes 1572872 | tf_op jit(solution)/shard_map/ppermute | solution.py:19
  2442.5 45.1 %collective-permute-start.8 = (bf16[2,256,4,128]{3,1,2,0:T(8,128)(2,1)}, bf16[2,256,4,128]{3,1,2,0:T(8,128)(2,1)}, u32[]{:S(2)}, u32[]{:S(2)}) collective-permute-start(bf16[2,256,4,128]{3,1,2,0:T(8,128)(2,1)} %get-tuple-element.123), channel_id=1, source_target_pairs={{8,0},{12,4},{16,8},{20,12},{24,16},{28,20},{9,1},{13,5},{17,9},{2... | collective-permute-start | bytes 1572872 | tf_op jit(solution)/shard_map/ppermute | solution.py:19
  2444.8 143.4 %all-reduce.8.cloned.1.call-start = ((), (), s32[]{:S(2)}) async-start(), calls=%async_computation.15 | async-start | bytes 2097152 | tf_op jit(solution)/shard_map/psum | solution.py:278
  2444.8 42.8 %copy-start.3 = (f32[2048,4,128]{2,0,1:T(8,128)S(1)}, f32[2048,4,128]{2,0,1:T(8,128)}, u32[]{:S(2)}) copy-start(f32[2048,4,128]{2,0,1:T(8,128)} %copy.273) | copy-start | bytes 12582916
  2444.9 42.8 %copy-start.4 = (f32[2048,4,128]{2,0,1:T(8,128)S(1)}, f32[2048,4,128]{2,0,1:T(8,128)}, u32[]{:S(2)}) copy-start(f32[2048,4,128]{2,0,1:T(8,128)} %copy.271) | copy-start | bytes 12582916
  2493.8 5.1 copy-start.50
  2508.0 149.2 %reduce-scatter.17.cloned.1.call-start = ((), (), s32[]{:S(2)}) async-start(), calls=%async_computation.19 | async-start | bytes 2359296 | tf_op jit(solution)/shard_map/reduce_scatter | solution.py:291
  2510.2 217.2 %reduce-scatter.11.cloned.1.call-start = ((), (), s32[]{:S(2)}) async-start(), calls=%async_computation.16 | async-start | bytes 2359296 | tf_op jit(solution)/shard_map/reduce_scatter | solution.py:282
  2513.7 34.9 %copy-start.43 = (bf16[256,512]{1,0:T(8,128)(2,1)S(1)}, bf16[256,512]{1,0:T(8,128)(2,1)}, u32[]{:S(2)}) copy-start(bf16[256,512]{1,0:T(8,128)(2,1)} %copy-done.42) | copy-start | bytes 786436
  2513.7 284.0 %reduce-scatter.15.cloned.1.call-start = ((), (), s32[]{:S(2)}) async-start(), calls=%async_computation.18 | async-start | bytes 2359296 | tf_op jit(solution)/shard_map/reduce_scatter | solution.py:288
  2516.0 351.9 %reduce-scatter.13.cloned.1.call-start = ((), (), s32[]{:S(2)}) async-start(), calls=%async_computation.17 | async-start | bytes 2359296 | tf_op jit(solution)/shard_map/reduce_scatter | solution.py:285
  2550.9 12.5 copy-start.24
  2563.4 12.4 copy-start.33
  2628.9 240.9 %copy-start.1 = (bf16[2,256,2048]{2,1,0:T(8,128)(2,1)S(1)}, bf16[2,256,2048]{2,1,0:T(8,128)(2,1)}, u32[]{:S(2)}) copy-start(bf16[2,256,2048]{2,1,0:T(8,128)(2,1)} %param.28) | copy-start | bytes 6291460
  (42 other events, 87.0 us)
Sparse Core Ops, SparseCore 0:
  143.9 55.3 all-reduce.5
  644.4 124.3 reduce-scatter.6
  770.4 105.9 all-gather.2
  1729.3 124.1 reduce-scatter.8
  1855.0 105.9 all-gather.4
  2444.9 102.1 all-reduce.9
  2549.5 35.9 all-reduce.7
  2589.1 68.0 reduce-scatter.16
  2660.8 66.5 reduce-scatter.10
  2730.8 66.8 reduce-scatter.14
  2801.2 66.6 reduce-scatter.12
where the time goes:
time: 2880 us
  waiting for transfers between devices  1550 us (54%)
  blocking collectives  777 us (27%)
  local copies, waits for them, and re-layouts  201 us (7%)
  matrix products  184 us (6%)
  other arithmetic  94.3 us (3%)
  starting transfers between devices  59 us (2%)
    all_to_all x1, blocking collectives, on_device(): lax.all_to_all(outgoing, 'expert', split_axis=0, concat_axis=0, tiled=True)  371 us
    all_to_all x1, blocking collectives, on_device(): lax.all_to_all(grad_slab, 'expert', split_axis=0, concat_axis=0, tiled=True)  370 us
    all_to_all x1, waiting for transfers between devices, on_device(): lax.all_to_all(leaving_grad, 'expert', split_axis=0, concat_axis=0, tiled...  356 us
    all_to_all x1, waiting for transfers between devices, on_device(): lax.all_to_all(leaving, 'expert', split_axis=0, concat_axis=0, tiled=True)  343 us
    reduce_scatter x1, waiting for transfers between devices, on_device(): lax.psum_scatter(partial_out.astype(jnp.bfloat16), 'head', scatter_dimens...  124 us
    reduce_scatter x1, waiting for transfers between devices, on_device(): lax.psum_scatter(grad_rows_in.reshape(expert_devs, slab_rows, width).asty...  124 us
    all_gather x1, waiting for transfers between devices, on_device(): leaving = lax.all_gather(rows_out, 'head', axis=2, tiled=True)  108 us
    all_gather x1, waiting for transfers between devices, on_device(): leaving_grad = lax.all_gather(grad_back, 'head', axis=2, tiled=True)  107 us
  transfers between devices with their start and end apart: 27, of which 22 were waited for; matrix products, arithmetic and copies ran while one was open for 6% of the time, Pallas kernels for 0%

commit v1 on v0

--- a/solution.py
+++ b/solution.py
@@ -1,11 +1,16 @@
 import jax
 import jax.numpy as jnp
 from jax import lax
+from jax.experimental import pallas as pl
+from jax.experimental.pallas import tpu as pltpu
 from jax.sharding import PartitionSpec as P
 
 HEAD_DIM = 128
 TOP = 8
 SEQ = 2048
+MESH = pl.DeviceIdType.MESH
+bf16 = jnp.bfloat16
+f32 = jnp.float32
 
 
 EPSILON = 1e-05
@@ -41,6 +46,447 @@
     return jnp.concatenate(
         [first_half * cosine - second_half * turned, second_half * cosine + first_half * turned], -1
     )
+
+
+def place():
+    block = lax.axis_index("expert")
+    lane = lax.axis_index("head")
+    return block // 2, block % 2, lane // 2, lane % 2
+
+
+def device(z, y, x, core):
+    return (z * 2 + y, x * 2 + core)
+
+
+def greet(z, y, x, core):
+    barrier = pltpu.get_barrier_semaphore()
+
+    def signal(target):
+        pl.semaphore_signal(barrier, inc=1, device_id=target, device_id_type=MESH)
+
+    signal(device(z, 1 - y, x, core))
+    signal(device(z, y, 1 - x, core))
+    signal(device(z, y, x, 1 - core))
+
+    @pl.when(z > 0)
+    def _():
+        signal(device(z - 1, y, x, core))
+
+    @pl.when(z < 3)
+    def _():
+        signal(device(z + 1, y, x, core))
+
+    pl.semaphore_wait(barrier, 3 + (z > 0).astype(jnp.int32) + (z < 3).astype(jnp.int32))
+
+
+def gather_kernel(own, whole, local_sem, send, recv):
+    z, y, x, core = place()
+    rows = own.shape[0]
+    eighth = rows // 8
+    me = z * 2 + y
+    slab = pl.ds(pl.multiple_of(core * 4 * eighth + x * eighth, eighth), 3 * eighth)
+    mine = pl.ds(pl.multiple_of(core * 4 * eighth + x * 3 * eighth, eighth), eighth)
+    theirs = pl.ds(pl.multiple_of(core * 4 * eighth + (1 - x) * 3 * eighth, eighth), eighth)
+    UP, DOWN, Y, X, CORE, CORE_X = range(6)
+
+    def copy(kind, block, part, target, from_own=False):
+        source = own.at[part] if from_own else whole.at[block, part]
+        return pltpu.make_async_remote_copy(
+            src_ref=source, dst_ref=whole.at[block, part],
+            send_sem=send.at[kind, block], recv_sem=recv.at[kind, block],
+            device_id=target, device_id_type=MESH)
+
+    up = lambda b, o=False: copy(UP, b, slab, device(z + 1, y, x, core), o)
+    down = lambda b, o=False: copy(DOWN, b, slab, device(z - 1, y, x, core), o)
+    over = lambda b, o=False: copy(Y, b, slab, device(z, 1 - y, x, core), o)
+    side = lambda b: copy(X, b, mine, device(z, y, 1 - x, core))
+    twin = lambda b: copy(CORE, b, slab, device(z, y, x, 1 - core))
+    twin_x = lambda b: copy(CORE_X, b, theirs, device(z, y, x, 1 - core))
+
+    greet(z, y, x, core)
+    keep = pltpu.make_async_copy(own, whole.at[me], local_sem)
+    keep.start()
+
+    @pl.when(z < 3)
+    def _():
+        up(me, True).start()
+
+    @pl.when(z > 0)
+    def _():
+        down(me, True).start()
+
+    over(me, True).start()
+
+    def spread(b):
+        side(b).start()
+        twin(b).start()
+
+    def from_y(zb):
+        b = zb * 2 + 1 - y
+        over(b).wait_recv()
+        spread(b)
+
+    for d in range(1, 4):
+        @pl.when(z >= d)
+        def _():
+            b = (z - d) * 2 + y
+            up(b).wait_recv()
+
+            @pl.when(z < 3)
+            def _():
+                up(b).start()
+            over(b).start()
+            spread(b)
+
+        @pl.when(z + d <= 3)
+        def _():
+            b = (z + d) * 2 + y
+            down(b).wait_recv()
+
+            @pl.when(z > 0)
+            def _():
+                down(b).start()
+            over(b).start()
+            spread(b)
+
+        if d == 1:
+            from_y(z)
+        else:
+            @pl.when(z >= d - 1)
+            def _():
+                from_y(z - (d - 1))
+
+            @pl.when(z + d - 1 <= 3)
+            def _():
+                from_y(z + d - 1)
+
+    @pl.when(z >= 3)
+    def _():
+        from_y(z - 3)
+
+    @pl.when(z <= 0)
+    def _():
+        from_y(z + 3)
+
+    for d in range(0, 4):
+        def through(zb):
+            for yb in (y, 1 - y):
+                b = zb * 2 + yb
+
+                def move():
+                    side_in = copy(X, b, theirs, device(z, y, 1 - x, core))
+                    side_in.wait_recv()
+                    twin_x(b).start()
+                if d == 0 and yb is y:
+                    continue
+                move()
+        if d == 0:
+            through(z)
+        else:
+            @pl.when(z >= d)
+            def _():
+                through(z - d)
+
+            @pl.when(z + d <= 3)
+            def _():
+                through(z + d)
+
+    other = pl.ds(pl.multiple_of((1 - core) * 4 * eighth + x * eighth, eighth), 3 * eighth)
+    other_x = pl.ds(pl.multiple_of((1 - core) * 4 * eighth + (1 - x) * 3 * eighth, eighth), eighth)
+    for b in range(8):
+        zb, yb = b // 2, b % 2
+
+        @pl.when(me != b)
+        def _():
+            copy(CORE, b, other, device(z, y, x, 1 - core)).wait_recv()
+            copy(CORE_X, b, other_x, device(z, y, x, 1 - core)).wait_recv()
+            side(b).wait_send()
+            twin(b).wait_send()
+            twin_x(b).wait_send()
+
+        @pl.when(yb == y)
+        def _():
+            over(b).wait_send()
+
+        @pl.when((yb == y) & (zb <= z) & (z < 3))
+        def _():
+            up(b).wait_send()
+
+        @pl.when((yb == y) & (zb >= z) & (z > 0))
+        def _():
+            down(b).wait_send()
+    keep.wait()
+
+
+def gather_all(own, number):
+    rows, width = own.shape
+    return pl.pallas_call(
+        gather_kernel,
+        out_shape=jax.ShapeDtypeStruct((8, rows, width), own.dtype),
+        in_specs=[pl.BlockSpec(memory_space=pl.ANY)],
+        out_specs=pl.BlockSpec(memory_space=pl.ANY),
+        scratch_shapes=[pltpu.SemaphoreType.DMA, pltpu.SemaphoreType.DMA((6, 8)), pltpu.SemaphoreType.DMA((6, 8))],
+        compiler_params=pltpu.CompilerParams(collective_id=number, has_side_effects=True),
+    )(own)
+
+
+def add_rows(target, source, rows):
+    step = 16
+
+    @pl.loop(0, rows // step)
+    def _(i):
+        part = pl.ds(pl.multiple_of(i * step, step), step)
+        target[part] = (target[part].astype(f32) + source[part].astype(f32)).astype(bf16)
+
+
+def scatter_kernel(parts, total, held, from_core, from_x, from_y, from_below, from_above, shared_in,
+                   load_sem, send, recv, end_send, end_recv):
+    z, y, x, core = place()
+    half = parts.shape[1] // 2
+    piece = half // 4
+    me = z * 2 + y
+    ahead = z // 2
+    order = (3 - 3 * ahead, 2 - ahead, z + 1 - 2 * (z % 2), z)
+    my_half = pl.ds(pl.multiple_of(core * half, half), half)
+    other_half = pl.ds(pl.multiple_of((1 - core) * half, half), half)
+    slab = pl.ds(pl.multiple_of(x * piece, piece), 3 * piece)
+    mine = pl.ds(pl.multiple_of(x * 3 * piece, piece), piece)
+    theirs = pl.ds(pl.multiple_of((1 - x) * 3 * piece, piece), piece)
+    shared = pl.ds(piece, 2 * piece)
+    CORE, X, Y, UP, DOWN = range(5)
+
+    def remote(kind, number, source, target, where):
+        return pltpu.make_async_remote_copy(
+            src_ref=source, dst_ref=target, send_sem=send.at[kind, number],
+            recv_sem=recv.at[kind, number], device_id=where, device_id_type=MESH)
+
+    def load(b):
+        return pltpu.make_async_copy(parts.at[b, my_half], held.at[b], load_sem.at[b])
+
+    def to_core(b):
+        return remote(CORE, b, parts.at[b, other_half], from_core.at[b], device(z, y, x, 1 - core))
+
+    def to_x(b):
+        return remote(X, b, held.at[b, theirs], from_x.at[b], device(z, y, 1 - x, core))
+
+    def to_y(zb):
+        return remote(Y, zb, held.at[zb * 2 + 1 - y, slab], from_y.at[zb], device(z, 1 - y, x, core))
+
+    def to_above(zb):
+        return remote(UP, zb, held.at[zb * 2 + y, slab], from_below.at[zb], device(z + 1, y, x, core))
+
+    def to_below(zb):
+        return remote(DOWN, zb, held.at[zb * 2 + y, slab], from_above.at[zb], device(z - 1, y, x, core))
+
+    greet(z, y, x, core)
+    for zb in order:
+        for yb in (1 - y, y):
+            load(zb * 2 + yb).start()
+            to_core(zb * 2 + yb).start()
+
+    def stage_core(zb, yb):
+        b = zb * 2 + yb
+        load(b).wait()
+        to_core(b).wait_recv()
+        add_rows(held.at[b], from_core.at[b], half)
+        to_x(b).start()
+
+    def stage_x(zb, yb):
+        b = zb * 2 + yb
+        to_x(b).wait_recv()
+        add_rows(held.at[b, mine], from_x.at[b], piece)
+
+    def stage_y(zb):
+        stage_x(zb, 1 - y)
+        to_y(zb).start()
+
+    def climb(zb):
+        @pl.when(z > 0)
+        def _():
+            to_above(zb).wait_recv()
+            add_rows(held.at[zb * 2 + y, slab], from_below.at[zb], 3 * piece)
+        to_above(zb).start()
+
+    def descend(zb):
+        @pl.when(z < 3)
+        def _():
+            to_below(zb).wait_recv()
+            add_rows(held.at[zb * 2 + y, slab], from_above.at[zb], 3 * piece)
+        to_below(zb).start()
+
+    def stage_z(i):
+        zb = order[i]
+        to_y(zb).wait_recv()
+        add_rows(held.at[zb * 2 + y, slab], from_y.at[zb], 3 * piece)
+        rises = (ahead == 0) if i < 2 else (z % 2 == 0)
+
+        @pl.when(rises)
+        def _():
+            climb(zb)
+
+        @pl.when(jnp.logical_not(rises))
+        def _():
+            descend(zb)
+
+    stage_core(order[0], 1 - y)
+    stage_core(order[0], y)
+    for i in range(4):
+        if i < 3:
+            stage_core(order[i + 1], 1 - y)
+        stage_y(order[i])
+        if i < 3:
+            stage_core(order[i + 1], y)
+        stage_x(order[i], y)
+        if i > 0:
+            stage_z(i - 1)
+
+    own = held.at[me]
+    to_y(z).wait_recv()
+    add_rows(own.at[slab], from_y.at[z], 3 * piece)
+
+    @pl.when(z > 0)
+    def _():
+        to_above(z).wait_recv()
+        add_rows(own.at[slab], from_below.at[z], 3 * piece)
+
+    @pl.when(z < 3)
+    def _():
+        to_below(z).wait_recv()
+        add_rows(own.at[slab], from_above.at[z], 3 * piece)
+
+    def at_end(number, source, target, where):
+        return pltpu.make_async_remote_copy(
+            src_ref=source, dst_ref=target, send_sem=end_send.at[number],
+            recv_sem=end_recv.at[number], device_id=where, device_id_type=MESH)
+
+    base = core * half
+    out_mine = pl.ds(pl.multiple_of(base + x * 3 * piece, piece), piece)
+    out_theirs = pl.ds(pl.multiple_of(base + (1 - x) * 3 * piece, piece), piece)
+    sums = at_end(0, held.at[me, shared], shared_in, device(z, y, 1 - x, core))
+    ready = at_end(1, held.at[me, mine], total.at[out_mine], device(z, y, 1 - x, core))
+    sums.start()
+    ready.start()
+    total[out_mine] = held[me, mine]
+    sums.wait_recv()
+    out_shared = pl.ds(pl.multiple_of(base + piece, piece), 2 * piece)
+    total[out_shared] = (held[me, shared].astype(f32) + shared_in[...].astype(f32)).astype(bf16)
+    at_end(1, held.at[me, mine], total.at[out_theirs], device(z, y, 1 - x, core)).wait_recv()
+    finished = at_end(2, total.at[my_half], total.at[my_half], device(z, y, x, 1 - core))
+    finished.start()
+    at_end(2, total.at[my_half], total.at[other_half], device(z, y, x, 1 - core)).wait_recv()
+    sums.wait_send()
+    ready.wait_send()
+    finished.wait_send()
+
+    for b in range(8):
+        zb, yb = b // 2, b % 2
+        to_core(b).wait_send()
+        to_x(b).wait_send()
+        if yb == 0:
+            to_y(zb).wait_send()
+
+            @pl.when(zb > z)
+            def _():
+                to_above(zb).wait_send()
+
+            @pl.when(zb < z)
+            def _():
+                to_below(zb).wait_send()
+
+
+def scatter_sum(parts, number):
+    _, rows, width = parts.shape
+    half, piece = rows // 2, rows // 8
+    return pl.pallas_call(
+        scatter_kernel,
+        out_shape=jax.ShapeDtypeStruct((rows, width), bf16),
+        in_specs=[pl.BlockSpec(memory_space=pl.ANY)],
+        out_specs=pl.BlockSpec(memory_space=pltpu.VMEM),
+        scratch_shapes=[
+            pltpu.VMEM((8, half, width), bf16),
+            pltpu.VMEM((8, half, width), bf16),
+            pltpu.VMEM((8, piece, width), bf16),
+            pltpu.VMEM((4, 3 * piece, width), bf16),
+            pltpu.VMEM((4, 3 * piece, width), bf16),
+            pltpu.VMEM((4, 3 * piece, width), bf16),
+            pltpu.VMEM((2 * piece, width), bf16),
+            pltpu.SemaphoreType.DMA((8,)),
+            pltpu.SemaphoreType.DMA((5, 8)),
+            pltpu.SemaphoreType.DMA((5, 8)),
+            pltpu.SemaphoreType.DMA((3,)),
+            pltpu.SemaphoreType.DMA((3,)),
+        ],
+        compiler_params=pltpu.CompilerParams(collective_id=number, has_side_effects=True, vmem_limit_bytes=48 * 2**20),
+    )(parts)
+def dot(a,b): return jnp.dot(a,b,preferred_element_type=f32)
+def dot_nt(a,b): return lax.dot_general(a,b,(((1,),(1,)),((),())),preferred_element_type=f32)
+def dot_tn(a,b): return lax.dot_general(a,b,(((0,),(0,)),((),())),preferred_element_type=f32)
+
+def moe_kernel(first, x_ref, g_ref, mask_ref, wr_ref, wg_ref, wu_ref, wd_ref, hg_ref, da_ref, gg_ref, out_ref, gx_ref):
+    x = x_ref[...]
+    g = g_ref[...]
+    logits = dot(x, wr_ref[...])
+    mask = mask_ref[...] > 0
+    top = jnp.max(jnp.where(mask, logits, -jnp.inf), -1, keepdims=True)
+    raised = jnp.where(mask, jnp.exp(jnp.where(mask, logits - top, 0.0)), 0.0)
+    gates = raised / jnp.sum(raised, -1, keepdims=True)
+    lanes = lax.broadcasted_iota(jnp.int32, gates.shape, 1)
+    ff = wg_ref.shape[2]
+    gx = None
+    out = None
+    gg = jnp.zeros(gates.shape, f32)
+    for j in range(wg_ref.shape[0]):
+        here = lanes == first[0] + j
+        gate = jnp.sum(jnp.where(here, gates, 0.0), -1, keepdims=True)
+        ga = dot(x, wg_ref[j])
+        ua = dot(x, wu_ref[j])
+        gw = dot_nt(g, wd_ref[j])
+        s = 1.0 / (1.0 + jnp.exp(-ga))
+        silu = ga * s
+        h = (silu * ua).astype(bf16).astype(f32)
+        gg = gg + jnp.where(here, jnp.sum(h * gw, -1, keepdims=True), 0.0)
+        gh = gw * gate
+        hg = (h * gate).astype(bf16)
+        du = (gh * silu).astype(bf16)
+        dg = (gh * ua * s * (1.0 + ga * (1.0 - s))).astype(bf16)
+        hg_ref[:, j * ff:(j + 1) * ff] = hg
+        da_ref[:, 2 * j * ff:(2 * j + 1) * ff] = dg
+        da_ref[:, (2 * j + 1) * ff:(2 * j + 2) * ff] = du
+        o = dot(hg, wd_ref[j])
+        b = dot_nt(dg, wg_ref[j]) + dot_nt(du, wu_ref[j])
+        out = o if out is None else out + o
+        gx = b if gx is None else gx + b
+    gg_ref[...] = gg
+    out_ref[...] = out.astype(bf16)
+    gx_ref[...] = gx.astype(bf16)
+
+def moe(first, X, G, mask, wr, wg, wu, wd, bt=256):
+    T, D = X.shape
+    E = mask.shape[1]
+    J, _, F = wg.shape
+    blk = lambda w: pl.BlockSpec((bt, w), lambda i, s: (i, 0))
+    full = lambda *shp: pl.BlockSpec(shp, lambda i, s: (0,) * len(shp))
+    return pl.pallas_call(moe_kernel,
+        grid_spec=pltpu.PrefetchScalarGridSpec(num_scalar_prefetch=1, grid=(T // bt,),
+        in_specs=[blk(D), blk(D), blk(E), full(D, E), full(J, D, F), full(J, D, F), full(J, F, D)],
+        out_specs=[blk(J * F), blk(2 * J * F), blk(E), blk(D), blk(D)]),
+        out_shape=[jax.ShapeDtypeStruct((T, J * F), bf16), jax.ShapeDtypeStruct((T, 2 * J * F), bf16), jax.ShapeDtypeStruct((T, E), f32),
+                   jax.ShapeDtypeStruct((T, D), bf16), jax.ShapeDtypeStruct((T, D), bf16)],
+        compiler_params=pltpu.CompilerParams(vmem_limit_bytes=56 * 2**20),
+    )(first, X, G, mask, wr, wg, wu, wd)
+
+def tn_kernel(a_ref, b_ref, o_ref):
+    o_ref[...] = dot_tn(a_ref[...], b_ref[...])
+
+def tn(a, b, bm=256, bn=None, fuse=False):
+    T, M = a.shape
+    N = b.shape[1]
+    bn = bn or N
+    return pl.pallas_call(tn_kernel, grid=(M // bm, N // bn),
+        in_specs=[pl.BlockSpec((T, bm), lambda i, j: (0, i)), pl.BlockSpec((T, bn), lambda i, j: (0, j))],
+        out_specs=pl.BlockSpec((bm, bn), lambda i, j: (i, j)),
+        out_shape=jax.ShapeDtypeStruct((M, N), f32),
+        compiler_params=pltpu.CompilerParams(vmem_limit_bytes=56 * 2**20, fuse_transposed_lhs_in_matmul=fuse))(a, b)
 
 
 def on_device(
@@ -317,9 +763,235 @@
     )
 
 
+def on_device_dense(
+    hidden_in,
+    norm1_gain,
+    w_query,
+    w_key,
+    w_value,
+    w_out,
+    query_gain,
+    key_gain,
+    norm2_gain,
+    w_router,
+    w_gate,
+    w_up,
+    w_down,
+    routes,
+    segments,
+    cotangent,
+):
+    seq_len, width = hidden_in.shape
+    local_width = w_query.shape[1]
+    head_count = local_width // HEAD_DIM
+    expert_devs = lax.axis_size("expert")
+    local_experts = w_gate.shape[0]
+    expert_total = w_router.shape[1]
+    capacity = 2 * seq_len * TOP // expert_total
+    slab_rows = local_experts * capacity
+    my_index = lax.axis_index("expert")
+    group = SEQ // seq_len
+    rank = my_index % group
+    f32 = jnp.float32
+    bf16 = jnp.bfloat16
+
+    def split_heads(values):
+        return values.reshape(seq_len, head_count, HEAD_DIM)
+
+    inputs = hidden_in.astype(f32)
+    inverse_attn = inverse_rms(inputs)
+    normed_attn = inputs * inverse_attn
+    attn_input = (normed_attn * norm1_gain).astype(bf16)
+    q_raw = split_heads(jnp.dot(attn_input, w_query, preferred_element_type=f32))
+    k_raw = split_heads(jnp.dot(attn_input, w_key, preferred_element_type=f32))
+    v_heads = split_heads(jnp.dot(attn_input, w_value, preferred_element_type=f32).astype(bf16))
+    q_gains = query_gain.reshape(head_count, HEAD_DIM)
+    k_gains = key_gain.reshape(head_count, HEAD_DIM)
+    q_inverse = inverse_rms(q_raw)
+    q_normed = q_raw * q_inverse
+    k_inverse = inverse_rms(k_raw)
+    k_normed = k_raw * k_inverse
+    local_places = lax.iota(jnp.int32, seq_len)
+    query_places = rank * seq_len + local_places
+    cosine, sine_part = rope_tables(query_places.astype(f32), HEAD_DIM // 2)
+    queries = rotate(q_normed * q_gains, cosine, sine_part, 1.0).astype(bf16)
+    key_rot = rotate(k_normed * k_gains, cosine, sine_part, 1.0).astype(bf16)
+    score_scale = HEAD_DIM ** (-0.5)
+    keys_values = jnp.stack([key_rot, v_heads])
+    pieces = [keys_values]
+    for offset in range(1, group):
+        keys_values = from_behind(keys_values, "expert", 1)
+        pieces.append(keys_values)
+    stacked = jnp.stack(pieces, 1).reshape(2, group * seq_len, head_count, HEAD_DIM)
+    keys_all = stacked[0]
+    values_all = stacked[1]
+    query_segs = lax.dynamic_slice_in_dim(segments, my_index * seq_len, seq_len, 0)
+    key_segs = jnp.concatenate(
+        [
+            lax.dynamic_slice_in_dim(
+                segments, jnp.maximum(my_index - offset, 0) * seq_len, seq_len, 0
+            )
+            for offset in range(group)
+        ],
+        0,
+    )
+    offsets = lax.iota(jnp.int32, group)
+    key_places = ((rank - offsets)[:, None] * seq_len + local_places[None, :]).reshape(-1)
+    key_valid = jnp.repeat(rank - offsets >= 0, seq_len)
+    allowed = (
+        key_valid[None, :]
+        & (query_places[:, None] >= key_places[None, :])
+        & (query_segs[:, None] == key_segs[None, :])
+    )
+
+    def scores_of():
+        raw_scores = (
+            jnp.einsum("thd,shd->hts", queries, keys_all, preferred_element_type=f32) * score_scale
+        )
+        return jnp.where(allowed[None], raw_scores, MASKED)
+
+    scores = scores_of()
+    row_max = jnp.max(scores, -1, keepdims=True)
+    raised = jnp.exp(scores - row_max)
+    exp_total = jnp.sum(raised, -1, keepdims=True)
+    log_total = row_max + jnp.log(exp_total)
+    attn_probs = (raised / exp_total).astype(bf16)
+    context = (
+        jnp.einsum("hts,shd->thd", attn_probs, values_all, preferred_element_type=f32)
+        .reshape(seq_len, local_width)
+        .astype(bf16)
+    )
+    attn_part = jnp.dot(context, w_out, preferred_element_type=f32)
+    middle = inputs + lax.psum(attn_part, "head")
+    inverse_moe = inverse_rms(middle)
+    normed_moe = middle * inverse_moe
+    moe_input = (normed_moe * norm2_gain).astype(bf16)
+    everyone = gather_all(moe_input, 1).reshape(expert_devs * seq_len, width)
+    all_grads = gather_all(cotangent, 2).reshape(expert_devs * seq_len, width)
+    all_routes = lax.all_gather(routes, "expert", axis=0, tiled=True)
+    catalog = lax.iota(jnp.int32, expert_total)
+    mask = jnp.sum((all_routes[:, :, None] == catalog).astype(f32), 1)
+    first = jnp.full((1,), local_experts, jnp.int32) * my_index
+    weighted, grad_acts, grad_gates, out_part, grad_part = moe(
+        first, everyone, all_grads, mask, w_router, w_gate, w_up, w_down
+    )
+    ff = w_gate.shape[2]
+    grad_down = tn(weighted, all_grads, 512, 512).reshape(local_experts, ff, width)
+    acts = tn(everyone, grad_acts, 512, 1024).reshape(width, local_experts, 2, ff)
+    grad_gate = acts[:, :, 0].transpose(1, 0, 2)
+    grad_up = acts[:, :, 1].transpose(1, 0, 2)
+    shape = (expert_devs, seq_len, width)
+    moe_out = scatter_sum(out_part.reshape(shape), 3)
+    home = scatter_sum(grad_part.reshape(shape), 4)
+    output = (middle + moe_out.astype(f32)).astype(bf16)
+    grad_final = cotangent.astype(f32)
+    grad_gates = lax.psum(grad_gates, ("expert", "head"))
+    grad_gates = lax.dynamic_slice_in_dim(grad_gates, my_index * seq_len, seq_len, 0)
+    own_mask = lax.dynamic_slice_in_dim(mask, my_index * seq_len, seq_len, 0) > 0
+    logits = jnp.where(own_mask, jnp.dot(moe_input, w_router, preferred_element_type=f32), -jnp.inf)
+    raised_gate = jnp.exp(logits - jnp.max(logits, -1, keepdims=True))
+    gate_weights = raised_gate / jnp.sum(raised_gate, -1, keepdims=True)
+    grad_logits = (
+        gate_weights * (grad_gates - jnp.sum(grad_gates * gate_weights, -1, keepdims=True))
+    ).astype(bf16)
+    grad_router = jnp.dot(moe_input.T, grad_logits, preferred_element_type=f32)
+    grad_moe_input = jnp.dot(grad_logits, w_router.T, preferred_element_type=f32) + home.astype(f32)
+    grad_norm2 = jnp.sum(grad_moe_input * normed_moe, 0)
+    grad_middle = grad_final + norm_back(grad_moe_input * norm2_gain, normed_moe, inverse_moe)
+    grad_attn = grad_middle.astype(bf16)
+    grad_out_turned = jnp.dot(grad_attn.T, context, preferred_element_type=f32)
+    grad_context = split_heads(jnp.dot(grad_attn, w_out.T, preferred_element_type=f32).astype(bf16))
+    attn_full = jnp.exp(scores_of() - log_total)
+    attn_low = attn_full.astype(bf16)
+    grad_values_all = jnp.einsum("hts,thd->shd", attn_low, grad_context, preferred_element_type=f32)
+    grad_probs = jnp.einsum("thd,shd->hts", grad_context, values_all, preferred_element_type=f32)
+    grad_scores = (
+        attn_full * (grad_probs - jnp.sum(grad_probs * attn_full, -1, keepdims=True))
+    ).astype(bf16)
+    grad_queries = (
+        jnp.einsum("hts,shd->thd", grad_scores, keys_all, preferred_element_type=f32) * score_scale
+    )
+    grad_keys_all = (
+        jnp.einsum("hts,thd->shd", grad_scores, queries, preferred_element_type=f32) * score_scale
+    )
+    kv_terms = jnp.stack([grad_keys_all, grad_values_all]).reshape(
+        2, group, seq_len, head_count, HEAD_DIM
+    )
+    kv_total = kv_terms[:, 0]
+    for offset in range(1, group):
+        kv_total = kv_total + from_behind(
+            kv_terms[:, offset].astype(jnp.bfloat16), "expert", -offset
+        ).astype(jnp.float32)
+    grad_keys = kv_total[0]
+    grad_values = kv_total[1]
+    grad_q_normed = rotate(grad_queries, cosine, sine_part, -1.0)
+    grad_k_normed = rotate(grad_keys, cosine, sine_part, -1.0)
+    grad_query_gain = jnp.sum(grad_q_normed * q_normed, 0).reshape(local_width)
+    grad_key_gain = jnp.sum(grad_k_normed * k_normed, 0).reshape(local_width)
+    grad_q_raw = (
+        norm_back(grad_q_normed * q_gains, q_normed, q_inverse)
+        .reshape(seq_len, local_width)
+        .astype(bf16)
+    )
+    grad_k_raw = (
+        norm_back(grad_k_normed * k_gains, k_normed, k_inverse)
+        .reshape(seq_len, local_width)
+        .astype(bf16)
+    )
+    grad_v_raw = grad_values.reshape(seq_len, local_width).astype(bf16)
+    grad_query = jnp.dot(attn_input.T, grad_q_raw, preferred_element_type=f32)
+    grad_key = jnp.dot(attn_input.T, grad_k_raw, preferred_element_type=f32)
+    grad_value = jnp.dot(attn_input.T, grad_v_raw, preferred_element_type=f32)
+    input_part = jnp.dot(grad_q_raw, w_query.T, preferred_element_type=f32)
+    input_part = input_part + jnp.dot(grad_k_raw, w_key.T, preferred_element_type=f32)
+    input_part = input_part + jnp.dot(grad_v_raw, w_value.T, preferred_element_type=f32)
+    grad_attn_input = lax.psum(input_part.astype(jnp.bfloat16), "head").astype(jnp.float32)
+    grad_norm1 = jnp.sum(grad_attn_input * normed_attn, 0)
+    grad_input = grad_middle + norm_back(grad_attn_input * norm1_gain, normed_attn, inverse_attn)
+    grad_query, grad_key, grad_value, grad_out_turned = (
+        lax.psum_scatter(
+            grad_query.astype(jnp.bfloat16), "expert", scatter_dimension=0, tiled=True
+        ).astype(jnp.float32),
+        lax.psum_scatter(
+            grad_key.astype(jnp.bfloat16), "expert", scatter_dimension=0, tiled=True
+        ).astype(jnp.float32),
+        lax.psum_scatter(
+            grad_value.astype(jnp.bfloat16), "expert", scatter_dimension=0, tiled=True
+        ).astype(jnp.float32),
+        lax.psum_scatter(
+            grad_out_turned.astype(jnp.bfloat16), "expert", scatter_dimension=0, tiled=True
+        ).astype(jnp.float32),
+    )
+    grad_router, grad_norm1, grad_norm2, grad_query_gain, grad_key_gain = (
+        lax.psum(grad_router.astype(jnp.bfloat16), "expert").astype(jnp.float32),
+        lax.psum(grad_norm1.astype(jnp.bfloat16), "expert").astype(jnp.float32),
+        lax.psum(grad_norm2.astype(jnp.bfloat16), "expert").astype(jnp.float32),
+        lax.psum(grad_query_gain.astype(jnp.bfloat16), "expert").astype(jnp.float32),
+        lax.psum(grad_key_gain.astype(jnp.bfloat16), "expert").astype(jnp.float32),
+    )
+    return (
+        output,
+        grad_input,
+        grad_norm1,
+        grad_query,
+        grad_key,
+        grad_value,
+        grad_out_turned.T,
+        grad_query_gain,
+        grad_key_gain,
+        grad_norm2,
+        grad_router,
+        grad_gate,
+        grad_up,
+        grad_down,
+    )
+
+
 def solution(mesh):
+    experts, heads = mesh.shape["expert"], mesh.shape["head"]
+    form = on_device_dense if (experts, heads) == (8, 4) else on_device
     return jax.shard_map(
-        on_device,
+        form,
         mesh=mesh,
         in_specs=(
             P("expert", None),

time: 2880 us -> 1030 us (0.36)
  waiting for transfers between devices: 1550 us -> 408 us
  blocking collectives: 777 us -> 75.4 us
  Pallas kernels: 0 us -> 288 us
  matrix products: 184 us -> 56.6 us
  local copies, waits for them, and re-layouts: 201 us -> 78.5 us
  other arithmetic: 94.3 us -> 52.7 us
    all_to_all x2 -> x0, blocking collectives: 741 us -> none  [the longest x1 371 us: on_device(): lax.all_to_all(outgoing, 'expert', split_axis=0, concat_axis=0, tiled=True)]
    all_to_all x2 -> x0, waiting for transfers between devices: 699 us -> none  [the longest x1 356 us: on_device(): lax.all_to_all(leaving_grad, 'expert', split_axis=0, concat_axis=0, tiled...]
    pallas_call x0 -> x7, Pallas kernels: none -> 288 us  [the longest x2 120 us: scatter_sum(): pl.pallas_call(scatter_kernel, out_shape=jax.ShapeDtypeStruct((rows, widt...]
    reduce_scatter x6 -> x4, waiting for transfers between devices: 478 us -> 225 us  [the longest x1 69.1 us: on_device_dense(): lax.psum_scatter(grad_value.astype(jnp.bfloat16), 'expert', scatter_dimen...]
    all_gather x2 -> x0, waiting for transfers between devices: 215 us -> none  [the longest x1 108 us: on_device(): leaving = lax.all_gather(rows_out, 'head', axis=2, tiled=True)]
    dot_general x31 -> x20, matrix products: 182 us -> 54.5 us  [the longest x1 7.15 us: on_device_dense(): jnp.einsum('hts,thd->shd', attn_low, grad_context, preferred_element_type...]
    gather x11 -> x0, local copies, waits for them, and re-layouts: 101 us -> none  [the longest x1 24.7 us: on_device(): grad_home.reshape(expert_total * capacity, width)[position]]
    all_gather x0 -> x1, blocking collectives: none -> 30.6 us  [on_device_dense(): all_routes = lax.all_gather(routes, 'expert', axis=0, tiled=True)]
  transfers between devices with their start and end apart: 27 -> 22, of which waited for: 22 -> 16; matrix products, arithmetic and copies ran while one was open for 6% -> 8% of each run, Pallas kernels for 0% -> 13%
where the time goes in v1:
time: 1030 us; the launch traced here: 1020 us
  waiting for transfers between devices  408 us (40%)
  Pallas kernels  288 us (28%)
  local copies, waits for them, and re-layouts  78.5 us (8%)
  blocking collectives  75.4 us (7%)
  matrix products  56.6 us (5%)
  other arithmetic  52.7 us (5%)
  starting transfers between devices  47.4 us (5%)
  between operations  15.3 us (1%)
    pallas_call x2, Pallas kernels, scatter_sum(): pl.pallas_call(scatter_kernel, out_shape=jax.ShapeDtypeStruct((rows, widt...  120 us
    ppermute x14, waiting for transfers between devices, from_behind(): return lax.ppermute(shard, axis, pairs)  97.2 us
    pallas_call x2, Pallas kernels, gather_all(): pl.pallas_call(gather_kernel, out_shape=jax.ShapeDtypeStruct((8, rows, wi...  95.3 us
    reduce_scatter x1, waiting for transfers between devices, on_device_dense(): lax.psum_scatter(grad_value.astype(jnp.bfloat16), 'expert', scatter_dimen...  69.1 us
    reduce_scatter x1, waiting for transfers between devices, on_device_dense(): lax.psum_scatter(grad_key.astype(jnp.bfloat16), 'expert', scatter_dimensi...  68.9 us
    reduce_scatter x1, waiting for transfers between devices, on_device_dense(): lax.psum_scatter(grad_query.astype(jnp.bfloat16), 'expert', scatter_dimen...  68.7 us
    psum x1, waiting for transfers between devices, on_device_dense(): grad_gates = lax.psum(grad_gates, ('expert', 'head'))  64.4 us
    pallas_call x1, Pallas kernels, moe(): pl.pallas_call(moe_kernel, grid_spec=pltpu.PrefetchScalarGridSpec(num_sca...  49.5 us
  transfers between devices with their start and end apart: 22, of which 16 were waited for; matrix products, arithmetic and copies ran while one was open for 8% of the time, Pallas kernels for 13%

profile of v1, /device:TPU:0, one launch (start us, length us, event | category | flops | bytes accessed | tf_op | source)
XLA Modules:
  0.0 1022.0 jit_solution(9271536840627669104)
XLA Ops:
  9.0 3.5 convolution_convert_fusion.6
  14.2 3.1 fusion.59
  17.3 2.0 reshape.378
  20.8 3.1 fusion.56
  24.0 2.0 reshape.379
  32.5 5.6 collective-permute-start
  38.2 10.4 %collective-permute-done = bf16[2,256,4,128]{3,1,2,0:T(8,128)(2,1)} collective-permute-done((bf16[2,256,4,128]{3,1,2,0:T(8,128)(2,1)S(1)}, bf16[2,256,4,128]{3,1,2,0:T(8,128)(2,1)}, u32[]{:S(2)}, u32[]{:S(2)}) %collective-permute-start) | collective-permute-done | bytes 524320 | tf_op jit(solution)/shard_map/ppermute | solution.py:24
  48.6 5.3 collective-permute-start.1
  53.9 9.8 collective-permute-done.1
  63.6 5.2 collective-permute-start.2
  69.2 8.5 collective-permute-done.2
  77.7 5.2 collective-permute-start.3
  83.4 8.3 collective-permute-done.3
  91.7 5.3 collective-permute-start.4
  97.7 6.7 collective-permute-done.4
  104.5 5.2 collective-permute-start.5
  116.5 5.8 collective-permute-start.6
  124.8 3.9 collective-permute-done.6
  129.6 2.5 fusion.62
  133.4 2.1 fusion.64
  136.8 2.0 copy-done.4
  138.7 2.3 fusion.22
  141.8 2.1 fusion.66
  143.9 50.3 %shard_map.264 = bf16[8,256,2048]{2,1,0:T(8,128)(2,1)} custom-call(bf16[256,2048]{1,0:T(8,128)(2,1)} %own.1), custom_call_target="tpu_custom_call" | custom-call | tf_op jit(solution)/shard_map/pallas_call | solution.py:223
  194.3 30.6 %all_gather.3 = s32[2048,8]{0,1:T(8,128)S(1)} all-gather(s32[256,8]{0,1:T(8,128)S(1)} %copy-done.61), channel_id=1, replica_groups=mesh['expert'=8,'head'=4] {'expert'}, dimensions={0}, use_global_device_ids=true | all-gather | bytes 73728 | tf_op jit(solution)/shard_map/all_gather | solution.py:871
  228.8 2.0 multiply_reduce_fusion.3
  233.3 45.0 %shard_map.263 = bf16[8,256,2048]{2,1,0:T(8,128)(2,1)} custom-call(bf16[256,2048]{1,0:T(8,128)(2,1)} %multiply_convert_fusion.1.own), custom_call_target="tpu_custom_call" | custom-call | tf_op jit(solution)/shard_map/pallas_call | solution.py:223
  278.3 2.0 fusion.65
  280.3 49.5 %shard_map.265 = (bf16[2048,512]{1,0:T(8,128)(2,1)}, bf16[2048,1024]{1,0:T(8,128)(2,1)}, f32[2048,16]{1,0:T(8,128)}, bf16[2048,2048]{1,0:T(8,128)(2,1)}, bf16[2048,2048]{1,0:T(8,128)(2,1)}) custom-call(s32[1]{0:T(128)} %bitcast.16.first, bf16[2048,2048]{1,0:T(8,128)(2,1)} %bitcast.194, bf16[2048,2048]{1,0:T(8,128)(2,1)} %bitcast.192, ...), custom_call_target="tpu_custom_call" | custom-call | tf_op jit(solution)/shard_map/pallas_call | solution.py:469
  329.8 57.6 %shard_map.267 = bf16[256,2048]{1,0:T(8,128)(2,1)S(1)} custom-call(bf16[8,256,2048]{2,1,0:T(8,128)(2,1)} %bitcast.203), custom_call_target="tpu_custom_call" | custom-call | tf_op jit(solution)/shard_map/pallas_call | solution.py:400
  387.5 62.1 %shard_map.266 = bf16[256,2048]{1,0:T(8,128)(2,1)S(1)} custom-call(bf16[8,256,2048]{2,1,0:T(8,128)(2,1)} %bitcast.202), custom_call_target="tpu_custom_call" | custom-call | tf_op jit(solution)/shard_map/pallas_call | solution.py:400
  451.3 64.4 %all-reduce.8.cloned.1.call-done = f32[2048,16]{1,0:T(8,128)} async-done(((f32[2048,16]{1,0:T(8,128)}), f32[2048,16]{1,0:T(8,128)}) %all-reduce.8.cloned.1.call-update) | async-done | bytes 131088 | tf_op jit(solution)/shard_map/psum | solution.py:888
  516.9 3.3 multiply_reduce_fusion.1
  524.3 7.2 fusion.6
  531.4 6.5 multiply_reduce_fusion
  538.0 5.3 copy.195
  543.3 6.8 multiply_convert_fusion
  550.1 2.0 copy-done.13
  552.2 3.0 multiply_bitcast_fusion
  555.2 5.4 copy.193
  560.6 4.8 slice_bitcast_fusion.8
  572.8 12.5 %collective-permute-done.13 = bf16[2,256,4,128]{3,1,2,0:T(8,128)(2,1)} collective-permute-done((bf16[2,256,4,128]{3,1,2,0:T(8,128)(2,1)}, bf16[2,256,4,128]{3,1,2,0:T(8,128)(2,1)}, u32[]{:S(2)}, u32[]{:S(2)}) %collective-permute-start.13) | collective-permute-done | bytes 524320 | tf_op jit(solution)/shard_map/ppermute | solution.py:24
  588.0 2.0 convolution_convert_fusion.4
  590.2 3.6 fusion.21
  593.8 35.4 %collective-permute-done.11 = bf16[2,256,4,128]{3,1,2,0:T(8,128)(2,1)} collective-permute-done((bf16[2,256,4,128]{3,1,2,0:T(8,128)(2,1)}, bf16[2,256,4,128]{3,1,2,0:T(8,128)(2,1)}, u32[]{:S(2)}, u32[]{:S(2)}) %collective-permute-start.11) | collective-permute-done | bytes 524320 | tf_op jit(solution)/shard_map/ppermute | solution.py:24
  629.6 2.6 fusion.29
  646.2 2.1 convolution_convert_fusion
  649.7 2.2 convolution_convert_fusion.3
  652.0 2.2 convolution_convert_fusion.2
  654.4 2.2 convolution_convert_fusion.1
  656.7 13.7 %shard_map.268 = f32[2048,1024]{1,0:T(8,128)} custom-call(bf16[2048,2048]{1,0:T(8,128)(2,1)} %bitcast.195, bf16[2048,1024]{1,0:T(8,128)(2,1)} %get-tuple-element.22.b_ref), custom_call_target="tpu_custom_call" | custom-call | tf_op jit(solution)/shard_map/pallas_call | solution.py:485
  670.4 11.7 %reshape.385 = f32[2048,2,2,256]{3,2,1,0:T(2,128)} reshape(f32[2048,1024]{1,0:T(8,128)} %shard_map.268) | data formatting | bytes 16777216 | tf_op jit(solution)/shard_map/reshape | solution.py:880
  682.1 9.9 fusion.61
  692.0 2.3 copy.253
  694.4 2.3 copy.252
  696.7 9.4 shard_map.269
  707.6 21.3 %all-reduce.10.cloned.1.call-done = bf16[256,2048]{1,0:T(8,128)(2,1)} async-done(((bf16[256,2048]{1,0:T(8,128)(2,1)}), bf16[256,2048]{1,0:T(8,128)(2,1)}) %all-reduce.10.cloned.1.call-update) | async-done | bytes 1048592 | tf_op jit(solution)/shard_map/psum | solution.py:948
  728.9 2.0 fusion.19
  730.9 44.7 %all-reduce = (bf16[2048]{0:T(1024)(128)(2,1)S(1)}, bf16[512]{0:T(512)(128)(2,1)S(1)}, bf16[512]{0:T(512)(128)(2,1)S(1)}, bf16[2048]{0:T(1024)(128)(2,1)S(1)}) all-reduce(bf16[2048]{0:T(1024)(128)(2,1)S(1)} %get-tuple-element.110, bf16[512]{0:T(512)(128)(2,1)S(1)} %get-tuple-element.135, ...), channel_id=1, replica_groups=mesh['expert'=8,'head'=4] {'expert'}, use_global_device_ids=true, to_apply=%region_19.20 | all-reduce | flops 5120 | bytes 20480 | tf_op jit(solution)/shard_map/psum | solution.py:967
  778.0 4.0 fusion.16
  782.0 18.8 %reduce-scatter.11.cloned.1.call-done = bf16[256,512]{1,0:T(8,128)(2,1)} async-done(((bf16[2048,512]{1,0:T(8,128)(2,1)}), bf16[256,512]{1,0:T(8,128)(2,1)}) %reduce-scatter.11.cloned.1.call-update) | async-done | bytes 262160 | tf_op jit(solution)/shard_map/reduce_scatter | solution.py:961
  802.8 68.7 %reduce-scatter.5.cloned.1.call-done = bf16[256,512]{1,0:T(8,128)(2,1)} async-done(((bf16[2048,512]{1,0:T(8,128)(2,1)}), bf16[256,512]{1,0:T(8,128)(2,1)}) %reduce-scatter.5.cloned.1.call-update) | async-done | bytes 262160 | tf_op jit(solution)/shard_map/reduce_scatter | solution.py:952
  873.3 68.9 %reduce-scatter.7.cloned.1.call-done = bf16[256,512]{1,0:T(8,128)(2,1)} async-done(((bf16[2048,512]{1,0:T(8,128)(2,1)}), bf16[256,512]{1,0:T(8,128)(2,1)}) %reduce-scatter.7.cloned.1.call-update) | async-done | bytes 262160 | tf_op jit(solution)/shard_map/reduce_scatter | solution.py:955
  944.0 69.1 %reduce-scatter.9.cloned.1.call-done = bf16[256,512]{1,0:T(8,128)(2,1)} async-done(((bf16[2048,512]{1,0:T(8,128)(2,1)}), bf16[256,512]{1,0:T(8,128)(2,1)}) %reduce-scatter.9.cloned.1.call-update) | async-done | bytes 262160 | tf_op jit(solution)/shard_map/reduce_scatter | solution.py:958
  (243 shorter events, 77.0 us)
Async XLA Ops:
  7.2 134.6 %copy-start = (bf16[512,2048]{1,0:T(8,128)(2,1)S(1)}, bf16[512,2048]{1,0:T(8,128)(2,1)}, u32[]{:S(2)}) copy-start(bf16[512,2048]{1,0:T(8,128)(2,1)} %param.21) | copy-start | bytes 6291460
  7.2 221.6 %all-reduce.6.cloned.1.call-start = ((), (), s32[]{:S(2)}) async-start(), calls=%async_computation.4 | async-start | bytes 4194304 | tf_op jit(solution)/shard_map/psum | solution.py:865
  8.9 11.9 %copy-start.52 = (f32[256]{0:T(256)}, f32[256]{0:T(256)S(1)}, u32[]{:S(2)}) copy-start(f32[256]{0:T(256)S(1)} %add_rsqrt_fusion.3) | copy-start | bytes 3076
  8.9 5.3 copy-start.11
  8.9 5.2 copy-start.41
  20.8 7.9 copy-start.44
  24.0 4.8 copy-start.48
  24.0 4.8 copy-start.50
  27.5 2.8 copy-start.46
  28.7 2.8 copy-start.30
  30.3 38.6 %copy-start.57 = (s32[2048]{0:T(1024)S(1)}, s32[2048]{0:T(1024)}, u32[]{:S(2)}) copy-start(s32[2048]{0:T(1024)} %param.30) | copy-start | bytes 24580
  32.5 16.0 %collective-permute-start = (bf16[2,256,4,128]{3,1,2,0:T(8,128)(2,1)S(1)}, bf16[2,256,4,128]{3,1,2,0:T(8,128)(2,1)}, u32[]{:S(2)}, u32[]{:S(2)}) collective-permute-start(bf16[2,256,4,128]{3,1,2,0:T(8,128)(2,1)S(1)} %get-tuple-element.119), channel_id=1, source_target_pairs={{0,4},{4,8},{8,12},{12,16},{16,20},{20,24},{24,28},{1,5},{5,9},{9,... | collective-permute-start | bytes 1572872 | tf_op jit(solution)/shard_map/ppermute | solution.py:24
  48.6 15.1 %collective-permute-start.1 = (bf16[2,256,4,128]{3,1,2,0:T(8,128)(2,1)}, bf16[2,256,4,128]{3,1,2,0:T(8,128)(2,1)}, u32[]{:S(2)}, u32[]{:S(2)}) collective-permute-start(bf16[2,256,4,128]{3,1,2,0:T(8,128)(2,1)} %collective-permute-done), channel_id=1, source_target_pairs={{0,4},{4,8},{8,12},{12,16},{16,20},{20,24},{24,28},{1,5},{5,9},{9,... | collective-permute-start | bytes 1572872 | tf_op jit(solution)/shard_map/ppermute | solution.py:24
  63.6 14.1 %collective-permute-start.2 = (bf16[2,256,4,128]{3,1,2,0:T(8,128)(2,1)}, bf16[2,256,4,128]{3,1,2,0:T(8,128)(2,1)}, u32[]{:S(2)}, u32[]{:S(2)}) collective-permute-start(bf16[2,256,4,128]{3,1,2,0:T(8,128)(2,1)} %collective-permute-done.1), channel_id=1, source_target_pairs={{0,4},{4,8},{8,12},{12,16},{16,20},{20,24},{24,28},{1,5},{5,9},{9,... | collective-permute-start | bytes 1572872 | tf_op jit(solution)/shard_map/ppermute | solution.py:24
  77.7 14.0 %collective-permute-start.3 = (bf16[2,256,4,128]{3,1,2,0:T(8,128)(2,1)}, bf16[2,256,4,128]{3,1,2,0:T(8,128)(2,1)S(1)}, u32[]{:S(2)}, u32[]{:S(2)}) collective-permute-start(bf16[2,256,4,128]{3,1,2,0:T(8,128)(2,1)} %collective-permute-done.2), channel_id=1, source_target_pairs={{0,4},{4,8},{8,12},{12,16},{16,20},{20,24},{24,28},{1,5},{5,9},{9,... | collective-permute-start | bytes 1572872 | tf_op jit(solution)/shard_map/ppermute | solution.py:24
  91.7 12.8 %collective-permute-start.4 = (bf16[2,256,4,128]{3,1,2,0:T(8,128)(2,1)S(1)}, bf16[2,256,4,128]{3,1,2,0:T(8,128)(2,1)S(1)}, u32[]{:S(2)}, u32[]{:S(2)}) collective-permute-start(bf16[2,256,4,128]{3,1,2,0:T(8,128)(2,1)S(1)} %collective-permute-done.3), channel_id=1, source_target_pairs={{0,4},{4,8},{8,12},{12,16},{16,20},{20,24},{24,28},{1,5},{5,9},{9,... | collective-permute-start | bytes 1572872 | tf_op jit(solution)/shard_map/ppermute | solution.py:24
  104.5 12.0 %collective-permute-start.5 = (bf16[2,256,4,128]{3,1,2,0:T(8,128)(2,1)S(1)}, bf16[2,256,4,128]{3,1,2,0:T(8,128)(2,1)S(1)}, u32[]{:S(2)}, u32[]{:S(2)}) collective-permute-start(bf16[2,256,4,128]{3,1,2,0:T(8,128)(2,1)S(1)} %collective-permute-done.4), channel_id=1, source_target_pairs={{0,4},{4,8},{8,12},{12,16},{16,20},{20,24},{24,28},{1,5},{5,9},{9,... | collective-permute-start | bytes 1572872 | tf_op jit(solution)/shard_map/ppermute | solution.py:24
  116.5 12.3 %collective-permute-start.6 = (bf16[2,256,4,128]{3,1,2,0:T(8,128)(2,1)S(1)}, bf16[2,256,4,128]{3,1,2,0:T(8,128)(2,1)S(1)}, u32[]{:S(2)}, u32[]{:S(2)}) collective-permute-start(bf16[2,256,4,128]{3,1,2,0:T(8,128)(2,1)S(1)} %collective-permute-done.5), channel_id=1, source_target_pairs={{0,4},{4,8},{8,12},{12,16},{16,20},{20,24},{24,28},{1,5},{5,9},{9,... | collective-permute-start | bytes 1572872 | tf_op jit(solution)/shard_map/ppermute | solution.py:24
  132.2 4.6 copy-start.14
  132.5 3.0 copy-start.18
  135.4 3.3 copy-start.4
  143.9 371.8 %all-reduce.8.cloned.1.call-start = ((), (), s32[]{:S(2)}) async-start(), calls=%async_computation.5 | async-start | bytes 2097152 | tf_op jit(solution)/shard_map/psum | solution.py:888
  143.9 50.3 %copy-start.61 = (s32[256,8]{0,1:T(8,128)S(1)}, s32[256,8]{0,1:T(8,128)}, u32[]{:S(2)}) copy-start(s32[256,8]{0,1:T(8,128)} %param.29) | copy-start | bytes 24580
  228.8 3.3 copy-start.42
  230.7 2.6 copy-start.54
  233.3 45.0 %copy-start.21 = (bf16[256,2048]{1,0:T(8,128)(2,1)S(1)}, bf16[256,2048]{1,0:T(8,128)(2,1)}, u32[]{:S(2)}) copy-start(bf16[256,2048]{1,0:T(8,128)(2,1)} %multiply_convert_fusion.1.own) | copy-start | bytes 3145732
  387.5 318.6 %all-reduce.12.cloned.1.call-start = ((), (), s32[]{:S(2)}) async-start(), calls=%async_computation.11 | async-start | bytes 131072 | tf_op jit(solution)/shard_map/psum | solution.py:966
  387.5 63.1 %copy-start.58 = (f32[256]{0:T(256)S(1)}, f32[256]{0:T(256)}, u32[]{:S(2)}) copy-start(f32[256]{0:T(256)} %get-tuple-element.160) | copy-start | bytes 3076
  516.8 3.4 copy-start.62
  516.8 3.4 copy-start.3
  516.9 3.4 copy-start.10
  516.9 3.4 copy-start.20
  516.9 3.4 copy-start.55
  524.3 7.2 copy-start.15
  543.3 8.9 copy-start.24
  550.1 2.0 copy-start.13
  560.5 7.4 copy-start.47
  560.5 7.6 copy-start.45
  560.5 27.4 %copy-start.22 = (bf16[256,2048]{1,0:T(8,128)(2,1)S(1)}, bf16[256,2048]{1,0:T(8,128)(2,1)}, u32[]{:S(2)}) copy-start(bf16[256,2048]{1,0:T(8,128)(2,1)} %multiply_convert_fusion.1.own) | copy-start | bytes 3145732
  560.5 27.4 %copy-start.59 = (f32[256]{0:T(256)S(1)}, f32[256]{0:T(256)}, u32[]{:S(2)}) copy-start(f32[256]{0:T(256)} %get-tuple-element.160) | copy-start | bytes 3076
  560.5 27.4 %copy-start.60 = (f32[256]{0:T(256)S(1)}, f32[256]{0:T(256)}, u32[]{:S(2)}) copy-start(f32[256]{0:T(256)} %fusion.47) | copy-start | bytes 3076
  560.6 27.4 %copy-start.63 = (f32[256]{0:T(256)S(1)}, f32[256]{0:T(256)}, u32[]{:S(2)}) copy-start(f32[256]{0:T(256)} %copy-done.62) | copy-start | bytes 3076
  560.6 29.6 %copy-start.19 = (bf16[1,8,256,4,128]{4,2,1,3,0:T(8,128)(2,1)S(1)}, bf16[1,8,256,4,128]{4,2,1,3,0:T(8,128)(2,1)}, u32[]{:S(2)}) copy-start(bf16[1,8,256,4,128]{4,2,1,3,0:T(8,128)(2,1)} %copy-done.18) | copy-start | bytes 6291460
  565.4 20.0 %collective-permute-start.13 = (bf16[2,256,4,128]{3,1,2,0:T(8,128)(2,1)}, bf16[2,256,4,128]{3,1,2,0:T(8,128)(2,1)}, u32[]{:S(2)}, u32[]{:S(2)}) collective-permute-start(bf16[2,256,4,128]{3,1,2,0:T(8,128)(2,1)} %get-tuple-element.123), channel_id=1, source_target_pairs={{28,0},{29,1},{30,2},{31,3}} | collective-permute-start | bytes 1572872 | tf_op jit(solution)/shard_map/ppermute | solution.py:24
  566.7 20.0 %collective-permute-start.12 = (bf16[2,256,4,128]{3,1,2,0:T(8,128)(2,1)}, bf16[2,256,4,128]{3,1,2,0:T(8,128)(2,1)}, u32[]{:S(2)}, u32[]{:S(2)}) collective-permute-start(bf16[2,256,4,128]{3,1,2,0:T(8,128)(2,1)} %get-tuple-element.124), channel_id=1, source_target_pairs={{24,0},{28,4},{25,1},{29,5},{26,2},{30,6},{27,3},{31,7}} | collective-permute-start | bytes 1572872 | tf_op jit(solution)/shard_map/ppermute | solution.py:24
  568.9 60.3 %collective-permute-start.11 = (bf16[2,256,4,128]{3,1,2,0:T(8,128)(2,1)}, bf16[2,256,4,128]{3,1,2,0:T(8,128)(2,1)}, u32[]{:S(2)}, u32[]{:S(2)}) collective-permute-start(bf16[2,256,4,128]{3,1,2,0:T(8,128)(2,1)} %get-tuple-element.125), channel_id=1, source_target_pairs={{20,0},{24,4},{28,8},{21,1},{25,5},{29,9},{22,2},{26,6},{30,10},{2... | collective-permute-start | bytes 1572872 | tf_op jit(solution)/shard_map/ppermute | solution.py:24
  570.2 59.4 %collective-permute-start.10 = (bf16[2,256,4,128]{3,1,2,0:T(8,128)(2,1)}, bf16[2,256,4,128]{3,1,2,0:T(8,128)(2,1)}, u32[]{:S(2)}, u32[]{:S(2)}) collective-permute-start(bf16[2,256,4,128]{3,1,2,0:T(8,128)(2,1)} %get-tuple-element.126), channel_id=1, source_target_pairs={{16,0},{20,4},{24,8},{28,12},{17,1},{21,5},{25,9},{29,13},{18,2},{... | collective-permute-start | bytes 1572872 | tf_op jit(solution)/shard_map/ppermute | solution.py:24
  571.5 58.1 %collective-permute-start.9 = (bf16[2,256,4,128]{3,1,2,0:T(8,128)(2,1)}, bf16[2,256,4,128]{3,1,2,0:T(8,128)(2,1)}, u32[]{:S(2)}, u32[]{:S(2)}) collective-permute-start(bf16[2,256,4,128]{3,1,2,0:T(8,128)(2,1)} %get-tuple-element.127), channel_id=1, source_target_pairs={{12,0},{16,4},{20,8},{24,12},{28,16},{13,1},{17,5},{21,9},{25,13},... | collective-permute-start | bytes 1572872 | tf_op jit(solution)/shard_map/ppermute | solution.py:24
  585.3 44.3 %collective-permute-start.8 = (bf16[2,256,4,128]{3,1,2,0:T(8,128)(2,1)}, bf16[2,256,4,128]{3,1,2,0:T(8,128)(2,1)}, u32[]{:S(2)}, u32[]{:S(2)}) collective-permute-start(bf16[2,256,4,128]{3,1,2,0:T(8,128)(2,1)} %get-tuple-element.128), channel_id=1, source_target_pairs={{8,0},{12,4},{16,8},{20,12},{24,16},{28,20},{9,1},{13,5},{17,9},{2... | collective-permute-start | bytes 1572872 | tf_op jit(solution)/shard_map/ppermute | solution.py:24
  586.6 43.0 %collective-permute-start.7 = (bf16[2,256,4,128]{3,1,2,0:T(8,128)(2,1)}, bf16[2,256,4,128]{3,1,2,0:T(8,128)(2,1)}, u32[]{:S(2)}, u32[]{:S(2)}) collective-permute-start(bf16[2,256,4,128]{3,1,2,0:T(8,128)(2,1)} %get-tuple-element.122), channel_id=1, source_target_pairs={{4,0},{8,4},{12,8},{16,12},{20,16},{24,20},{28,24},{5,1},{9,5},{13... | collective-permute-start | bytes 1572872 | tf_op jit(solution)/shard_map/ppermute | solution.py:24
  590.0 138.9 %all-reduce.10.cloned.1.call-start = ((), (), s32[]{:S(2)}) async-start(), calls=%async_computation.6 | async-start | bytes 2097152 | tf_op jit(solution)/shard_map/psum | solution.py:948
  590.2 39.4 %copy-start.5 = (f32[2048,4,128]{2,0,1:T(8,128)S(1)}, f32[2048,4,128]{2,0,1:T(8,128)}, u32[]{:S(2)}) copy-start(f32[2048,4,128]{2,0,1:T(8,128)} %copy.195) | copy-start | bytes 12582916
  590.2 39.4 %copy-start.6 = (f32[2048,4,128]{2,0,1:T(8,128)S(1)}, f32[2048,4,128]{2,0,1:T(8,128)}, u32[]{:S(2)}) copy-start(f32[2048,4,128]{2,0,1:T(8,128)} %copy.193) | copy-start | bytes 12582916
  593.8 39.2 %copy-start.31 = (f32[256,64]{1,0:T(8,128)S(1)}, f32[256,64]{1,0:T(8,128)}, u32[]{:S(2)}) copy-start(f32[256,64]{1,0:T(8,128)} %copy-done.30) | copy-start | bytes 196612
  593.8 39.2 %copy-start.39 = (f32[256,64]{1,0:T(8,128)S(1)}, f32[256,64]{1,0:T(8,128)}, u32[]{:S(2)}) copy-start(f32[256,64]{1,0:T(8,128)} %get-tuple-element.155) | copy-start | bytes 196612
  637.2 3.5 copy-start.40
  638.8 3.7 copy-start.27
  646.2 154.6 %reduce-scatter.11.cloned.1.call-start = ((), (), s32[]{:S(2)}) async-start(), calls=%async_computation.10 | async-start | bytes 2359296 | tf_op jit(solution)/shard_map/reduce_scatter | solution.py:961
  648.4 3.6 copy-start.37
  648.4 223.0 %reduce-scatter.5.cloned.1.call-start = ((), (), s32[]{:S(2)}) async-start(), calls=%async_computation.7 | async-start | bytes 2359296 | tf_op jit(solution)/shard_map/reduce_scatter | solution.py:952
  651.9 290.3 %reduce-scatter.7.cloned.1.call-start = ((), (), s32[]{:S(2)}) async-start(), calls=%async_computation.8 | async-start | bytes 2359296 | tf_op jit(solution)/shard_map/reduce_scatter | solution.py:955
  654.2 358.9 %reduce-scatter.9.cloned.1.call-start = ((), (), s32[]{:S(2)}) async-start(), calls=%async_computation.9 | async-start | bytes 2359296 | tf_op jit(solution)/shard_map/reduce_scatter | solution.py:958
  706.1 24.8 %copy-start.56 = (bf16[2048]{0:T(1024)(128)(2,1)S(1)}, bf16[2048]{0:T(1024)(128)(2,1)}, u32[]{:S(2)}) copy-start(bf16[2048]{0:T(1024)(128)(2,1)} %get-tuple-element.108) | copy-start | bytes 12292
  778.0 236.9 %copy-start.1 = (bf16[512,2048]{1,0:T(8,128)(2,1)S(1)}, bf16[512,2048]{1,0:T(8,128)(2,1)}, u32[]{:S(2)}) copy-start(bf16[512,2048]{1,0:T(8,128)(2,1)} %param.21) | copy-start | bytes 6291460
  (22 other events, 28.3 us)
Sparse Core Ops, SparseCore 0:
  144.0 69.9 all-reduce.5
  387.6 128.0 all-reduce.7
  590.1 100.5 all-reduce.11
  692.9 35.9 all-reduce.9
  732.7 68.0 reduce-scatter.10
  804.6 66.8 reduce-scatter.4
  875.4 66.7 reduce-scatter.6
  946.2 66.8 reduce-scatter.8

commit v2 on v1

--- a/solution.py
+++ b/solution.py
@@ -1,3 +1,5 @@
+import functools
+
 import jax
 import jax.numpy as jnp
 from jax import lax
@@ -230,13 +232,30 @@
     )(own)
 
 
+def add_split(a, b):
+    pair = a.astype(f32) + b.astype(f32)
+    lanes = lax.broadcasted_iota(jnp.int32, pair.shape, 1)
+    whole = jnp.where(lanes < 16, pair + pltpu.roll(pair, 112, 1), 0.0)
+    high = whole.astype(bf16).astype(f32)
+    return (high + pltpu.roll(whole - high, 16, 1)).astype(bf16)
+
+
+def sum_of(a, b):
+    width = a.shape[-1]
+    main = width - width % 2048
+    total = (a[:, :main].astype(f32) + b[:, :main].astype(f32)).astype(bf16)
+    if main == width:
+        return total
+    return jnp.concatenate([total, add_split(a[:, main:], b[:, main:])], 1)
+
+
 def add_rows(target, source, rows):
     step = 16
 
     @pl.loop(0, rows // step)
     def _(i):
         part = pl.ds(pl.multiple_of(i * step, step), step)
-        target[part] = (target[part].astype(f32) + source[part].astype(f32)).astype(bf16)
+        target[part] = sum_of(target[part], source[part])
 
 
 def scatter_kernel(parts, total, held, from_core, from_x, from_y, from_below, from_above, shared_in,
@@ -369,7 +388,7 @@
     total[out_mine] = held[me, mine]
     sums.wait_recv()
     out_shared = pl.ds(pl.multiple_of(base + piece, piece), 2 * piece)
-    total[out_shared] = (held[me, shared].astype(f32) + shared_in[...].astype(f32)).astype(bf16)
+    total[out_shared] = sum_of(held[me, shared], shared_in[...])
     at_end(1, held.at[me, mine], total.at[out_theirs], device(z, y, 1 - x, core)).wait_recv()
     finished = at_end(2, total.at[my_half], total.at[my_half], device(z, y, x, 1 - core))
     finished.start()
@@ -422,11 +441,11 @@
 def dot_nt(a,b): return lax.dot_general(a,b,(((1,),(1,)),((),())),preferred_element_type=f32)
 def dot_tn(a,b): return lax.dot_general(a,b,(((0,),(0,)),((),())),preferred_element_type=f32)
 
-def moe_kernel(first, x_ref, g_ref, mask_ref, wr_ref, wg_ref, wu_ref, wd_ref, hg_ref, da_ref, gg_ref, out_ref, gx_ref):
+def moe_kernel(first, x_ref, g_ref, mask_ref, wr_ref, wg_ref, wu_ref, wd_ref, hg_ref, da_ref, parts_ref):
     x = x_ref[...]
     g = g_ref[...]
     logits = dot(x, wr_ref[...])
-    mask = mask_ref[...] > 0
+    mask = mask_ref[:, :wr_ref.shape[1]].astype(f32) > 0
     top = jnp.max(jnp.where(mask, logits, -jnp.inf), -1, keepdims=True)
     raised = jnp.where(mask, jnp.exp(jnp.where(mask, logits - top, 0.0)), 0.0)
     gates = raised / jnp.sum(raised, -1, keepdims=True)
@@ -456,37 +475,487 @@
         b = dot_nt(dg, wg_ref[j]) + dot_nt(du, wu_ref[j])
         out = o if out is None else out + o
         gx = b if gx is None else gx + b
-    gg_ref[...] = gg
-    out_ref[...] = out.astype(bf16)
-    gx_ref[...] = gx.astype(bf16)
-
-def moe(first, X, G, mask, wr, wg, wu, wd, bt=256):
+    D = x.shape[1]
+    parts_ref[:, :D] = out.astype(bf16)
+    parts_ref[:, D:2 * D] = gx.astype(bf16)
+    high = gg.astype(bf16)
+    low = (gg - high.astype(f32)).astype(bf16)
+    spare = jnp.zeros((gg.shape[0], 128 - 2 * gg.shape[1]), bf16)
+    parts_ref[:, 2 * D:] = jnp.concatenate([high, low, spare], 1)
+
+def moe(first, X, G, wr, wg, wu, wd, bt=512):
     T, D = X.shape
-    E = mask.shape[1]
+    E = wr.shape[1]
     J, _, F = wg.shape
     blk = lambda w: pl.BlockSpec((bt, w), lambda i, s: (i, 0))
     full = lambda *shp: pl.BlockSpec(shp, lambda i, s: (0,) * len(shp))
     return pl.pallas_call(moe_kernel,
         grid_spec=pltpu.PrefetchScalarGridSpec(num_scalar_prefetch=1, grid=(T // bt,),
-        in_specs=[blk(D), blk(D), blk(E), full(D, E), full(J, D, F), full(J, D, F), full(J, F, D)],
-        out_specs=[blk(J * F), blk(2 * J * F), blk(E), blk(D), blk(D)]),
-        out_shape=[jax.ShapeDtypeStruct((T, J * F), bf16), jax.ShapeDtypeStruct((T, 2 * J * F), bf16), jax.ShapeDtypeStruct((T, E), f32),
-                   jax.ShapeDtypeStruct((T, D), bf16), jax.ShapeDtypeStruct((T, D), bf16)],
+        in_specs=[blk(D), blk(D), pl.BlockSpec((bt, 128), lambda i, s: (i, D // 128)), full(D, E), full(J, D, F), full(J, D, F), full(J, F, D)],
+        out_specs=[blk(J * F), blk(2 * J * F), blk(2 * D + 128)]),
+        out_shape=[jax.ShapeDtypeStruct((T, J * F), bf16), jax.ShapeDtypeStruct((T, 2 * J * F), bf16),
+                   jax.ShapeDtypeStruct((T, 2 * D + 128), bf16)],
         compiler_params=pltpu.CompilerParams(vmem_limit_bytes=56 * 2**20),
-    )(first, X, G, mask, wr, wg, wu, wd)
+    )(first, X, G, G, wr, wg, wu, wd)
 
 def tn_kernel(a_ref, b_ref, o_ref):
     o_ref[...] = dot_tn(a_ref[...], b_ref[...])
 
-def tn(a, b, bm=256, bn=None, fuse=False):
+def tn(a, b, bm, bn, N):
     T, M = a.shape
-    N = b.shape[1]
-    bn = bn or N
     return pl.pallas_call(tn_kernel, grid=(M // bm, N // bn),
         in_specs=[pl.BlockSpec((T, bm), lambda i, j: (0, i)), pl.BlockSpec((T, bn), lambda i, j: (0, j))],
         out_specs=pl.BlockSpec((bm, bn), lambda i, j: (i, j)),
         out_shape=jax.ShapeDtypeStruct((M, N), f32),
-        compiler_params=pltpu.CompilerParams(vmem_limit_bytes=56 * 2**20, fuse_transposed_lhs_in_matmul=fuse))(a, b)
+        compiler_params=pltpu.CompilerParams(vmem_limit_bytes=56 * 2**20))(a, b)
+
+
+def expert_grads_kernel(a_ref, b_ref, gate_ref, up_ref):
+    both = dot_tn(a_ref[...], b_ref[...])
+    ff = gate_ref.shape[2]
+    for j in range(gate_ref.shape[0]):
+        gate_ref[j] = both[:, 2 * j * ff:(2 * j + 1) * ff]
+        up_ref[j] = both[:, (2 * j + 1) * ff:(2 * j + 2) * ff]
+
+
+def expert_grads(a, b, J, bm=512):
+    T, D = a.shape
+    F = b.shape[1] // (2 * J)
+    spec = pl.BlockSpec((J, bm, F), lambda i: (0, i, 0))
+    shape = jax.ShapeDtypeStruct((J, D, F), f32)
+    return pl.pallas_call(expert_grads_kernel, grid=(D // bm,),
+        in_specs=[pl.BlockSpec((T, bm), lambda i: (0, i)), pl.BlockSpec((T, 2 * J * F), lambda i: (0, 0))],
+        out_specs=[spec, spec], out_shape=[shape, shape],
+        compiler_params=pltpu.CompilerParams(vmem_limit_bytes=56 * 2**20))(a, b)
+
+
+EPS = 1e-05
+HD = 128
+BLOCK = 256
+
+
+def block_of(r, parity):
+    return 2 * r + (parity if r % 2 == 0 else 1 - parity)
+
+
+def norm_factor(v):
+    return lax.rsqrt(jnp.mean(v * v, -1, keepdims=True) + EPS)
+
+
+def project_kernel(x_ref, gain_ref, w_ref, qg_ref, kg_ref, cos_ref, sin_ref, a_ref, q_ref, k_ref, v_ref, qr_ref, kr_ref):
+    x = x_ref[...].astype(f32)
+    a = (x * norm_factor(x) * gain_ref[...]).astype(bf16)
+    a_ref[...] = a
+    raw = dot(a, w_ref[...])
+    cosine, sine = cos_ref[...], sin_ref[...]
+
+    def turned(part, gain):
+        n = part * norm_factor(part) * gain
+        return (n * cosine + pltpu.roll(n, HD // 2, 1) * sine).astype(bf16)
+
+    q_raw, k_raw = raw[:, :HD], raw[:, HD:2 * HD]
+    qr_ref[...] = q_raw
+    kr_ref[...] = k_raw
+    q_ref[...] = turned(q_raw, qg_ref[...])
+    k_ref[...] = turned(k_raw, kg_ref[...])
+    v_ref[...] = raw[:, 2 * HD:].astype(bf16)
+
+
+def project(x, gain, w, qg, kg, cosine, sine, bt=256):
+    T, D = x.shape
+    blk = lambda n: pl.BlockSpec((bt, n), lambda i: (i, 0))
+    full = lambda *s: pl.BlockSpec(s, lambda i: (0,) * len(s))
+    sd = jax.ShapeDtypeStruct
+    return pl.pallas_call(
+        project_kernel, grid=(T // bt,),
+        in_specs=[blk(D), full(1, D), full(D, 3 * HD), full(1, HD), full(1, HD), blk(HD), blk(HD)],
+        out_specs=[blk(D)] + [blk(HD)] * 5,
+        out_shape=[sd((T, D), bf16)] + [sd((T, HD), bf16)] * 3 + [sd((T, HD), f32)] * 2,
+        compiler_params=pltpu.CompilerParams(vmem_limit_bytes=40 * 2**20),
+    )(x, gain, w, qg, kg, cosine, sine)
+
+
+def probabilities(r, start, q, k_ref, segc_ref, segr_ref):
+    keys = (2 * r + 2) * BLOCK
+    scores = dot_nt(q, k_ref[:keys]) * (HD ** -0.5)
+    rows = start + lax.broadcasted_iota(jnp.int32, scores.shape, 0)
+    columns = lax.broadcasted_iota(jnp.int32, scores.shape, 1)
+    same = segc_ref[pl.ds(start, BLOCK)] == segr_ref[:, :keys]
+    scores = jnp.where((rows >= columns) & same, scores, -1000000000.0)
+    raised = jnp.exp(scores - jnp.max(scores, -1, keepdims=True))
+    return raised / jnp.sum(raised, -1, keepdims=True)
+
+
+def attend_kernel(q_ref, k_ref, v_ref, segc_ref, segr_ref, out_ref):
+    parity = lax.axis_index("expert") % 2
+    for r in range(4):
+        start = pl.multiple_of(block_of(r, parity) * BLOCK, BLOCK)
+        probs = probabilities(r, start, q_ref[pl.ds(start, BLOCK)], k_ref, segc_ref, segr_ref)
+        out_ref[r] = dot(probs.astype(bf16), v_ref[:(2 * r + 2) * BLOCK]).astype(bf16)
+
+
+VM = pl.BlockSpec(memory_space=pltpu.VMEM)
+
+
+def attend(q, k, v, segc, segr):
+    return pl.pallas_call(
+        attend_kernel, in_specs=[VM] * 5, out_specs=VM,
+        out_shape=jax.ShapeDtypeStruct((4, BLOCK, HD), bf16),
+        compiler_params=pltpu.CompilerParams(vmem_limit_bytes=40 * 2**20),
+    )(q, k, v, segc, segr)
+
+
+def attend_back_kernel(q_ref, k_ref, v_ref, segc_ref, segr_ref, g_ref, dq_ref, own_ref, other_ref, dk, dv):
+    parity = lax.axis_index("expert") % 2
+    for r in (3, 2, 1, 0):
+        keys = (2 * r + 2) * BLOCK
+        start = pl.multiple_of(block_of(r, parity) * BLOCK, BLOCK)
+        q = q_ref[pl.ds(start, BLOCK)]
+        g = g_ref[r]
+        probs = probabilities(r, start, q, k_ref, segc_ref, segr_ref)
+        gv = dot_tn(probs.astype(bf16), g)
+        gp = dot_nt(g, v_ref[:keys])
+        gs = (probs * (gp - jnp.sum(gp * probs, -1, keepdims=True))).astype(bf16)
+        dq_ref[r] = dot(gs, k_ref[:keys]) * (HD ** -0.5)
+        gk = dot_tn(gs, q) * (HD ** -0.5)
+        if r == 3:
+            dv[...] = gv
+            dk[...] = gk
+        else:
+            dv[:keys] += gv
+            dk[:keys] += gk
+    for r in range(4):
+        mine = pl.ds(pl.multiple_of(block_of(r, parity) * BLOCK, BLOCK), BLOCK)
+        other = pl.ds(pl.multiple_of(block_of(r, 1 - parity) * BLOCK, BLOCK), BLOCK)
+        own_ref[r, :, :HD] = dk[mine]
+        own_ref[r, :, HD:] = dv[mine]
+        other_ref[r, :, :HD] = dk[other].astype(bf16)
+        other_ref[r, :, HD:] = dv[other].astype(bf16)
+
+
+def attend_back(q, k, v, segc, segr, g):
+    T = q.shape[0]
+    sd = jax.ShapeDtypeStruct
+    return pl.pallas_call(
+        attend_back_kernel, in_specs=[VM] * 6, out_specs=[VM] * 3,
+        out_shape=[sd((4, BLOCK, HD), f32), sd((4, BLOCK, 2 * HD), f32), sd((4, BLOCK, 2 * HD), bf16)],
+        scratch_shapes=[pltpu.VMEM((T, HD), f32), pltpu.VMEM((T, HD), f32)],
+        compiler_params=pltpu.CompilerParams(vmem_limit_bytes=48 * 2**20),
+    )(q, k, v, segc, segr, g)
+
+
+def settle_kernel(dq_ref, own_ref, other_ref, qr_ref, kr_ref, qg_ref, kg_ref, cos_ref, sin_ref,
+                  raw_ref, gains_ref, arrived, send, recv):
+    z, y, x, core = place()
+    barrier = pltpu.get_barrier_semaphore()
+    partner = device(z, 1 - y, x, core)
+    pl.semaphore_signal(barrier, inc=1, device_id=partner, device_id_type=MESH)
+    pl.semaphore_wait(barrier, 1)
+    copies = []
+    for r in range(4):
+        copy = pltpu.make_async_remote_copy(
+            src_ref=other_ref.at[r], dst_ref=arrived.at[r], send_sem=send.at[r], recv_sem=recv.at[r],
+            device_id=partner, device_id_type=MESH)
+        copy.start()
+        copies.append(copy)
+    gain_sums = [jnp.zeros((1, HD), f32), jnp.zeros((1, HD), f32)]
+
+    def back(turned, raw, gain, which, cosine, sine):
+        g = turned * cosine - pltpu.roll(turned, HD // 2, 1) * sine
+        factor = norm_factor(raw)
+        n = raw * factor
+        gain_sums[which] = gain_sums[which] + jnp.sum(g * n, 0, keepdims=True)
+        g = g * gain
+        return (factor * (g - n * jnp.mean(g * n, -1, keepdims=True))).astype(bf16)
+
+    for r in range(4):
+        rows = pl.ds(pl.multiple_of(block_of(r, y) * BLOCK, BLOCK), BLOCK)
+        raw_ref[r, :, :HD] = back(dq_ref[r], qr_ref[rows], qg_ref[...], 0, cos_ref[rows], sin_ref[rows])
+    for r in range(4):
+        rows = pl.ds(pl.multiple_of(block_of(r, y) * BLOCK, BLOCK), BLOCK)
+        copies[r].wait_recv()
+        dk = own_ref[r, :, :HD] + arrived[r, :, :HD].astype(f32)
+        raw_ref[r, :, HD:2 * HD] = back(dk, kr_ref[rows], kg_ref[...], 1, cos_ref[rows], sin_ref[rows])
+        raw_ref[r, :, 2 * HD:] = (own_ref[r, :, HD:] + arrived[r, :, HD:].astype(f32)).astype(bf16)
+    gains_ref[0:1] = gain_sums[0]
+    gains_ref[1:2] = gain_sums[1]
+    for copy in copies:
+        copy.wait_send()
+
+
+def settle(dq, own, other, qr, kr, qg, kg, cosine, sine, number):
+    sd = jax.ShapeDtypeStruct
+    return pl.pallas_call(
+        settle_kernel, in_specs=[VM] * 9, out_specs=[VM] * 2,
+        out_shape=[sd((4, BLOCK, 3 * HD), bf16), sd((2, HD), f32)],
+        scratch_shapes=[pltpu.VMEM((4, BLOCK, 2 * HD), bf16), pltpu.SemaphoreType.DMA((4,)), pltpu.SemaphoreType.DMA((4,))],
+        compiler_params=pltpu.CompilerParams(collective_id=number, has_side_effects=True, vmem_limit_bytes=48 * 2**20),
+    )(dq, own, other, qr, kr, qg, kg, cosine, sine)
+
+
+def greet_owners(z, y, x, core, sources):
+    barrier = pltpu.get_barrier_semaphore()
+    for r in range(4):
+        target = device(r, sources(r), x, core)
+
+        def signal():
+            pl.semaphore_signal(barrier, inc=1, device_id=target, device_id_type=MESH)
+        pl.when((z != r) | (z % 2 == 1))(signal)
+    return barrier
+
+
+def blend_kernel(parts, groups, multiply, part_ref, *refs):
+    weights = refs[:groups]
+    total, gathered, out_half, in_half, kept, held, from_x, send, recv, pair_send, pair_recv, local = refs[groups:]
+    z, y, x, core = place()
+    targets = lambda r: (y if r % 2 == 0 else 1 - y)
+    source_y = (y + z) % 2
+    barrier = greet_owners(z, y, x, core, lambda r: source_y)
+    for where in (device(z, y, 1 - x, core), device(z, y, x, 1 - core)):
+        pl.semaphore_signal(barrier, inc=1, device_id=where, device_id_type=MESH)
+    pl.semaphore_wait(barrier, 5 + z % 2)
+    width = HD * 4
+
+    def lanes(g, n):
+        return pl.ds(pl.multiple_of(g * width + n * HD, HD), HD)
+
+    def remote(r, g):
+        return pltpu.make_async_remote_copy(
+            src_ref=part_ref.at[r, :, pl.ds(g * HD, HD)], dst_ref=gathered.at[:, lanes(g, z)],
+            send_sem=send.at[r, g], recv_sem=recv.at[z, g],
+            device_id=device(r, targets(r), x, core), device_id_type=MESH)
+
+    def arriving(n, g):
+        return pltpu.make_async_remote_copy(
+            src_ref=part_ref.at[n, :, pl.ds(g * HD, HD)], dst_ref=gathered.at[:, lanes(g, n)],
+            send_sem=send.at[n, g], recv_sem=recv.at[n, g],
+            device_id=device(n, source_y, x, core), device_id_type=MESH)
+
+    def own(r, g):
+        return pltpu.make_async_copy(
+            part_ref.at[r, :, pl.ds(g * HD, HD)], gathered.at[:, lanes(g, r)], local.at[g])
+
+    for r in range(4):
+        here = (z == r) & (z % 2 == 0)
+
+        @pl.when(here)
+        def _():
+            for g in range(groups):
+                own(r, g).start()
+
+        @pl.when(jnp.logical_not(here))
+        def _():
+            for g in range(groups):
+                remote(r, g).start()
+    for r in range(4):
+        here = (z == r) & (z % 2 == 0)
+
+        @pl.when(here)
+        def _():
+            for g in range(groups):
+                own(r, g).wait()
+
+        @pl.when(jnp.logical_not(here))
+        def _():
+            for g in range(groups):
+                arriving(r, g).wait_recv()
+
+    rows = total.shape[0]
+    half = rows // 2
+    chunk = half // 2
+    my_half = core * half
+    other_half = (1 - core) * half
+
+    def pair(kind, c, source, target, where):
+        return pltpu.make_async_remote_copy(
+            src_ref=source, dst_ref=target, send_sem=pair_send.at[kind, c], recv_sem=pair_recv.at[kind, c],
+            device_id=where, device_id_type=MESH)
+
+    twin = device(z, y, x, 1 - core)
+    across = device(z, y, 1 - x, core)
+    piece = lambda c: pl.ds(c * chunk, chunk)
+    first = [pair(0, c, out_half.at[piece(c)], in_half.at[piece(c)], twin) for c in range(2)]
+    second = [pair(1, c, held.at[piece(c)], from_x.at[piece(c)], across) for c in range(2)]
+    at = lambda base, c: pl.ds(pl.multiple_of(base + c * chunk, chunk), chunk)
+    third = [pair(2, c, total.at[at(my_half, c)], total.at[at(my_half, c)], twin) for c in range(2)]
+    for c in range(2):
+        out_half[piece(c)] = multiply(gathered[at(other_half, c)], weights).astype(bf16)
+        first[c].start()
+    for c in range(2):
+        kept[...] = multiply(gathered[at(my_half, c)], weights)
+        first[c].wait_recv()
+        held[piece(c)] = (kept[...] + in_half[piece(c)].astype(f32)).astype(bf16)
+        second[c].start()
+    for c in range(2):
+        second[c].wait_recv()
+        total[at(my_half, c)] = (held[piece(c)].astype(f32) + from_x[piece(c)].astype(f32)).astype(bf16)
+        third[c].start()
+    for c in range(2):
+        pair(2, c, total.at[at(my_half, c)], total.at[at(other_half, c)], twin).wait_recv()
+        first[c].wait_send()
+        second[c].wait_send()
+        third[c].wait_send()
+    for r in range(4):
+        here = (z == r) & (z % 2 == 0)
+
+        @pl.when(jnp.logical_not(here))
+        def _():
+            for g in range(groups):
+                remote(r, g).wait_send()
+
+
+def blend(parts, weights, multiply, number):
+    groups = parts.shape[2] // HD
+    rows, width = BLOCK, 2048
+    sd = jax.ShapeDtypeStruct
+    half = rows // 2
+    return pl.pallas_call(
+        functools.partial(blend_kernel, 4, groups, multiply),
+        in_specs=[VM] * (1 + groups), out_specs=[VM] * 2,
+        out_shape=[sd((rows, width), bf16), sd((rows, 4 * groups * HD), bf16)],
+        scratch_shapes=[
+            pltpu.VMEM((half, width), bf16), pltpu.VMEM((half, width), bf16), pltpu.VMEM((half // 2, width), f32),
+            pltpu.VMEM((half, width), bf16), pltpu.VMEM((half, width), bf16),
+            pltpu.SemaphoreType.DMA((4, groups)), pltpu.SemaphoreType.DMA((4, groups)),
+            pltpu.SemaphoreType.DMA((3, 2)), pltpu.SemaphoreType.DMA((3, 2)), pltpu.SemaphoreType.DMA((groups,)),
+        ],
+        compiler_params=pltpu.CompilerParams(collective_id=number, has_side_effects=True, vmem_limit_bytes=48 * 2**20),
+    )(parts, *weights)
+
+
+def hand_back_kernel(g_ref, out_ref, send, recv, local):
+    z, y, x, core = place()
+    source_y = (y + z) % 2
+    barrier = pltpu.get_barrier_semaphore()
+    for r in range(4):
+        def signal():
+            pl.semaphore_signal(barrier, inc=1, device_id=device(r, y if r % 2 == 0 else 1 - y, x, core), device_id_type=MESH)
+        pl.when((z != r) | (z % 2 == 1))(signal)
+    pl.semaphore_wait(barrier, 3 + z % 2)
+
+    def remote(n):
+        return pltpu.make_async_remote_copy(
+            src_ref=g_ref.at[:, pl.ds(n * HD, HD)], dst_ref=out_ref.at[z], send_sem=send.at[n], recv_sem=recv.at[z],
+            device_id=device(n, source_y, x, core), device_id_type=MESH)
+
+    def arriving(r):
+        return pltpu.make_async_remote_copy(
+            src_ref=g_ref.at[:, pl.ds(r * HD, HD)], dst_ref=out_ref.at[r], send_sem=send.at[r], recv_sem=recv.at[r],
+            device_id=device(r, y if r % 2 == 0 else 1 - y, x, core), device_id_type=MESH)
+
+    def own(n):
+        return pltpu.make_async_copy(g_ref.at[:, pl.ds(n * HD, HD)], out_ref.at[n], local)
+
+    for n in range(4):
+        here = (z == n) & (z % 2 == 0)
+        pl.when(here)(lambda: own(n).start())
+        pl.when(jnp.logical_not(here))(lambda: remote(n).start())
+    for n in range(4):
+        here = (z == n) & (z % 2 == 0)
+        pl.when(here)(lambda: own(n).wait())
+        pl.when(jnp.logical_not(here))(lambda: arriving(n).wait_recv())
+        pl.when(jnp.logical_not(here))(lambda: remote(n).wait_send())
+
+
+def hand_back(g, number):
+    return pl.pallas_call(
+        hand_back_kernel, in_specs=[VM], out_specs=VM,
+        out_shape=jax.ShapeDtypeStruct((4, BLOCK, HD), bf16),
+        scratch_shapes=[pltpu.SemaphoreType.DMA((4,)), pltpu.SemaphoreType.DMA((4,)), pltpu.SemaphoreType.DMA],
+        compiler_params=pltpu.CompilerParams(collective_id=number, has_side_effects=True),
+    )(g)
+
+
+def grad_weight_kernel(parity, a_ref, raw_ref, out_ref, acc):
+    r = pl.program_id(0)
+    part = dot_tn(a_ref[...], raw_ref[0])
+
+    @pl.when(r == 0)
+    def _():
+        acc[...] = part
+
+    @pl.when(r > 0)
+    def _():
+        acc[...] += part
+
+    @pl.when(r == 3)
+    def _():
+        out_ref[...] = acc[...].astype(bf16)
+
+
+def grad_weight(parity, a, raw):
+    T, D = a.shape
+    W = raw.shape[2]
+    return pl.pallas_call(
+        grad_weight_kernel,
+        grid_spec=pltpu.PrefetchScalarGridSpec(
+            num_scalar_prefetch=1, grid=(4,),
+            in_specs=[pl.BlockSpec((BLOCK, D), lambda r, p: (2 * r + (r + p[0]) % 2, 0)),
+                      pl.BlockSpec((1, BLOCK, W), lambda r, p: (r, 0, 0))],
+            out_specs=pl.BlockSpec((D, W), lambda r, p: (0, 0)),
+            scratch_shapes=[pltpu.VMEM((D, W), f32)]),
+        out_shape=jax.ShapeDtypeStruct((D, W), bf16),
+        compiler_params=pltpu.CompilerParams(vmem_limit_bytes=40 * 2**20),
+    )(parity, a, raw)
+
+
+def deliver_kernel(add_up, part_ref, out_ref, held, from_y, from_z, send, recv, local):
+    z, y, x, core = place()
+    barrier = pltpu.get_barrier_semaphore()
+    partner = device(z, 1 - y, x, core)
+    pl.semaphore_signal(barrier, inc=1, device_id=partner, device_id_type=MESH)
+    for n in range(4):
+        pl.when(z != n)(lambda: pl.semaphore_signal(barrier, inc=1, device_id=device(n, y, x, core), device_id_type=MESH))
+    pl.semaphore_wait(barrier, 4)
+
+    def pair(n):
+        return pltpu.make_async_remote_copy(
+            src_ref=part_ref.at[n * 2 + 1 - y], dst_ref=from_y.at[n], send_sem=send.at[0, n], recv_sem=recv.at[0, n],
+            device_id=partner, device_id_type=MESH)
+
+    def along(n):
+        return pltpu.make_async_remote_copy(
+            src_ref=held.at[n], dst_ref=from_z.at[z], send_sem=send.at[1, n], recv_sem=recv.at[1, z],
+            device_id=device(n, y, x, core), device_id_type=MESH)
+
+    def arriving(n):
+        return pltpu.make_async_remote_copy(
+            src_ref=held.at[n], dst_ref=from_z.at[n], send_sem=send.at[1, n], recv_sem=recv.at[1, n],
+            device_id=device(n, y, x, core), device_id_type=MESH)
+
+    ahead = z // 2
+    order = (3 - 3 * ahead, 2 - ahead, z + 1 - 2 * (z % 2), z)
+    for n in order:
+        pair(n).start()
+    for i, n in enumerate(order):
+        pair(n).wait_recv()
+        held[n] = (part_ref[n * 2 + y].astype(f32) + from_y[n].astype(f32)).astype(bf16)
+        if i < 3:
+            along(n).start()
+    from_z[z] = held[z]
+    for n in range(4):
+        pl.when(z != n)(lambda: arriving(n).wait_recv())
+    if add_up:
+        out_ref[...] = (from_z[0].astype(f32) + from_z[1].astype(f32)) + (from_z[2].astype(f32) + from_z[3].astype(f32))
+    else:
+        for n in range(4):
+            for g in range(3):
+                out_ref[g, :, n * HD:(n + 1) * HD] = from_z[n, :, g * HD:(g + 1) * HD].astype(f32)
+    for n in range(4):
+        pair(n).wait_send()
+        pl.when(z != n)(lambda: along(n).wait_send())
+
+
+def deliver(parts, add_up, number):
+    _, rows, width = parts.shape
+    shape = (rows, width) if add_up else (3, rows, 4 * HD)
+    return pl.pallas_call(
+        functools.partial(deliver_kernel, add_up),
+        in_specs=[VM], out_specs=VM, out_shape=jax.ShapeDtypeStruct(shape, f32),
+        scratch_shapes=[pltpu.VMEM((4, rows, width), bf16)] * 3 + [
+            pltpu.SemaphoreType.DMA((2, 4)), pltpu.SemaphoreType.DMA((2, 4)), pltpu.SemaphoreType.DMA],
+        compiler_params=pltpu.CompilerParams(collective_id=number, has_side_effects=True, vmem_limit_bytes=48 * 2**20),
+    )(parts)
 
 
 def on_device(
@@ -763,222 +1232,103 @@
     )
 
 
-def on_device_dense(
-    hidden_in,
-    norm1_gain,
-    w_query,
-    w_key,
-    w_value,
-    w_out,
-    query_gain,
-    key_gain,
-    norm2_gain,
-    w_router,
-    w_gate,
-    w_up,
-    w_down,
-    routes,
-    segments,
-    cotangent,
+def dense_layer(
+    hidden_in, norm1_gain, w_query, w_key, w_value, w_out, query_gain, key_gain, norm2_gain, w_router,
+    w_gate, w_up, w_down, routes, segments, cotangent,
 ):
-    seq_len, width = hidden_in.shape
-    local_width = w_query.shape[1]
-    head_count = local_width // HEAD_DIM
-    expert_devs = lax.axis_size("expert")
+    rows, width = hidden_in.shape
+    experts = w_router.shape[1]
+    devices = lax.axis_size("expert")
+    tokens = devices * rows
     local_experts = w_gate.shape[0]
-    expert_total = w_router.shape[1]
-    capacity = 2 * seq_len * TOP // expert_total
-    slab_rows = local_experts * capacity
+    ff = w_gate.shape[2]
     my_index = lax.axis_index("expert")
-    group = SEQ // seq_len
-    rank = my_index % group
-    f32 = jnp.float32
-    bf16 = jnp.bfloat16
-
-    def split_heads(values):
-        return values.reshape(seq_len, head_count, HEAD_DIM)
+    head = my_index // 2
+    parity = jnp.full((1,), 1, jnp.int32) * (my_index % 2)
+
+    def own_head(v):
+        return lax.dynamic_slice_in_dim(v, head * HEAD_DIM, HEAD_DIM, v.ndim - 1)
+
+    hidden_all = gather_all(hidden_in, 1).reshape(tokens, width)
+    weights = jnp.concatenate([own_head(w_query), own_head(w_key), own_head(w_value)], 1)
+    q_gain, k_gain = own_head(query_gain)[None], own_head(key_gain)[None]
+    cosine, sine = rope_tables(lax.iota(jnp.int32, tokens).astype(f32), HEAD_DIM // 2)
+    cosine, sine = cosine[:, 0], sine[:, 0]
+    cosine = jnp.concatenate([cosine, cosine], 1)
+    sine = jnp.concatenate([-sine, sine], 1)
+    attn_all, queries, keys, values, q_raw, k_raw = project(
+        hidden_all, norm1_gain[None], weights, q_gain, k_gain, cosine, sine
+    )
+    segc, segr = segments[:, None], segments[None]
+    context = attend(queries, keys, values, segc, segr)
+    attn_out, own_context = blend(context, [w_out], lambda a, w: dot(a, w[0][...]), 2)
 
     inputs = hidden_in.astype(f32)
-    inverse_attn = inverse_rms(inputs)
-    normed_attn = inputs * inverse_attn
-    attn_input = (normed_attn * norm1_gain).astype(bf16)
-    q_raw = split_heads(jnp.dot(attn_input, w_query, preferred_element_type=f32))
-    k_raw = split_heads(jnp.dot(attn_input, w_key, preferred_element_type=f32))
-    v_heads = split_heads(jnp.dot(attn_input, w_value, preferred_element_type=f32).astype(bf16))
-    q_gains = query_gain.reshape(head_count, HEAD_DIM)
-    k_gains = key_gain.reshape(head_count, HEAD_DIM)
-    q_inverse = inverse_rms(q_raw)
-    q_normed = q_raw * q_inverse
-    k_inverse = inverse_rms(k_raw)
-    k_normed = k_raw * k_inverse
-    local_places = lax.iota(jnp.int32, seq_len)
-    query_places = rank * seq_len + local_places
-    cosine, sine_part = rope_tables(query_places.astype(f32), HEAD_DIM // 2)
-    queries = rotate(q_normed * q_gains, cosine, sine_part, 1.0).astype(bf16)
-    key_rot = rotate(k_normed * k_gains, cosine, sine_part, 1.0).astype(bf16)
-    score_scale = HEAD_DIM ** (-0.5)
-    keys_values = jnp.stack([key_rot, v_heads])
-    pieces = [keys_values]
-    for offset in range(1, group):
-        keys_values = from_behind(keys_values, "expert", 1)
-        pieces.append(keys_values)
-    stacked = jnp.stack(pieces, 1).reshape(2, group * seq_len, head_count, HEAD_DIM)
-    keys_all = stacked[0]
-    values_all = stacked[1]
-    query_segs = lax.dynamic_slice_in_dim(segments, my_index * seq_len, seq_len, 0)
-    key_segs = jnp.concatenate(
-        [
-            lax.dynamic_slice_in_dim(
-                segments, jnp.maximum(my_index - offset, 0) * seq_len, seq_len, 0
-            )
-            for offset in range(group)
-        ],
-        0,
-    )
-    offsets = lax.iota(jnp.int32, group)
-    key_places = ((rank - offsets)[:, None] * seq_len + local_places[None, :]).reshape(-1)
-    key_valid = jnp.repeat(rank - offsets >= 0, seq_len)
-    allowed = (
-        key_valid[None, :]
-        & (query_places[:, None] >= key_places[None, :])
-        & (query_segs[:, None] == key_segs[None, :])
-    )
-
-    def scores_of():
-        raw_scores = (
-            jnp.einsum("thd,shd->hts", queries, keys_all, preferred_element_type=f32) * score_scale
-        )
-        return jnp.where(allowed[None], raw_scores, MASKED)
-
-    scores = scores_of()
-    row_max = jnp.max(scores, -1, keepdims=True)
-    raised = jnp.exp(scores - row_max)
-    exp_total = jnp.sum(raised, -1, keepdims=True)
-    log_total = row_max + jnp.log(exp_total)
-    attn_probs = (raised / exp_total).astype(bf16)
-    context = (
-        jnp.einsum("hts,shd->thd", attn_probs, values_all, preferred_element_type=f32)
-        .reshape(seq_len, local_width)
-        .astype(bf16)
-    )
-    attn_part = jnp.dot(context, w_out, preferred_element_type=f32)
-    middle = inputs + lax.psum(attn_part, "head")
+    middle = inputs + attn_out.astype(f32)
     inverse_moe = inverse_rms(middle)
     normed_moe = middle * inverse_moe
     moe_input = (normed_moe * norm2_gain).astype(bf16)
-    everyone = gather_all(moe_input, 1).reshape(expert_devs * seq_len, width)
-    all_grads = gather_all(cotangent, 2).reshape(expert_devs * seq_len, width)
-    all_routes = lax.all_gather(routes, "expert", axis=0, tiled=True)
-    catalog = lax.iota(jnp.int32, expert_total)
-    mask = jnp.sum((all_routes[:, :, None] == catalog).astype(f32), 1)
+    own_mask = jnp.sum((routes[:, :, None] == lax.iota(jnp.int32, experts)).astype(f32), 1)
+    sent = jnp.concatenate([cotangent, jnp.pad(own_mask.astype(bf16), ((0, 0), (0, 128 - experts)))], 1)
+    grads_all = gather_all(sent, 3).reshape(tokens, width + 128)
+    everyone = gather_all(moe_input, 4).reshape(tokens, width)
     first = jnp.full((1,), local_experts, jnp.int32) * my_index
-    weighted, grad_acts, grad_gates, out_part, grad_part = moe(
-        first, everyone, all_grads, mask, w_router, w_gate, w_up, w_down
-    )
-    ff = w_gate.shape[2]
-    grad_down = tn(weighted, all_grads, 512, 512).reshape(local_experts, ff, width)
-    acts = tn(everyone, grad_acts, 512, 1024).reshape(width, local_experts, 2, ff)
-    grad_gate = acts[:, :, 0].transpose(1, 0, 2)
-    grad_up = acts[:, :, 1].transpose(1, 0, 2)
-    shape = (expert_devs, seq_len, width)
-    moe_out = scatter_sum(out_part.reshape(shape), 3)
-    home = scatter_sum(grad_part.reshape(shape), 4)
-    output = (middle + moe_out.astype(f32)).astype(bf16)
+    weighted, grad_acts, parts = moe(first, everyone, grads_all, w_router, w_gate, w_up, w_down)
+    grad_down = tn(weighted, grads_all, 512, 512, width).reshape(local_experts, ff, width)
+    grad_gate, grad_up = expert_grads(everyone, grad_acts, local_experts)
+    total = scatter_sum(parts.reshape(devices, rows, 2 * width + 128), 5)
+    output = (middle + total[:, :width].astype(f32)).astype(bf16)
     grad_final = cotangent.astype(f32)
-    grad_gates = lax.psum(grad_gates, ("expert", "head"))
-    grad_gates = lax.dynamic_slice_in_dim(grad_gates, my_index * seq_len, seq_len, 0)
-    own_mask = lax.dynamic_slice_in_dim(mask, my_index * seq_len, seq_len, 0) > 0
-    logits = jnp.where(own_mask, jnp.dot(moe_input, w_router, preferred_element_type=f32), -jnp.inf)
+    tail = total[:, 2 * width :].astype(f32)
+    grad_gates = tail[:, :experts] + tail[:, experts : 2 * experts]
+    logits = jnp.where(
+        own_mask > 0, jnp.dot(moe_input, w_router, preferred_element_type=f32), -jnp.inf
+    )
     raised_gate = jnp.exp(logits - jnp.max(logits, -1, keepdims=True))
     gate_weights = raised_gate / jnp.sum(raised_gate, -1, keepdims=True)
     grad_logits = (
         gate_weights * (grad_gates - jnp.sum(grad_gates * gate_weights, -1, keepdims=True))
     ).astype(bf16)
     grad_router = jnp.dot(moe_input.T, grad_logits, preferred_element_type=f32)
-    grad_moe_input = jnp.dot(grad_logits, w_router.T, preferred_element_type=f32) + home.astype(f32)
+    grad_moe_input = jnp.dot(grad_logits, w_router.T, preferred_element_type=f32)
+    grad_moe_input = grad_moe_input + total[:, width : 2 * width].astype(f32)
     grad_norm2 = jnp.sum(grad_moe_input * normed_moe, 0)
     grad_middle = grad_final + norm_back(grad_moe_input * norm2_gain, normed_moe, inverse_moe)
+    grad_router, grad_norm2 = lax.psum((grad_router, grad_norm2), "expert")
+
     grad_attn = grad_middle.astype(bf16)
-    grad_out_turned = jnp.dot(grad_attn.T, context, preferred_element_type=f32)
-    grad_context = split_heads(jnp.dot(grad_attn, w_out.T, preferred_element_type=f32).astype(bf16))
-    attn_full = jnp.exp(scores_of() - log_total)
-    attn_low = attn_full.astype(bf16)
-    grad_values_all = jnp.einsum("hts,thd->shd", attn_low, grad_context, preferred_element_type=f32)
-    grad_probs = jnp.einsum("thd,shd->hts", grad_context, values_all, preferred_element_type=f32)
-    grad_scores = (
-        attn_full * (grad_probs - jnp.sum(grad_probs * attn_full, -1, keepdims=True))
-    ).astype(bf16)
-    grad_queries = (
-        jnp.einsum("hts,shd->thd", grad_scores, keys_all, preferred_element_type=f32) * score_scale
-    )
-    grad_keys_all = (
-        jnp.einsum("hts,thd->shd", grad_scores, queries, preferred_element_type=f32) * score_scale
-    )
-    kv_terms = jnp.stack([grad_keys_all, grad_values_all]).reshape(
-        2, group, seq_len, head_count, HEAD_DIM
-    )
-    kv_total = kv_terms[:, 0]
-    for offset in range(1, group):
-        kv_total = kv_total + from_behind(
-            kv_terms[:, offset].astype(jnp.bfloat16), "expert", -offset
-        ).astype(jnp.float32)
-    grad_keys = kv_total[0]
-    grad_values = kv_total[1]
-    grad_q_normed = rotate(grad_queries, cosine, sine_part, -1.0)
-    grad_k_normed = rotate(grad_keys, cosine, sine_part, -1.0)
-    grad_query_gain = jnp.sum(grad_q_normed * q_normed, 0).reshape(local_width)
-    grad_key_gain = jnp.sum(grad_k_normed * k_normed, 0).reshape(local_width)
-    grad_q_raw = (
-        norm_back(grad_q_normed * q_gains, q_normed, q_inverse)
-        .reshape(seq_len, local_width)
-        .astype(bf16)
-    )
-    grad_k_raw = (
-        norm_back(grad_k_normed * k_gains, k_normed, k_inverse)
-        .reshape(seq_len, local_width)
-        .astype(bf16)
-    )
-    grad_v_raw = grad_values.reshape(seq_len, local_width).astype(bf16)
-    grad_query = jnp.dot(attn_input.T, grad_q_raw, preferred_element_type=f32)
-    grad_key = jnp.dot(attn_input.T, grad_k_raw, preferred_element_type=f32)
-    grad_value = jnp.dot(attn_input.T, grad_v_raw, preferred_element_type=f32)
-    input_part = jnp.dot(grad_q_raw, w_query.T, preferred_element_type=f32)
-    input_part = input_part + jnp.dot(grad_k_raw, w_key.T, preferred_element_type=f32)
-    input_part = input_part + jnp.dot(grad_v_raw, w_value.T, preferred_element_type=f32)
-    grad_attn_input = lax.psum(input_part.astype(jnp.bfloat16), "head").astype(jnp.float32)
+    grad_context = jnp.dot(grad_attn, w_out.T, preferred_element_type=f32).astype(bf16)
+    head_grad = hand_back(grad_context, 6)
+    out_part = dot_tn(grad_attn, own_context).astype(bf16)
+    grad_w_out = deliver(out_part.reshape(devices, rows, -1), True, 7)
+    grad_q, own_kv, other_kv = attend_back(queries, keys, values, segc, segr, head_grad)
+    raw_grads, gains = settle(grad_q, own_kv, other_kv, q_raw, k_raw, q_gain, k_gain, cosine, sine, 8)
+
+    def back_through(a, w):
+        span = 4 * HEAD_DIM
+        return sum(dot_nt(a[:, g * span : (g + 1) * span], w[g][...]) for g in range(3))
+
+    grad_attn_input, _ = blend(raw_grads, [w_query, w_key, w_value], back_through, 9)
+    weight_part = grad_weight(parity, attn_all, raw_grads)
+    grad_qkv = deliver(weight_part.reshape(devices, rows, -1), False, 10)
+    grad_attn_input = grad_attn_input.astype(f32)
+    inverse_attn = inverse_rms(inputs)
+    normed_attn = inputs * inverse_attn
     grad_norm1 = jnp.sum(grad_attn_input * normed_attn, 0)
     grad_input = grad_middle + norm_back(grad_attn_input * norm1_gain, normed_attn, inverse_attn)
-    grad_query, grad_key, grad_value, grad_out_turned = (
-        lax.psum_scatter(
-            grad_query.astype(jnp.bfloat16), "expert", scatter_dimension=0, tiled=True
-        ).astype(jnp.float32),
-        lax.psum_scatter(
-            grad_key.astype(jnp.bfloat16), "expert", scatter_dimension=0, tiled=True
-        ).astype(jnp.float32),
-        lax.psum_scatter(
-            grad_value.astype(jnp.bfloat16), "expert", scatter_dimension=0, tiled=True
-        ).astype(jnp.float32),
-        lax.psum_scatter(
-            grad_out_turned.astype(jnp.bfloat16), "expert", scatter_dimension=0, tiled=True
-        ).astype(jnp.float32),
-    )
-    grad_router, grad_norm1, grad_norm2, grad_query_gain, grad_key_gain = (
-        lax.psum(grad_router.astype(jnp.bfloat16), "expert").astype(jnp.float32),
-        lax.psum(grad_norm1.astype(jnp.bfloat16), "expert").astype(jnp.float32),
-        lax.psum(grad_norm2.astype(jnp.bfloat16), "expert").astype(jnp.float32),
-        lax.psum(grad_query_gain.astype(jnp.bfloat16), "expert").astype(jnp.float32),
-        lax.psum(grad_key_gain.astype(jnp.bfloat16), "expert").astype(jnp.float32),
-    )
+    wide = jnp.zeros((2, query_gain.shape[0]), f32)
+    wide = lax.dynamic_update_slice_in_dim(wide, gains, head * HEAD_DIM, 1)
+    grad_norm1, wide = lax.psum((grad_norm1, wide), "expert")
     return (
         output,
         grad_input,
         grad_norm1,
-        grad_query,
-        grad_key,
-        grad_value,
-        grad_out_turned.T,
-        grad_query_gain,
-        grad_key_gain,
+        grad_qkv[0],
+        grad_qkv[1],
+        grad_qkv[2],
+        grad_w_out.T,
+        wide[0],
+        wide[1],
         grad_norm2,
         grad_router,
         grad_gate,
@@ -987,11 +1337,16 @@
     )
 
 
+def layer(*arrays):
+    rows, experts = arrays[0].shape[0], arrays[9].shape[1]
+    whole = 2 * rows * TOP // experts >= rows and rows * lax.axis_size("expert") == SEQ
+    grid = (lax.axis_size("expert"), lax.axis_size("head")) == (8, 4)
+    return dense_layer(*arrays) if whole and grid else on_device(*arrays)
+
+
 def solution(mesh):
-    experts, heads = mesh.shape["expert"], mesh.shape["head"]
-    form = on_device_dense if (experts, heads) == (8, 4) else on_device
     return jax.shard_map(
-        form,
+        layer,
         mesh=mesh,
         in_specs=(
             P("expert", None),

time: 1030 us -> 608 us (0.59)
  waiting for transfers between devices: 408 us -> 0.02 us
  Pallas kernels: 288 us -> 500 us
  local copies, waits for them, and re-layouts: 78.5 us -> 22.3 us
  matrix products: 56.6 us -> 7.51 us
  starting transfers between devices: 47.4 us -> 0.04 us
  blocking collectives: 75.4 us -> 35.7 us
  other arithmetic: 52.7 us -> 18.8 us
    reduce_scatter x4 -> x0, waiting for transfers between devices: 225 us -> none  [the longest x1 69.1 us: on_device_dense(): lax.psum_scatter(grad_value.astype(jnp.bfloat16), 'expert', scatter_dimen...]
    pallas_call x0 -> x11, Pallas kernels: none -> 193 us  [the longest x2 64.2 us: blend(): pl.pallas_call(functools.partial(blend_kernel, 4, groups, multiply), in_s...]
    ppermute x14 -> x0, waiting for transfers between devices: 97.2 us -> none  [from_behind(): return lax.ppermute(shard, axis, pairs)]
    psum x4 -> x1, waiting for transfers between devices: 85.6 us -> 0.01 us  [dense_layer(): grad_router, grad_norm2 = lax.psum((grad_router, grad_norm2), 'expert')]
    pallas_call x2 -> x3, Pallas kernels: 95.3 us -> 148 us  [gather_all(): pl.pallas_call(gather_kernel, out_shape=jax.ShapeDtypeStruct((8, rows, wi...]
    dot_general x21 -> x5, matrix products: 56.6 us -> 7.51 us  [the longest x1 3.88 us: dense_layer(): jnp.dot(grad_logits, w_router.T, preferred_element_type=f32)]
    ppermute x14 -> x0, starting transfers between devices: 46.7 us -> none  [from_behind(): return lax.ppermute(shard, axis, pairs)]
    all_gather x1 -> x0, blocking collectives: 30.6 us -> none  [on_device_dense(): all_routes = lax.all_gather(routes, 'expert', axis=0, tiled=True)]
  transfers between devices with their start and end apart: 22 -> 1, of which waited for: 16 -> 0; matrix products, arithmetic and copies ran while one was open for 8% -> 3% of each run, Pallas kernels for 13% -> 27%
where the time goes in v2:
time: 608 us; the launch traced here: 599 us
  Pallas kernels  500 us (82%)
  blocking collectives  35.7 us (6%)
  local copies, waits for them, and re-layouts  22.3 us (4%)
  other arithmetic  18.8 us (3%)
  between operations  14.6 us (2%)
  matrix products  7.51 us (1%)
    pallas_call x3, Pallas kernels, gather_all(): pl.pallas_call(gather_kernel, out_shape=jax.ShapeDtypeStruct((8, rows, wi...  148 us
    pallas_call x1, Pallas kernels, scatter_sum(): pl.pallas_call(scatter_kernel, out_shape=jax.ShapeDtypeStruct((rows, widt...  108 us
    pallas_call x2, Pallas kernels, blend(): pl.pallas_call(functools.partial(blend_kernel, 4, groups, multiply), in_s...  64.2 us
    pallas_call x2, Pallas kernels, deliver(): pl.pallas_call(functools.partial(deliver_kernel, add_up), in_specs=[VM],...  58.5 us
    pallas_call x1, Pallas kernels, moe(): pl.pallas_call(moe_kernel, grid_spec=pltpu.PrefetchScalarGridSpec(num_sca...  41.1 us
    psum x1, blocking collectives, dense_layer(): grad_norm1, wide = lax.psum((grad_norm1, wide), 'expert')  35.7 us
    unnamed x55, local copies, waits for them, and re-layouts  16.8 us
    pallas_call x1, Pallas kernels, settle(): pl.pallas_call(settle_kernel, in_specs=[VM] * 9, out_specs=[VM] * 2, out_...  15.1 us
  transfers between devices with their start and end apart: 1, of which 0 were waited for; matrix products, arithmetic and copies ran while one was open for 3% of the time, Pallas kernels for 27%

profile of v2, /device:TPU:0, one launch (start us, length us, event | category | flops | bytes accessed | tf_op | source)
XLA Modules:
  0.0 598.8 jit_solution(13761528145747640390)
XLA Ops:
  7.2 0.0 all-reduce.4.cloned.1.call-start
  7.3 0.7 convert_reduce_fusion
  8.0 0.0 copy-start.17
  8.0 50.0 %shard_map.263 = bf16[8,256,2048]{2,1,0:T(8,128)(2,1)} custom-call(bf16[256,2048]{1,0:T(8,128)(2,1)} %own.1), custom_call_target="tpu_custom_call" | custom-call | tf_op jit(solution)/shard_map/pallas_call | solution.py:225
  58.1 0.4 copy.48.segc_ref
  58.5 1.1 constant_dynamic-slice_fusion.2
  59.5 1.3 constant_dynamic-slice_fusion
  60.8 0.8 dynamic-slice_bitcast_fusion
  61.6 3.7 fusion.14
  65.3 0.2 pad_maximum_fusion.w_ref
  65.6 0.0 copy-start.18
  65.6 0.6 pad_maximum_fusion.1
  66.2 0.1 copy-done.18
  66.3 13.0 %shard_map.264 = (bf16[2048,2048]{1,0:T(8,128)(2,1)}, bf16[2048,128]{1,0:T(8,128)(2,1)S(1)}, bf16[2048,128]{1,0:T(8,128)(2,1)S(1)}, bf16[2048,128]{1,0:T(8,128)(...) custom-call(bf16[2048,2048]{1,0:T(8,128)(2,1)} %bitcast.45, f32[1,2048]{1,0:T(1,128)S(1)} %bitcast.39, ...), custom_call_target="tpu_custom_call" | custom-call | tf_op jit(solution)/shard_map/pallas_call | solution.py:569
  79.2 1.0 copy-done.12
  80.2 1.0 copy-done.14
  81.2 3.6 shard_map.265.part_ref
  84.8 0.8 copy-done.6
  85.6 0.8 copy-done.8
  86.4 0.8 copy-done.10
  87.1 23.8 %shard_map.266 = (bf16[256,2048]{1,0:T(8,128)(2,1)S(1)}, bf16[256,512]{1,0:T(8,128)(2,1)S(1)}) custom-call(bf16[4,256,128]{2,1,0:T(8,128)(2,1)S(1)} %shard_map.265.part_ref, bf16[512,2048]{1,0:T(8,128)(2,1)S(1)} %copy-done.2), custom_call_target="tpu_custom_call" | custom-call | tf_op jit(solution)/shard_map/pallas_call | solution.py:812
  110.9 0.4 multiply_reduce_fusion.2
  111.4 2.6 multiply_convert_fusion.own
  114.0 48.9 %shard_map.267 = bf16[8,256,2048]{2,1,0:T(8,128)(2,1)} custom-call(bf16[256,2048]{1,0:T(8,128)(2,1)} %multiply_convert_fusion.own), custom_call_target="tpu_custom_call" | custom-call | tf_op jit(solution)/shard_map/pallas_call | solution.py:225
  162.9 0.1 copy.49
  163.0 2.3 fusion.11.own
  165.3 48.9 %shard_map.268 = bf16[8,256,2176]{2,1,0:T(8,128)(2,1)} custom-call(bf16[256,2176]{1,0:T(8,128)(2,1)} %fusion.11.own), custom_call_target="tpu_custom_call" | custom-call | tf_op jit(solution)/shard_map/pallas_call | solution.py:225
  214.3 1.0 copy.50.wr_ref
  215.3 41.1 %shard_map.269 = (bf16[2048,512]{1,0:T(8,128)(2,1)}, bf16[2048,1024]{1,0:T(8,128)(2,1)}, bf16[2048,4224]{1,0:T(8,128)(2,1)}) custom-call(s32[1]{0:T(128)} %bitcast.6.first, bf16[2048,2048]{1,0:T(8,128)(2,1)} %bitcast.43, bf16[2048,2176]{1,0:T(8,128)(2,1)} %bitcast.40, bf16[2048,2176]{1,0:T(8,128)(2,1)} %bitcast.41, bf16[2048,16]{1,0:T(8,128)(2,1)} %copy.50.wr_ref, ...), custom_call_target="tpu_custom_call" | custom-call | tf_op jit(solution)/shard_map/pallas_call | solution.py:492
  256.4 108.4 %shard_map.270 = bf16[256,4224]{1,0:T(8,128)(2,1)S(1)} custom-call(bf16[8,256,4224]{2,1,0:T(8,128)(2,1)} %bitcast.46), custom_call_target="tpu_custom_call" | custom-call | tf_op jit(solution)/shard_map/pallas_call | solution.py:419
  364.7 1.3 copy-done.4
  366.1 0.1 copy.51
  366.2 0.5 fusion.18
  366.7 0.2 fusion.16
  366.9 0.3 multiply_reduce_fusion.3
  367.1 0.2 multiply_convert_fusion.1
  367.4 0.9 fusion.19
  368.3 0.0 all-reduce.4.cloned.1.call-update
  368.3 3.9 multiply_reduce_fusion
  372.2 4.8 multiply_add_fusion
  377.0 1.3 copy-done.21
  378.3 1.5 convolution_convert_fusion.1.g_ref
  379.8 14.8 %shard_map.271.g_ref = bf16[4,256,128]{2,1,0:T(8,128)(2,1)} custom-call(bf16[256,512]{1,0:T(8,128)(2,1)} %convolution_convert_fusion.1.g_ref), custom_call_target="tpu_custom_call" | custom-call | tf_op jit(solution)/shard_map/pallas_call | solution.py:861
  394.6 1.0 copy-done.11
  395.7 0.9 copy-done.16
  396.6 6.0 %shard_map.272 = (f32[4,256,128]{2,1,0:T(8,128)S(1)}, f32[4,256,256]{2,1,0:T(8,128)S(1)}, bf16[4,256,256]{2,1,0:T(8,128)(2,1)S(1)}) custom-call(bf16[2048,128]{1,0:T(8,128)(2,1)S(1)} %copy-done.7, bf16[2048,128]{1,0:T(8,128)(2,1)S(1)} %copy-done.9, bf16[2048,128]{1,0:T(8,128)(2,1)S(1)} %copy-done.11, s32[2048,1]{1,0:T(8,128)S(1)} %copy.48.segc_ref, ...), custom_call_target="tpu_custom_call" | custom-call | tf_op jit(solution)/shard_map/pallas_call | solution.py:639
  402.7 15.1 %shard_map.273 = (bf16[4,256,384]{2,1,0:T(8,128)(2,1)S(1)}, f32[2,128]{1,0:T(2,128)S(1)}) custom-call(f32[4,256,128]{2,1,0:T(8,128)S(1)} %get-tuple-element.38.dq_ref, f32[4,256,256]{2,1,0:T(8,128)S(1)} %get-tuple-element.39.own_ref, bf16[4,256,256]{2,1,0:T(8,128)(2,1)S(1)} %get-tuple-element.40.other_ref, f32[2048,128]{1,0:T(8,128)S(1)} %copy-done.13, ...), custom_call_target="tpu_custom_call" | custom-call | tf_op jit(solution)/shard_map/pallas_call | solution.py:688
  417.8 40.5 %shard_map.274 = (bf16[256,2048]{1,0:T(8,128)(2,1)S(1)}, bf16[256,1536]{1,0:T(8,128)(2,1)}) custom-call(bf16[4,256,384]{2,1,0:T(8,128)(2,1)S(1)} %get-tuple-element.43.part_ref.raw_ref, bf16[2048,512]{1,0:T(8,128)(2,1)S(1)} %copy-done.5, bf16[2048,512]{1,0:T(8,128)(2,1)} %refs_1_.1, bf16[2048,512]{1,0:T(8,128)(2,1)} %refs_2_.1), custom_call_target="tpu_custom_call" | custom-call | tf_op jit(solution)/shard_map/pallas_call | solution.py:812
  458.3 0.0 copy-start.22
  458.3 0.8 fusion.8
  459.1 0.8 copy-done.22
  459.9 2.0 fusion.6
  461.8 3.4 copy-done.1
  465.2 4.4 shard_map.275
  469.6 29.5 %shard_map.276 = f32[3,256,512]{2,1,0:T(8,128)S(1)} custom-call(bf16[8,256,384]{2,1,0:T(8,128)(2,1)S(1)} %bitcast.34), custom_call_target="tpu_custom_call" | custom-call | tf_op jit(solution)/shard_map/pallas_call | solution.py:952
  499.1 1.2 slice_bitcast_fusion
  500.3 0.7 convolution_convert_fusion
  501.0 29.0 %shard_map.277 = f32[256,512]{1,0:T(8,128)S(1)} custom-call(bf16[8,256,512]{2,1,0:T(8,128)(2,1)S(1)} %bitcast.33), custom_call_target="tpu_custom_call" | custom-call | tf_op jit(solution)/shard_map/pallas_call | solution.py:952
  530.0 1.0 copy.54
  531.0 13.6 %shard_map.278 = (f32[2,2048,256]{2,1,0:T(8,128)}, f32[2,2048,256]{2,1,0:T(8,128)}) custom-call(bf16[2048,2048]{1,0:T(8,128)(2,1)} %bitcast.44, bf16[2048,1024]{1,0:T(8,128)(2,1)} %get-tuple-element.48.b_ref), custom_call_target="tpu_custom_call" | custom-call | tf_op jit(solution)/shard_map/pallas_call | solution.py:526
  544.7 9.2 %shard_map.279 = f32[512,2048]{1,0:T(8,128)} custom-call(bf16[2048,512]{1,0:T(8,128)(2,1)} %get-tuple-element.51.a_ref, bf16[2048,2176]{1,0:T(8,128)(2,1)} %bitcast.42), custom_call_target="tpu_custom_call" | custom-call | tf_op jit(solution)/shard_map/pallas_call | solution.py:506
  553.8 35.7 %all-reduce.1 = (f32[2048]{0:T(1024)}, f32[2,512]{1,0:T(2,128)S(1)}, f32[2048]{0:T(1024)}) all-reduce(f32[2048]{0:T(1024)S(1)} %get-tuple-element.110, f32[2,512]{1,0:T(2,128)S(1)} %constant_dynamic-update-slice_fusion, f32[2048]{0:T(1024)S(1)} %get-tuple-element.108), channel_id=1, replica_groups=mesh['expert'=8,'head'=4] {'expert'}, use_global_device_ids=true, to_apply=%region_9.10 | all-reduce | flops 5120 | bytes 40960 | tf_op jit(solution)/shard_map/psum | solution.py:1321
  589.6 0.6 fusion.17
  590.2 1.6 copy.59
  (49 shorter events, 0.1 us)
Async XLA Ops:
  7.2 583.0 %all-reduce.4.cloned.1.call-start = ((), (), s32[]{:S(2)}) async-start(), calls=%async_computation | async-start | bytes 262144 | tf_op jit(solution)/shard_map/psum | solution.py:1297
  8.0 50.1 %copy-start.17 = (s32[2048]{0:T(1024)S(1)}, s32[2048]{0:T(1024)}, u32[]{:S(2)}) copy-start(s32[2048]{0:T(1024)} %param.30) | copy-start | bytes 24580
  65.6 0.7 copy-start.18
  66.2 13.0 %copy-start = (f32[2048,128]{1,0:T(8,128)}, f32[2048,128]{1,0:T(8,128)S(1)}, u32[]{:S(2)}) copy-start(f32[2048,128]{1,0:T(8,128)S(1)} %get-tuple-element.134.sin_ref) | copy-start | bytes 3145732
  79.2 1.0 copy-start.12
  80.2 1.0 copy-start.14
  81.2 6.0 copy-start.2
  81.2 29.7 %copy-start.19 = (bf16[256,2048]{1,0:T(8,128)(2,1)S(1)}, bf16[256,2048]{1,0:T(8,128)(2,1)}, u32[]{:S(2)}) copy-start(bf16[256,2048]{1,0:T(8,128)(2,1)} %own.1) | copy-start | bytes 3145732
  84.8 0.8 copy-start.6
  85.6 0.8 copy-start.8
  86.3 0.8 copy-start.10
  87.1 24.2 %copy-start.25 = (f32[2048]{0:T(1024)S(1)}, f32[2048]{0:T(1024)}, u32[]{:S(2)}) copy-start(f32[2048]{0:T(1024)} %param.24) | copy-start | bytes 24580
  165.3 48.9 %copy-start.24 = (bf16[2048,16]{0,1:T(8,128)(2,1)S(1)}, bf16[2048,16]{0,1:T(8,128)(2,1)}, u32[]{:S(2)}) copy-start(bf16[2048,16]{0,1:T(8,128)(2,1)} %param.25) | copy-start | bytes 196612
  256.4 109.8 %copy-start.23 = (bf16[256,2048]{1,0:T(8,128)(2,1)S(1)}, bf16[256,2048]{1,0:T(8,128)(2,1)}, u32[]{:S(2)}) copy-start(bf16[256,2048]{1,0:T(8,128)(2,1)} %multiply_convert_fusion.own) | copy-start | bytes 3145732
  364.7 1.3 copy-start.4
  372.2 6.1 %copy-start.3 = (bf16[512,2048]{1,0:T(8,128)(2,1)S(1)}, bf16[512,2048]{1,0:T(8,128)(2,1)}, u32[]{:S(2)}) copy-start(bf16[512,2048]{1,0:T(8,128)(2,1)} %refs_0_.2) | copy-start | bytes 6291460
  377.0 1.3 copy-start.21
  378.3 16.3 %copy-start.7 = (bf16[2048,128]{1,0:T(8,128)(2,1)S(1)}, bf16[2048,128]{1,0:T(8,128)(2,1)}, u32[]{:S(2)}) copy-start(bf16[2048,128]{1,0:T(8,128)(2,1)} %copy-done.6) | copy-start | bytes 1572868
  378.3 16.3 %copy-start.9 = (bf16[2048,128]{1,0:T(8,128)(2,1)S(1)}, bf16[2048,128]{1,0:T(8,128)(2,1)}, u32[]{:S(2)}) copy-start(bf16[2048,128]{1,0:T(8,128)(2,1)} %copy-done.8) | copy-start | bytes 1572868
  394.6 1.0 copy-start.11
  395.7 0.9 copy-start.16
  396.6 6.0 %copy-start.13 = (f32[2048,128]{1,0:T(8,128)S(1)}, f32[2048,128]{1,0:T(8,128)}, u32[]{:S(2)}) copy-start(f32[2048,128]{1,0:T(8,128)} %copy-done.12) | copy-start | bytes 3145732
  396.6 6.0 %copy-start.15 = (f32[2048,128]{1,0:T(8,128)S(1)}, f32[2048,128]{1,0:T(8,128)}, u32[]{:S(2)}) copy-start(f32[2048,128]{1,0:T(8,128)} %copy-done.14) | copy-start | bytes 3145732
  402.7 15.1 %copy-start.5 = (bf16[2048,512]{1,0:T(8,128)(2,1)S(1)}, bf16[2048,512]{1,0:T(8,128)(2,1)}, u32[]{:S(2)}) copy-start(bf16[2048,512]{1,0:T(8,128)(2,1)} %refs_0_.3) | copy-start | bytes 6291460
  417.8 40.5 %copy-start.20 = (bf16[256,2048]{1,0:T(8,128)(2,1)S(1)}, bf16[256,2048]{1,0:T(8,128)(2,1)}, u32[]{:S(2)}) copy-start(bf16[256,2048]{1,0:T(8,128)(2,1)} %own.1) | copy-start | bytes 3145732
  458.3 1.6 copy-start.22
  461.8 3.4 copy-start.1
Sparse Core Ops, SparseCore 0:
  368.5 74.5 all-reduce.3

commit v3 on v2

--- a/solution.py
+++ b/solution.py
@@ -605,94 +605,6 @@
     )(q, k, v, segc, segr)
 
 
-def attend_back_kernel(q_ref, k_ref, v_ref, segc_ref, segr_ref, g_ref, dq_ref, own_ref, other_ref, dk, dv):
-    parity = lax.axis_index("expert") % 2
-    for r in (3, 2, 1, 0):
-        keys = (2 * r + 2) * BLOCK
-        start = pl.multiple_of(block_of(r, parity) * BLOCK, BLOCK)
-        q = q_ref[pl.ds(start, BLOCK)]
-        g = g_ref[r]
-        probs = probabilities(r, start, q, k_ref, segc_ref, segr_ref)
-        gv = dot_tn(probs.astype(bf16), g)
-        gp = dot_nt(g, v_ref[:keys])
-        gs = (probs * (gp - jnp.sum(gp * probs, -1, keepdims=True))).astype(bf16)
-        dq_ref[r] = dot(gs, k_ref[:keys]) * (HD ** -0.5)
-        gk = dot_tn(gs, q) * (HD ** -0.5)
-        if r == 3:
-            dv[...] = gv
-            dk[...] = gk
-        else:
-            dv[:keys] += gv
-            dk[:keys] += gk
-    for r in range(4):
-        mine = pl.ds(pl.multiple_of(block_of(r, parity) * BLOCK, BLOCK), BLOCK)
-        other = pl.ds(pl.multiple_of(block_of(r, 1 - parity) * BLOCK, BLOCK), BLOCK)
-        own_ref[r, :, :HD] = dk[mine]
-        own_ref[r, :, HD:] = dv[mine]
-        other_ref[r, :, :HD] = dk[other].astype(bf16)
-        other_ref[r, :, HD:] = dv[other].astype(bf16)
-
-
-def attend_back(q, k, v, segc, segr, g):
-    T = q.shape[0]
-    sd = jax.ShapeDtypeStruct
-    return pl.pallas_call(
-        attend_back_kernel, in_specs=[VM] * 6, out_specs=[VM] * 3,
-        out_shape=[sd((4, BLOCK, HD), f32), sd((4, BLOCK, 2 * HD), f32), sd((4, BLOCK, 2 * HD), bf16)],
-        scratch_shapes=[pltpu.VMEM((T, HD), f32), pltpu.VMEM((T, HD), f32)],
-        compiler_params=pltpu.CompilerParams(vmem_limit_bytes=48 * 2**20),
-    )(q, k, v, segc, segr, g)
-
-
-def settle_kernel(dq_ref, own_ref, other_ref, qr_ref, kr_ref, qg_ref, kg_ref, cos_ref, sin_ref,
-                  raw_ref, gains_ref, arrived, send, recv):
-    z, y, x, core = place()
-    barrier = pltpu.get_barrier_semaphore()
-    partner = device(z, 1 - y, x, core)
-    pl.semaphore_signal(barrier, inc=1, device_id=partner, device_id_type=MESH)
-    pl.semaphore_wait(barrier, 1)
-    copies = []
-    for r in range(4):
-        copy = pltpu.make_async_remote_copy(
-            src_ref=other_ref.at[r], dst_ref=arrived.at[r], send_sem=send.at[r], recv_sem=recv.at[r],
-            device_id=partner, device_id_type=MESH)
-        copy.start()
-        copies.append(copy)
-    gain_sums = [jnp.zeros((1, HD), f32), jnp.zeros((1, HD), f32)]
-
-    def back(turned, raw, gain, which, cosine, sine):
-        g = turned * cosine - pltpu.roll(turned, HD // 2, 1) * sine
-        factor = norm_factor(raw)
-        n = raw * factor
-        gain_sums[which] = gain_sums[which] + jnp.sum(g * n, 0, keepdims=True)
-        g = g * gain
-        return (factor * (g - n * jnp.mean(g * n, -1, keepdims=True))).astype(bf16)
-
-    for r in range(4):
-        rows = pl.ds(pl.multiple_of(block_of(r, y) * BLOCK, BLOCK), BLOCK)
-        raw_ref[r, :, :HD] = back(dq_ref[r], qr_ref[rows], qg_ref[...], 0, cos_ref[rows], sin_ref[rows])
-    for r in range(4):
-        rows = pl.ds(pl.multiple_of(block_of(r, y) * BLOCK, BLOCK), BLOCK)
-        copies[r].wait_recv()
-        dk = own_ref[r, :, :HD] + arrived[r, :, :HD].astype(f32)
-        raw_ref[r, :, HD:2 * HD] = back(dk, kr_ref[rows], kg_ref[...], 1, cos_ref[rows], sin_ref[rows])
-        raw_ref[r, :, 2 * HD:] = (own_ref[r, :, HD:] + arrived[r, :, HD:].astype(f32)).astype(bf16)
-    gains_ref[0:1] = gain_sums[0]
-    gains_ref[1:2] = gain_sums[1]
-    for copy in copies:
-        copy.wait_send()
-
-
-def settle(dq, own, other, qr, kr, qg, kg, cosine, sine, number):
-    sd = jax.ShapeDtypeStruct
-    return pl.pallas_call(
-        settle_kernel, in_specs=[VM] * 9, out_specs=[VM] * 2,
-        out_shape=[sd((4, BLOCK, 3 * HD), bf16), sd((2, HD), f32)],
-        scratch_shapes=[pltpu.VMEM((4, BLOCK, 2 * HD), bf16), pltpu.SemaphoreType.DMA((4,)), pltpu.SemaphoreType.DMA((4,))],
-        compiler_params=pltpu.CompilerParams(collective_id=number, has_side_effects=True, vmem_limit_bytes=48 * 2**20),
-    )(dq, own, other, qr, kr, qg, kg, cosine, sine)
-
-
 def greet_owners(z, y, x, core, sources):
     barrier = pltpu.get_barrier_semaphore()
     for r in range(4):
@@ -823,139 +735,368 @@
     )(parts, *weights)
 
 
-def hand_back_kernel(g_ref, out_ref, send, recv, local):
+def masked_probs(b, q, k_ref, segc_ref, segr_ref):
+    keys = (b + 1) * BLOCK
+    scores = dot_nt(q, k_ref[:keys]) * (HD ** -0.5)
+    rows = b * BLOCK + lax.broadcasted_iota(jnp.int32, scores.shape, 0)
+    columns = lax.broadcasted_iota(jnp.int32, scores.shape, 1)
+    same = segc_ref[b * BLOCK:keys] == segr_ref[:, :keys]
+    scores = jnp.where((rows >= columns) & same, scores, -1000000000.0)
+    raised = jnp.exp(scores - jnp.max(scores, -1, keepdims=True))
+    return raised / jnp.sum(raised, -1, keepdims=True)
+
+
+def far_first(z):
+    ahead = z // 2
+    return (3 - 3 * ahead, 2 - ahead, z + 1 - 2 * (z % 2), z)
+
+
+def greet_peers(z, y, x, core, others):
+    barrier = pltpu.get_barrier_semaphore()
+
+    def signal(where):
+        pl.semaphore_signal(barrier, inc=1, device_id=where, device_id_type=MESH)
+
+    for n in range(4):
+        pl.when(z != n)(lambda: signal(device(n, y, x, core)))
+        pl.when(z != n)(lambda: signal(device(n, 1 - y, x, core)))
+    signal(device(z, 1 - y, x, core))
+    for where in others:
+        signal(where)
+    pl.semaphore_wait(barrier, 7 + len(others))
+
+
+def heads_back_kernel(ga_ref, w_ref, ctx_ref, q_ref, k_ref, v_ref, segc_ref, segr_ref, qr_ref, kr_ref, qg_ref, kg_ref,
+                      cos_ref, sin_ref, small_ref, raw_ref, gains_ref, wout_ref, small_out,
+                      g_own, g_all, dk, dv, terms, from_y, held, from_z, small_y, small_sum, small_z,
+                      send, recv, y_send, y_recv, z_send, z_recv, s_send, s_recv):
     z, y, x, core = place()
-    source_y = (y + z) % 2
-    barrier = pltpu.get_barrier_semaphore()
-    for r in range(4):
-        def signal():
-            pl.semaphore_signal(barrier, inc=1, device_id=device(r, y if r % 2 == 0 else 1 - y, x, core), device_id_type=MESH)
-        pl.when((z != r) | (z % 2 == 1))(signal)
-    pl.semaphore_wait(barrier, 3 + z % 2)
-
-    def remote(n):
+    me = z * 2 + y
+    across, twin, corner = device(z, y, 1 - x, core), device(z, y, x, 1 - core), device(z, y, 1 - x, 1 - core)
+    partner = device(z, 1 - y, x, core)
+    greet_peers(z, y, x, core, (across, twin, corner))
+
+    def remote(source, target, ssem, rsem, where):
         return pltpu.make_async_remote_copy(
-            src_ref=g_ref.at[:, pl.ds(n * HD, HD)], dst_ref=out_ref.at[z], send_sem=send.at[n], recv_sem=recv.at[z],
-            device_id=device(n, source_y, x, core), device_id_type=MESH)
-
-    def arriving(r):
+            src_ref=source, dst_ref=target, send_sem=ssem, recv_sem=rsem, device_id=where, device_id_type=MESH)
+
+    quarter = small_ref.shape[1] // 4
+
+    def lanes(cx, cc):
+        return pl.ds(pl.multiple_of((cx * 2 + cc) * quarter, quarter), quarter)
+
+    own_lanes = lanes(x, core)
+    small_pair = remote(small_ref.at[:, own_lanes], small_y, s_send.at[0], s_recv.at[0], partner)
+    small_pair.start()
+
+    g_context = dot_nt(ga_ref[...], w_ref[...]).astype(bf16)
+    for n in range(4):
+        g_own[n] = g_context[:, n * HD:(n + 1) * HD]
+
+    def to_head(n, yt):
+        return remote(g_own.at[n], g_all.at[me], send.at[n * 2 + yt], recv.at[me], device(n, yt, x, core))
+
+    def from_block(b):
+        return remote(g_own.at[b // 2], g_all.at[b], send.at[b], recv.at[b], device(b // 2, b % 2, x, core))
+
+    for b in range(8):
+        pl.when(me != b)(lambda: to_head(b // 2, b % 2).start())
+    g_all[me] = g_own[z]
+
+    for b in range(8):
+        terms[b] = dot_tn(ga_ref[:, b * BLOCK:(b + 1) * BLOCK], ctx_ref[...]).astype(bf16)
+    order = far_first(z)
+
+    def term_pair(n):
+        return remote(terms.at[n * 2 + 1 - y], from_y.at[n], y_send.at[n], y_recv.at[n], partner)
+
+    def term_along(n):
+        return remote(held.at[n], from_z.at[z], z_send.at[n], z_recv.at[z], device(n, y, x, core))
+
+    def term_arriving(n):
+        return remote(held.at[n], from_z.at[n], z_send.at[n], z_recv.at[n], device(n, y, x, core))
+
+    for n in order:
+        term_pair(n).start()
+
+    def small_along(n):
+        return remote(small_sum, small_z.at[z], s_send.at[1 + n], s_recv.at[1 + z], device(n, y, x, core))
+
+    def small_arriving(n):
+        return remote(small_sum, small_z.at[n], s_send.at[1 + n], s_recv.at[1 + n], device(n, y, x, core))
+
+    def small_spread(i):
+        where = (across, twin, corner)[i]
+        return remote(small_out.at[:, own_lanes], small_out.at[:, own_lanes], s_send.at[5 + i], s_recv.at[5 + i], where)
+
+    def small_spread_in(i):
+        theirs = (lanes(1 - x, core), lanes(x, 1 - core), lanes(1 - x, 1 - core))[i]
+        where = (across, twin, corner)[i]
+        return remote(small_out.at[:, own_lanes], small_out.at[:, theirs], s_send.at[5 + i], s_recv.at[5 + i], where)
+
+    for b in range(8):
+        pl.when(me != b)(lambda: from_block(b).wait_recv())
+
+    gain_sums = [jnp.zeros((1, HD), f32), jnp.zeros((1, HD), f32)]
+
+    def back(turned, b, raw_in, gain, which):
+        rows = slice(b * BLOCK, (b + 1) * BLOCK)
+        g = turned * cos_ref[rows] - pltpu.roll(turned, HD // 2, 1) * sin_ref[rows]
+        raw = raw_in[rows]
+        factor = norm_factor(raw)
+        n = raw * factor
+        gain_sums[which] = gain_sums[which] + jnp.sum(g * n, 0, keepdims=True)
+        g = g * gain[...]
+        return (factor * (g - n * jnp.mean(g * n, -1, keepdims=True))).astype(bf16)
+
+    for b in range(7, -1, -1):
+        keys = (b + 1) * BLOCK
+        q = q_ref[b * BLOCK:keys]
+        g = g_all[b]
+        probs = masked_probs(b, q, k_ref, segc_ref, segr_ref)
+        gv = dot_tn(probs.astype(bf16), g)
+        gp = dot_nt(g, v_ref[:keys])
+        gs = (probs * (gp - jnp.sum(gp * probs, -1, keepdims=True))).astype(bf16)
+        gk = dot_tn(gs, q)
+        if b == 7:
+            dv[...] = gv
+            dk[...] = gk
+        else:
+            dv[:keys] += gv
+            dk[:keys] += gk
+        raw_ref[b, :, :HD] = back(dot(gs, k_ref[:keys]) * (HD ** -0.5), b, qr_ref, qg_ref, 0)
+        if b == 5:
+            small_pair.wait_recv()
+            small_sum[...] = small_ref[:, own_lanes] + small_y[...]
+            for n in range(4):
+                pl.when(z != n)(lambda: small_along(n).start())
+            small_z[z] = small_sum[...]
+        if b in (4, 3, 2):
+            n = order[4 - b]
+            term_pair(n).wait_recv()
+            held[n] = (terms[n * 2 + y].astype(f32) + from_y[n].astype(f32)).astype(bf16)
+            term_along(n).start()
+        if b == 1:
+            for n in range(4):
+                pl.when(z != n)(lambda: small_arriving(n).wait_recv())
+            small_out[:, own_lanes] = (small_z[0] + small_z[1]) + (small_z[2] + small_z[3])
+            for i in range(3):
+                small_spread(i).start()
+    term_pair(z).wait_recv()
+    from_z[z] = (terms[me].astype(f32) + from_y[z].astype(f32)).astype(bf16)
+    for b in range(8):
+        rows = slice(b * BLOCK, (b + 1) * BLOCK)
+        raw_ref[b, :, HD:2 * HD] = back(dk[rows] * (HD ** -0.5), b, kr_ref, kg_ref, 1)
+        raw_ref[b, :, 2 * HD:] = dv[rows].astype(bf16)
+    gains_ref[0:1] = gain_sums[0]
+    gains_ref[1:2] = gain_sums[1]
+    for n in range(4):
+        pl.when(z != n)(lambda: term_arriving(n).wait_recv())
+    wout_ref[...] = (from_z[0].astype(f32) + from_z[1].astype(f32)) + (from_z[2].astype(f32) + from_z[3].astype(f32))
+    for i in range(3):
+        small_spread_in(i).wait_recv()
+        small_spread(i).wait_send()
+    small_pair.wait_send()
+    for b in range(8):
+        pl.when(me != b)(lambda: to_head(b // 2, b % 2).wait_send())
+    for n in range(4):
+        term_pair(n).wait_send()
+        pl.when(z != n)(lambda: term_along(n).wait_send())
+        pl.when(z != n)(lambda: small_along(n).wait_send())
+
+
+def heads_back(ga, w, ctx, q, k, v, segc, segr, qr, kr, qg, kg, cosine, sine, small, number):
+    T, D = q.shape[0], ga.shape[1]
+    S = small.shape[0]
+    span = 4 * HD
+    sd = jax.ShapeDtypeStruct
+    dma = pltpu.SemaphoreType.DMA
+    return pl.pallas_call(
+        heads_back_kernel, in_specs=[VM] * 15, out_specs=[VM] * 4,
+        out_shape=[sd((8, BLOCK, 3 * HD), bf16), sd((2, HD), f32), sd((BLOCK, span), f32), sd((S, D), f32)],
+        scratch_shapes=[
+            pltpu.VMEM((4, BLOCK, HD), bf16), pltpu.VMEM((8, BLOCK, HD), bf16),
+            pltpu.VMEM((T, HD), f32), pltpu.VMEM((T, HD), f32),
+            pltpu.VMEM((8, BLOCK, span), bf16), pltpu.VMEM((4, BLOCK, span), bf16),
+            pltpu.VMEM((4, BLOCK, span), bf16), pltpu.VMEM((4, BLOCK, span), bf16),
+            pltpu.VMEM((S, D // 4), f32), pltpu.VMEM((S, D // 4), f32), pltpu.VMEM((4, S, D // 4), f32),
+            dma((8,)), dma((8,)), dma((4,)), dma((4,)), dma((4,)), dma((4,)), dma((8,)), dma((8,)),
+        ],
+        compiler_params=pltpu.CompilerParams(collective_id=number, has_side_effects=True, vmem_limit_bytes=56 * 2**20),
+    )(ga, w, ctx, q, k, v, segc, segr, qr, kr, qg, kg, cosine, sine, small)
+
+
+def finish_kernel(raw_ref, a_ref, wq_ref, wk_ref, wv_ref, gains_ref, hidden_ref, gain_ref, middle_ref,
+                  grad_ref, weights_ref, norm_ref, gains_out,
+                  columns, gathered, products, from_z, out_half, in_half, held, from_x, total, gains_in, norm_in,
+                  load, send, recv, w_send, w_recv, pair_send, pair_recv, g_send, g_recv, n_send, n_recv):
+    z, y, x, core = place()
+    me = z * 2 + y
+    across, twin = device(z, y, 1 - x, core), device(z, y, x, 1 - core)
+    greet_peers(z, y, x, core, (across, twin))
+    order = far_first(z)
+    span = 4 * HD
+
+    def remote(source, target, ssem, rsem, where):
         return pltpu.make_async_remote_copy(
-            src_ref=g_ref.at[:, pl.ds(r * HD, HD)], dst_ref=out_ref.at[r], send_sem=send.at[r], recv_sem=recv.at[r],
-            device_id=device(r, y if r % 2 == 0 else 1 - y, x, core), device_id_type=MESH)
-
-    def own(n):
-        return pltpu.make_async_copy(g_ref.at[:, pl.ds(n * HD, HD)], out_ref.at[n], local)
+            src_ref=source, dst_ref=target, send_sem=ssem, recv_sem=rsem, device_id=where, device_id_type=MESH)
+
+    def lanes(g, n):
+        return pl.ds(pl.multiple_of(g * span + n * HD, HD), HD)
+
+    def rows_to(n, g):
+        return remote(raw_ref.at[n * 2 + y, :, pl.ds(g * HD, HD)], gathered.at[:, lanes(g, z)],
+                      send.at[n, g], recv.at[z, g], device(n, y, x, core))
+
+    def rows_from(n, g):
+        return remote(raw_ref.at[n * 2 + y, :, pl.ds(g * HD, HD)], gathered.at[:, lanes(g, n)],
+                      send.at[n, g], recv.at[n, g], device(n, y, x, core))
+
+    def column_load(n):
+        block = pl.ds(pl.multiple_of((n * 2 + y) * BLOCK, BLOCK), BLOCK)
+        return pltpu.make_async_copy(a_ref.at[:, block], columns.at[n], load.at[n])
+
+    for n in order[:3]:
+        for g in range(3):
+            rows_to(n, g).start()
+    for n in order:
+        column_load(n).start()
+
+    def gains_to(n):
+        return remote(gains_ref, gains_in.at[z], g_send.at[n], g_recv.at[z], device(n, y, x, core))
+
+    def gains_from(n):
+        return remote(gains_ref, gains_in.at[n], g_send.at[n], g_recv.at[n], device(n, y, x, core))
 
     for n in range(4):
-        here = (z == n) & (z % 2 == 0)
-        pl.when(here)(lambda: own(n).start())
-        pl.when(jnp.logical_not(here))(lambda: remote(n).start())
+        pl.when(z != n)(lambda: gains_to(n).start())
+    gains_in[z] = gains_ref[...]
+    for g in range(3):
+        gathered[:, lanes(g, z)] = raw_ref[me, :, g * HD:(g + 1) * HD]
+
+    def products_to(n):
+        return remote(products.at[n], from_z.at[z], w_send.at[n], w_recv.at[z], device(n, y, x, core))
+
+    def products_from(n):
+        return remote(products.at[n], from_z.at[n], w_send.at[n], w_recv.at[n], device(n, y, x, core))
+
+    raw_all = raw_ref[...].reshape(8 * BLOCK, 3 * HD)
+    for i, n in enumerate(order):
+        column_load(n).wait()
+        product = dot_tn(columns[n], raw_all).astype(bf16)
+        if i < 3:
+            products[n] = product
+            products_to(n).start()
+        else:
+            from_z[z] = product
+
     for n in range(4):
-        here = (z == n) & (z % 2 == 0)
-        pl.when(here)(lambda: own(n).wait())
-        pl.when(jnp.logical_not(here))(lambda: arriving(n).wait_recv())
-        pl.when(jnp.logical_not(here))(lambda: remote(n).wait_send())
-
-
-def hand_back(g, number):
+        for g in range(3):
+            pl.when(z != n)(lambda: rows_from(n, g).wait_recv())
+
+    rows = total.shape[0]
+    half = rows // 2
+    chunk = half // 2
+    my_half = core * half
+    other_half = (1 - core) * half
+    piece = lambda c: pl.ds(c * chunk, chunk)
+    at = lambda base, c: pl.ds(pl.multiple_of(base + c * chunk, chunk), chunk)
+
+    def pair(kind, c, source, target, where):
+        return remote(source, target, pair_send.at[kind, c], pair_recv.at[kind, c], where)
+
+    def multiply(part):
+        return (dot_nt(part[:, :span], wq_ref[...]) + dot_nt(part[:, span:2 * span], wk_ref[...])
+                + dot_nt(part[:, 2 * span:], wv_ref[...]))
+
+    first = [pair(0, c, out_half.at[piece(c)], in_half.at[piece(c)], twin) for c in range(2)]
+    second = [pair(1, c, held.at[piece(c)], from_x.at[piece(c)], across) for c in range(2)]
+    third = [pair(2, c, total.at[at(my_half, c)], total.at[at(my_half, c)], twin) for c in range(2)]
+    for c in range(2):
+        out_half[piece(c)] = multiply(gathered[at(other_half, c)]).astype(bf16)
+        first[c].start()
+    for c in range(2):
+        kept = multiply(gathered[at(my_half, c)])
+        first[c].wait_recv()
+        held[piece(c)] = (kept + in_half[piece(c)].astype(f32)).astype(bf16)
+        second[c].start()
+    for n in range(4):
+        pl.when(z != n)(lambda: products_from(n).wait_recv())
+    for n in range(4):
+        for g in range(3):
+            weights_ref[g, :, n * HD:(n + 1) * HD] = from_z[n, :, g * HD:(g + 1) * HD].astype(f32)
+    for n in range(4):
+        pl.when(z != n)(lambda: gains_from(n).wait_recv())
+        gains_out[:, n * HD:(n + 1) * HD] = gains_in[n]
+    for c in range(2):
+        second[c].wait_recv()
+        total[at(my_half, c)] = (held[piece(c)].astype(f32) + from_x[piece(c)].astype(f32)).astype(bf16)
+        third[c].start()
+    for c in range(2):
+        pair(2, c, total.at[at(my_half, c)], total.at[at(other_half, c)], twin).wait_recv()
+
+    norm_part = jnp.zeros((1, total.shape[1]), f32)
+    step = 32
+
+    def norm_rows(i, norm_part):
+        part = pl.ds(pl.multiple_of(i * step, step), step)
+        e = total[part].astype(f32)
+        v = hidden_ref[part].astype(f32)
+        factor = norm_factor(v)
+        n = v * factor
+        norm_part = norm_part + jnp.sum(e * n, 0, keepdims=True)
+        e = e * gain_ref[...]
+        grad_ref[part] = middle_ref[part] + factor * (e - n * jnp.mean(e * n, -1, keepdims=True))
+        return norm_part
+
+    norm_part = lax.fori_loop(0, rows // step, norm_rows, norm_part)
+    norm_in[me] = jnp.broadcast_to(norm_part, (8, total.shape[1]))
+
+    def norm_to(b):
+        return remote(norm_in.at[me], norm_in.at[me], n_send.at[b], n_recv.at[me], device(b // 2, b % 2, x, core))
+
+    def norm_from(b):
+        return remote(norm_in.at[b], norm_in.at[b], n_send.at[b], n_recv.at[b], device(b // 2, b % 2, x, core))
+
+    for b in range(8):
+        pl.when(me != b)(lambda: norm_to(b).start())
+    for b in range(8):
+        pl.when(me != b)(lambda: norm_from(b).wait_recv())
+    sums = [norm_in[b, 0:1] for b in range(8)]
+    norm_ref[...] = ((sums[0] + sums[1]) + (sums[2] + sums[3])) + ((sums[4] + sums[5]) + (sums[6] + sums[7]))
+
+    for c in range(2):
+        first[c].wait_send()
+        second[c].wait_send()
+        third[c].wait_send()
+    for b in range(8):
+        pl.when(me != b)(lambda: norm_to(b).wait_send())
+    for n in range(4):
+        for g in range(3):
+            pl.when(z != n)(lambda: rows_to(n, g).wait_send())
+        pl.when(z != n)(lambda: products_to(n).wait_send())
+        pl.when(z != n)(lambda: gains_to(n).wait_send())
+
+
+def finish(raw, a, wq, wk, wv, gains, hidden, gain, middle, number):
+    T, D = a.shape
+    rows, half = BLOCK, BLOCK // 2
+    span = 4 * HD
+    sd = jax.ShapeDtypeStruct
+    dma = pltpu.SemaphoreType.DMA
+    vm = pltpu.VMEM
     return pl.pallas_call(
-        hand_back_kernel, in_specs=[VM], out_specs=VM,
-        out_shape=jax.ShapeDtypeStruct((4, BLOCK, HD), bf16),
-        scratch_shapes=[pltpu.SemaphoreType.DMA((4,)), pltpu.SemaphoreType.DMA((4,)), pltpu.SemaphoreType.DMA],
-        compiler_params=pltpu.CompilerParams(collective_id=number, has_side_effects=True),
-    )(g)
-
-
-def grad_weight_kernel(parity, a_ref, raw_ref, out_ref, acc):
-    r = pl.program_id(0)
-    part = dot_tn(a_ref[...], raw_ref[0])
-
-    @pl.when(r == 0)
-    def _():
-        acc[...] = part
-
-    @pl.when(r > 0)
-    def _():
-        acc[...] += part
-
-    @pl.when(r == 3)
-    def _():
-        out_ref[...] = acc[...].astype(bf16)
-
-
-def grad_weight(parity, a, raw):
-    T, D = a.shape
-    W = raw.shape[2]
-    return pl.pallas_call(
-        grad_weight_kernel,
-        grid_spec=pltpu.PrefetchScalarGridSpec(
-            num_scalar_prefetch=1, grid=(4,),
-            in_specs=[pl.BlockSpec((BLOCK, D), lambda r, p: (2 * r + (r + p[0]) % 2, 0)),
-                      pl.BlockSpec((1, BLOCK, W), lambda r, p: (r, 0, 0))],
-            out_specs=pl.BlockSpec((D, W), lambda r, p: (0, 0)),
-            scratch_shapes=[pltpu.VMEM((D, W), f32)]),
-        out_shape=jax.ShapeDtypeStruct((D, W), bf16),
-        compiler_params=pltpu.CompilerParams(vmem_limit_bytes=40 * 2**20),
-    )(parity, a, raw)
-
-
-def deliver_kernel(add_up, part_ref, out_ref, held, from_y, from_z, send, recv, local):
-    z, y, x, core = place()
-    barrier = pltpu.get_barrier_semaphore()
-    partner = device(z, 1 - y, x, core)
-    pl.semaphore_signal(barrier, inc=1, device_id=partner, device_id_type=MESH)
-    for n in range(4):
-        pl.when(z != n)(lambda: pl.semaphore_signal(barrier, inc=1, device_id=device(n, y, x, core), device_id_type=MESH))
-    pl.semaphore_wait(barrier, 4)
-
-    def pair(n):
-        return pltpu.make_async_remote_copy(
-            src_ref=part_ref.at[n * 2 + 1 - y], dst_ref=from_y.at[n], send_sem=send.at[0, n], recv_sem=recv.at[0, n],
-            device_id=partner, device_id_type=MESH)
-
-    def along(n):
-        return pltpu.make_async_remote_copy(
-            src_ref=held.at[n], dst_ref=from_z.at[z], send_sem=send.at[1, n], recv_sem=recv.at[1, z],
-            device_id=device(n, y, x, core), device_id_type=MESH)
-
-    def arriving(n):
-        return pltpu.make_async_remote_copy(
-            src_ref=held.at[n], dst_ref=from_z.at[n], send_sem=send.at[1, n], recv_sem=recv.at[1, n],
-            device_id=device(n, y, x, core), device_id_type=MESH)
-
-    ahead = z // 2
-    order = (3 - 3 * ahead, 2 - ahead, z + 1 - 2 * (z % 2), z)
-    for n in order:
-        pair(n).start()
-    for i, n in enumerate(order):
-        pair(n).wait_recv()
-        held[n] = (part_ref[n * 2 + y].astype(f32) + from_y[n].astype(f32)).astype(bf16)
-        if i < 3:
-            along(n).start()
-    from_z[z] = held[z]
-    for n in range(4):
-        pl.when(z != n)(lambda: arriving(n).wait_recv())
-    if add_up:
-        out_ref[...] = (from_z[0].astype(f32) + from_z[1].astype(f32)) + (from_z[2].astype(f32) + from_z[3].astype(f32))
-    else:
-        for n in range(4):
-            for g in range(3):
-                out_ref[g, :, n * HD:(n + 1) * HD] = from_z[n, :, g * HD:(g + 1) * HD].astype(f32)
-    for n in range(4):
-        pair(n).wait_send()
-        pl.when(z != n)(lambda: along(n).wait_send())
-
-
-def deliver(parts, add_up, number):
-    _, rows, width = parts.shape
-    shape = (rows, width) if add_up else (3, rows, 4 * HD)
-    return pl.pallas_call(
-        functools.partial(deliver_kernel, add_up),
-        in_specs=[VM], out_specs=VM, out_shape=jax.ShapeDtypeStruct(shape, f32),
-        scratch_shapes=[pltpu.VMEM((4, rows, width), bf16)] * 3 + [
-            pltpu.SemaphoreType.DMA((2, 4)), pltpu.SemaphoreType.DMA((2, 4)), pltpu.SemaphoreType.DMA],
-        compiler_params=pltpu.CompilerParams(collective_id=number, has_side_effects=True, vmem_limit_bytes=48 * 2**20),
-    )(parts)
+        finish_kernel, in_specs=[VM, pl.BlockSpec(memory_space=pl.ANY)] + [VM] * 7, out_specs=[VM] * 4,
+        out_shape=[sd((rows, D), f32), sd((3, BLOCK, span), f32), sd((1, D), f32), sd((2, span), f32)],
+        scratch_shapes=[
+            vm((4, T, BLOCK), bf16), vm((rows, 3 * span), bf16), vm((4, BLOCK, 3 * HD), bf16), vm((4, BLOCK, 3 * HD), bf16),
+            vm((half, D), bf16), vm((half, D), bf16), vm((half, D), bf16), vm((half, D), bf16), vm((rows, D), bf16),
+            vm((4, 2, HD), f32), vm((8, 8, D), f32),
+            dma((4,)), dma((4, 3)), dma((4, 3)), dma((4,)), dma((4,)), dma((3, 2)), dma((3, 2)),
+            dma((4,)), dma((4,)), dma((8,)), dma((8,)),
+        ],
+        compiler_params=pltpu.CompilerParams(collective_id=number, has_side_effects=True, vmem_limit_bytes=56 * 2**20),
+    )(raw, a, wq, wk, wv, gains, hidden, gain, middle)
 
 
 def on_device(
@@ -1244,7 +1385,6 @@
     ff = w_gate.shape[2]
     my_index = lax.axis_index("expert")
     head = my_index // 2
-    parity = jnp.full((1,), 1, jnp.int32) * (my_index % 2)
 
     def own_head(v):
         return lax.dynamic_slice_in_dim(v, head * HEAD_DIM, HEAD_DIM, v.ndim - 1)
@@ -1289,48 +1429,37 @@
     grad_logits = (
         gate_weights * (grad_gates - jnp.sum(grad_gates * gate_weights, -1, keepdims=True))
     ).astype(bf16)
-    grad_router = jnp.dot(moe_input.T, grad_logits, preferred_element_type=f32)
     grad_moe_input = jnp.dot(grad_logits, w_router.T, preferred_element_type=f32)
     grad_moe_input = grad_moe_input + total[:, width : 2 * width].astype(f32)
-    grad_norm2 = jnp.sum(grad_moe_input * normed_moe, 0)
     grad_middle = grad_final + norm_back(grad_moe_input * norm2_gain, normed_moe, inverse_moe)
-    grad_router, grad_norm2 = lax.psum((grad_router, grad_norm2), "expert")
-
-    grad_attn = grad_middle.astype(bf16)
-    grad_context = jnp.dot(grad_attn, w_out.T, preferred_element_type=f32).astype(bf16)
-    head_grad = hand_back(grad_context, 6)
-    out_part = dot_tn(grad_attn, own_context).astype(bf16)
-    grad_w_out = deliver(out_part.reshape(devices, rows, -1), True, 7)
-    grad_q, own_kv, other_kv = attend_back(queries, keys, values, segc, segr, head_grad)
-    raw_grads, gains = settle(grad_q, own_kv, other_kv, q_raw, k_raw, q_gain, k_gain, cosine, sine, 8)
-
-    def back_through(a, w):
-        span = 4 * HEAD_DIM
-        return sum(dot_nt(a[:, g * span : (g + 1) * span], w[g][...]) for g in range(3))
-
-    grad_attn_input, _ = blend(raw_grads, [w_query, w_key, w_value], back_through, 9)
-    weight_part = grad_weight(parity, attn_all, raw_grads)
-    grad_qkv = deliver(weight_part.reshape(devices, rows, -1), False, 10)
-    grad_attn_input = grad_attn_input.astype(f32)
-    inverse_attn = inverse_rms(inputs)
-    normed_attn = inputs * inverse_attn
-    grad_norm1 = jnp.sum(grad_attn_input * normed_attn, 0)
-    grad_input = grad_middle + norm_back(grad_attn_input * norm1_gain, normed_attn, inverse_attn)
-    wide = jnp.zeros((2, query_gain.shape[0]), f32)
-    wide = lax.dynamic_update_slice_in_dim(wide, gains, head * HEAD_DIM, 1)
-    grad_norm1, wide = lax.psum((grad_norm1, wide), "expert")
+    small = jnp.concatenate(
+        [
+            lax.dot_general(grad_logits, moe_input, (((0,), (0,)), ((), ())), preferred_element_type=f32),
+            jnp.sum(grad_moe_input * normed_moe, 0, keepdims=True),
+            jnp.zeros((7, width), f32),
+        ],
+        0,
+    )
+
+    raw_grads, gains, grad_w_out, small = heads_back(
+        grad_middle.astype(bf16), w_out, own_context, queries, keys, values, segc, segr,
+        q_raw, k_raw, q_gain, k_gain, cosine, sine, small, 6,
+    )
+    grad_input, grad_qkv, grad_norm1, gains = finish(
+        raw_grads, attn_all, w_query, w_key, w_value, gains, hidden_in, norm1_gain[None], grad_middle, 7
+    )
     return (
         output,
         grad_input,
-        grad_norm1,
+        grad_norm1[0],
         grad_qkv[0],
         grad_qkv[1],
         grad_qkv[2],
         grad_w_out.T,
-        wide[0],
-        wide[1],
-        grad_norm2,
-        grad_router,
+        gains[0],
+        gains[1],
+        small[experts],
+        small[:experts].T,
         grad_gate,
         grad_up,
         grad_down,

time: 608 us -> 532 us (0.88)
  blocking collectives: 35.7 us -> 0 us
  between operations: 14.6 us -> 1.16 us
  other arithmetic: 18.8 us -> 12 us
    psum x1 -> x0, blocking collectives: 35.7 us -> none  [dense_layer(): grad_norm1, wide = lax.psum((grad_norm1, wide), 'expert')]
    pallas_call x2 -> x1, Pallas kernels: 64.2 us -> 29.7 us  [blend(): pl.pallas_call(functools.partial(blend_kernel, 4, groups, multiply), in_s...]
    pallas_call x6 -> x2, Pallas kernels: 98.8 us -> 122 us  [the longest x1 68.5 us: finish(): pl.pallas_call(finish_kernel, in_specs=[VM, pl.BlockSpec(memory_space=pl....]
    add x2 -> x0, other arithmetic: 6.73 us -> none  [the longest x1 4.77 us: dense_layer(): grad_final + norm_back(grad_moe_input * norm2_gain, normed_moe, inverse_moe)]
    unnamed x55 -> x58, local copies, waits for them, and re-layouts: 16.8 us -> 11 us
  transfers between devices with their start and end apart: 1 -> 0, of which waited for: 0 -> 0; matrix products, arithmetic and copies ran while one was open for 3% -> 0% of each run, Pallas kernels for 27% -> 0%
where the time goes in v3:
time: 532 us; the launch traced here: 529 us
  Pallas kernels  495 us (93%)
  local copies, waits for them, and re-layouts  19.2 us (4%)
  other arithmetic  12 us (2%)
    pallas_call x3, Pallas kernels, gather_all(): pl.pallas_call(gather_kernel, out_shape=jax.ShapeDtypeStruct((8, rows, wi...  153 us
    pallas_call x1, Pallas kernels, scatter_sum(): pl.pallas_call(scatter_kernel, out_shape=jax.ShapeDtypeStruct((rows, widt...  108 us
    pallas_call x1, Pallas kernels, finish(): pl.pallas_call(finish_kernel, in_specs=[VM, pl.BlockSpec(memory_space=pl....  68.5 us
    pallas_call x1, Pallas kernels, heads_back(): pl.pallas_call(heads_back_kernel, in_specs=[VM] * 15, out_specs=[VM] * 4,...  53.5 us
    pallas_call x1, Pallas kernels, moe(): pl.pallas_call(moe_kernel, grid_spec=pltpu.PrefetchScalarGridSpec(num_sca...  41.1 us
    pallas_call x1, Pallas kernels, blend(): pl.pallas_call(functools.partial(blend_kernel, 4, groups, multiply), in_s...  29.7 us
    pallas_call x1, Pallas kernels, expert_grads(): pl.pallas_call(expert_grads_kernel, grid=(D // bm,), in_specs=[pl.BlockSp...  13.6 us
    pallas_call x1, Pallas kernels, project(): pl.pallas_call(project_kernel, grid=(T // bt,), in_specs=[blk(D), full(1,...  13.5 us

profile of v3, /device:TPU:0, one launch (start us, length us, event | category | flops | bytes accessed | tf_op | source)
XLA Modules:
  0.0 528.7 jit_solution(10308967898119343142)
XLA Ops:
  0.6 50.0 %shard_map.263 = bf16[8,256,2048]{2,1,0:T(8,128)(2,1)} custom-call(bf16[256,2048]{1,0:T(8,128)(2,1)} %hidden_ref.1), custom_call_target="tpu_custom_call" | custom-call | tf_op jit(solution)/shard_map/pallas_call | solution.py:225
  50.7 1.3 constant_dynamic-slice_fusion
  52.0 1.1 constant_dynamic-slice_fusion.2
  53.1 0.2 pad_maximum_fusion.w_ref
  53.3 0.8 dynamic-slice_bitcast_fusion
  54.1 3.7 fusion.3
  57.8 0.0 copy-start.12
  57.8 0.6 pad_maximum_fusion.1
  58.4 0.0 copy-start.1
  58.5 0.0 copy-start.2
  58.5 0.0 copy-done.13
  58.5 0.0 copy-done.12
  58.5 13.5 %shard_map.264 = (bf16[2048,2048]{1,0:T(8,128)(2,1)}, bf16[2048,128]{1,0:T(8,128)(2,1)S(1)}, bf16[2048,128]{1,0:T(8,128)(2,1)S(1)}, bf16[2048,128]{1,0:T(8,128)(...) custom-call(bf16[2048,2048]{1,0:T(8,128)(2,1)} %bitcast.43, f32[1,2048]{1,0:T(1,128)S(1)} %bitcast.37, ...), custom_call_target="tpu_custom_call" | custom-call | tf_op jit(solution)/shard_map/pallas_call | solution.py:569
  72.0 0.0 copy-done.1
  72.0 0.8 copy-done.6
  72.8 1.0 copy-done.8
  73.8 1.0 copy-done.9
  74.8 0.0 copy-done.11
  74.8 0.4 copy.48.segc_ref
  75.2 0.4 copy-done.4
  75.6 0.2 copy-done.5
  75.8 1.0 copy-done.7
  76.8 3.6 shard_map.265.part_ref
  80.4 0.0 copy-start.3
  80.4 1.6 copy-done.3
  82.0 29.7 %shard_map.266 = (bf16[256,2048]{1,0:T(8,128)(2,1)S(1)}, bf16[256,512]{1,0:T(8,128)(2,1)S(1)}) custom-call(bf16[4,256,128]{2,1,0:T(8,128)(2,1)S(1)} %shard_map.265.part_ref, bf16[512,2048]{1,0:T(8,128)(2,1)S(1)} %copy-done.3), custom_call_target="tpu_custom_call" | custom-call | tf_op jit(solution)/shard_map/pallas_call | solution.py:724
  111.6 0.0 copy-done
  111.7 0.0 copy-start.10
  111.7 0.7 copy-done.10
  112.4 0.0 copy-done.15
  112.4 0.4 multiply_reduce_fusion.2
  112.8 1.5 multiply_convert_fusion.own
  114.3 54.5 %shard_map.267 = bf16[8,256,2048]{2,1,0:T(8,128)(2,1)} custom-call(bf16[256,2048]{1,0:T(8,128)(2,1)} %multiply_convert_fusion.own), custom_call_target="tpu_custom_call" | custom-call | tf_op jit(solution)/shard_map/pallas_call | solution.py:225
  168.9 0.1 copy.49
  169.0 1.1 fusion.2.own
  170.1 48.9 %shard_map.268 = bf16[8,256,2176]{2,1,0:T(8,128)(2,1)} custom-call(bf16[256,2176]{1,0:T(8,128)(2,1)} %fusion.2.own), custom_call_target="tpu_custom_call" | custom-call | tf_op jit(solution)/shard_map/pallas_call | solution.py:225
  219.0 0.0 copy-done.22
  219.0 1.0 copy.50.wr_ref
  220.1 41.1 %shard_map.269 = (bf16[2048,512]{1,0:T(8,128)(2,1)}, bf16[2048,1024]{1,0:T(8,128)(2,1)}, bf16[2048,4224]{1,0:T(8,128)(2,1)}) custom-call(s32[1]{0:T(128)} %bitcast.6.first, bf16[2048,2048]{1,0:T(8,128)(2,1)} %bitcast.41, bf16[2048,2176]{1,0:T(8,128)(2,1)} %bitcast.38, bf16[2048,2176]{1,0:T(8,128)(2,1)} %bitcast.39, bf16[2048,16]{1,0:T(8,128)(2,1)} %copy.50.wr_ref, ...), custom_call_target="tpu_custom_call" | custom-call | tf_op jit(solution)/shard_map/pallas_call | solution.py:492
  261.1 108.4 %shard_map.270 = bf16[256,4224]{1,0:T(8,128)(2,1)S(1)} custom-call(bf16[8,256,4224]{2,1,0:T(8,128)(2,1)} %bitcast.44), custom_call_target="tpu_custom_call" | custom-call | tf_op jit(solution)/shard_map/pallas_call | solution.py:419
  369.5 0.1 copy.51
  369.7 0.5 fusion.8
  370.1 0.2 fusion.5
  370.3 0.3 multiply_reduce_fusion.3
  370.6 0.2 multiply_convert_fusion.1
  370.8 0.0 copy-start.18
  370.8 0.9 multiply_reduce_fusion
  371.8 0.3 copy-done.18
  372.0 3.0 fusion.6
  375.0 0.3 fusion.9
  375.3 0.1 pad.7.clone
  375.4 0.8 maximum_maximum_fusion.small_ref
  376.2 53.5 %shard_map.271 = (bf16[8,256,384]{2,1,0:T(8,128)(2,1)}, f32[2,128]{1,0:T(2,128)}, f32[256,512]{1,0:T(8,128)}, f32[24,2048]{1,0:T(8,128)}) custom-call(bf16[256,2048]{1,0:T(8,128)(2,1)} %get-tuple-element.114.ga_ref, bf16[512,2048]{1,0:T(8,128)(2,1)} %w_ref.1, bf16[256,512]{1,0:T(8,128)(2,1)} %copy-done.10, bf16[2048,128]{1,0:T(8,128)(2,1)} %copy-done.4, ...), custom_call_target="tpu_custom_call" | custom-call | tf_op jit(solution)/shard_map/pallas_call | solution.py:914
  429.6 68.5 %shard_map.272 = (f32[256,2048]{1,0:T(8,128)}, f32[3,256,512]{2,1,0:T(8,128)}, f32[1,2048]{1,0:T(1,128)}, f32[2,512]{1,0:T(2,128)}) custom-call(bf16[8,256,384]{2,1,0:T(8,128)(2,1)} %get-tuple-element.43.raw_ref, bf16[2048,2048]{1,0:T(8,128)(2,1)} %get-tuple-element.44.a_ref, bf16[2048,512]{1,0:T(8,128)(2,1)} %wq_ref.1, bf16[2048,512]{1,0:T(8,128)(2,1)} %wk_ref.1, ...), custom_call_target="tpu_custom_call" | custom-call | tf_op jit(solution)/shard_map/pallas_call | solution.py:1088
  498.2 2.6 slice_bitcast_fusion
  500.8 1.0 copy.54
  501.8 0.6 fusion.7
  502.4 0.6 slice.46
  503.0 0.7 slice_bitcast_fusion.3
  503.6 13.6 %shard_map.273 = (f32[2,2048,256]{2,1,0:T(8,128)}, f32[2,2048,256]{2,1,0:T(8,128)}) custom-call(bf16[2048,2048]{1,0:T(8,128)(2,1)} %bitcast.42, bf16[2048,1024]{1,0:T(8,128)(2,1)} %get-tuple-element.52.b_ref), custom_call_target="tpu_custom_call" | custom-call | tf_op jit(solution)/shard_map/pallas_call | solution.py:526
  517.3 9.4 %shard_map.274 = f32[512,2048]{1,0:T(8,128)} custom-call(bf16[2048,512]{1,0:T(8,128)(2,1)} %get-tuple-element.55.a_ref, bf16[2048,2176]{1,0:T(8,128)(2,1)} %bitcast.40), custom_call_target="tpu_custom_call" | custom-call | tf_op jit(solution)/shard_map/pallas_call | solution.py:506
  526.6 1.3 copy.59
  528.0 0.0 copy-done.25
  528.0 0.6 copy.60
  (40 shorter events, 0.1 us)
Async XLA Ops:
  54.1 4.4 copy-start.13
  54.1 4.4 copy-start.14
  57.8 0.7 copy-start.12
  58.4 13.6 %copy-start.1 = (f32[2048,128]{1,0:T(8,128)}, f32[2048,128]{1,0:T(8,128)S(1)}, u32[]{:S(2)}) copy-start(f32[2048,128]{1,0:T(8,128)S(1)} %get-tuple-element.132.cos_ref) | copy-start | bytes 3145732
  58.5 13.6 %copy-start.2 = (f32[2048,128]{1,0:T(8,128)}, f32[2048,128]{1,0:T(8,128)S(1)}, u32[]{:S(2)}) copy-start(f32[2048,128]{1,0:T(8,128)S(1)} %get-tuple-element.133.sin_ref) | copy-start | bytes 3145732
  58.5 16.3 %copy-start.11 = (s32[2048]{0:T(1024)S(1)}, s32[2048]{0:T(1024)}, u32[]{:S(2)}) copy-start(s32[2048]{0:T(1024)} %param.30) | copy-start | bytes 24580
  72.0 0.8 copy-start.6
  72.8 1.0 copy-start.8
  73.8 1.0 copy-start.9
  74.8 0.8 copy-start.4
  74.8 1.0 copy-start.5
  75.2 36.5 %copy-start = (s32[2048,1]{1,0:T(8,128)}, s32[2048,1]{1,0:T(8,128)S(1)}, u32[]{:S(2)}) copy-start(s32[2048,1]{1,0:T(8,128)S(1)} %copy.48.segc_ref) | copy-start | bytes 24580
  75.8 1.0 copy-start.7
  76.8 35.6 %copy-start.15 = (bf16[256,2048]{1,0:T(8,128)(2,1)S(1)}, bf16[256,2048]{1,0:T(8,128)(2,1)}, u32[]{:S(2)}) copy-start(bf16[256,2048]{1,0:T(8,128)(2,1)} %hidden_ref.1) | copy-start | bytes 3145732
  80.4 1.6 copy-start.3
  82.0 30.8 %copy-start.23 = (f32[2048]{0:T(1024)S(1)}, f32[2048]{0:T(1024)}, u32[]{:S(2)}) copy-start(f32[2048]{0:T(1024)} %param.24) | copy-start | bytes 24580
  111.7 0.7 copy-start.10
  114.3 54.6 %copy-start.24 = (s32[256,8]{0,1:T(8,128)S(1)}, s32[256,8]{0,1:T(8,128)}, u32[]{:S(2)}) copy-start(s32[256,8]{0,1:T(8,128)} %param.29) | copy-start | bytes 24580
  114.3 54.7 %copy-start.17 = (bf16[256,2048]{1,0:T(8,128)(2,1)S(1)}, bf16[256,2048]{1,0:T(8,128)(2,1)}, u32[]{:S(2)}) copy-start(bf16[256,2048]{1,0:T(8,128)(2,1)} %param.31) | copy-start | bytes 3145732
  170.1 48.9 %copy-start.22 = (bf16[2048,16]{0,1:T(8,128)(2,1)S(1)}, bf16[2048,16]{0,1:T(8,128)(2,1)}, u32[]{:S(2)}) copy-start(bf16[2048,16]{0,1:T(8,128)(2,1)} %param.25) | copy-start | bytes 196612
  261.1 108.5 %copy-start.16 = (bf16[256,2048]{1,0:T(8,128)(2,1)S(1)}, bf16[256,2048]{1,0:T(8,128)(2,1)}, u32[]{:S(2)}) copy-start(bf16[256,2048]{1,0:T(8,128)(2,1)} %multiply_convert_fusion.own) | copy-start | bytes 3145732
  370.8 1.2 copy-start.18
  498.1 2.6 copy-start.20
  498.1 3.6 copy-start.26
  498.2 4.2 copy-start.21
  517.3 9.4 %copy-start.19 = (f32[256,2048]{1,0:T(8,128)S(1)}, f32[256,2048]{1,0:T(8,128)}, u32[]{:S(2)}) copy-start(f32[256,2048]{1,0:T(8,128)} %get-tuple-element.149) | copy-start | bytes 6291460
  526.6 1.3 copy-start.25

commit v4 on v0

--- a/solution.py
+++ b/solution.py
@@ -1,11 +1,18 @@
+import functools
+
 import jax
 import jax.numpy as jnp
 from jax import lax
+from jax.experimental import pallas as pl
+from jax.experimental.pallas import tpu as pltpu
 from jax.sharding import PartitionSpec as P
 
 HEAD_DIM = 128
 TOP = 8
 SEQ = 2048
+MESH = pl.DeviceIdType.MESH
+bf16 = jnp.bfloat16
+f32 = jnp.float32
 
 
 EPSILON = 1e-05
@@ -41,6 +48,1222 @@
     return jnp.concatenate(
         [first_half * cosine - second_half * turned, second_half * cosine + first_half * turned], -1
     )
+
+
+def place():
+    block = lax.axis_index("expert")
+    lane = lax.axis_index("head")
+    return block // 2, block % 2, lane // 2, lane % 2
+
+
+def device(z, y, x, core):
+    return (z * 2 + y, x * 2 + core)
+
+
+def greet(z, y, x, core):
+    barrier = pltpu.get_barrier_semaphore()
+
+    def signal(target):
+        pl.semaphore_signal(barrier, inc=1, device_id=target, device_id_type=MESH)
+
+    signal(device(z, 1 - y, x, core))
+    signal(device(z, y, 1 - x, core))
+    signal(device(z, y, x, 1 - core))
+
+    @pl.when(z > 0)
+    def _():
+        signal(device(z - 1, y, x, core))
+
+    @pl.when(z < 3)
+    def _():
+        signal(device(z + 1, y, x, core))
+
+    pl.semaphore_wait(barrier, 3 + (z > 0).astype(jnp.int32) + (z < 3).astype(jnp.int32))
+
+
+def add_split(a, b):
+    pair = a.astype(f32) + b.astype(f32)
+    lanes = lax.broadcasted_iota(jnp.int32, pair.shape, 1)
+    whole = jnp.where(lanes < 16, pair + pltpu.roll(pair, 112, 1), 0.0)
+    high = whole.astype(bf16).astype(f32)
+    return (high + pltpu.roll(whole - high, 16, 1)).astype(bf16)
+
+
+def dot(a,b): return jnp.dot(a,b,preferred_element_type=f32)
+def dot_nt(a,b): return lax.dot_general(a,b,(((1,),(1,)),((),())),preferred_element_type=f32)
+def dot_tn(a,b): return lax.dot_general(a,b,(((0,),(0,)),((),())),preferred_element_type=f32)
+
+
+EPS = 1e-05
+HD = 128
+BLOCK = 256
+
+
+def block_of(r, parity):
+    return 2 * r + (parity if r % 2 == 0 else 1 - parity)
+
+
+def norm_factor(v):
+    return lax.rsqrt(jnp.mean(v * v, -1, keepdims=True) + EPS)
+
+
+def probabilities(r, start, q, k_ref, segc_ref, segr_ref):
+    keys = (2 * r + 2) * BLOCK
+    scores = dot_nt(q, k_ref[:keys]) * (HD ** -0.5)
+    rows = start + lax.broadcasted_iota(jnp.int32, scores.shape, 0)
+    columns = lax.broadcasted_iota(jnp.int32, scores.shape, 1)
+    same = segc_ref[pl.ds(start, BLOCK)] == segr_ref[:, :keys]
+    scores = jnp.where((rows >= columns) & same, scores, -1000000000.0)
+    raised = jnp.exp(scores - jnp.max(scores, -1, keepdims=True))
+    return raised / jnp.sum(raised, -1, keepdims=True)
+
+
+VM = pl.BlockSpec(memory_space=pltpu.VMEM)
+
+
+def masked_probs(b, q, k_ref, segc_ref, segr_ref):
+    keys = (b + 1) * BLOCK
+    scores = dot_nt(q, k_ref[:keys]) * (HD ** -0.5)
+    rows = b * BLOCK + lax.broadcasted_iota(jnp.int32, scores.shape, 0)
+    columns = lax.broadcasted_iota(jnp.int32, scores.shape, 1)
+    same = segc_ref[b * BLOCK:keys] == segr_ref[:, :keys]
+    scores = jnp.where((rows >= columns) & same, scores, -1000000000.0)
+    raised = jnp.exp(scores - jnp.max(scores, -1, keepdims=True))
+    return raised / jnp.sum(raised, -1, keepdims=True)
+
+
+def far_first(z):
+    ahead = z // 2
+    return (3 - 3 * ahead, 2 - ahead, z + 1 - 2 * (z % 2), z)
+
+
+def greet_peers(z, y, x, core, others):
+    barrier = pltpu.get_barrier_semaphore()
+
+    def signal(where):
+        pl.semaphore_signal(barrier, inc=1, device_id=where, device_id_type=MESH)
+
+    for n in range(4):
+        pl.when(z != n)(lambda: signal(device(n, y, x, core)))
+        pl.when(z != n)(lambda: signal(device(n, 1 - y, x, core)))
+    signal(device(z, 1 - y, x, core))
+    for where in others:
+        signal(where)
+    pl.semaphore_wait(barrier, 7 + len(others))
+
+
+def picked(i, values):
+    if isinstance(i, int):
+        return values[i]
+    return sum((i == k).astype(jnp.int32) * v for k, v in enumerate(values))
+
+
+class Gather:
+    def __init__(self, own, whole, local_sem, send, recv, rows=BLOCK):
+        self.own, self.whole, self.send, self.recv, self.rows = own, whole, send, recv, rows
+        z, y, x, core = self.place = place()
+        self.me = z * 2 + y
+        half, eighth = rows // 2, rows // 8
+        self.unit = eighth // 2
+        self.keep = pltpu.make_async_copy(own, self.at(self.me, 0, rows), local_sem)
+
+        def chunks(c):
+            return ((c * half + x * 5 * self.unit, 3 * self.unit), (c * half + (3 - x) * self.unit, 3 * self.unit))
+
+        def quarter(c, of):
+            return (c * half + of * 3 * eighth, eighth)
+
+        self.slab, self.twin_slab = chunks(core), chunks(1 - core)
+        self.mine, self.theirs = quarter(core, x), quarter(core, 1 - x)
+        self.twin_theirs = quarter(1 - core, 1 - x)
+
+    def at(self, b, start, size):
+        return self.whole.at[pl.ds(pl.multiple_of(b * self.rows + start, self.unit), size)]
+
+    def copy(self, kind, c, b, part, where, own=False):
+        if own:
+            source = self.own.at[pl.ds(pl.multiple_of(part[0], self.unit), part[1])]
+        else:
+            source = self.at(b, *part)
+        return pltpu.make_async_remote_copy(
+            src_ref=source, dst_ref=self.at(b, *part), send_sem=self.send.at[kind, c, b], recv_sem=self.recv.at[kind, c, b],
+            device_id=where, device_id_type=MESH)
+
+    def up(self, b, c, own=False):
+        z, y, x, core = self.place
+        return self.copy(0, c, b, self.slab[c], device(z + 1, y, x, core), own)
+
+    def down(self, b, c, own=False):
+        z, y, x, core = self.place
+        return self.copy(1, c, b, self.slab[c], device(z - 1, y, x, core), own)
+
+    def over(self, b, c, own=False):
+        z, y, x, core = self.place
+        return self.copy(2, c, b, self.slab[c], device(z, 1 - y, x, core), own)
+
+    def side(self, b, part):
+        z, y, x, core = self.place
+        return self.copy(3, 0, b, part, device(z, y, 1 - x, core))
+
+    def twin(self, b, c, part):
+        z, y, x, core = self.place
+        return self.copy(4, c, b, part, device(z, y, x, 1 - core))
+
+    def twin_x(self, b, part):
+        z, y, x, core = self.place
+        return self.copy(5, 0, b, part, device(z, y, x, 1 - core))
+
+    def group(self, i):
+        z = self.place[0]
+        ahead = z // 2
+        return picked(i, (z, z + 1 - 2 * (z % 2), 2 - ahead, 3 - 3 * ahead))
+
+    def start(self):
+        z, y, x, core = self.place
+        for c in range(2):
+            pl.when(z < 3)(lambda: self.up(self.me, c, True).start())
+            pl.when(z > 0)(lambda: self.down(self.me, c, True).start())
+            self.over(self.me, c, True).start()
+        self.keep.start()
+
+    def spread(self, b, c):
+        if c == 0:
+            self.side(b, self.mine).start()
+        self.twin(b, c, self.slab[c]).start()
+
+    def hop(self, i):
+        z, y, x, core = self.place
+        b = self.group(i) * 2 + y
+        below = picked(i, (0, z % 2, z // 2, z // 2)) == 1
+        for c in range(2):
+            @pl.when(below)
+            def _():
+                self.up(b, c).wait_recv()
+                pl.when(z < 3)(lambda: self.up(b, c).start())
+
+            @pl.when(jnp.logical_not(below))
+            def _():
+                self.down(b, c).wait_recv()
+                pl.when(z > 0)(lambda: self.down(b, c).start())
+
+            self.over(b, c).start()
+            self.spread(b, c)
+
+    def hop_inside(self, i):
+        z = self.place[0]
+        pl.when((z > 0) & (z < 3))(lambda: self.hop(i))
+
+    def hop_outside(self, i):
+        z = self.place[0]
+        pl.when(z % 3 == 0)(lambda: self.hop(i))
+
+    def cross(self, i):
+        b = self.group(i) * 2 + 1 - self.place[1]
+        for c in range(2):
+            self.over(b, c).wait_recv()
+            self.spread(b, c)
+
+    def blocks(self, i, act):
+        y = self.place[1]
+        n = self.group(i)
+        act(n * 2 + 1 - y)
+        if isinstance(i, int):
+            if i > 0:
+                act(n * 2 + y)
+        else:
+            pl.when(i > 0)(lambda: act(n * 2 + y))
+
+    def flank(self, i):
+        def act(b):
+            self.side(b, self.theirs).wait_recv()
+            self.twin_x(b, self.theirs).start()
+        self.blocks(i, act)
+
+    def complete(self, i):
+        def act(b):
+            for c in range(2):
+                self.twin(b, c, self.twin_slab[c]).wait_recv()
+            self.twin_x(b, self.twin_theirs).wait_recv()
+        self.blocks(i, act)
+
+    def drain(self):
+        z, y, x, core = self.place
+        for b in range(8):
+            zb, yb = b // 2, b % 2
+
+            @pl.when(self.me != b)
+            def _():
+                self.side(b, self.mine).wait_send()
+                self.twin_x(b, self.theirs).wait_send()
+
+            for c in range(2):
+                pl.when(self.me != b)(lambda: self.twin(b, c, self.slab[c]).wait_send())
+                pl.when(yb == y)(lambda: self.over(b, c).wait_send())
+                pl.when((yb == y) & (zb <= z) & (z < 3))(lambda: self.up(b, c).wait_send())
+                pl.when((yb == y) & (zb >= z) & (z > 0))(lambda: self.down(b, c).wait_send())
+
+    def whole_run(self):
+        self.start()
+        self.hop(1)
+        self.cross(0)
+        self.hop_inside(2)
+        self.flank(0)
+        self.hop_outside(2)
+        self.cross(1)
+        self.hop_inside(3)
+        self.flank(1)
+        self.hop_outside(3)
+        self.cross(2)
+        self.cross(3)
+        self.flank(2)
+        self.flank(3)
+        for i in range(4):
+            self.complete(i)
+        self.keep.wait()
+        self.drain()
+
+
+GATHER_SEMS = [pltpu.SemaphoreType.DMA, pltpu.SemaphoreType.DMA((6, 2, 8)), pltpu.SemaphoreType.DMA((6, 2, 8))]
+
+
+ANY = pl.BlockSpec(memory_space=pl.ANY)
+
+
+def project_all_kernel(own_ref, gain_ref, w_ref, qg_ref, kg_ref, cos_ref, sin_ref,
+                       a_out, q_ref, k_ref, v_ref, qr_ref, kr_ref,
+                       whole, a_buf, local_sem, send, recv, a_sem):
+    greet(*place())
+    gather = Gather(own_ref, whole, local_sem, send, recv)
+    gather.start()
+    gather.hop(1)
+    gather.cross(0)
+    gather.hop_inside(2)
+    gather.flank(0)
+    gather.keep.wait()
+    span = 2 * BLOCK
+
+    def rows_of(i):
+        return pl.ds(pl.multiple_of(gather.group(i) * span, span), span)
+
+    def stored(i, slot):
+        return pltpu.make_async_copy(a_buf.at[slot], a_out.at[rows_of(i)], a_sem.at[slot])
+
+    def step(i, _):
+        gather.complete(i)
+        pl.when(i == 0)(lambda: gather.hop_inside(3))
+        rows = rows_of(i)
+        slot = i % 2
+        pl.when(i >= 2)(lambda: stored(i - 2, slot).wait())
+        x = whole[rows].astype(f32)
+        a = (x * norm_factor(x) * gain_ref[...]).astype(bf16)
+        a_buf[slot] = a
+        stored(i, slot).start()
+        raw = dot(a, w_ref[...])
+        cosine, sine = cos_ref[rows], sin_ref[rows]
+
+        def turned(part, gain):
+            n = part * norm_factor(part) * gain
+            return (n * cosine + pltpu.roll(n, HD // 2, 1) * sine).astype(bf16)
+
+        q_raw, k_raw = raw[:, :HD], raw[:, HD:2 * HD]
+        qr_ref[rows] = q_raw
+        kr_ref[rows] = k_raw
+        q_ref[rows] = turned(q_raw, qg_ref[...])
+        k_ref[rows] = turned(k_raw, kg_ref[...])
+        v_ref[rows] = raw[:, 2 * HD:].astype(bf16)
+        pl.when(i < 2)(lambda: gather.hop_outside(i + 2))
+        pl.when(i < 3)(lambda: gather.cross(i + 1))
+        pl.when(i < 3)(lambda: gather.flank(i + 1))
+        return 0
+
+    lax.fori_loop(0, 4, step, 0)
+    stored(2, 0).wait()
+    stored(3, 1).wait()
+    gather.drain()
+
+
+def project_all(own, gain, w, qg, kg, cosine, sine, number):
+    rows, D = own.shape
+    T = 8 * rows
+    sd = jax.ShapeDtypeStruct
+    return pl.pallas_call(
+        project_all_kernel, in_specs=[ANY] + [VM] * 6, out_specs=[ANY] + [VM] * 5,
+        out_shape=[sd((T, D), bf16)] + [sd((T, HD), bf16)] * 3 + [sd((T, HD), f32)] * 2,
+        scratch_shapes=[pltpu.VMEM((T, D), bf16), pltpu.VMEM((2, 2 * rows, D), bf16)] + GATHER_SEMS + [pltpu.SemaphoreType.DMA((2,))],
+        compiler_params=pltpu.CompilerParams(collective_id=number, has_side_effects=True, vmem_limit_bytes=56 * 2**20),
+    )(own, gain, w, qg, kg, cosine, sine)
+
+
+def attend_all_kernel(sent_ref, q_ref, k_ref, v_ref, segc_ref, segr_ref, w_ref, total, gathered, whole,
+                      part, arrived, out_half, in_half, held, from_x, local_sem, g_send, g_recv,
+                      send, recv, pair_send, pair_recv):
+    z, y, x, core = place()
+    across, twin = device(z, y, 1 - x, core), device(z, y, x, 1 - core)
+    greet_peers(z, y, x, core, (across, twin))
+    gather = Gather(sent_ref, whole, local_sem, g_send, g_recv)
+    targets = lambda r: (y if r % 2 == 0 else 1 - y)
+    source_y = (y + z) % 2
+
+    def remote(source, target, ssem, rsem, where):
+        return pltpu.make_async_remote_copy(
+            src_ref=source, dst_ref=target, send_sem=ssem, recv_sem=rsem, device_id=where, device_id_type=MESH)
+
+    def to_block(r):
+        return remote(part.at[r], arrived.at[z], send.at[r], recv.at[z], device(r, targets(r), x, core))
+
+    def from_head(n):
+        return remote(part.at[n], arrived.at[n], send.at[n], recv.at[n], device(n, source_y, x, core))
+
+    here = lambda r: (z == r) & (z % 2 == 0)
+    gather.start()
+    for r in range(3, -1, -1):
+        start = pl.multiple_of(block_of(r, y) * BLOCK, BLOCK)
+        probs = probabilities(r, start, q_ref[pl.ds(start, BLOCK)], k_ref, segc_ref, segr_ref)
+        part[r] = dot(probs.astype(bf16), v_ref[:(2 * r + 2) * BLOCK]).astype(bf16)
+        pl.when(jnp.logical_not(here(r)))(lambda: to_block(r).start())
+
+    gather.hop(1)
+    gather.cross(0)
+    gather.hop_inside(2)
+
+    @pl.when(z % 2 == 0)
+    def _():
+        arrived[z] = part[z]
+
+    for n in range(4):
+        pl.when(jnp.logical_not(here(n)))(lambda: from_head(n).wait_recv())
+        gathered[:, n * HD:(n + 1) * HD] = arrived[n]
+
+    rows = total.shape[0]
+    half = rows // 2
+    chunk = half // 2
+    my_half = core * half
+    other_half = (1 - core) * half
+    piece = lambda c: pl.ds(c * chunk, chunk)
+    at = lambda base, c: pl.ds(pl.multiple_of(base + c * chunk, chunk), chunk)
+
+    def pair(kind, c, source, target, where):
+        return remote(source, target, pair_send.at[kind, c], pair_recv.at[kind, c], where)
+
+    first = [pair(0, c, out_half.at[piece(c)], in_half.at[piece(c)], twin) for c in range(2)]
+    second = [pair(1, c, held.at[piece(c)], from_x.at[piece(c)], across) for c in range(2)]
+    third = [pair(2, c, total.at[at(my_half, c)], total.at[at(my_half, c)], twin) for c in range(2)]
+    for c in range(2):
+        out_half[piece(c)] = dot(gathered[at(other_half, c)], w_ref[...]).astype(bf16)
+        first[c].start()
+    for c in range(2):
+        kept = dot(gathered[at(my_half, c)], w_ref[...])
+        first[c].wait_recv()
+        held[piece(c)] = (kept + in_half[piece(c)].astype(f32)).astype(bf16)
+        second[c].start()
+    gather.flank(0)
+    gather.hop_outside(2)
+    gather.cross(1)
+    gather.hop_inside(3)
+    for c in range(2):
+        second[c].wait_recv()
+        total[at(my_half, c)] = (held[piece(c)].astype(f32) + from_x[piece(c)].astype(f32)).astype(bf16)
+        third[c].start()
+    gather.flank(1)
+    gather.hop_outside(3)
+    gather.cross(2)
+    for c in range(2):
+        pair(2, c, total.at[at(my_half, c)], total.at[at(other_half, c)], twin).wait_recv()
+    gather.cross(3)
+    gather.flank(2)
+    gather.flank(3)
+    for i in range(4):
+        gather.complete(i)
+    gather.keep.wait()
+    gather.drain()
+    for c in range(2):
+        first[c].wait_send()
+        second[c].wait_send()
+        third[c].wait_send()
+    for r in range(4):
+        pl.when(jnp.logical_not(here(r)))(lambda: to_block(r).wait_send())
+
+
+def attend_all(sent, q, k, v, segc, segr, w, number):
+    rows, width = sent.shape
+    D = w.shape[1]
+    half = rows // 2
+    sd = jax.ShapeDtypeStruct
+    dma = pltpu.SemaphoreType.DMA
+    return pl.pallas_call(
+        attend_all_kernel, in_specs=[ANY] + [VM] * 6, out_specs=[VM, VM, ANY],
+        out_shape=[sd((rows, D), bf16), sd((rows, 4 * HD), bf16), sd((8 * rows, width), bf16)],
+        scratch_shapes=[pltpu.VMEM((4, BLOCK, HD), bf16)] * 2 + [pltpu.VMEM((half, D), bf16)] * 4 + GATHER_SEMS + [
+            dma((4,)), dma((4,)), dma((3, 2)), dma((3, 2))],
+        compiler_params=pltpu.CompilerParams(collective_id=number, has_side_effects=True, vmem_limit_bytes=56 * 2**20),
+    )(sent, q, k, v, segc, segr, w)
+
+
+def experts_kernel(own_ref, grads_ref, wr_ref, wg_in, wu_in, wd_in, x_out, weighted_out, acts_out, parts_out,
+                   whole, wg, wu, wd, g_buf, mask_all, gw, w_buf, a_buf, p_buf,
+                   local_sem, send, recv, weight_sem, g_sem, out_sem):
+    z, y, x_place, core = place()
+    first = (z * 2 + y) * wg_in.shape[0]
+    D, ff = wg_in.shape[1], wg_in.shape[2]
+    span = 2 * BLOCK
+    weights = [pltpu.make_async_copy(source, target, weight_sem.at[k])
+               for k, (source, target) in enumerate(((wd_in, wd), (wg_in, wg), (wu_in, wu)))]
+
+    def grads_load(g):
+        return pltpu.make_async_copy(grads_ref.at[pl.ds(g * span, span)], g_buf.at[g % 2], g_sem.at[g % 2])
+
+    weights[0].start()
+    grads_load(0).start()
+    grads_load(1).start()
+    weights[1].start()
+    weights[2].start()
+    greet(z, y, x_place, core)
+    gather = Gather(own_ref, whole, local_sem, send, recv)
+    gather.start()
+    weights[0].wait()
+    for g in range(4):
+        grads_load(g).wait()
+        rows = slice(g * span, (g + 1) * span)
+        mask_all[rows] = g_buf[g % 2, :, D:]
+        for j in range(2):
+            gw[rows, j * ff:(j + 1) * ff] = dot_nt(g_buf[g % 2, :, :D], wd[j])
+        if g < 2:
+            grads_load(g + 2).start()
+    gather.hop(1)
+    gather.cross(0)
+    gather.hop_inside(2)
+    gather.flank(0)
+    gather.keep.wait()
+    weights[1].wait()
+    weights[2].wait()
+
+    def rows_of(i):
+        return pl.ds(pl.multiple_of(gather.group(i) * span, span), span)
+
+    def stores(i, slot):
+        rows = rows_of(i)
+        return [
+            pltpu.make_async_copy(w_buf.at[slot], weighted_out.at[rows], out_sem.at[slot, 0]),
+            pltpu.make_async_copy(a_buf.at[slot], acts_out.at[rows], out_sem.at[slot, 1]),
+            pltpu.make_async_copy(p_buf.at[slot], parts_out.at[rows], out_sem.at[slot, 2]),
+        ]
+
+    def x_store(i, slot):
+        return pltpu.make_async_copy(whole.at[rows_of(i)], x_out.at[rows_of(i)], out_sem.at[slot, 3])
+
+    def step(i, _):
+        gather.complete(i)
+        slot = i % 2
+
+        @pl.when(i >= 2)
+        def _():
+            for copy in stores(i - 2, slot):
+                copy.wait()
+            x_store(i - 2, slot).wait()
+
+        x_store(i, slot).start()
+        rows = rows_of(i)
+        x = whole[rows]
+        logits = dot(x, wr_ref[...])
+        count = logits.shape[1]
+        mask = mask_all[rows, :count].astype(f32) > 0
+        top = jnp.max(jnp.where(mask, logits, -jnp.inf), -1, keepdims=True)
+        raised = jnp.where(mask, jnp.exp(jnp.where(mask, logits - top, 0.0)), 0.0)
+        gates = raised / jnp.sum(raised, -1, keepdims=True)
+        lane = lax.broadcasted_iota(jnp.int32, gates.shape, 1)
+        gg = jnp.zeros(gates.shape, f32)
+        for j in range(2):
+            here = lane == first + j
+            gate = jnp.sum(jnp.where(here, gates, 0.0), -1, keepdims=True)
+            ga = dot(x, wg[j])
+            ua = dot(x, wu[j])
+            gw_j = gw[rows, j * ff:(j + 1) * ff]
+            s = 1.0 / (1.0 + jnp.exp(-ga))
+            silu = ga * s
+            h = (silu * ua).astype(bf16).astype(f32)
+            gg = gg + jnp.where(here, jnp.sum(h * gw_j, -1, keepdims=True), 0.0)
+            gh = gw_j * gate
+            w_buf[slot, :, j * ff:(j + 1) * ff] = (h * gate).astype(bf16)
+            a_buf[slot, :, 2 * j * ff:(2 * j + 1) * ff] = (gh * ua * s * (1.0 + ga * (1.0 - s))).astype(bf16)
+            a_buf[slot, :, (2 * j + 1) * ff:(2 * j + 2) * ff] = (gh * silu).astype(bf16)
+            if j == 0:
+                pl.when(i == 0)(lambda: gather.hop_inside(3))
+        pl.when(i < 2)(lambda: gather.hop_outside(i + 2))
+        pl.when(i < 3)(lambda: gather.cross(i + 1))
+        p_buf[slot, :, :D] = dot(w_buf[slot], wd[...].reshape(2 * ff, D)).astype(bf16)
+        gx = dot_nt(a_buf[slot, :, :ff], wg[0])
+        for k, weight in ((1, wu[0]), (2, wg[1]), (3, wu[1])):
+            gx = gx + dot_nt(a_buf[slot, :, k * ff:(k + 1) * ff], weight)
+        p_buf[slot, :, D:2 * D] = gx.astype(bf16)
+        high = gg.astype(bf16)
+        low = (gg - high.astype(f32)).astype(bf16)
+        spare = jnp.zeros((span, 128 - 2 * count), bf16)
+        p_buf[slot, :, 2 * D:] = jnp.concatenate([high, low, spare], 1)
+        for copy in stores(i, slot):
+            copy.start()
+        pl.when(i < 3)(lambda: gather.flank(i + 1))
+        return 0
+
+    lax.fori_loop(0, 4, step, 0)
+    for i in (2, 3):
+        for copy in stores(i, i % 2):
+            copy.wait()
+        x_store(i, i % 2).wait()
+    gather.drain()
+
+
+def experts_all(own, grads, wr, wg, wu, wd, number):
+    rows, D = own.shape
+    T = 8 * rows
+    J, _, F = wg.shape
+    span = 2 * rows
+    sd = jax.ShapeDtypeStruct
+    dma = pltpu.SemaphoreType.DMA
+    vm = pltpu.VMEM
+    return pl.pallas_call(
+        experts_kernel, in_specs=[ANY, ANY, VM, ANY, ANY, ANY], out_specs=[ANY] * 4,
+        out_shape=[sd((T, D), bf16), sd((T, J * F), bf16), sd((T, 2 * J * F), bf16), sd((T, 2 * D + 128), bf16)],
+        scratch_shapes=[
+            vm((T, D), bf16), vm((J, D, F), bf16), vm((J, D, F), bf16), vm((J, F, D), bf16),
+            vm((2, span, D + 128), bf16), vm((T, 128), bf16), vm((T, J * F), f32),
+            vm((2, span, J * F), bf16), vm((2, span, 2 * J * F), bf16), vm((2, span, 2 * D + 128), bf16),
+        ] + GATHER_SEMS + [dma((3,)), dma((2,)), dma((2, 4))],
+        compiler_params=pltpu.CompilerParams(collective_id=number, has_side_effects=True, vmem_limit_bytes=60 * 2**20),
+    )(own, grads, wr, wg, wu, wd)
+
+
+def sum_rows(target, source, cols, rows):
+    step = 16
+    main = cols.size - cols.size % 2048
+
+    @pl.loop(0, rows // step)
+    def _(i):
+        part = pl.ds(pl.multiple_of(i * step, step), step)
+        wide = pl.ds(cols.start, main)
+        target[part, wide] = (target[part, wide].astype(f32) + source[part, wide].astype(f32)).astype(bf16)
+        if main < cols.size:
+            tail = pl.ds(cols.start + main, cols.size - main)
+            target[part, tail] = add_split(target[part, tail], source[part, tail])
+
+
+def sums_kernel(parts, x_ref, acts_ref, grads_ref, weighted_ref, total, gate_out, up_out, down_out,
+                held, from_core, from_x, from_y, from_below, from_above, shared_in,
+                acts, weighted, x_buf, g_buf, gu_buf, down_buf,
+                load_sem, send, recv, end_send, end_recv, fixed_sem, x_sem, g_sem, gu_sem, down_sem):
+    z, y, x, core = place()
+    D = x_ref.shape[1]
+    half = parts.shape[1] // 2
+    piece = half // 4
+    me = z * 2 + y
+    order = far_first(z)
+    my_half = pl.ds(pl.multiple_of(core * half, half), half)
+    other_half = pl.ds(pl.multiple_of((1 - core) * half, half), half)
+    slab = pl.ds(pl.multiple_of(x * piece, piece), 3 * piece)
+    mine = pl.ds(pl.multiple_of(x * 3 * piece, piece), piece)
+    theirs = pl.ds(pl.multiple_of((1 - x) * 3 * piece, piece), piece)
+    shared = pl.ds(piece, 2 * piece)
+    spans = (pl.ds(0, D), pl.ds(D, parts.shape[2] - D))
+    CORE, X, Y, UP, DOWN = range(5)
+    everything = pl.ds(0, half)
+
+    def remote(kind, h, number, source, target, where):
+        return pltpu.make_async_remote_copy(
+            src_ref=source, dst_ref=target, send_sem=send.at[kind, h, number],
+            recv_sem=recv.at[kind, h, number], device_id=where, device_id_type=MESH)
+
+    def load(b, h):
+        return pltpu.make_async_copy(parts.at[b, my_half, spans[h]], held.at[b, everything, spans[h]], load_sem.at[h, b])
+
+    def to_core(b, h):
+        return remote(CORE, h, b, parts.at[b, other_half, spans[h]], from_core.at[b, everything, spans[h]], device(z, y, x, 1 - core))
+
+    def to_x(b, h):
+        return remote(X, h, b, held.at[b, theirs, spans[h]], from_x.at[b, pl.ds(0, piece), spans[h]], device(z, y, 1 - x, core))
+
+    def to_y(zb, h):
+        return remote(Y, h, zb, held.at[zb * 2 + 1 - y, slab, spans[h]], from_y.at[zb, pl.ds(0, 3 * piece), spans[h]], device(z, 1 - y, x, core))
+
+    def to_above(zb, h):
+        return remote(UP, h, zb, held.at[zb * 2 + y, slab, spans[h]], from_below.at[zb, pl.ds(0, 3 * piece), spans[h]], device(z + 1, y, x, core))
+
+    def to_below(zb, h):
+        return remote(DOWN, h, zb, held.at[zb * 2 + y, slab, spans[h]], from_above.at[zb, pl.ds(0, 3 * piece), spans[h]], device(z - 1, y, x, core))
+
+    fixed = [pltpu.make_async_copy(acts_ref, acts, fixed_sem.at[0]), pltpu.make_async_copy(weighted_ref, weighted, fixed_sem.at[1])]
+    ff = weighted.shape[1] // 2
+    x_pieces, g_pieces = D // BLOCK, D // 512
+
+    def x_load(k):
+        return pltpu.make_async_copy(x_ref.at[:, pl.ds(k * BLOCK, BLOCK)], x_buf.at[k % 2], x_sem.at[k % 2])
+
+    def g_load(k):
+        return pltpu.make_async_copy(grads_ref.at[:, pl.ds(k * 512, 512)], g_buf.at[k % 2], g_sem.at[k % 2])
+
+    def gu_store(k):
+        rows = pl.ds(k * BLOCK, BLOCK)
+        return [pltpu.make_async_copy(gu_buf.at[k % 2, u, j], (gate_out, up_out)[u].at[j, rows], gu_sem.at[k % 2, u, j])
+                for u in range(2) for j in range(2)]
+
+    def down_store(k):
+        return [pltpu.make_async_copy(down_buf.at[k % 2, j], down_out.at[j, :, pl.ds(k * 512, 512)], down_sem.at[k % 2, j])
+                for j in range(2)]
+
+    def x_piece(k):
+        if k == 0:
+            fixed[0].wait()
+        x_load(k).wait()
+        if k >= 2:
+            for copy in gu_store(k - 2):
+                copy.wait()
+        both = dot_tn(x_buf[k % 2], acts[...])
+        for j in range(2):
+            for u in range(2):
+                gu_buf[k % 2, u, j] = both[:, (2 * j + u) * ff:(2 * j + u + 1) * ff]
+        for copy in gu_store(k):
+            copy.start()
+        if k + 2 < x_pieces:
+            x_load(k + 2).start()
+
+    def g_piece(k):
+        if k == 0:
+            fixed[1].wait()
+        g_load(k).wait()
+        if k >= 2:
+            for copy in down_store(k - 2):
+                copy.wait()
+        both = dot_tn(weighted[...], g_buf[k % 2])
+        for j in range(2):
+            down_buf[k % 2, j] = both[j * ff:(j + 1) * ff]
+        for copy in down_store(k):
+            copy.start()
+        if k + 2 < g_pieces:
+            g_load(k + 2).start()
+
+    fillers = [functools.partial(x_piece, k) for k in range(x_pieces)]
+    for k in range(g_pieces):
+        fillers.insert(3 * k + 2, functools.partial(g_piece, k))
+
+    greet(z, y, x, core)
+    items = [(zb, h) for zb in order for h in (1, 0)]
+    for k, (zb, h) in enumerate(items):
+        for yb in (1 - y, y):
+            load(zb * 2 + yb, h).start()
+            to_core(zb * 2 + yb, h).start()
+        if k == 1:
+            for copy in fixed:
+                copy.start()
+            for j in range(2):
+                x_load(j).start()
+                g_load(j).start()
+
+    def stage_core(zb, h, yb):
+        b = zb * 2 + yb
+        load(b, h).wait()
+        to_core(b, h).wait_recv()
+        sum_rows(held.at[b], from_core.at[b], spans[h], half)
+        to_x(b, h).start()
+
+    def stage_x(zb, h, yb):
+        b = zb * 2 + yb
+        to_x(b, h).wait_recv()
+        sum_rows(held.at[b, mine], from_x.at[b], spans[h], piece)
+
+    def stage_y(zb, h):
+        stage_x(zb, h, 1 - y)
+        to_y(zb, h).start()
+
+    def climb(zb, h):
+        @pl.when(z > 0)
+        def _():
+            to_above(zb, h).wait_recv()
+            sum_rows(held.at[zb * 2 + y, slab], from_below.at[zb], spans[h], 3 * piece)
+        to_above(zb, h).start()
+
+    def descend(zb, h):
+        @pl.when(z < 3)
+        def _():
+            to_below(zb, h).wait_recv()
+            sum_rows(held.at[zb * 2 + y, slab], from_above.at[zb], spans[h], 3 * piece)
+        to_below(zb, h).start()
+
+    def stage_z(k):
+        zb, h = items[k]
+        to_y(zb, h).wait_recv()
+        sum_rows(held.at[zb * 2 + y, slab], from_y.at[zb], spans[h], 3 * piece)
+        rises = (z // 2 == 0) if k < 4 else (z % 2 == 0)
+        pl.when(rises)(lambda: climb(zb, h))
+        pl.when(jnp.logical_not(rises))(lambda: descend(zb, h))
+
+    base = core * half
+    out_mine = pl.ds(pl.multiple_of(base + x * 3 * piece, piece), piece)
+    out_theirs = pl.ds(pl.multiple_of(base + (1 - x) * 3 * piece, piece), piece)
+    out_shared = pl.ds(pl.multiple_of(base + piece, piece), 2 * piece)
+
+    def at_end(number, h, source, target, where):
+        return pltpu.make_async_remote_copy(
+            src_ref=source, dst_ref=target, send_sem=end_send.at[h, number],
+            recv_sem=end_recv.at[h, number], device_id=where, device_id_type=MESH)
+
+    across, twin = device(z, y, 1 - x, core), device(z, y, x, 1 - core)
+    end_sums = lambda h: at_end(0, h, held.at[me, shared, spans[h]], shared_in.at[pl.ds(0, 2 * piece), spans[h]], across)
+    end_ready = lambda h, rows: at_end(1, h, held.at[me, mine, spans[h]], total.at[rows, spans[h]], across)
+    end_twin = lambda h, rows: at_end(2, h, total.at[my_half, spans[h]], total.at[rows, spans[h]], twin)
+
+    def own_sum(h):
+        own = held.at[me]
+        to_y(z, h).wait_recv()
+        sum_rows(own.at[slab], from_y.at[z], spans[h], 3 * piece)
+
+        @pl.when(z > 0)
+        def _():
+            to_above(z, h).wait_recv()
+            sum_rows(own.at[slab], from_below.at[z], spans[h], 3 * piece)
+
+        @pl.when(z < 3)
+        def _():
+            to_below(z, h).wait_recv()
+            sum_rows(own.at[slab], from_above.at[z], spans[h], 3 * piece)
+        end_sums(h).start()
+        end_ready(h, out_mine).start()
+        total[out_mine, spans[h]] = held[me, mine, spans[h]]
+
+    def own_end(h):
+        end_sums(h).wait_recv()
+        sum_rows(held.at[me, shared], shared_in, spans[h], 2 * piece)
+        total[out_shared, spans[h]] = held[me, shared, spans[h]]
+        end_ready(h, out_theirs).wait_recv()
+        end_twin(h, my_half).start()
+
+    zb, h = items[0]
+    stage_core(zb, h, 1 - y)
+    stage_core(zb, h, y)
+    for k, (zb, h) in enumerate(items):
+        if k < 7:
+            stage_core(*items[k + 1], 1 - y)
+        stage_y(zb, h)
+        if k < 7:
+            stage_core(*items[k + 1], y)
+        stage_x(zb, h, y)
+        if 0 < k < 7:
+            stage_z(k - 1)
+        if k < 7:
+            for fill in fillers[2 * k:2 * k + 2]:
+                fill()
+    for fill in fillers[14:]:
+        fill()
+    own_sum(1)
+    own_sum(0)
+    end_sums(1).wait_send()
+    own_end(1)
+    end_sums(0).wait_send()
+    own_end(0)
+    for h in (1, 0):
+        end_twin(h, other_half).wait_recv()
+        end_ready(h, out_mine).wait_send()
+        end_twin(h, my_half).wait_send()
+        for b in range(8):
+            zb, yb = b // 2, b % 2
+            to_core(b, h).wait_send()
+            to_x(b, h).wait_send()
+            if yb == 0:
+                to_y(zb, h).wait_send()
+                pl.when(zb > z)(lambda: to_above(zb, h).wait_send())
+                pl.when(zb < z)(lambda: to_below(zb, h).wait_send())
+    for k in (x_pieces - 2, x_pieces - 1):
+        for copy in gu_store(k):
+            copy.wait()
+    for k in (g_pieces - 2, g_pieces - 1):
+        for copy in down_store(k):
+            copy.wait()
+
+
+def sums_all(parts, x, acts, grads, weighted, number):
+    _, rows, width = parts.shape
+    T, D = x.shape
+    ff = weighted.shape[1] // 2
+    half, piece = rows // 2, rows // 8
+    sd = jax.ShapeDtypeStruct
+    dma = pltpu.SemaphoreType.DMA
+    vm = pltpu.VMEM
+    return pl.pallas_call(
+        sums_kernel, in_specs=[ANY] * 5, out_specs=[VM, ANY, ANY, ANY],
+        out_shape=[sd((rows, width), bf16), sd((2, D, ff), f32), sd((2, D, ff), f32), sd((2, ff, D), f32)],
+        scratch_shapes=[
+            vm((8, half, width), bf16), vm((8, half, width), bf16), vm((8, piece, width), bf16),
+            vm((4, 3 * piece, width), bf16), vm((4, 3 * piece, width), bf16), vm((4, 3 * piece, width), bf16),
+            vm((2 * piece, width), bf16),
+            vm(acts.shape, bf16), vm(weighted.shape, bf16), vm((2, T, BLOCK), bf16), vm((2, T, 512), bf16),
+            vm((2, 2, 2, BLOCK, ff), f32), vm((2, 2, ff, 512), f32),
+            dma((2, 8)), dma((5, 2, 8)), dma((5, 2, 8)), dma((2, 3)), dma((2, 3)),
+            dma((2,)), dma((2,)), dma((2,)), dma((2, 2, 2)), dma((2, 2)),
+        ],
+        compiler_params=pltpu.CompilerParams(collective_id=number, has_side_effects=True, vmem_limit_bytes=62 * 2**20),
+    )(parts, x, acts, grads, weighted)
+
+
+def backward_kernel(ga_ref, segc_ref, segr_ref, qg_ref, kg_ref, gains_small, gain_ref,
+                    w_in, ctx_ref, q_in, k_in, v_in, qr_in, kr_in, cos_in, sin_in, wq_in, wk_in, wv_in, a_in, hidden_in, middle_in,
+                    grad_ref, weights_ref, norm_ref, gains_out, wout_ref, small_out,
+                    w_ref, q_ref, k_ref, v_ref, qr_ref, kr_ref, cos_ref, sin_ref, wq_ref, wk_ref, wv_ref, columns, hidden_ref, middle_ref,
+                    raw_ref, g_own, g_all, dk, dv, terms, from_y, held_terms, from_below, from_above,
+                    small_y, small_sum, small_z, raw_in, gathered, products, from_z, out_half, in_half, held, from_x, total, gains_own, gains_in, norm_in,
+                    load, g_send, g_recv, f_send, f_recv, t_send, t_recv, s_send, s_recv, send, recv, w_send, w_recv,
+                    pair_send, pair_recv, e_send, e_recv, n_send, n_recv):
+    small_ref = gains_small
+    z, y, x, core = place()
+    me = z * 2 + y
+    order = far_first(z)
+    span = 4 * HD
+    across, twin, corner = device(z, y, 1 - x, core), device(z, y, x, 1 - core), device(z, y, 1 - x, 1 - core)
+    partner = device(z, 1 - y, x, core)
+
+    loads = [pltpu.make_async_copy(source, target, load.at[k]) for k, (source, target) in enumerate((
+        (w_in, w_ref), (q_in, q_ref), (k_in, k_ref), (v_in, v_ref), (qr_in, qr_ref), (kr_in, kr_ref), (cos_in, cos_ref),
+        (sin_in, sin_ref), (wq_in, wq_ref), (wk_in, wk_ref), (wv_in, wv_ref), (hidden_in, hidden_ref), (middle_in, middle_ref)))]
+
+    def column_load(n):
+        block = pl.ds(pl.multiple_of((n * 2 + y) * BLOCK, BLOCK), BLOCK)
+        return pltpu.make_async_copy(a_in.at[:, block], columns.at[n], load.at[13 + n])
+
+    for copy in loads:
+        copy.start()
+    for n in range(4):
+        column_load(n).start()
+    greet_peers(z, y, x, core, (across, twin, corner))
+
+    def remote(source, target, ssem, rsem, where):
+        return pltpu.make_async_remote_copy(
+            src_ref=source, dst_ref=target, send_sem=ssem, recv_sem=rsem, device_id=where, device_id_type=MESH)
+
+    def when_away(n, act):
+        pl.when(z != n)(act)
+
+    loads[0].wait()
+    g_context = dot_nt(ga_ref[...], w_ref[...]).astype(bf16)
+    for n in range(4):
+        g_own[n] = g_context[:, n * HD:(n + 1) * HD]
+
+    def g_to(n):
+        return remote(g_own.at[n], g_all.at[me], g_send.at[n], g_recv.at[z], device(n, y, x, core))
+
+    def g_from(n):
+        return remote(g_own.at[n], g_all.at[n * 2 + y], g_send.at[n], g_recv.at[n], device(n, y, x, core))
+
+    def g_over(n):
+        return remote(g_all.at[n * 2 + y], g_all.at[n * 2 + y], f_send.at[n], f_recv.at[n], partner)
+
+    def g_over_in(n):
+        return remote(g_all.at[n * 2 + 1 - y], g_all.at[n * 2 + 1 - y], f_send.at[n], f_recv.at[n], partner)
+
+    for n in range(4):
+        when_away(n, lambda: g_to(n).start())
+    g_all[me] = g_own[z]
+    g_over(z).start()
+
+    quarter = small_ref.shape[1] // 4
+
+    def lanes(cx, cc):
+        return pl.ds(pl.multiple_of((cx * 2 + cc) * quarter, quarter), quarter)
+
+    own_lanes = lanes(x, core)
+    small_pair = remote(small_ref.at[:, own_lanes], small_y, s_send.at[0], s_recv.at[0], partner)
+    small_pair.start()
+
+    def small_along(n):
+        return remote(small_sum, small_z.at[z], s_send.at[1 + n], s_recv.at[1 + z], device(n, y, x, core))
+
+    def small_arriving(n):
+        return remote(small_sum, small_z.at[n], s_send.at[1 + n], s_recv.at[1 + n], device(n, y, x, core))
+
+    fans = (across, twin, corner)
+    fan_lanes = (lanes(1 - x, core), lanes(x, 1 - core), lanes(1 - x, 1 - core))
+
+    def small_spread(i):
+        return remote(small_out.at[:, own_lanes], small_out.at[:, own_lanes], s_send.at[5 + i], s_recv.at[5 + i], fans[i])
+
+    def small_spread_in(i):
+        return remote(small_out.at[:, own_lanes], small_out.at[:, fan_lanes[i]], s_send.at[5 + i], s_recv.at[5 + i], fans[i])
+
+    for b in range(8):
+        terms[b] = dot_tn(ga_ref[:, b * BLOCK:(b + 1) * BLOCK], ctx_ref[...]).astype(bf16)
+
+    def term_pair(n):
+        return remote(terms.at[n * 2 + 1 - y], from_y.at[n], t_send.at[0, n], t_recv.at[0, n], partner)
+
+    def term_up(n):
+        return remote(held_terms.at[n], from_below.at[n], t_send.at[1, n], t_recv.at[1, n], device(z + 1, y, x, core))
+
+    def term_down(n):
+        return remote(held_terms.at[n], from_above.at[n], t_send.at[2, n], t_recv.at[2, n], device(z - 1, y, x, core))
+
+    def paired(n):
+        return terms[n * 2 + y].astype(f32) + from_y[n].astype(f32)
+
+    def term_stage(k):
+        n = order[k]
+        term_pair(n).wait_recv()
+        held_terms[n] = paired(n).astype(bf16)
+        rises = (z // 2 == 0) if k < 2 else (z % 2 == 0)
+
+        @pl.when(rises)
+        def _():
+            @pl.when(z > 0)
+            def _():
+                term_up(n).wait_recv()
+                held_terms[n] = (paired(n) + from_below[n].astype(f32)).astype(bf16)
+            term_up(n).start()
+
+        @pl.when(jnp.logical_not(rises))
+        def _():
+            @pl.when(z < 3)
+            def _():
+                term_down(n).wait_recv()
+                held_terms[n] = (paired(n) + from_above[n].astype(f32)).astype(bf16)
+            term_down(n).start()
+
+    for n in range(4):
+        when_away(n, lambda: g_from(n).wait_recv())
+        when_away(n, lambda: g_over(n).start())
+    for n in order:
+        term_pair(n).start()
+
+    def rows_to(n):
+        return remote(raw_ref.at[n * 2 + y], raw_in.at[z], send.at[n], recv.at[z], device(n, y, x, core))
+
+    def rows_from(n):
+        return remote(raw_ref.at[n * 2 + y], raw_in.at[n], send.at[n], recv.at[n], device(n, y, x, core))
+
+    gain_sums = [jnp.zeros((1, HD), f32), jnp.zeros((1, HD), f32)]
+
+    def back(turned, b, raw_in, gain, which):
+        rows = slice(b * BLOCK, (b + 1) * BLOCK)
+        g = turned * cos_ref[rows] - pltpu.roll(turned, HD // 2, 1) * sin_ref[rows]
+        raw = raw_in[rows]
+        factor = norm_factor(raw)
+        n = raw * factor
+        gain_sums[which] = gain_sums[which] + jnp.sum(g * n, 0, keepdims=True)
+        g = g * gain[...]
+        return (factor * (g - n * jnp.mean(g * n, -1, keepdims=True))).astype(bf16)
+
+    for copy in loads[1:8]:
+        copy.wait()
+    for b in range(7, -1, -1):
+        keys = (b + 1) * BLOCK
+        rows = slice(b * BLOCK, keys)
+        pl.when(y != b % 2)(lambda: g_over_in(b // 2).wait_recv())
+        q = q_ref[rows]
+        g = g_all[b]
+        probs = masked_probs(b, q, k_ref, segc_ref, segr_ref)
+        gv = dot_tn(probs.astype(bf16), g)
+        gp = dot_nt(g, v_ref[:keys])
+        gs = (probs * (gp - jnp.sum(gp * probs, -1, keepdims=True))).astype(bf16)
+        gk = dot_tn(gs, q)
+        if b == 7:
+            dv[...] = gv
+            dk[...] = gk
+        else:
+            dv[:keys] += gv
+            dk[:keys] += gk
+        raw_ref[b, :, :HD] = back(dot(gs, k_ref[:keys]) * (HD ** -0.5), b, qr_ref, qg_ref, 0)
+        raw_ref[b, :, HD:2 * HD] = back(dk[rows] * (HD ** -0.5), b, kr_ref, kg_ref, 1)
+        raw_ref[b, :, 2 * HD:] = dv[rows].astype(bf16)
+
+        @pl.when(y == b % 2)
+        def _():
+            when_away(b // 2, lambda: rows_to(b // 2).start())
+
+        if b == 5:
+            small_pair.wait_recv()
+            small_sum[...] = small_ref[:, own_lanes] + small_y[...]
+            for n in range(4):
+                when_away(n, lambda: small_along(n).start())
+            small_z[z] = small_sum[...]
+        if b == 1:
+            for n in range(4):
+                when_away(n, lambda: small_arriving(n).wait_recv())
+            small_out[:, own_lanes] = (small_z[0] + small_z[1]) + (small_z[2] + small_z[3])
+            for i in range(3):
+                small_spread(i).start()
+
+    gains_own[0:1] = gain_sums[0]
+    gains_own[1:2] = gain_sums[1]
+
+    def gains_to(n):
+        return remote(gains_own, gains_in.at[z], e_send.at[n], e_recv.at[z], device(n, y, x, core))
+
+    def gains_from(n):
+        return remote(gains_own, gains_in.at[n], e_send.at[n], e_recv.at[n], device(n, y, x, core))
+
+    for n in range(4):
+        when_away(n, lambda: gains_to(n).start())
+    gains_in[z] = gains_own[...]
+    raw_in[z] = raw_ref[me]
+
+    def products_to(n):
+        return remote(products.at[n], from_z.at[z], w_send.at[n], w_recv.at[z], device(n, y, x, core))
+
+    def products_from(n):
+        return remote(products.at[n], from_z.at[n], w_send.at[n], w_recv.at[n], device(n, y, x, core))
+
+    raw_all = raw_ref[...].reshape(8 * BLOCK, 3 * HD)
+    for i, n in enumerate(order):
+        column_load(n).wait()
+        product = dot_tn(columns[n], raw_all).astype(bf16)
+        if i < 3:
+            products[n] = product
+            products_to(n).start()
+        else:
+            from_z[z] = product
+
+    for copy in loads[8:]:
+        copy.wait()
+    term_stage(0)
+    for n in range(4):
+        when_away(n, lambda: rows_from(n).wait_recv())
+        for g in range(3):
+            gathered[:, g * span + n * HD:g * span + (n + 1) * HD] = raw_in[n, :, g * HD:(g + 1) * HD]
+
+    rows = total.shape[0]
+    half = rows // 2
+    chunk = half // 2
+    my_half = core * half
+    other_half = (1 - core) * half
+    piece = lambda c: pl.ds(c * chunk, chunk)
+    at = lambda base, c: pl.ds(pl.multiple_of(base + c * chunk, chunk), chunk)
+
+    def pair(kind, c, source, target, where):
+        return remote(source, target, pair_send.at[kind, c], pair_recv.at[kind, c], where)
+
+    def multiply(part):
+        return (dot_nt(part[:, :span], wq_ref[...]) + dot_nt(part[:, span:2 * span], wk_ref[...])
+                + dot_nt(part[:, 2 * span:], wv_ref[...]))
+
+    first = [pair(0, c, out_half.at[piece(c)], in_half.at[piece(c)], twin) for c in range(2)]
+    second = [pair(1, c, held.at[piece(c)], from_x.at[piece(c)], across) for c in range(2)]
+    third = [pair(2, c, total.at[at(my_half, c)], total.at[at(my_half, c)], twin) for c in range(2)]
+    for c in range(2):
+        out_half[piece(c)] = multiply(gathered[at(other_half, c)]).astype(bf16)
+        first[c].start()
+    for c in range(2):
+        kept = multiply(gathered[at(my_half, c)])
+        first[c].wait_recv()
+        held[piece(c)] = (kept + in_half[piece(c)].astype(f32)).astype(bf16)
+        second[c].start()
+
+    term_stage(1)
+    term_stage(2)
+    term_pair(z).wait_recv()
+    wout_ref[...] = paired(z)
+
+    @pl.when(z > 0)
+    def _():
+        term_up(z).wait_recv()
+        wout_ref[...] += from_below[z].astype(f32)
+
+    @pl.when(z < 3)
+    def _():
+        term_down(z).wait_recv()
+        wout_ref[...] += from_above[z].astype(f32)
+
+    for n in range(4):
+        when_away(n, lambda: gains_from(n).wait_recv())
+        gains_out[:, n * HD:(n + 1) * HD] = gains_in[n]
+    for c in range(2):
+        second[c].wait_recv()
+        total[at(my_half, c)] = (held[piece(c)].astype(f32) + from_x[piece(c)].astype(f32)).astype(bf16)
+        third[c].start()
+
+    step = 32
+
+    def norm_rows(base):
+        def body(i, norm_part):
+            part = pl.ds(pl.multiple_of(base + i * step, step), step)
+            e = total[part].astype(f32)
+            v = hidden_ref[part].astype(f32)
+            factor = norm_factor(v)
+            n = v * factor
+            norm_part = norm_part + jnp.sum(e * n, 0, keepdims=True)
+            e = e * gain_ref[...]
+            grad_ref[part] = middle_ref[part] + factor * (e - n * jnp.mean(e * n, -1, keepdims=True))
+            return norm_part
+        return body
+
+    nothing = jnp.zeros((1, total.shape[1]), f32)
+    mine_part = lax.fori_loop(0, half // step, norm_rows(my_half), nothing)
+    for c in range(2):
+        pair(2, c, total.at[at(my_half, c)], total.at[at(other_half, c)], twin).wait_recv()
+    other_part = lax.fori_loop(0, half // step, norm_rows(other_half), nothing)
+    norm_part = mine_part + other_part
+    for t in range(norm_in.shape[1]):
+        norm_in[me, t:t + 1] = norm_part[:, t * 128:(t + 1) * 128]
+
+    def norm_to(b):
+        return remote(norm_in.at[me], norm_in.at[me], n_send.at[b], n_recv.at[me], device(b // 2, b % 2, x, core))
+
+    def norm_from(b):
+        return remote(norm_in.at[b], norm_in.at[b], n_send.at[b], n_recv.at[b], device(b // 2, b % 2, x, core))
+
+    for b in range(8):
+        pl.when(me != b)(lambda: norm_to(b).start())
+    for n in range(4):
+        when_away(n, lambda: products_from(n).wait_recv())
+    for n in range(4):
+        for g in range(3):
+            weights_ref[g, :, n * HD:(n + 1) * HD] = from_z[n, :, g * HD:(g + 1) * HD].astype(f32)
+    for b in range(8):
+        pl.when(me != b)(lambda: norm_from(b).wait_recv())
+    sums = [norm_in[b] for b in range(8)]
+    norm_sum = ((sums[0] + sums[1]) + (sums[2] + sums[3])) + ((sums[4] + sums[5]) + (sums[6] + sums[7]))
+    for t in range(norm_in.shape[1]):
+        norm_ref[:, t * 128:(t + 1) * 128] = norm_sum[t:t + 1]
+
+    for i in range(3):
+        small_spread_in(i).wait_recv()
+        small_spread(i).wait_send()
+    small_pair.wait_send()
+    for c in range(2):
+        first[c].wait_send()
+        second[c].wait_send()
+        third[c].wait_send()
+    for b in range(8):
+        pl.when(me != b)(lambda: norm_to(b).wait_send())
+    for n in range(4):
+        when_away(n, lambda: g_to(n).wait_send())
+        g_over(n).wait_send()
+        term_pair(n).wait_send()
+        pl.when(n > z)(lambda: term_up(n).wait_send())
+        pl.when(n < z)(lambda: term_down(n).wait_send())
+        when_away(n, lambda: small_along(n).wait_send())
+        when_away(n, lambda: rows_to(n).wait_send())
+        when_away(n, lambda: products_to(n).wait_send())
+        when_away(n, lambda: gains_to(n).wait_send())
+
+
+def backward_all(ga, segc, segr, qg, kg, small, gain, w, ctx, q, k, v, qr, kr, cosine, sine, wq, wk, wv, a, hidden, middle, number):
+    T, D = a.shape
+    rows, half = BLOCK, BLOCK // 2
+    span = 4 * HD
+    S = small.shape[0]
+    sd = jax.ShapeDtypeStruct
+    dma = pltpu.SemaphoreType.DMA
+    vm = pltpu.VMEM
+    like = lambda m: vm(m.shape, m.dtype)
+    return pl.pallas_call(
+        backward_kernel, in_specs=[VM] * 7 + [ANY, VM] + [ANY] * 13, out_specs=[VM] * 6,
+        out_shape=[sd((rows, D), f32), sd((3, BLOCK, span), f32), sd((1, D), f32), sd((2, span), f32),
+                   sd((BLOCK, span), f32), sd((S, D), f32)],
+        scratch_shapes=[like(m) for m in (w, q, k, v, qr, kr, cosine, sine, wq, wk, wv)] + [
+            vm((4, T, BLOCK), bf16), like(hidden), like(middle),
+            vm((8, BLOCK, 3 * HD), bf16), vm((4, BLOCK, HD), bf16), vm((8, BLOCK, HD), bf16), vm((T, HD), f32), vm((T, HD), f32),
+            vm((8, BLOCK, span), bf16)] + [vm((4, BLOCK, span), bf16)] * 4 + [
+            vm((S, D // 4), f32), vm((S, D // 4), f32), vm((4, S, D // 4), f32),
+            vm((4, BLOCK, 3 * HD), bf16), vm((rows, 3 * span), bf16), vm((4, BLOCK, 3 * HD), bf16), vm((4, BLOCK, 3 * HD), bf16)] + [vm((half, D), bf16)] * 4 + [
+            vm((rows, D), bf16), vm((2, HD), f32), vm((4, 2, HD), f32), vm((8, D // 128, 128), f32),
+            dma((17,)), dma((4,)), dma((4,)), dma((4,)), dma((4,)), dma((3, 4)), dma((3, 4)), dma((8,)), dma((8,)),
+            dma((4,)), dma((4,)), dma((4,)), dma((4,)), dma((3, 2)), dma((3, 2)), dma((4,)), dma((4,)), dma((8,)), dma((8,)),
+        ],
+        compiler_params=pltpu.CompilerParams(collective_id=number, has_side_effects=True, vmem_limit_bytes=60 * 2**20),
+    )(ga, segc, segr, qg, kg, small, gain, w, ctx, q, k, v, qr, kr, cosine, sine, wq, wk, wv, a, hidden, middle)
 
 
 def on_device(
@@ -317,9 +1540,111 @@
     )
 
 
+def full_tables(tokens):
+    half_dim = HEAD_DIM // 2
+    fine_cos, fine_sin = rope_tables(lax.iota(jnp.int32, 64).astype(f32), half_dim)
+    coarse = (64 * lax.iota(jnp.int32, tokens // 64)).astype(f32)
+    coarse_cos, coarse_sin = rope_tables(coarse, half_dim)
+    fine_cos, fine_sin = fine_cos.reshape(1, 64, half_dim), fine_sin.reshape(1, 64, half_dim)
+    cosine = (coarse_cos * fine_cos - coarse_sin * fine_sin).reshape(tokens, half_dim)
+    sine = (coarse_sin * fine_cos + coarse_cos * fine_sin).reshape(tokens, half_dim)
+    return jnp.concatenate([cosine, cosine], 1), jnp.concatenate([-sine, sine], 1)
+
+
+def dense_layer(
+    hidden_in, norm1_gain, w_query, w_key, w_value, w_out, query_gain, key_gain, norm2_gain, w_router,
+    w_gate, w_up, w_down, routes, segments, cotangent,
+):
+    rows, width = hidden_in.shape
+    experts = w_router.shape[1]
+    devices = lax.axis_size("expert")
+    tokens = devices * rows
+    my_index = lax.axis_index("expert")
+    head = my_index // 2
+
+    def own_head(v):
+        return lax.dynamic_slice_in_dim(v, head * HEAD_DIM, HEAD_DIM, v.ndim - 1)
+
+    weights = jnp.concatenate([own_head(w_query), own_head(w_key), own_head(w_value)], 1)
+    q_gain, k_gain = own_head(query_gain)[None], own_head(key_gain)[None]
+    cosine, sine = full_tables(tokens)
+    attn_all, queries, keys, values, q_raw, k_raw = project_all(
+        hidden_in, norm1_gain[None], weights, q_gain, k_gain, cosine, sine, 1
+    )
+    segc, segr = segments[:, None], segments[None]
+    own_mask = jnp.sum((routes[:, :, None] == lax.iota(jnp.int32, experts)).astype(f32), 1)
+    sent = jnp.concatenate([cotangent, jnp.pad(own_mask.astype(bf16), ((0, 0), (0, 128 - experts)))], 1)
+    attn_out, own_context, grads_all = attend_all(
+        sent, queries, keys, values, segc, segr, w_out, 2
+    )
+
+    inputs = hidden_in.astype(f32)
+    middle = inputs + attn_out.astype(f32)
+    inverse_moe = inverse_rms(middle)
+    normed_moe = middle * inverse_moe
+    moe_input = (normed_moe * norm2_gain).astype(bf16)
+    everyone, weighted, grad_acts, parts = experts_all(
+        moe_input, grads_all, w_router, w_gate, w_up, w_down, 3
+    )
+    total, grad_gate, grad_up, grad_down = sums_all(
+        parts.reshape(devices, rows, 2 * width + 128), everyone, grad_acts, grads_all, weighted, 4
+    )
+    output = (middle + total[:, :width].astype(f32)).astype(bf16)
+    grad_final = cotangent.astype(f32)
+    tail = total[:, 2 * width :].astype(f32)
+    grad_gates = tail[:, :experts] + tail[:, experts : 2 * experts]
+    logits = jnp.where(
+        own_mask > 0, jnp.dot(moe_input, w_router, preferred_element_type=f32), -jnp.inf
+    )
+    raised_gate = jnp.exp(logits - jnp.max(logits, -1, keepdims=True))
+    gate_weights = raised_gate / jnp.sum(raised_gate, -1, keepdims=True)
+    grad_logits = (
+        gate_weights * (grad_gates - jnp.sum(grad_gates * gate_weights, -1, keepdims=True))
+    ).astype(bf16)
+    grad_moe_input = jnp.dot(grad_logits, w_router.T, preferred_element_type=f32)
+    grad_moe_input = grad_moe_input + total[:, width : 2 * width].astype(f32)
+    grad_middle = grad_final + norm_back(grad_moe_input * norm2_gain, normed_moe, inverse_moe)
+    small = jnp.concatenate(
+        [
+            lax.dot_general(grad_logits, moe_input, (((0,), (0,)), ((), ())), preferred_element_type=f32),
+            jnp.sum(grad_moe_input * normed_moe, 0, keepdims=True),
+            jnp.zeros((7, width), f32),
+        ],
+        0,
+    )
+
+    grad_input, grad_qkv, grad_norm1, gains, grad_w_out, small = backward_all(
+        grad_middle.astype(bf16), segc, segr, q_gain, k_gain, small, norm1_gain[None], w_out, own_context,
+        queries, keys, values, q_raw, k_raw, cosine, sine, w_query, w_key, w_value, attn_all, hidden_in, grad_middle, 5,
+    )
+    return (
+        output,
+        grad_input,
+        grad_norm1[0],
+        grad_qkv[0],
+        grad_qkv[1],
+        grad_qkv[2],
+        grad_w_out.T,
+        gains[0],
+        gains[1],
+        small[experts],
+        small[:experts].T,
+        grad_gate,
+        grad_up,
+        grad_down,
+    )
+
+
+def layer(*arrays):
+    rows, experts = arrays[0].shape[0], arrays[9].shape[1]
+    whole = 2 * rows * TOP // experts >= rows and rows * lax.axis_size("expert") == SEQ
+    grid = (lax.axis_size("expert"), lax.axis_size("head")) == (8, 4)
+    return dense_layer(*arrays) if whole and grid else on_device(*arrays)
+
+
 def solution(mesh):
     return jax.shard_map(
-        on_device,
+        layer,
         mesh=mesh,
         in_specs=(
             P("expert", None),

time: 2880 us -> 445 us (0.15)
  waiting for transfers between devices: 1550 us -> 0 us
  blocking collectives: 777 us -> 0 us
  Pallas kernels: 0 us -> 391 us
  matrix products: 184 us -> 4.25 us
  local copies, waits for them, and re-layouts: 201 us -> 24.3 us
  other arithmetic: 94.3 us -> 15.1 us
  starting transfers between devices: 59 us -> 0 us
    all_to_all x2 -> x0, blocking collectives: 741 us -> none  [the longest x1 371 us: on_device(): lax.all_to_all(outgoing, 'expert', split_axis=0, concat_axis=0, tiled=True)]
    all_to_all x2 -> x0, waiting for transfers between devices: 699 us -> none  [the longest x1 356 us: on_device(): lax.all_to_all(leaving_grad, 'expert', split_axis=0, concat_axis=0, tiled...]
    reduce_scatter x6 -> x0, waiting for transfers between devices: 478 us -> none  [the longest x1 124 us: on_device(): lax.psum_scatter(partial_out.astype(jnp.bfloat16), 'head', scatter_dimens...]
    pallas_call x0 -> x5, Pallas kernels: none -> 391 us  [the longest x1 106 us: backward_all(): pl.pallas_call(backward_kernel, in_specs=[VM] * 7 + [ANY, VM] + [ANY] * 1...]
    all_gather x2 -> x0, waiting for transfers between devices: 215 us -> none  [the longest x1 108 us: on_device(): leaving = lax.all_gather(rows_out, 'head', axis=2, tiled=True)]
    dot_general x32 -> x3, matrix products: 184 us -> 4.25 us  [the longest x1 2.27 us: dense_layer(): jnp.dot(grad_logits, w_router.T, preferred_element_type=f32)]
    gather x11 -> x0, local copies, waits for them, and re-layouts: 101 us -> none  [the longest x1 24.7 us: on_device(): grad_home.reshape(expert_total * capacity, width)[position]]
    ppermute x14 -> x0, waiting for transfers between devices: 90.7 us -> none  [from_behind(): return lax.ppermute(shard, axis, pairs)]
  transfers between devices with their start and end apart: 27 -> 0, of which waited for: 22 -> 0; matrix products, arithmetic and copies ran while one was open for 6% -> 0% of each run, Pallas kernels for 0% -> 0%
where the time goes in v4:
time: 445 us; the launch traced here: 436 us
  Pallas kernels  391 us (88%)
  local copies, waits for them, and re-layouts  24.3 us (5%)
  other arithmetic  15.1 us (3%)
    pallas_call x1, Pallas kernels, backward_all(): pl.pallas_call(backward_kernel, in_specs=[VM] * 7 + [ANY, VM] + [ANY] * 1...  106 us
    pallas_call x1, Pallas kernels, sums_all(): pl.pallas_call(sums_kernel, in_specs=[ANY] * 5, out_specs=[VM, ANY, ANY,...  101 us
    pallas_call x1, Pallas kernels, experts_all(): pl.pallas_call(experts_kernel, in_specs=[ANY, ANY, VM, ANY, ANY, ANY], ou...  64.8 us
    pallas_call x1, Pallas kernels, attend_all(): pl.pallas_call(attend_all_kernel, in_specs=[ANY] + [VM] * 6, out_specs=[V...  61.7 us
    pallas_call x1, Pallas kernels, project_all(): pl.pallas_call(project_all_kernel, in_specs=[ANY] + [VM] * 6, out_specs=[...  57.3 us
    unnamed x43, local copies, waits for them, and re-layouts  14.4 us

profile of v4, /device:TPU:0, one launch (start us, length us, event | category | flops | bytes accessed | tf_op | source)
XLA Modules:
  0.0 436.0 jit_solution(12033044941425814329)
XLA Ops:
  0.7 1.3 constant_dynamic-slice_fusion
  2.0 1.1 constant_dynamic-slice_fusion.2
  3.0 1.3 pad_maximum_fusion.w_ref
  4.4 1.3 dynamic-slice_bitcast_fusion
  5.7 0.2 multiply_cosine_fusion
  5.9 0.1 multiply_cosine_fusion.1
  6.0 0.3 multiply_add_fusion.1
  6.4 0.1 bitcast_negate_fusion
  6.4 1.9 pad_maximum_fusion.1
  8.4 57.3 %shard_map.263 = (bf16[2048,2048]{1,0:T(8,128)(2,1)}, bf16[2048,128]{1,0:T(8,128)(2,1)}, bf16[2048,128]{1,0:T(8,128)(2,1)}, bf16[2048,128]{1,0:T(8,128)(2,1)}, f32[2048,128]{1,0:T(8,128)}, /*index=5*/f32[2048,128]{1,0:T(8,128)}) custom-call(bf16[256,2048]{1,0:T(8,128)(2,1)} %hidden_in.1, f32[1,2048]{1,0:T(1,128)} %bitcast.38, ...), custom_call_target="tpu_custom_call" | custom-call | tf_op jit(solution)/shard_map/pallas_call | solution.py:389
  65.7 0.0 copy-start.12
  65.7 0.0 copy-done.15
  65.8 0.1 copy.48
  65.9 0.0 copy-done.4
  65.9 1.1 fusion.2.sent_ref
  67.0 0.0 copy-done.12
  67.0 1.3 copy.49.segc_ref
  68.3 61.7 %shard_map.264 = (bf16[256,2048]{1,0:T(8,128)(2,1)}, bf16[256,512]{1,0:T(8,128)(2,1)}, bf16[2048,2176]{1,0:T(8,128)(2,1)}) custom-call(bf16[256,2176]{1,0:T(8,128)(2,1)} %fusion.2.sent_ref, bf16[2048,128]{1,0:T(8,128)(2,1)} %get-tuple-element.37.q_ref.q_in, bf16[2048,128]{1,0:T(8,128)(2,1)} %get-tuple-element.38.k_ref.k_in, ...), custom_call_target="tpu_custom_call" | custom-call | tf_op jit(solution)/shard_map/pallas_call | solution.py:493
  130.0 0.0 copy-start.1
  130.0 0.0 copy-start.14
  130.0 0.0 copy-done
  130.0 1.7 multiply_reduce_fusion.2
  131.8 0.0 copy-done.1
  131.8 0.0 copy-done.14
  131.8 1.5 multiply_convert_fusion.own_ref
  133.3 0.0 copy-done.13
  133.3 1.0 copy.50.wr_ref
  134.3 64.8 %shard_map.265 = (bf16[2048,2048]{1,0:T(8,128)(2,1)}, bf16[2048,512]{1,0:T(8,128)(2,1)}, bf16[2048,1024]{1,0:T(8,128)(2,1)}, bf16[2048,4224]{1,0:T(8,128)(2,1)}) custom-call(bf16[256,2048]{1,0:T(8,128)(2,1)} %multiply_convert_fusion.own_ref, bf16[2048,2176]{1,0:T(8,128)(2,1)} %get-tuple-element.41.grads_ref, bf16[2048,16]{1,0:T(8,128)(2,1)} %copy.50.wr_ref, ...), custom_call_target="tpu_custom_call" | custom-call | tf_op jit(solution)/shard_map/pallas_call | solution.py:623
  199.2 101.1 %shard_map.266 = (bf16[256,4224]{1,0:T(8,128)(2,1)}, f32[2,2048,256]{2,1,0:T(8,128)}, f32[2,2048,256]{2,1,0:T(8,128)}, f32[2,256,2048]{2,1,0:T(8,128)}) custom-call(bf16[8,256,4224]{2,1,0:T(8,128)(2,1)} %bitcast.31, bf16[2048,2048]{1,0:T(8,128)(2,1)} %get-tuple-element.43.x_ref, bf16[2048,1024]{1,0:T(8,128)(2,1)} %get-tuple-element.44.acts_ref, ...), custom_call_target="tpu_custom_call" | custom-call | tf_op jit(solution)/shard_map/pallas_call | solution.py:888
  300.2 0.0 copy-start.3
  300.2 0.0 copy-start.2
  300.2 1.0 slice_convert_fusion
  301.3 0.1 copy.51
  301.4 1.7 fusion.7
  303.1 0.2 fusion.4
  303.3 0.3 multiply_reduce_fusion.3
  303.5 0.2 multiply_convert_fusion.1
  303.8 0.0 copy-done.3
  303.8 0.3 fusion.8
  304.0 0.0 copy-done.2
  304.0 2.3 multiply_reduce_fusion
  306.3 0.1 pad.7.clone
  306.4 0.8 maximum_maximum_fusion.gains_small
  307.2 0.0 copy-done.5
  307.2 4.3 fusion.5
  311.5 106.4 %shard_map.267 = (f32[256,2048]{1,0:T(8,128)}, f32[3,256,512]{2,1,0:T(8,128)}, f32[1,2048]{1,0:T(1,128)}, f32[2,512]{1,0:T(2,128)}, f32[256,512]{1,0:T(8,128)}, /*index=5*/f32[24,2048]{1,0:T(8,128)}) custom-call(bf16[256,2048]{1,0:T(8,128)(2,1)} %get-tuple-element.118.ga_ref, s32[2048,1]{1,0:T(8,128)} %copy.49.segc_ref, s32[1,2048]{1,0:T(1,128)} %bitcast.36, ...), custom_call_target="tpu_custom_call" | custom-call | tf_op jit(solution)/shard_map/pallas_call | solution.py:1251
  417.8 0.0 copy-start.10
  417.8 0.0 copy-start.11
  417.8 0.0 copy-start.17
  417.9 0.0 copy-start.9
  417.9 2.7 slice_bitcast_fusion
  420.6 1.0 copy.54
  421.5 0.0 copy-done.11
  421.6 0.7 slice_bitcast_fusion.3
  422.2 0.6 slice.46
  422.8 0.6 fusion.6
  423.4 1.3 copy.62
  424.7 0.6 copy.63
  425.3 1.0 copy-done.8
  426.4 2.1 copy.64
  428.5 1.6 copy-done.7
  430.1 2.1 copy.65
  432.2 1.6 copy-done.6
  433.8 2.0 copy.66
  (22 shorter events, 0.1 us)
Async XLA Ops:
  8.4 57.4 %copy-start.15 = (s32[256,8]{0,1:T(8,128)S(1)}, s32[256,8]{0,1:T(8,128)}, u32[]{:S(2)}) copy-start(s32[256,8]{0,1:T(8,128)} %param.29) | copy-start | bytes 24580
  8.4 57.5 %copy-start.4 = (bf16[256,2048]{1,0:T(8,128)(2,1)S(1)}, bf16[256,2048]{1,0:T(8,128)(2,1)}, u32[]{:S(2)}) copy-start(bf16[256,2048]{1,0:T(8,128)(2,1)} %param.31) | copy-start | bytes 3145732
  65.7 1.3 copy-start.12
  68.3 61.7 %copy-start = (bf16[256,2048]{1,0:T(8,128)(2,1)S(1)}, bf16[256,2048]{1,0:T(8,128)(2,1)}, u32[]{:S(2)}) copy-start(bf16[256,2048]{1,0:T(8,128)(2,1)} %hidden_in.1) | copy-start | bytes 3145732
  130.0 1.8 copy-start.1
  130.0 1.8 copy-start.14
  131.8 1.5 copy-start.13
  300.2 3.5 copy-start.3
  300.2 3.8 copy-start.2
  304.0 3.1 copy-start.5
  417.8 2.7 copy-start.10
  417.8 3.7 copy-start.11
  417.8 5.0 %copy-start.17 = (f32[2,512]{1,0:T(2,128)S(1)}, f32[2,512]{1,0:T(2,128)}, u32[]{:S(2)}) copy-start(f32[2,512]{1,0:T(2,128)} %get-tuple-element.55) | copy-start | bytes 12292
  417.9 5.6 %copy-start.9 = (f32[256,2048]{1,0:T(8,128)S(1)}, f32[256,2048]{1,0:T(8,128)}, u32[]{:S(2)}) copy-start(f32[256,2048]{1,0:T(8,128)} %get-tuple-element.156) | copy-start | bytes 6291460
  421.6 3.2 copy-start.16
  423.4 3.0 copy-start.8
  426.4 3.7 copy-start.7
  430.1 3.7 copy-start.6

commit v5 on v4

--- a/solution.py
+++ b/solution.py
@@ -180,50 +180,53 @@
     def at(self, b, start, size):
         return self.whole.at[pl.ds(pl.multiple_of(b * self.rows + start, self.unit), size)]
 
-    def copy(self, kind, c, b, part, where, own=False):
+    def copy(self, first, c, index, b, part, where, own=False):
         if own:
             source = self.own.at[pl.ds(pl.multiple_of(part[0], self.unit), part[1])]
         else:
             source = self.at(b, *part)
         return pltpu.make_async_remote_copy(
-            src_ref=source, dst_ref=self.at(b, *part), send_sem=self.send.at[kind, c, b], recv_sem=self.recv.at[kind, c, b],
+            src_ref=source, dst_ref=self.at(b, *part), send_sem=self.send.at[first + index], recv_sem=self.recv.at[first + index],
             device_id=where, device_id_type=MESH)
 
     def up(self, b, c, own=False):
         z, y, x, core = self.place
-        return self.copy(0, c, b, self.slab[c], device(z + 1, y, x, core), own)
+        return self.copy(0, c, c * 4 + b // 2, b, self.slab[c], device(z + 1, y, x, core), own)
 
     def down(self, b, c, own=False):
         z, y, x, core = self.place
-        return self.copy(1, c, b, self.slab[c], device(z - 1, y, x, core), own)
+        return self.copy(8, c, c * 4 + b // 2, b, self.slab[c], device(z - 1, y, x, core), own)
 
     def over(self, b, c, own=False):
         z, y, x, core = self.place
-        return self.copy(2, c, b, self.slab[c], device(z, 1 - y, x, core), own)
+        return self.copy(16, c, c * 4 + b // 2, b, self.slab[c], device(z, 1 - y, x, core), own)
 
     def side(self, b, part):
         z, y, x, core = self.place
-        return self.copy(3, 0, b, part, device(z, y, 1 - x, core))
+        return self.copy(24, 0, b, b, part, device(z, y, 1 - x, core))
 
     def twin(self, b, c, part):
         z, y, x, core = self.place
-        return self.copy(4, c, b, part, device(z, y, x, 1 - core))
+        return self.copy(32, c, c * 8 + b, b, part, device(z, y, x, 1 - core))
 
     def twin_x(self, b, part):
         z, y, x, core = self.place
-        return self.copy(5, 0, b, part, device(z, y, x, 1 - core))
+        return self.copy(48, 0, b, b, part, device(z, y, x, 1 - core))
 
     def group(self, i):
         z = self.place[0]
         ahead = z // 2
         return picked(i, (z, z + 1 - 2 * (z % 2), 2 - ahead, 3 - 3 * ahead))
 
+    def start_chunk(self, c):
+        z, y, x, core = self.place
+        pl.when(z < 3)(lambda: self.up(self.me, c, True).start())
+        pl.when(z > 0)(lambda: self.down(self.me, c, True).start())
+        self.over(self.me, c, True).start()
+
     def start(self):
-        z, y, x, core = self.place
-        for c in range(2):
-            pl.when(z < 3)(lambda: self.up(self.me, c, True).start())
-            pl.when(z > 0)(lambda: self.down(self.me, c, True).start())
-            self.over(self.me, c, True).start()
+        self.start_chunk(0)
+        self.start_chunk(1)
         self.keep.start()
 
     def spread(self, b, c):
@@ -323,313 +326,10 @@
         self.drain()
 
 
-GATHER_SEMS = [pltpu.SemaphoreType.DMA, pltpu.SemaphoreType.DMA((6, 2, 8)), pltpu.SemaphoreType.DMA((6, 2, 8))]
+GATHER_SEMS = [pltpu.SemaphoreType.DMA, pltpu.SemaphoreType.DMA((56,)), pltpu.SemaphoreType.DMA((56,))]
 
 
 ANY = pl.BlockSpec(memory_space=pl.ANY)
-
-
-def project_all_kernel(own_ref, gain_ref, w_ref, qg_ref, kg_ref, cos_ref, sin_ref,
-                       a_out, q_ref, k_ref, v_ref, qr_ref, kr_ref,
-                       whole, a_buf, local_sem, send, recv, a_sem):
-    greet(*place())
-    gather = Gather(own_ref, whole, local_sem, send, recv)
-    gather.start()
-    gather.hop(1)
-    gather.cross(0)
-    gather.hop_inside(2)
-    gather.flank(0)
-    gather.keep.wait()
-    span = 2 * BLOCK
-
-    def rows_of(i):
-        return pl.ds(pl.multiple_of(gather.group(i) * span, span), span)
-
-    def stored(i, slot):
-        return pltpu.make_async_copy(a_buf.at[slot], a_out.at[rows_of(i)], a_sem.at[slot])
-
-    def step(i, _):
-        gather.complete(i)
-        pl.when(i == 0)(lambda: gather.hop_inside(3))
-        rows = rows_of(i)
-        slot = i % 2
-        pl.when(i >= 2)(lambda: stored(i - 2, slot).wait())
-        x = whole[rows].astype(f32)
-        a = (x * norm_factor(x) * gain_ref[...]).astype(bf16)
-        a_buf[slot] = a
-        stored(i, slot).start()
-        raw = dot(a, w_ref[...])
-        cosine, sine = cos_ref[rows], sin_ref[rows]
-
-        def turned(part, gain):
-            n = part * norm_factor(part) * gain
-            return (n * cosine + pltpu.roll(n, HD // 2, 1) * sine).astype(bf16)
-
-        q_raw, k_raw = raw[:, :HD], raw[:, HD:2 * HD]
-        qr_ref[rows] = q_raw
-        kr_ref[rows] = k_raw
-        q_ref[rows] = turned(q_raw, qg_ref[...])
-        k_ref[rows] = turned(k_raw, kg_ref[...])
-        v_ref[rows] = raw[:, 2 * HD:].astype(bf16)
-        pl.when(i < 2)(lambda: gather.hop_outside(i + 2))
-        pl.when(i < 3)(lambda: gather.cross(i + 1))
-        pl.when(i < 3)(lambda: gather.flank(i + 1))
-        return 0
-
-    lax.fori_loop(0, 4, step, 0)
-    stored(2, 0).wait()
-    stored(3, 1).wait()
-    gather.drain()
-
-
-def project_all(own, gain, w, qg, kg, cosine, sine, number):
-    rows, D = own.shape
-    T = 8 * rows
-    sd = jax.ShapeDtypeStruct
-    return pl.pallas_call(
-        project_all_kernel, in_specs=[ANY] + [VM] * 6, out_specs=[ANY] + [VM] * 5,
-        out_shape=[sd((T, D), bf16)] + [sd((T, HD), bf16)] * 3 + [sd((T, HD), f32)] * 2,
-        scratch_shapes=[pltpu.VMEM((T, D), bf16), pltpu.VMEM((2, 2 * rows, D), bf16)] + GATHER_SEMS + [pltpu.SemaphoreType.DMA((2,))],
-        compiler_params=pltpu.CompilerParams(collective_id=number, has_side_effects=True, vmem_limit_bytes=56 * 2**20),
-    )(own, gain, w, qg, kg, cosine, sine)
-
-
-def attend_all_kernel(sent_ref, q_ref, k_ref, v_ref, segc_ref, segr_ref, w_ref, total, gathered, whole,
-                      part, arrived, out_half, in_half, held, from_x, local_sem, g_send, g_recv,
-                      send, recv, pair_send, pair_recv):
-    z, y, x, core = place()
-    across, twin = device(z, y, 1 - x, core), device(z, y, x, 1 - core)
-    greet_peers(z, y, x, core, (across, twin))
-    gather = Gather(sent_ref, whole, local_sem, g_send, g_recv)
-    targets = lambda r: (y if r % 2 == 0 else 1 - y)
-    source_y = (y + z) % 2
-
-    def remote(source, target, ssem, rsem, where):
-        return pltpu.make_async_remote_copy(
-            src_ref=source, dst_ref=target, send_sem=ssem, recv_sem=rsem, device_id=where, device_id_type=MESH)
-
-    def to_block(r):
-        return remote(part.at[r], arrived.at[z], send.at[r], recv.at[z], device(r, targets(r), x, core))
-
-    def from_head(n):
-        return remote(part.at[n], arrived.at[n], send.at[n], recv.at[n], device(n, source_y, x, core))
-
-    here = lambda r: (z == r) & (z % 2 == 0)
-    gather.start()
-    for r in range(3, -1, -1):
-        start = pl.multiple_of(block_of(r, y) * BLOCK, BLOCK)
-        probs = probabilities(r, start, q_ref[pl.ds(start, BLOCK)], k_ref, segc_ref, segr_ref)
-        part[r] = dot(probs.astype(bf16), v_ref[:(2 * r + 2) * BLOCK]).astype(bf16)
-        pl.when(jnp.logical_not(here(r)))(lambda: to_block(r).start())
-
-    gather.hop(1)
-    gather.cross(0)
-    gather.hop_inside(2)
-
-    @pl.when(z % 2 == 0)
-    def _():
-        arrived[z] = part[z]
-
-    for n in range(4):
-        pl.when(jnp.logical_not(here(n)))(lambda: from_head(n).wait_recv())
-        gathered[:, n * HD:(n + 1) * HD] = arrived[n]
-
-    rows = total.shape[0]
-    half = rows // 2
-    chunk = half // 2
-    my_half = core * half
-    other_half = (1 - core) * half
-    piece = lambda c: pl.ds(c * chunk, chunk)
-    at = lambda base, c: pl.ds(pl.multiple_of(base + c * chunk, chunk), chunk)
-
-    def pair(kind, c, source, target, where):
-        return remote(source, target, pair_send.at[kind, c], pair_recv.at[kind, c], where)
-
-    first = [pair(0, c, out_half.at[piece(c)], in_half.at[piece(c)], twin) for c in range(2)]
-    second = [pair(1, c, held.at[piece(c)], from_x.at[piece(c)], across) for c in range(2)]
-    third = [pair(2, c, total.at[at(my_half, c)], total.at[at(my_half, c)], twin) for c in range(2)]
-    for c in range(2):
-        out_half[piece(c)] = dot(gathered[at(other_half, c)], w_ref[...]).astype(bf16)
-        first[c].start()
-    for c in range(2):
-        kept = dot(gathered[at(my_half, c)], w_ref[...])
-        first[c].wait_recv()
-        held[piece(c)] = (kept + in_half[piece(c)].astype(f32)).astype(bf16)
-        second[c].start()
-    gather.flank(0)
-    gather.hop_outside(2)
-    gather.cross(1)
-    gather.hop_inside(3)
-    for c in range(2):
-        second[c].wait_recv()
-        total[at(my_half, c)] = (held[piece(c)].astype(f32) + from_x[piece(c)].astype(f32)).astype(bf16)
-        third[c].start()
-    gather.flank(1)
-    gather.hop_outside(3)
-    gather.cross(2)
-    for c in range(2):
-        pair(2, c, total.at[at(my_half, c)], total.at[at(other_half, c)], twin).wait_recv()
-    gather.cross(3)
-    gather.flank(2)
-    gather.flank(3)
-    for i in range(4):
-        gather.complete(i)
-    gather.keep.wait()
-    gather.drain()
-    for c in range(2):
-        first[c].wait_send()
-        second[c].wait_send()
-        third[c].wait_send()
-    for r in range(4):
-        pl.when(jnp.logical_not(here(r)))(lambda: to_block(r).wait_send())
-
-
-def attend_all(sent, q, k, v, segc, segr, w, number):
-    rows, width = sent.shape
-    D = w.shape[1]
-    half = rows // 2
-    sd = jax.ShapeDtypeStruct
-    dma = pltpu.SemaphoreType.DMA
-    return pl.pallas_call(
-        attend_all_kernel, in_specs=[ANY] + [VM] * 6, out_specs=[VM, VM, ANY],
-        out_shape=[sd((rows, D), bf16), sd((rows, 4 * HD), bf16), sd((8 * rows, width), bf16)],
-        scratch_shapes=[pltpu.VMEM((4, BLOCK, HD), bf16)] * 2 + [pltpu.VMEM((half, D), bf16)] * 4 + GATHER_SEMS + [
-            dma((4,)), dma((4,)), dma((3, 2)), dma((3, 2))],
-        compiler_params=pltpu.CompilerParams(collective_id=number, has_side_effects=True, vmem_limit_bytes=56 * 2**20),
-    )(sent, q, k, v, segc, segr, w)
-
-
-def experts_kernel(own_ref, grads_ref, wr_ref, wg_in, wu_in, wd_in, x_out, weighted_out, acts_out, parts_out,
-                   whole, wg, wu, wd, g_buf, mask_all, gw, w_buf, a_buf, p_buf,
-                   local_sem, send, recv, weight_sem, g_sem, out_sem):
-    z, y, x_place, core = place()
-    first = (z * 2 + y) * wg_in.shape[0]
-    D, ff = wg_in.shape[1], wg_in.shape[2]
-    span = 2 * BLOCK
-    weights = [pltpu.make_async_copy(source, target, weight_sem.at[k])
-               for k, (source, target) in enumerate(((wd_in, wd), (wg_in, wg), (wu_in, wu)))]
-
-    def grads_load(g):
-        return pltpu.make_async_copy(grads_ref.at[pl.ds(g * span, span)], g_buf.at[g % 2], g_sem.at[g % 2])
-
-    weights[0].start()
-    grads_load(0).start()
-    grads_load(1).start()
-    weights[1].start()
-    weights[2].start()
-    greet(z, y, x_place, core)
-    gather = Gather(own_ref, whole, local_sem, send, recv)
-    gather.start()
-    weights[0].wait()
-    for g in range(4):
-        grads_load(g).wait()
-        rows = slice(g * span, (g + 1) * span)
-        mask_all[rows] = g_buf[g % 2, :, D:]
-        for j in range(2):
-            gw[rows, j * ff:(j + 1) * ff] = dot_nt(g_buf[g % 2, :, :D], wd[j])
-        if g < 2:
-            grads_load(g + 2).start()
-    gather.hop(1)
-    gather.cross(0)
-    gather.hop_inside(2)
-    gather.flank(0)
-    gather.keep.wait()
-    weights[1].wait()
-    weights[2].wait()
-
-    def rows_of(i):
-        return pl.ds(pl.multiple_of(gather.group(i) * span, span), span)
-
-    def stores(i, slot):
-        rows = rows_of(i)
-        return [
-            pltpu.make_async_copy(w_buf.at[slot], weighted_out.at[rows], out_sem.at[slot, 0]),
-            pltpu.make_async_copy(a_buf.at[slot], acts_out.at[rows], out_sem.at[slot, 1]),
-            pltpu.make_async_copy(p_buf.at[slot], parts_out.at[rows], out_sem.at[slot, 2]),
-        ]
-
-    def x_store(i, slot):
-        return pltpu.make_async_copy(whole.at[rows_of(i)], x_out.at[rows_of(i)], out_sem.at[slot, 3])
-
-    def step(i, _):
-        gather.complete(i)
-        slot = i % 2
-
-        @pl.when(i >= 2)
-        def _():
-            for copy in stores(i - 2, slot):
-                copy.wait()
-            x_store(i - 2, slot).wait()
-
-        x_store(i, slot).start()
-        rows = rows_of(i)
-        x = whole[rows]
-        logits = dot(x, wr_ref[...])
-        count = logits.shape[1]
-        mask = mask_all[rows, :count].astype(f32) > 0
-        top = jnp.max(jnp.where(mask, logits, -jnp.inf), -1, keepdims=True)
-        raised = jnp.where(mask, jnp.exp(jnp.where(mask, logits - top, 0.0)), 0.0)
-        gates = raised / jnp.sum(raised, -1, keepdims=True)
-        lane = lax.broadcasted_iota(jnp.int32, gates.shape, 1)
-        gg = jnp.zeros(gates.shape, f32)
-        for j in range(2):
-            here = lane == first + j
-            gate = jnp.sum(jnp.where(here, gates, 0.0), -1, keepdims=True)
-            ga = dot(x, wg[j])
-            ua = dot(x, wu[j])
-            gw_j = gw[rows, j * ff:(j + 1) * ff]
-            s = 1.0 / (1.0 + jnp.exp(-ga))
-            silu = ga * s
-            h = (silu * ua).astype(bf16).astype(f32)
-            gg = gg + jnp.where(here, jnp.sum(h * gw_j, -1, keepdims=True), 0.0)
-            gh = gw_j * gate
-            w_buf[slot, :, j * ff:(j + 1) * ff] = (h * gate).astype(bf16)
-            a_buf[slot, :, 2 * j * ff:(2 * j + 1) * ff] = (gh * ua * s * (1.0 + ga * (1.0 - s))).astype(bf16)
-            a_buf[slot, :, (2 * j + 1) * ff:(2 * j + 2) * ff] = (gh * silu).astype(bf16)
-            if j == 0:
-                pl.when(i == 0)(lambda: gather.hop_inside(3))
-        pl.when(i < 2)(lambda: gather.hop_outside(i + 2))
-        pl.when(i < 3)(lambda: gather.cross(i + 1))
-        p_buf[slot, :, :D] = dot(w_buf[slot], wd[...].reshape(2 * ff, D)).astype(bf16)
-        gx = dot_nt(a_buf[slot, :, :ff], wg[0])
-        for k, weight in ((1, wu[0]), (2, wg[1]), (3, wu[1])):
-            gx = gx + dot_nt(a_buf[slot, :, k * ff:(k + 1) * ff], weight)
-        p_buf[slot, :, D:2 * D] = gx.astype(bf16)
-        high = gg.astype(bf16)
-        low = (gg - high.astype(f32)).astype(bf16)
-        spare = jnp.zeros((span, 128 - 2 * count), bf16)
-        p_buf[slot, :, 2 * D:] = jnp.concatenate([high, low, spare], 1)
-        for copy in stores(i, slot):
-            copy.start()
-        pl.when(i < 3)(lambda: gather.flank(i + 1))
-        return 0
-
-    lax.fori_loop(0, 4, step, 0)
-    for i in (2, 3):
-        for copy in stores(i, i % 2):
-            copy.wait()
-        x_store(i, i % 2).wait()
-    gather.drain()
-
-
-def experts_all(own, grads, wr, wg, wu, wd, number):
-    rows, D = own.shape
-    T = 8 * rows
-    J, _, F = wg.shape
-    span = 2 * rows
-    sd = jax.ShapeDtypeStruct
-    dma = pltpu.SemaphoreType.DMA
-    vm = pltpu.VMEM
-    return pl.pallas_call(
-        experts_kernel, in_specs=[ANY, ANY, VM, ANY, ANY, ANY], out_specs=[ANY] * 4,
-        out_shape=[sd((T, D), bf16), sd((T, J * F), bf16), sd((T, 2 * J * F), bf16), sd((T, 2 * D + 128), bf16)],
-        scratch_shapes=[
-            vm((T, D), bf16), vm((J, D, F), bf16), vm((J, D, F), bf16), vm((J, F, D), bf16),
-            vm((2, span, D + 128), bf16), vm((T, 128), bf16), vm((T, J * F), f32),
-            vm((2, span, J * F), bf16), vm((2, span, 2 * J * F), bf16), vm((2, span, 2 * D + 128), bf16),
-        ] + GATHER_SEMS + [dma((3,)), dma((2,)), dma((2, 4))],
-        compiler_params=pltpu.CompilerParams(collective_id=number, has_side_effects=True, vmem_limit_bytes=60 * 2**20),
-    )(own, grads, wr, wg, wu, wd)
 
 
 def sum_rows(target, source, cols, rows):
@@ -901,9 +601,311 @@
     )(parts, x, acts, grads, weighted)
 
 
+def forward_kernel(hidden, sent_ref, gain1_ref, gain2_ref, qg_ref, kg_ref, segc_ref, segr_ref, wr_ref,
+                   wq_in, wk_in, wv_in, cos_in, sin_in, wout_in, wg_in, wu_in, wd_in,
+                   gathered, middle_out, moe_out, x_all, a_out, q_out, k_out, v_out, qr_out, kr_out, grads_all,
+                   m_out, weighted_out, acts_out, parts_out,
+                   w_qkv, cos_ref, sin_ref, w_out, wg, wu, wd, q_ref, k_ref, v_ref, qr_ref, kr_ref,
+                   part, arrived, out_half, in_half, held, from_x, total, middle_ref, moe, whole, mask_all, w_buf, a_buf, p_buf,
+                   x_keep, x_send, x_recv, c_keep, c_send, c_recv, m_keep, m_send, m_recv,
+                   load, stream, out_sem, kept_sem, send, recv, pair_send, pair_recv):
+    z, y, x, core = place()
+    across, twin = device(z, y, 1 - x, core), device(z, y, x, 1 - core)
+    first_expert = (z * 2 + y) * wg_in.shape[0]
+    D, ff = wg_in.shape[1], wg_in.shape[2]
+    span = 2 * BLOCK
+    head = pl.ds(pl.multiple_of(z * HD, HD), HD)
+    loads = [pltpu.make_async_copy(source, target, load.at[k]) for k, (source, target) in enumerate((
+        (wq_in.at[:, head], w_qkv.at[:, pl.ds(0, HD)]), (wk_in.at[:, head], w_qkv.at[:, pl.ds(HD, HD)]),
+        (wv_in.at[:, head], w_qkv.at[:, pl.ds(2 * HD, HD)]), (cos_in, cos_ref), (sin_in, sin_ref),
+        (wout_in, w_out), (wd_in, wd), (wg_in, wg), (wu_in, wu)))]
+    for copy in loads:
+        copy.start()
+    greet_peers(z, y, x, core, (across, twin))
+    gather = Gather(hidden, x_all, x_keep, x_send, x_recv)
+    cot = Gather(sent_ref, grads_all, c_keep, c_send, c_recv)
+    experts = Gather(moe, whole, m_keep, m_send, m_recv)
+
+    def remote(source, target, ssem, rsem, where):
+        return pltpu.make_async_remote_copy(
+            src_ref=source, dst_ref=target, send_sem=ssem, recv_sem=rsem, device_id=where, device_id_type=MESH)
+
+    gather.start()
+    gather.hop(1)
+    gather.cross(0)
+    gather.hop_inside(2)
+    gather.flank(0)
+    gather.keep.wait()
+    for copy in loads[:5]:
+        copy.wait()
+
+    def rows_of(i):
+        return pl.ds(pl.multiple_of(gather.group(i) * span, span), span)
+
+    x_part, a_part = p_buf.at[:, pl.ds(0, D)], p_buf.at[:, pl.ds(D, D)]
+
+    def a_store(i):
+        return pltpu.make_async_copy(a_part, a_out.at[rows_of(i)], stream.at[1])
+
+    def project(i):
+        gather.complete(i)
+        rows = rows_of(i)
+        fetch = pltpu.make_async_copy(x_all.at[rows], x_part, stream.at[0])
+        fetch.start()
+        if i > 0:
+            a_store(i - 1).wait()
+        fetch.wait()
+        v = p_buf[:, :D].astype(f32)
+        a = (v * norm_factor(v) * gain1_ref[...]).astype(bf16)
+        p_buf[:, D:2 * D] = a
+        a_store(i).start()
+        raw = dot(a, w_qkv[...])
+        cosine, sine = cos_ref[rows], sin_ref[rows]
+
+        def turned(part, gain):
+            n = part * norm_factor(part) * gain
+            return (n * cosine + pltpu.roll(n, HD // 2, 1) * sine).astype(bf16)
+
+        q_raw, k_raw = raw[:, :HD], raw[:, HD:2 * HD]
+        qr_ref[rows] = q_raw
+        kr_ref[rows] = k_raw
+        q_ref[rows] = turned(q_raw, qg_ref[:, head])
+        k_ref[rows] = turned(k_raw, kg_ref[:, head])
+        v_ref[rows] = raw[:, 2 * HD:].astype(bf16)
+
+    for i in range(4):
+        if i < 2:
+            gather.hop_outside(i + 2)
+        if i < 3:
+            gather.cross(i + 1)
+        if i == 0:
+            gather.hop_inside(3)
+        if i == 1:
+            cot.start()
+        project(i)
+        if i < 3:
+            gather.flank(i + 1)
+    a_store(3).wait()
+    keeps = [pltpu.make_async_copy(source, target, kept_sem.at[k]) for k, (source, target) in enumerate((
+        (q_ref, q_out), (k_ref, k_out), (v_ref, v_out), (qr_ref, qr_out), (kr_ref, kr_out),
+        (middle_ref, middle_out), (moe, moe_out)))]
+    for copy in keeps[:5]:
+        copy.start()
+    cot.hop(1)
+    cot.cross(0)
+    cot.hop_inside(2)
+
+    targets = lambda r: (y if r % 2 == 0 else 1 - y)
+    source_y = (y + z) % 2
+
+    def to_block(r):
+        return remote(part.at[r], arrived.at[z], send.at[r], recv.at[z], device(r, targets(r), x, core))
+
+    def from_head(n):
+        return remote(part.at[n], arrived.at[n], send.at[n], recv.at[n], device(n, source_y, x, core))
+
+    here = lambda r: (z == r) & (z % 2 == 0)
+    for r in range(3, -1, -1):
+        start = pl.multiple_of(block_of(r, y) * BLOCK, BLOCK)
+        probs = probabilities(r, start, q_ref[pl.ds(start, BLOCK)], k_ref, segc_ref, segr_ref)
+        part[r] = dot(probs.astype(bf16), v_ref[:(2 * r + 2) * BLOCK]).astype(bf16)
+        pl.when(jnp.logical_not(here(r)))(lambda: to_block(r).start())
+    cot.flank(0)
+
+    @pl.when(z % 2 == 0)
+    def _():
+        arrived[z] = part[z]
+
+    loads[5].wait()
+    for n in range(4):
+        pl.when(jnp.logical_not(here(n)))(lambda: from_head(n).wait_recv())
+        gathered[:, n * HD:(n + 1) * HD] = arrived[n]
+    cot.hop_outside(2)
+    cot.cross(1)
+    cot.hop_inside(3)
+
+    half = BLOCK // 2
+    chunk = half // 2
+    my_half = core * half
+    other_half = (1 - core) * half
+    piece = lambda c: pl.ds(pl.multiple_of(c * chunk, chunk), chunk)
+    at = lambda base, c: pl.ds(pl.multiple_of(base + c * chunk, chunk), chunk)
+
+    def pair(kind, c, source, target, where):
+        return remote(source, target, pair_send.at[kind, c], pair_recv.at[kind, c], where)
+
+    first = lambda c: pair(0, c, out_half.at[piece(c)], in_half.at[piece(c)], twin)
+    second = lambda c: pair(1, c, held.at[piece(c)], from_x.at[piece(c)], across)
+    third = lambda c: pair(2, c, total.at[at(my_half, c)], total.at[at(my_half, c)], twin)
+    for c in (1 - x, x):
+        out_half[piece(c)] = dot(gathered[at(other_half, c)], w_out[...]).astype(bf16)
+        first(c).start()
+    for c in (1 - x, x):
+        kept = dot(gathered[at(my_half, c)], w_out[...])
+        first(c).wait_recv()
+        held[piece(c)] = (kept + in_half[piece(c)].astype(f32)).astype(bf16)
+        second(c).start()
+    cot.flank(1)
+    step = 32
+
+    def norm_rows(base, count):
+        def body(i, _):
+            rows = pl.ds(pl.multiple_of(base + i * step, step), step)
+            v = hidden[rows].astype(f32) + total[rows].astype(f32)
+            middle_ref[rows] = v
+            moe[rows] = (v * norm_factor(v) * gain2_ref[...]).astype(bf16)
+            return 0
+        lax.fori_loop(0, count // step, body, 0)
+
+    for k, c in enumerate((x, 1 - x)):
+        second(c).wait_recv()
+        total[at(my_half, c)] = (held[piece(c)].astype(f32) + from_x[piece(c)].astype(f32)).astype(bf16)
+        third(c).start()
+        norm_rows(my_half + c * chunk, chunk)
+        experts.start_chunk(k)
+        if k == 0:
+            cot.hop_outside(3)
+            cot.cross(2)
+    for c in (x, 1 - x):
+        pair(2, c, total.at[at(my_half, c)], total.at[at(other_half, c)], twin).wait_recv()
+    norm_rows(other_half, half)
+    experts.keep.start()
+    for copy in keeps[5:]:
+        copy.start()
+    cot.flank(2)
+    experts.hop(1)
+    experts.cross(0)
+    cot.cross(3)
+    experts.hop_inside(2)
+    experts.flank(0)
+    cot.flank(3)
+    experts.keep.wait()
+    cot.keep.wait()
+    for copy in loads[6:]:
+        copy.wait()
+
+    def grads_load(i):
+        rows = rows_of(i)
+        return [pltpu.make_async_copy(grads_all.at[rows, pl.ds(0, D)], p_buf.at[:, pl.ds(0, D)], stream.at[1]),
+                pltpu.make_async_copy(grads_all.at[rows, pl.ds(D, 128)], mask_all, stream.at[2])]
+
+    def stores(i):
+        rows = rows_of(i)
+        return [
+            pltpu.make_async_copy(w_buf.at[i % 2], weighted_out.at[rows], out_sem.at[i % 2, 0]),
+            pltpu.make_async_copy(a_buf.at[i % 2], acts_out.at[rows], out_sem.at[i % 2, 1]),
+            pltpu.make_async_copy(whole.at[rows], m_out.at[rows], out_sem.at[i % 2, 2]),
+        ]
+
+    def parts_store(i):
+        return pltpu.make_async_copy(p_buf, parts_out.at[rows_of(i)], stream.at[0])
+
+    def run_experts(i):
+        cot.complete(i)
+        if i > 0:
+            parts_store(i - 1).wait()
+        fetches = grads_load(i)
+        for copy in fetches:
+            copy.start()
+        experts.complete(i)
+        slot = i % 2
+        if i >= 2:
+            for copy in stores(i - 2):
+                copy.wait()
+
+        rows = rows_of(i)
+        v = whole[rows]
+        logits = dot(v, wr_ref[...])
+        count = logits.shape[1]
+        for copy in fetches:
+            copy.wait()
+        mask = mask_all[:, :count].astype(f32) > 0
+        top = jnp.max(jnp.where(mask, logits, -jnp.inf), -1, keepdims=True)
+        raised = jnp.where(mask, jnp.exp(jnp.where(mask, logits - top, 0.0)), 0.0)
+        gates = raised / jnp.sum(raised, -1, keepdims=True)
+        lane = lax.broadcasted_iota(jnp.int32, gates.shape, 1)
+        gg = jnp.zeros(gates.shape, f32)
+        for j in range(2):
+            mine = lane == first_expert + j
+            gate = jnp.sum(jnp.where(mine, gates, 0.0), -1, keepdims=True)
+            ga = dot(v, wg[j])
+            ua = dot(v, wu[j])
+            gw_j = dot_nt(p_buf[:, :D], wd[j])
+            s = 1.0 / (1.0 + jnp.exp(-ga))
+            silu = ga * s
+            h = (silu * ua).astype(bf16).astype(f32)
+            gg = gg + jnp.where(mine, jnp.sum(h * gw_j, -1, keepdims=True), 0.0)
+            gh = gw_j * gate
+            w_buf[slot, :, j * ff:(j + 1) * ff] = (h * gate).astype(bf16)
+            a_buf[slot, :, 2 * j * ff:(2 * j + 1) * ff] = (gh * ua * s * (1.0 + ga * (1.0 - s))).astype(bf16)
+            a_buf[slot, :, (2 * j + 1) * ff:(2 * j + 2) * ff] = (gh * silu).astype(bf16)
+        for copy in stores(i):
+            copy.start()
+        if i < 3:
+            experts.flank(i + 1)
+        p_buf[:, :D] = dot(w_buf[slot], wd[...].reshape(2 * ff, D)).astype(bf16)
+        gx = dot_nt(a_buf[slot, :, :ff], wg[0])
+        for k, weight in ((1, wu[0]), (2, wg[1]), (3, wu[1])):
+            gx = gx + dot_nt(a_buf[slot, :, k * ff:(k + 1) * ff], weight)
+        p_buf[:, D:2 * D] = gx.astype(bf16)
+        high = gg.astype(bf16)
+        low = (gg - high.astype(f32)).astype(bf16)
+        spare = jnp.zeros((span, 128 - 2 * count), bf16)
+        p_buf[:, 2 * D:] = jnp.concatenate([high, low, spare], 1)
+        parts_store(i).start()
+
+    for i in range(4):
+        if i < 2:
+            experts.hop_outside(i + 2)
+        if i < 3:
+            experts.cross(i + 1)
+        if i == 0:
+            experts.hop_inside(3)
+        run_experts(i)
+    parts_store(3).wait()
+    for i in (2, 3):
+        for copy in stores(i):
+            copy.wait()
+    for copy in keeps:
+        copy.wait()
+    gather.drain()
+    cot.drain()
+    experts.drain()
+    for c in range(2):
+        first(c).wait_send()
+        second(c).wait_send()
+        third(c).wait_send()
+    for r in range(4):
+        pl.when(jnp.logical_not(here(r)))(lambda: to_block(r).wait_send())
+
+
+def forward_all(hidden, sent, gain1, gain2, qg, kg, segc, segr, wr, wq, wk, wv, cosine, sine, wout, wg, wu, wd, number):
+    rows, D = hidden.shape
+    T = 8 * rows
+    J, _, F = wg.shape
+    half, span = rows // 2, 2 * rows
+    sd = jax.ShapeDtypeStruct
+    dma = pltpu.SemaphoreType.DMA
+    vm = pltpu.VMEM
+    like = lambda m: vm(m.shape, m.dtype)
+    heads = [((T, HD), bf16)] * 3 + [((T, HD), f32)] * 2
+    return pl.pallas_call(
+        forward_kernel, in_specs=[VM] * 9 + [ANY] * 9, out_specs=[VM] + [ANY] * 14,
+        out_shape=[sd((rows, 4 * HD), bf16), sd((rows, D), f32), sd((rows, D), bf16), sd((T, D), bf16), sd((T, D), bf16)]
+        + [sd(*m) for m in heads] + [sd((T, D + 128), bf16), sd((T, D), bf16), sd((T, J * F), bf16), sd((T, 2 * J * F), bf16),
+                                     sd((T, 2 * D + 128), bf16)],
+        scratch_shapes=[vm((D, 3 * HD), bf16)] + [like(m) for m in (cosine, sine, wout, wg, wu, wd)]
+        + [vm(*m) for m in heads] + [vm((4, BLOCK, HD), bf16)] * 2 + [vm((half, D), bf16)] * 4 + [vm((rows, D), bf16), vm((rows, D), f32), vm((rows, D), bf16)] + [
+            vm((T, D), bf16), vm((span, 128), bf16), vm((2, span, J * F), bf16), vm((2, span, 2 * J * F), bf16),
+            vm((span, 2 * D + 128), bf16)] + GATHER_SEMS * 3 + [
+            dma((9,)), dma((3,)), dma((2, 3)), dma((7,)), dma((4,)), dma((4,)), dma((3, 2)), dma((3, 2))],
+        compiler_params=pltpu.CompilerParams(collective_id=number, has_side_effects=True, vmem_limit_bytes=62 * 2**20),
+    )(hidden, sent, gain1, gain2, qg, kg, segc, segr, wr, wq, wk, wv, cosine, sine, wout, wg, wu, wd)
+
+
 def backward_kernel(ga_ref, segc_ref, segr_ref, qg_ref, kg_ref, gains_small, gain_ref,
                     w_in, ctx_ref, q_in, k_in, v_in, qr_in, kr_in, cos_in, sin_in, wq_in, wk_in, wv_in, a_in, hidden_in, middle_in,
-                    grad_ref, weights_ref, norm_ref, gains_out, wout_ref, small_out,
+                    grad_ref, weights_q, weights_k, weights_v, norm_ref, gains_out, wout_ref, small_out,
                     w_ref, q_ref, k_ref, v_ref, qr_ref, kr_ref, cos_ref, sin_ref, wq_ref, wk_ref, wv_ref, columns, hidden_ref, middle_ref,
                     raw_ref, g_own, g_all, dk, dv, terms, from_y, held_terms, from_below, from_above,
                     small_y, small_sum, small_z, raw_in, gathered, products, from_z, out_half, in_half, held, from_x, total, gains_own, gains_in, norm_in,
@@ -985,7 +987,7 @@
         return remote(small_out.at[:, own_lanes], small_out.at[:, fan_lanes[i]], s_send.at[5 + i], s_recv.at[5 + i], fans[i])
 
     for b in range(8):
-        terms[b] = dot_tn(ga_ref[:, b * BLOCK:(b + 1) * BLOCK], ctx_ref[...]).astype(bf16)
+        terms[b] = dot_tn(ctx_ref[...], ga_ref[:, b * BLOCK:(b + 1) * BLOCK]).astype(bf16)
 
     def term_pair(n):
         return remote(terms.at[n * 2 + 1 - y], from_y.at[n], t_send.at[0, n], t_recv.at[0, n], partner)
@@ -1042,7 +1044,7 @@
         factor = norm_factor(raw)
         n = raw * factor
         gain_sums[which] = gain_sums[which] + jnp.sum(g * n, 0, keepdims=True)
-        g = g * gain[...]
+        g = g * gain[:, pl.ds(pl.multiple_of(z * HD, HD), HD)]
         return (factor * (g - n * jnp.mean(g * n, -1, keepdims=True))).astype(bf16)
 
     for copy in loads[1:8]:
@@ -1072,19 +1074,11 @@
         def _():
             when_away(b // 2, lambda: rows_to(b // 2).start())
 
-        if b == 5:
-            small_pair.wait_recv()
-            small_sum[...] = small_ref[:, own_lanes] + small_y[...]
-            for n in range(4):
-                when_away(n, lambda: small_along(n).start())
-            small_z[z] = small_sum[...]
-        if b == 1:
-            for n in range(4):
-                when_away(n, lambda: small_arriving(n).wait_recv())
-            small_out[:, own_lanes] = (small_z[0] + small_z[1]) + (small_z[2] + small_z[3])
-            for i in range(3):
-                small_spread(i).start()
-
+    small_pair.wait_recv()
+    small_sum[...] = small_ref[:, own_lanes] + small_y[...]
+    for n in range(4):
+        when_away(n, lambda: small_along(n).start())
+    small_z[z] = small_sum[...]
     gains_own[0:1] = gain_sums[0]
     gains_own[1:2] = gain_sums[1]
 
@@ -1114,10 +1108,11 @@
             products_to(n).start()
         else:
             from_z[z] = product
+        if i % 2 == 0:
+            term_stage(i // 2)
 
     for copy in loads[8:]:
         copy.wait()
-    term_stage(0)
     for n in range(4):
         when_away(n, lambda: rows_from(n).wait_recv())
         for g in range(3):
@@ -1150,7 +1145,6 @@
         held[piece(c)] = (kept + in_half[piece(c)].astype(f32)).astype(bf16)
         second[c].start()
 
-    term_stage(1)
     term_stage(2)
     term_pair(z).wait_recv()
     wout_ref[...] = paired(z)
@@ -1165,6 +1159,11 @@
         term_down(z).wait_recv()
         wout_ref[...] += from_above[z].astype(f32)
 
+    for n in range(4):
+        when_away(n, lambda: small_arriving(n).wait_recv())
+    small_out[:, own_lanes] = (small_z[0] + small_z[1]) + (small_z[2] + small_z[3])
+    for i in range(3):
+        small_spread(i).start()
     for n in range(4):
         when_away(n, lambda: gains_from(n).wait_recv())
         gains_out[:, n * HD:(n + 1) * HD] = gains_in[n]
@@ -1209,7 +1208,7 @@
         when_away(n, lambda: products_from(n).wait_recv())
     for n in range(4):
         for g in range(3):
-            weights_ref[g, :, n * HD:(n + 1) * HD] = from_z[n, :, g * HD:(g + 1) * HD].astype(f32)
+            (weights_q, weights_k, weights_v)[g][:, n * HD:(n + 1) * HD] = from_z[n, :, g * HD:(g + 1) * HD].astype(f32)
     for b in range(8):
         pl.when(me != b)(lambda: norm_from(b).wait_recv())
     sums = [norm_in[b] for b in range(8)]
@@ -1249,13 +1248,13 @@
     vm = pltpu.VMEM
     like = lambda m: vm(m.shape, m.dtype)
     return pl.pallas_call(
-        backward_kernel, in_specs=[VM] * 7 + [ANY, VM] + [ANY] * 13, out_specs=[VM] * 6,
-        out_shape=[sd((rows, D), f32), sd((3, BLOCK, span), f32), sd((1, D), f32), sd((2, span), f32),
-                   sd((BLOCK, span), f32), sd((S, D), f32)],
+        backward_kernel, in_specs=[VM] * 7 + [ANY, VM] + [ANY] * 13, out_specs=[VM] * 8,
+        out_shape=[sd((rows, D), f32), sd((BLOCK, span), f32), sd((BLOCK, span), f32), sd((BLOCK, span), f32), sd((1, D), f32), sd((2, span), f32),
+                   sd((span, BLOCK), f32), sd((S, D), f32)],
         scratch_shapes=[like(m) for m in (w, q, k, v, qr, kr, cosine, sine, wq, wk, wv)] + [
             vm((4, T, BLOCK), bf16), like(hidden), like(middle),
             vm((8, BLOCK, 3 * HD), bf16), vm((4, BLOCK, HD), bf16), vm((8, BLOCK, HD), bf16), vm((T, HD), f32), vm((T, HD), f32),
-            vm((8, BLOCK, span), bf16)] + [vm((4, BLOCK, span), bf16)] * 4 + [
+            vm((8, span, BLOCK), bf16)] + [vm((4, span, BLOCK), bf16)] * 4 + [
             vm((S, D // 4), f32), vm((S, D // 4), f32), vm((4, S, D // 4), f32),
             vm((4, BLOCK, 3 * HD), bf16), vm((rows, 3 * span), bf16), vm((4, BLOCK, 3 * HD), bf16), vm((4, BLOCK, 3 * HD), bf16)] + [vm((half, D), bf16)] * 4 + [
             vm((rows, D), bf16), vm((2, HD), f32), vm((4, 2, HD), f32), vm((8, D // 128, 128), f32),
@@ -1559,35 +1558,21 @@
     experts = w_router.shape[1]
     devices = lax.axis_size("expert")
     tokens = devices * rows
-    my_index = lax.axis_index("expert")
-    head = my_index // 2
-
-    def own_head(v):
-        return lax.dynamic_slice_in_dim(v, head * HEAD_DIM, HEAD_DIM, v.ndim - 1)
-
-    weights = jnp.concatenate([own_head(w_query), own_head(w_key), own_head(w_value)], 1)
-    q_gain, k_gain = own_head(query_gain)[None], own_head(key_gain)[None]
+
     cosine, sine = full_tables(tokens)
-    attn_all, queries, keys, values, q_raw, k_raw = project_all(
-        hidden_in, norm1_gain[None], weights, q_gain, k_gain, cosine, sine, 1
-    )
     segc, segr = segments[:, None], segments[None]
     own_mask = jnp.sum((routes[:, :, None] == lax.iota(jnp.int32, experts)).astype(f32), 1)
     sent = jnp.concatenate([cotangent, jnp.pad(own_mask.astype(bf16), ((0, 0), (0, 128 - experts)))], 1)
-    attn_out, own_context, grads_all = attend_all(
-        sent, queries, keys, values, segc, segr, w_out, 2
-    )
-
-    inputs = hidden_in.astype(f32)
-    middle = inputs + attn_out.astype(f32)
+    own_context, middle, moe_input, _, attn_all, queries, keys, values, q_raw, k_raw, grads_all, everyone, weighted, grad_acts, parts = (
+        forward_all(
+            hidden_in, sent, norm1_gain[None], norm2_gain[None], query_gain[None], key_gain[None], segc, segr, w_router,
+            w_query, w_key, w_value, cosine, sine, w_out, w_gate, w_up, w_down, 1,
+        )
+    )
     inverse_moe = inverse_rms(middle)
     normed_moe = middle * inverse_moe
-    moe_input = (normed_moe * norm2_gain).astype(bf16)
-    everyone, weighted, grad_acts, parts = experts_all(
-        moe_input, grads_all, w_router, w_gate, w_up, w_down, 3
-    )
     total, grad_gate, grad_up, grad_down = sums_all(
-        parts.reshape(devices, rows, 2 * width + 128), everyone, grad_acts, grads_all, weighted, 4
+        parts.reshape(devices, rows, 2 * width + 128), everyone, grad_acts, grads_all, weighted, 2
     )
     output = (middle + total[:, :width].astype(f32)).astype(bf16)
     grad_final = cotangent.astype(f32)
@@ -1613,18 +1598,18 @@
         0,
     )
 
-    grad_input, grad_qkv, grad_norm1, gains, grad_w_out, small = backward_all(
-        grad_middle.astype(bf16), segc, segr, q_gain, k_gain, small, norm1_gain[None], w_out, own_context,
-        queries, keys, values, q_raw, k_raw, cosine, sine, w_query, w_key, w_value, attn_all, hidden_in, grad_middle, 5,
+    grad_input, grad_query, grad_key, grad_value, grad_norm1, gains, grad_w_out, small = backward_all(
+        grad_middle.astype(bf16), segc, segr, query_gain[None], key_gain[None], small, norm1_gain[None], w_out, own_context,
+        queries, keys, values, q_raw, k_raw, cosine, sine, w_query, w_key, w_value, attn_all, hidden_in, grad_middle, 3,
     )
     return (
         output,
         grad_input,
         grad_norm1[0],
-        grad_qkv[0],
-        grad_qkv[1],
-        grad_qkv[2],
-        grad_w_out.T,
+        grad_query,
+        grad_key,
+        grad_value,
+        grad_w_out,
         gains[0],
         gains[1],
         small[experts],

time: 445 us -> 414 us (0.930)
  Pallas kernels: 391 us -> 365 us
    pallas_call x3 -> x1, Pallas kernels: 184 us -> 164 us  [forward_all(): pl.pallas_call(forward_kernel, in_specs=[VM] * 9 + [ANY] * 9, out_specs=[...]
    pallas_call x1, Pallas kernels: 106 us -> 100 us  [backward_all(): pl.pallas_call(backward_kernel, in_specs=[VM] * 7 + [ANY, VM] + [ANY] * 1...]
    unnamed x43 -> x38, local copies, waits for them, and re-layouts: 14.4 us -> 17.5 us
where the time goes in v5:
time: 414 us; the launch traced here: 407 us
  Pallas kernels  365 us (88%)
  local copies, waits for them, and re-layouts  23.5 us (6%)
  other arithmetic  14 us (3%)
    pallas_call x1, Pallas kernels, forward_all(): pl.pallas_call(forward_kernel, in_specs=[VM] * 9 + [ANY] * 9, out_specs=[...  164 us
    pallas_call x1, Pallas kernels, sums_all(): pl.pallas_call(sums_kernel, in_specs=[ANY] * 5, out_specs=[VM, ANY, ANY,...  101 us
    pallas_call x1, Pallas kernels, backward_all(): pl.pallas_call(backward_kernel, in_specs=[VM] * 7 + [ANY, VM] + [ANY] * 1...  100 us
    unnamed x38, local copies, waits for them, and re-layouts  17.5 us

profile of v5, /device:TPU:0, one launch (start us, length us, event | category | flops | bytes accessed | tf_op | source)
XLA Modules:
  0.0 406.6 jit_solution(5144366432498916406)
XLA Ops:
  0.6 0.0 copy-start.12
  0.7 0.0 copy-start.10
  0.7 0.8 convert_reduce_fusion
  1.4 0.1 copy.45
  1.6 2.3 fusion.1.sent_ref
  3.9 0.0 copy-done.12
  3.9 1.3 copy.46.segc_ref
  5.2 0.0 copy-done.10
  5.2 1.0 copy.47.wr_ref
  6.2 0.2 multiply_cosine_fusion
  6.4 0.1 multiply_cosine_fusion.1
  6.6 0.3 multiply_add_fusion.1
  6.9 0.1 bitcast_negate_fusion
  7.0 1.9 pad_maximum_fusion
  8.9 164.3 %shard_map.263 = (bf16[256,512]{1,0:T(8,128)(2,1)}, f32[256,2048]{1,0:T(8,128)}, bf16[256,2048]{1,0:T(8,128)(2,1)}, bf16[2048,2048]{1,0:T(8,128)(2,1)}, bf16[204...) custom-call(bf16[256,2048]{1,0:T(8,128)(2,1)} %hidden_in.1, ...), custom_call_target="tpu_custom_call" | custom-call | tf_op jit(solution)/shard_map/pallas_call | solution.py:892
  173.2 1.8 multiply_reduce_fusion.2
  175.0 0.0 copy-start.5
  175.0 100.5 %shard_map.264 = (bf16[256,4224]{1,0:T(8,128)(2,1)}, f32[2,2048,256]{2,1,0:T(8,128)}, f32[2,2048,256]{2,1,0:T(8,128)}, f32[2,256,2048]{2,1,0:T(8,128)}) custom-call(bf16[8,256,4224]{2,1,0:T(8,128)(2,1)} %bitcast.23, bf16[2048,2048]{1,0:T(8,128)(2,1)} %get-tuple-element.42.x_ref, bf16[2048,1024]{1,0:T(8,128)(2,1)} %get-tuple-element.43.acts_ref, ...), custom_call_target="tpu_custom_call" | custom-call | tf_op jit(solution)/shard_map/pallas_call | solution.py:588
  275.6 0.0 copy-start
  275.6 0.0 copy-start.11
  275.6 1.0 slice_convert_fusion
  276.6 0.1 copy.48
  276.7 0.0 copy-done.5
  276.7 0.5 fusion.6
  277.2 0.2 fusion.3
  277.4 0.3 multiply_reduce_fusion.3
  277.7 0.2 multiply_convert_fusion
  277.9 0.0 copy-done
  277.9 0.0 copy-done.11
  277.9 0.0 copy-start.1
  277.9 2.1 multiply_reduce_fusion
  280.1 0.0 copy-done.1
  280.1 4.1 fusion.4
  284.1 0.3 fusion.7
  284.4 0.1 pad.7.clone
  284.5 0.8 maximum_maximum_fusion.gains_small
  285.3 100.2 %shard_map.265 = (f32[256,2048]{1,0:T(8,128)}, f32[256,512]{1,0:T(8,128)}, f32[256,512]{1,0:T(8,128)}, f32[256,512]{1,0:T(8,128)}, f32[1,2048]{1,0:T(1,128)}, /*...) custom-call(bf16[256,2048]{1,0:T(8,128)(2,1)} %get-tuple-element.68.ga_ref, s32[2048,1]{1,0:T(8,128)} %copy.46.segc_ref, ...), custom_call_target="tpu_custom_call" | custom-call | tf_op jit(solution)/shard_map/pallas_call | solution.py:1250
  385.5 1.3 fusion.5
  386.8 1.4 slice.34
  388.2 1.6 slice_bitcast_fusion
  389.8 0.0 copy-start.13
  389.8 0.0 copy-start.9
  389.8 0.0 copy-start.8
  389.8 0.0 copy-start.7
  389.8 0.0 copy-start.6
  389.8 3.3 copy.62
  393.1 0.0 copy-done.13
  393.1 0.0 copy-start.4
  393.1 0.6 copy.63
  393.7 0.0 copy-done.9
  393.7 0.8 copy.64
  394.5 0.0 copy-done.8
  394.5 0.8 copy.65
  395.3 0.0 copy-done.7
  395.3 0.8 copy.66
  396.1 0.0 copy-done.6
  396.1 0.8 copy.67
  396.9 0.0 copy-done.4
  396.9 0.0 copy-start.3
  396.9 2.1 copy.68
  399.0 1.6 copy-done.3
  400.6 2.1 copy.69
  402.7 1.6 copy-done.2
  404.3 2.0 copy.70
  (9 shorter events, 0.0 us)
Async XLA Ops:
  0.6 3.2 copy-start.12
  0.7 4.6 %copy-start.10 = (bf16[2048,16]{0,1:T(8,128)(2,1)S(1)}, bf16[2048,16]{0,1:T(8,128)(2,1)}, u32[]{:S(2)}) copy-start(bf16[2048,16]{0,1:T(8,128)(2,1)} %param.25) | copy-start | bytes 196612
  175.0 101.7 %copy-start.5 = (bf16[256,2048]{1,0:T(8,128)(2,1)S(1)}, bf16[256,2048]{1,0:T(8,128)(2,1)}, u32[]{:S(2)}) copy-start(bf16[256,2048]{1,0:T(8,128)(2,1)} %get-tuple-element.47) | copy-start | bytes 3145732
  275.6 2.3 copy-start
  275.6 2.3 copy-start.11
  277.9 2.2 copy-start.1
  389.8 3.3 copy-start.13
  389.8 3.9 copy-start.9
  389.8 4.7 %copy-start.8 = (f32[256,512]{1,0:T(8,128)S(1)}, f32[256,512]{1,0:T(8,128)}, u32[]{:S(2)}) copy-start(f32[256,512]{1,0:T(8,128)} %get-tuple-element.102) | copy-start | bytes 1572868
  389.8 5.5 %copy-start.7 = (f32[256,512]{1,0:T(8,128)S(1)}, f32[256,512]{1,0:T(8,128)}, u32[]{:S(2)}) copy-start(f32[256,512]{1,0:T(8,128)} %get-tuple-element.103) | copy-start | bytes 1572868
  389.8 6.3 %copy-start.6 = (f32[512,256]{1,0:T(8,128)S(1)}, f32[512,256]{1,0:T(8,128)}, u32[]{:S(2)}) copy-start(f32[512,256]{1,0:T(8,128)} %get-tuple-element.104) | copy-start | bytes 1572868
  393.1 3.8 copy-start.4
  396.9 3.7 copy-start.3
  400.6 3.7 copy-start.2

commit v6 on v5

--- a/solution.py
+++ b/solution.py
@@ -159,23 +159,24 @@
 
 
 class Gather:
-    def __init__(self, own, whole, local_sem, send, recv, rows=BLOCK):
+    def __init__(self, own, whole, local_sem, send, recv, lone=2, rows=BLOCK):
         self.own, self.whole, self.send, self.recv, self.rows = own, whole, send, recv, rows
         z, y, x, core = self.place = place()
         self.me = z * 2 + y
         half, eighth = rows // 2, rows // 8
         self.unit = eighth // 2
+        lone, lead = lone * self.unit, 3 * self.unit
         self.keep = pltpu.make_async_copy(own, self.at(self.me, 0, rows), local_sem)
 
         def chunks(c):
-            return ((c * half + x * 5 * self.unit, 3 * self.unit), (c * half + (3 - x) * self.unit, 3 * self.unit))
-
-        def quarter(c, of):
-            return (c * half + of * 3 * eighth, eighth)
+            return ((c * half + x * (half - lead), lead), (c * half + (1 - x) * lead + x * lone, half - lead - lone))
+
+        def edge(c, of):
+            return (c * half + of * (half - lone), lone)
 
         self.slab, self.twin_slab = chunks(core), chunks(1 - core)
-        self.mine, self.theirs = quarter(core, x), quarter(core, 1 - x)
-        self.twin_theirs = quarter(1 - core, 1 - x)
+        self.mine, self.theirs = edge(core, x), edge(core, 1 - x)
+        self.twin_theirs = edge(1 - core, 1 - x)
 
     def at(self, b, start, size):
         return self.whole.at[pl.ds(pl.multiple_of(b * self.rows + start, self.unit), size)]
@@ -332,62 +333,188 @@
 ANY = pl.BlockSpec(memory_space=pl.ANY)
 
 
-def sum_rows(target, source, cols, rows):
-    step = 16
-    main = cols.size - cols.size % 2048
+def sum_rows(target, source, rows):
+    step = 32
+    width = target.shape[-1]
+    main = width - width % 1024
 
     @pl.loop(0, rows // step)
     def _(i):
         part = pl.ds(pl.multiple_of(i * step, step), step)
-        wide = pl.ds(cols.start, main)
+        wide = pl.ds(0, main)
         target[part, wide] = (target[part, wide].astype(f32) + source[part, wide].astype(f32)).astype(bf16)
-        if main < cols.size:
-            tail = pl.ds(cols.start + main, cols.size - main)
+        if main < width:
+            tail = pl.ds(main, width - main)
             target[part, tail] = add_split(target[part, tail], source[part, tail])
 
 
-def sums_kernel(parts, x_ref, acts_ref, grads_ref, weighted_ref, total, gate_out, up_out, down_out,
-                held, from_core, from_x, from_y, from_below, from_above, shared_in,
-                acts, weighted, x_buf, g_buf, gu_buf, down_buf,
-                load_sem, send, recv, end_send, end_recv, fixed_sem, x_sem, g_sem, gu_sem, down_sem):
+class Scatter:
+    def __init__(self, parts, start, total, buffers, sems):
+        self.parts, self.total = parts, total
+        self.cols = pl.ds(start, total.shape[1])
+        self.held, self.from_core, self.from_x, self.from_y, self.from_below, self.from_above, self.shared_in = buffers
+        self.load_sem, self.sems, self.recv_sems, self.end_send, self.end_recv = sems
+        z, y, x, core = self.place = place()
+        self.me = z * 2 + y
+        self.order = far_first(z)
+        self.half = half = parts.shape[1] // 2
+        self.piece = piece = half // 4
+        ds = lambda start, size: pl.ds(pl.multiple_of(start, piece), size)
+        self.my_half, self.other_half = ds(core * half, half), ds((1 - core) * half, half)
+        self.slab, self.mine, self.theirs = ds(x * piece, 3 * piece), ds(x * 3 * piece, piece), ds((1 - x) * 3 * piece, piece)
+        self.shared = pl.ds(piece, 2 * piece)
+        base = core * half
+        self.out_mine, self.out_theirs = ds(base + x * 3 * piece, piece), ds(base + (1 - x) * 3 * piece, piece)
+        self.out_shared = ds(base + piece, 2 * piece)
+        self.across, self.twin = device(z, y, 1 - x, core), device(z, y, x, 1 - core)
+
+    def remote(self, number, source, target, where):
+        return pltpu.make_async_remote_copy(
+            src_ref=source, dst_ref=target, send_sem=self.sems.at[number], recv_sem=self.recv_sems.at[number],
+            device_id=where, device_id_type=MESH)
+
+    def load(self, b):
+        return pltpu.make_async_copy(self.parts.at[b, self.my_half, self.cols], self.held.at[b], self.load_sem.at[b])
+
+    def to_core(self, b):
+        return self.remote(b, self.parts.at[b, self.other_half, self.cols], self.from_core.at[b], self.twin)
+
+    def to_x(self, b):
+        return self.remote(8 + b, self.held.at[b, self.theirs], self.from_x.at[b], self.across)
+
+    def to_y(self, zb):
+        z, y, x, core = self.place
+        return self.remote(16 + zb, self.held.at[zb * 2 + 1 - y, self.slab], self.from_y.at[zb], device(z, 1 - y, x, core))
+
+    def to_above(self, zb):
+        z, y, x, core = self.place
+        return self.remote(20 + zb, self.held.at[zb * 2 + y, self.slab], self.from_below.at[zb], device(z + 1, y, x, core))
+
+    def to_below(self, zb):
+        z, y, x, core = self.place
+        return self.remote(24 + zb, self.held.at[zb * 2 + y, self.slab], self.from_above.at[zb], device(z - 1, y, x, core))
+
+    def begin(self, k):
+        y = self.place[1]
+        for yb in (1 - y, y):
+            self.load(self.order[k] * 2 + yb).start()
+            self.to_core(self.order[k] * 2 + yb).start()
+
+    def stage_core(self, k, other):
+        y = self.place[1]
+        b = self.order[k] * 2 + (1 - y if other else y)
+        self.load(b).wait()
+        self.to_core(b).wait_recv()
+        sum_rows(self.held.at[b], self.from_core.at[b], self.half)
+        self.to_x(b).start()
+
+    def stage_x(self, k, other=False):
+        y = self.place[1]
+        b = self.order[k] * 2 + (1 - y if other else y)
+        self.to_x(b).wait_recv()
+        sum_rows(self.held.at[b, self.mine], self.from_x.at[b], self.piece)
+
+    def stage_y(self, k):
+        self.stage_x(k, True)
+        self.to_y(self.order[k]).start()
+
+    def add_slab(self, zb, source):
+        sum_rows(self.held.at[zb * 2 + self.place[1], self.slab], source.at[zb], 3 * self.piece)
+
+    def stage_z(self, k):
+        z = self.place[0]
+        zb = self.order[k]
+        self.to_y(zb).wait_recv()
+        self.add_slab(zb, self.from_y)
+        rises = (z // 2 == 0) if k < 2 else (z % 2 == 0)
+
+        @pl.when(rises)
+        def _():
+            @pl.when(z > 0)
+            def _():
+                self.to_above(zb).wait_recv()
+                self.add_slab(zb, self.from_below)
+            self.to_above(zb).start()
+
+        @pl.when(jnp.logical_not(rises))
+        def _():
+            @pl.when(z < 3)
+            def _():
+                self.to_below(zb).wait_recv()
+                self.add_slab(zb, self.from_above)
+            self.to_below(zb).start()
+
+    def at_end(self, number, source, target, where):
+        return pltpu.make_async_remote_copy(
+            src_ref=source, dst_ref=target, send_sem=self.end_send.at[number], recv_sem=self.end_recv.at[number],
+            device_id=where, device_id_type=MESH)
+
+    def end_sums(self):
+        return self.at_end(0, self.held.at[self.me, self.shared], self.shared_in, self.across)
+
+    def end_ready(self, rows):
+        return self.at_end(1, self.held.at[self.me, self.mine], self.total.at[rows], self.across)
+
+    def end_twin(self, rows):
+        return self.at_end(2, self.total.at[self.my_half], self.total.at[rows], self.twin)
+
+    def own_sum(self):
+        z = self.place[0]
+        self.to_y(z).wait_recv()
+        self.add_slab(z, self.from_y)
+
+        @pl.when(z > 0)
+        def _():
+            self.to_above(z).wait_recv()
+            self.add_slab(z, self.from_below)
+
+        @pl.when(z < 3)
+        def _():
+            self.to_below(z).wait_recv()
+            self.add_slab(z, self.from_above)
+        self.end_sums().start()
+        self.end_ready(self.out_mine).start()
+        self.total[self.out_mine] = self.held[self.me, self.mine]
+
+    def own_end(self):
+        self.end_sums().wait()
+        sum_rows(self.held.at[self.me, self.shared], self.shared_in, 2 * self.piece)
+        self.total[self.out_shared] = self.held[self.me, self.shared]
+        self.end_ready(self.out_theirs).wait_recv()
+        self.end_twin(self.my_half).start()
+
+    def finish(self):
+        z = self.place[0]
+        self.end_twin(self.other_half).wait_recv()
+        self.end_ready(self.out_mine).wait_send()
+        self.end_twin(self.my_half).wait_send()
+        for b in range(8):
+            self.to_core(b).wait_send()
+            self.to_x(b).wait_send()
+        for zb in range(4):
+            self.to_y(zb).wait_send()
+            pl.when(zb > z)(lambda: self.to_above(zb).wait_send())
+            pl.when(zb < z)(lambda: self.to_below(zb).wait_send())
+
+
+def scatter_buffers(rows, width):
+    half, piece = rows // 2, rows // 8
+    vm = pltpu.VMEM
+    return [vm((8, half, width), bf16), vm((8, half, width), bf16), vm((8, piece, width), bf16)] + [
+        vm((4, 3 * piece, width), bf16)] * 3 + [vm((2 * piece, width), bf16)]
+
+
+SCATTER_SEMS = [pltpu.SemaphoreType.DMA((n,)) for n in (8, 28, 28, 3, 3)]
+
+
+def sums_kernel(parts, x_ref, acts_ref, grads_ref, weighted_ref, total_a, total_b, gate_out, up_out, down_out, *rest):
+    buffers_a, buffers_b, rest = rest[:7], rest[7:14], rest[14:]
+    acts, weighted, x_buf, g_buf, gu_buf, down_buf = rest[:6]
+    sems_a, sems_b, rest = rest[6:11], rest[11:16], rest[16:]
+    fixed_sem, x_sem, g_sem, gu_sem, down_sem = rest
     z, y, x, core = place()
     D = x_ref.shape[1]
-    half = parts.shape[1] // 2
-    piece = half // 4
-    me = z * 2 + y
-    order = far_first(z)
-    my_half = pl.ds(pl.multiple_of(core * half, half), half)
-    other_half = pl.ds(pl.multiple_of((1 - core) * half, half), half)
-    slab = pl.ds(pl.multiple_of(x * piece, piece), 3 * piece)
-    mine = pl.ds(pl.multiple_of(x * 3 * piece, piece), piece)
-    theirs = pl.ds(pl.multiple_of((1 - x) * 3 * piece, piece), piece)
-    shared = pl.ds(piece, 2 * piece)
-    spans = (pl.ds(0, D), pl.ds(D, parts.shape[2] - D))
-    CORE, X, Y, UP, DOWN = range(5)
-    everything = pl.ds(0, half)
-
-    def remote(kind, h, number, source, target, where):
-        return pltpu.make_async_remote_copy(
-            src_ref=source, dst_ref=target, send_sem=send.at[kind, h, number],
-            recv_sem=recv.at[kind, h, number], device_id=where, device_id_type=MESH)
-
-    def load(b, h):
-        return pltpu.make_async_copy(parts.at[b, my_half, spans[h]], held.at[b, everything, spans[h]], load_sem.at[h, b])
-
-    def to_core(b, h):
-        return remote(CORE, h, b, parts.at[b, other_half, spans[h]], from_core.at[b, everything, spans[h]], device(z, y, x, 1 - core))
-
-    def to_x(b, h):
-        return remote(X, h, b, held.at[b, theirs, spans[h]], from_x.at[b, pl.ds(0, piece), spans[h]], device(z, y, 1 - x, core))
-
-    def to_y(zb, h):
-        return remote(Y, h, zb, held.at[zb * 2 + 1 - y, slab, spans[h]], from_y.at[zb, pl.ds(0, 3 * piece), spans[h]], device(z, 1 - y, x, core))
-
-    def to_above(zb, h):
-        return remote(UP, h, zb, held.at[zb * 2 + y, slab, spans[h]], from_below.at[zb, pl.ds(0, 3 * piece), spans[h]], device(z + 1, y, x, core))
-
-    def to_below(zb, h):
-        return remote(DOWN, h, zb, held.at[zb * 2 + y, slab, spans[h]], from_above.at[zb, pl.ds(0, 3 * piece), spans[h]], device(z - 1, y, x, core))
+    sums = (Scatter(parts, D + total_a.shape[1], total_b, buffers_b, sems_b), Scatter(parts, D, total_a, buffers_a, sems_a))
 
     fixed = [pltpu.make_async_copy(acts_ref, acts, fixed_sem.at[0]), pltpu.make_async_copy(weighted_ref, weighted, fixed_sem.at[1])]
     ff = weighted.shape[1] // 2
@@ -444,131 +571,38 @@
         fillers.insert(3 * k + 2, functools.partial(g_piece, k))
 
     greet(z, y, x, core)
-    items = [(zb, h) for zb in order for h in (1, 0)]
-    for k, (zb, h) in enumerate(items):
-        for yb in (1 - y, y):
-            load(zb * 2 + yb, h).start()
-            to_core(zb * 2 + yb, h).start()
-        if k == 1:
+    for k in range(4):
+        for s in sums:
+            s.begin(k)
+        if k == 0:
             for copy in fixed:
                 copy.start()
             for j in range(2):
                 x_load(j).start()
                 g_load(j).start()
-
-    def stage_core(zb, h, yb):
-        b = zb * 2 + yb
-        load(b, h).wait()
-        to_core(b, h).wait_recv()
-        sum_rows(held.at[b], from_core.at[b], spans[h], half)
-        to_x(b, h).start()
-
-    def stage_x(zb, h, yb):
-        b = zb * 2 + yb
-        to_x(b, h).wait_recv()
-        sum_rows(held.at[b, mine], from_x.at[b], spans[h], piece)
-
-    def stage_y(zb, h):
-        stage_x(zb, h, 1 - y)
-        to_y(zb, h).start()
-
-    def climb(zb, h):
-        @pl.when(z > 0)
-        def _():
-            to_above(zb, h).wait_recv()
-            sum_rows(held.at[zb * 2 + y, slab], from_below.at[zb], spans[h], 3 * piece)
-        to_above(zb, h).start()
-
-    def descend(zb, h):
-        @pl.when(z < 3)
-        def _():
-            to_below(zb, h).wait_recv()
-            sum_rows(held.at[zb * 2 + y, slab], from_above.at[zb], spans[h], 3 * piece)
-        to_below(zb, h).start()
-
-    def stage_z(k):
-        zb, h = items[k]
-        to_y(zb, h).wait_recv()
-        sum_rows(held.at[zb * 2 + y, slab], from_y.at[zb], spans[h], 3 * piece)
-        rises = (z // 2 == 0) if k < 4 else (z % 2 == 0)
-        pl.when(rises)(lambda: climb(zb, h))
-        pl.when(jnp.logical_not(rises))(lambda: descend(zb, h))
-
-    base = core * half
-    out_mine = pl.ds(pl.multiple_of(base + x * 3 * piece, piece), piece)
-    out_theirs = pl.ds(pl.multiple_of(base + (1 - x) * 3 * piece, piece), piece)
-    out_shared = pl.ds(pl.multiple_of(base + piece, piece), 2 * piece)
-
-    def at_end(number, h, source, target, where):
-        return pltpu.make_async_remote_copy(
-            src_ref=source, dst_ref=target, send_sem=end_send.at[h, number],
-            recv_sem=end_recv.at[h, number], device_id=where, device_id_type=MESH)
-
-    across, twin = device(z, y, 1 - x, core), device(z, y, x, 1 - core)
-    end_sums = lambda h: at_end(0, h, held.at[me, shared, spans[h]], shared_in.at[pl.ds(0, 2 * piece), spans[h]], across)
-    end_ready = lambda h, rows: at_end(1, h, held.at[me, mine, spans[h]], total.at[rows, spans[h]], across)
-    end_twin = lambda h, rows: at_end(2, h, total.at[my_half, spans[h]], total.at[rows, spans[h]], twin)
-
-    def own_sum(h):
-        own = held.at[me]
-        to_y(z, h).wait_recv()
-        sum_rows(own.at[slab], from_y.at[z], spans[h], 3 * piece)
-
-        @pl.when(z > 0)
-        def _():
-            to_above(z, h).wait_recv()
-            sum_rows(own.at[slab], from_below.at[z], spans[h], 3 * piece)
-
-        @pl.when(z < 3)
-        def _():
-            to_below(z, h).wait_recv()
-            sum_rows(own.at[slab], from_above.at[z], spans[h], 3 * piece)
-        end_sums(h).start()
-        end_ready(h, out_mine).start()
-        total[out_mine, spans[h]] = held[me, mine, spans[h]]
-
-    def own_end(h):
-        end_sums(h).wait_recv()
-        sum_rows(held.at[me, shared], shared_in, spans[h], 2 * piece)
-        total[out_shared, spans[h]] = held[me, shared, spans[h]]
-        end_ready(h, out_theirs).wait_recv()
-        end_twin(h, my_half).start()
-
-    zb, h = items[0]
-    stage_core(zb, h, 1 - y)
-    stage_core(zb, h, y)
-    for k, (zb, h) in enumerate(items):
-        if k < 7:
-            stage_core(*items[k + 1], 1 - y)
-        stage_y(zb, h)
-        if k < 7:
-            stage_core(*items[k + 1], y)
-        stage_x(zb, h, y)
-        if 0 < k < 7:
-            stage_z(k - 1)
-        if k < 7:
-            for fill in fillers[2 * k:2 * k + 2]:
+    items = [(k, s) for k in range(4) for s in sums]
+    for other in (True, False):
+        sums[0].stage_core(0, other)
+    for i, (k, s) in enumerate(items):
+        if i < 7:
+            items[i + 1][1].stage_core(items[i + 1][0], True)
+        s.stage_y(k)
+        if i < 7:
+            items[i + 1][1].stage_core(items[i + 1][0], False)
+        s.stage_x(k)
+        if 0 < i < 7:
+            items[i - 1][1].stage_z(items[i - 1][0])
+        if i < 7:
+            for fill in fillers[2 * i:2 * i + 2]:
                 fill()
     for fill in fillers[14:]:
         fill()
-    own_sum(1)
-    own_sum(0)
-    end_sums(1).wait_send()
-    own_end(1)
-    end_sums(0).wait_send()
-    own_end(0)
-    for h in (1, 0):
-        end_twin(h, other_half).wait_recv()
-        end_ready(h, out_mine).wait_send()
-        end_twin(h, my_half).wait_send()
-        for b in range(8):
-            zb, yb = b // 2, b % 2
-            to_core(b, h).wait_send()
-            to_x(b, h).wait_send()
-            if yb == 0:
-                to_y(zb, h).wait_send()
-                pl.when(zb > z)(lambda: to_above(zb, h).wait_send())
-                pl.when(zb < z)(lambda: to_below(zb, h).wait_send())
+    for s in sums:
+        s.own_sum()
+    for s in sums:
+        s.own_end()
+    for s in sums:
+        s.finish()
     for k in (x_pieces - 2, x_pieces - 1):
         for copy in gu_store(k):
             copy.wait()
@@ -581,22 +615,17 @@
     _, rows, width = parts.shape
     T, D = x.shape
     ff = weighted.shape[1] // 2
-    half, piece = rows // 2, rows // 8
+    widths = (D // 2, D // 2 + 128)
     sd = jax.ShapeDtypeStruct
     dma = pltpu.SemaphoreType.DMA
     vm = pltpu.VMEM
     return pl.pallas_call(
-        sums_kernel, in_specs=[ANY] * 5, out_specs=[VM, ANY, ANY, ANY],
-        out_shape=[sd((rows, width), bf16), sd((2, D, ff), f32), sd((2, D, ff), f32), sd((2, ff, D), f32)],
-        scratch_shapes=[
-            vm((8, half, width), bf16), vm((8, half, width), bf16), vm((8, piece, width), bf16),
-            vm((4, 3 * piece, width), bf16), vm((4, 3 * piece, width), bf16), vm((4, 3 * piece, width), bf16),
-            vm((2 * piece, width), bf16),
+        sums_kernel, in_specs=[ANY] * 5, out_specs=[VM, VM, ANY, ANY, ANY],
+        out_shape=[sd((rows, w), bf16) for w in widths] + [sd((2, D, ff), f32), sd((2, D, ff), f32), sd((2, ff, D), f32)],
+        scratch_shapes=scatter_buffers(rows, widths[0]) + scatter_buffers(rows, widths[1]) + [
             vm(acts.shape, bf16), vm(weighted.shape, bf16), vm((2, T, BLOCK), bf16), vm((2, T, 512), bf16),
-            vm((2, 2, 2, BLOCK, ff), f32), vm((2, 2, ff, 512), f32),
-            dma((2, 8)), dma((5, 2, 8)), dma((5, 2, 8)), dma((2, 3)), dma((2, 3)),
-            dma((2,)), dma((2,)), dma((2,)), dma((2, 2, 2)), dma((2, 2)),
-        ],
+            vm((2, 2, 2, BLOCK, ff), f32), vm((2, 2, ff, 512), f32)] + SCATTER_SEMS * 2 + [
+            dma((2,)), dma((2,)), dma((2,)), dma((2, 2, 2)), dma((2, 2))],
         compiler_params=pltpu.CompilerParams(collective_id=number, has_side_effects=True, vmem_limit_bytes=62 * 2**20),
     )(parts, x, acts, grads, weighted)
 
@@ -622,7 +651,7 @@
     for copy in loads:
         copy.start()
     greet_peers(z, y, x, core, (across, twin))
-    gather = Gather(hidden, x_all, x_keep, x_send, x_recv)
+    gather = Gather(hidden, x_all, x_keep, x_send, x_recv, 3)
     cot = Gather(sent_ref, grads_all, c_keep, c_send, c_recv)
     experts = Gather(moe, whole, m_keep, m_send, m_recv)
 
@@ -904,13 +933,13 @@
 
 
 def backward_kernel(ga_ref, segc_ref, segr_ref, qg_ref, kg_ref, gains_small, gain_ref,
-                    w_in, ctx_ref, q_in, k_in, v_in, qr_in, kr_in, cos_in, sin_in, wq_in, wk_in, wv_in, a_in, hidden_in, middle_in,
-                    grad_ref, weights_q, weights_k, weights_v, norm_ref, gains_out, wout_ref, small_out,
+                    w_in, ctx_ref, q_in, k_in, v_in, qr_in, kr_in, cos_in, sin_in, wq_in, wk_in, wv_in, a_in, hidden_in, middle_in, parts,
+                    grad_ref, weights_q, weights_k, weights_v, norm_ref, gains_out, wout_ref, small_out, sum_ref,
                     w_ref, q_ref, k_ref, v_ref, qr_ref, kr_ref, cos_ref, sin_ref, wq_ref, wk_ref, wv_ref, columns, hidden_ref, middle_ref,
                     raw_ref, g_own, g_all, dk, dv, terms, from_y, held_terms, from_below, from_above,
                     small_y, small_sum, small_z, raw_in, gathered, products, from_z, out_half, in_half, held, from_x, total, gains_own, gains_in, norm_in,
                     load, g_send, g_recv, f_send, f_recv, t_send, t_recv, s_send, s_recv, send, recv, w_send, w_recv,
-                    pair_send, pair_recv, e_send, e_recv, n_send, n_recv):
+                    pair_send, pair_recv, e_send, e_recv, n_send, n_recv, *scatter):
     small_ref = gains_small
     z, y, x, core = place()
     me = z * 2 + y
@@ -924,14 +953,17 @@
         (sin_in, sin_ref), (wq_in, wq_ref), (wk_in, wk_ref), (wv_in, wv_ref), (hidden_in, hidden_ref), (middle_in, middle_ref)))]
 
     def column_load(n):
-        block = pl.ds(pl.multiple_of((n * 2 + y) * BLOCK, BLOCK), BLOCK)
-        return pltpu.make_async_copy(a_in.at[:, block], columns.at[n], load.at[13 + n])
+        block = pl.ds(pl.multiple_of((order[n] * 2 + y) * BLOCK, BLOCK), BLOCK)
+        return pltpu.make_async_copy(a_in.at[:, block], columns.at[n % 2], load.at[13 + n % 2])
 
     for copy in loads:
         copy.start()
-    for n in range(4):
-        column_load(n).start()
     greet_peers(z, y, x, core, (across, twin, corner))
+    sums = Scatter(parts, 0, sum_ref, scatter[:7], scatter[7:])
+    for k in range(4):
+        sums.begin(k)
+    column_load(0).start()
+    column_load(1).start()
 
     def remote(source, target, ssem, rsem, where):
         return pltpu.make_async_remote_copy(
@@ -1023,6 +1055,9 @@
                 held_terms[n] = (paired(n) + from_above[n].astype(f32)).astype(bf16)
             term_down(n).start()
 
+    for k in range(3):
+        sums.stage_core(k, True)
+        sums.stage_core(k, False)
     for n in range(4):
         when_away(n, lambda: g_from(n).wait_recv())
         when_away(n, lambda: g_over(n).start())
@@ -1074,6 +1109,10 @@
         def _():
             when_away(b // 2, lambda: rows_to(b // 2).start())
 
+    for k in range(3):
+        sums.stage_y(k)
+        sums.stage_x(k)
+
     small_pair.wait_recv()
     small_sum[...] = small_ref[:, own_lanes] + small_y[...]
     for n in range(4):
@@ -1101,15 +1140,15 @@
 
     raw_all = raw_ref[...].reshape(8 * BLOCK, 3 * HD)
     for i, n in enumerate(order):
-        column_load(n).wait()
-        product = dot_tn(columns[n], raw_all).astype(bf16)
+        column_load(i).wait()
+        product = dot_tn(columns[i % 2], raw_all).astype(bf16)
+        if i < 2:
+            column_load(i + 2).start()
         if i < 3:
             products[n] = product
             products_to(n).start()
         else:
             from_z[z] = product
-        if i % 2 == 0:
-            term_stage(i // 2)
 
     for copy in loads[8:]:
         copy.wait()
@@ -1145,28 +1184,11 @@
         held[piece(c)] = (kept + in_half[piece(c)].astype(f32)).astype(bf16)
         second[c].start()
 
-    term_stage(2)
-    term_pair(z).wait_recv()
-    wout_ref[...] = paired(z)
-
-    @pl.when(z > 0)
-    def _():
-        term_up(z).wait_recv()
-        wout_ref[...] += from_below[z].astype(f32)
-
-    @pl.when(z < 3)
-    def _():
-        term_down(z).wait_recv()
-        wout_ref[...] += from_above[z].astype(f32)
-
-    for n in range(4):
-        when_away(n, lambda: small_arriving(n).wait_recv())
-    small_out[:, own_lanes] = (small_z[0] + small_z[1]) + (small_z[2] + small_z[3])
-    for i in range(3):
-        small_spread(i).start()
-    for n in range(4):
-        when_away(n, lambda: gains_from(n).wait_recv())
-        gains_out[:, n * HD:(n + 1) * HD] = gains_in[n]
+    term_stage(0)
+    sums.stage_core(3, True)
+    sums.stage_core(3, False)
+    sums.stage_z(0)
+    term_stage(1)
     for c in range(2):
         second[c].wait_recv()
         total[at(my_half, c)] = (held[piece(c)].astype(f32) + from_x[piece(c)].astype(f32)).astype(bf16)
@@ -1204,18 +1226,47 @@
 
     for b in range(8):
         pl.when(me != b)(lambda: norm_to(b).start())
+    sums.stage_y(3)
+    sums.stage_x(3)
+    sums.stage_z(1)
+    term_stage(2)
+    sums.stage_z(2)
+    term_pair(z).wait_recv()
+    wout_ref[...] = paired(z)
+
+    @pl.when(z > 0)
+    def _():
+        term_up(z).wait_recv()
+        wout_ref[...] += from_below[z].astype(f32)
+
+    @pl.when(z < 3)
+    def _():
+        term_down(z).wait_recv()
+        wout_ref[...] += from_above[z].astype(f32)
+
+    for n in range(4):
+        when_away(n, lambda: small_arriving(n).wait_recv())
+    small_out[:, own_lanes] = (small_z[0] + small_z[1]) + (small_z[2] + small_z[3])
+    for i in range(3):
+        small_spread(i).start()
+    for n in range(4):
+        when_away(n, lambda: gains_from(n).wait_recv())
+        gains_out[:, n * HD:(n + 1) * HD] = gains_in[n]
+    sums.own_sum()
     for n in range(4):
         when_away(n, lambda: products_from(n).wait_recv())
     for n in range(4):
         for g in range(3):
             (weights_q, weights_k, weights_v)[g][:, n * HD:(n + 1) * HD] = from_z[n, :, g * HD:(g + 1) * HD].astype(f32)
+    sums.own_end()
     for b in range(8):
         pl.when(me != b)(lambda: norm_from(b).wait_recv())
-    sums = [norm_in[b] for b in range(8)]
-    norm_sum = ((sums[0] + sums[1]) + (sums[2] + sums[3])) + ((sums[4] + sums[5]) + (sums[6] + sums[7]))
+    norms = [norm_in[b] for b in range(8)]
+    norm_sum = ((norms[0] + norms[1]) + (norms[2] + norms[3])) + ((norms[4] + norms[5]) + (norms[6] + norms[7]))
     for t in range(norm_in.shape[1]):
         norm_ref[:, t * 128:(t + 1) * 128] = norm_sum[t:t + 1]
 
+    sums.finish()
     for i in range(3):
         small_spread_in(i).wait_recv()
         small_spread(i).wait_send()
@@ -1238,7 +1289,7 @@
         when_away(n, lambda: gains_to(n).wait_send())
 
 
-def backward_all(ga, segc, segr, qg, kg, small, gain, w, ctx, q, k, v, qr, kr, cosine, sine, wq, wk, wv, a, hidden, middle, number):
+def backward_all(ga, segc, segr, qg, kg, small, gain, w, ctx, q, k, v, qr, kr, cosine, sine, wq, wk, wv, a, hidden, middle, parts, number):
     T, D = a.shape
     rows, half = BLOCK, BLOCK // 2
     span = 4 * HD
@@ -1248,21 +1299,21 @@
     vm = pltpu.VMEM
     like = lambda m: vm(m.shape, m.dtype)
     return pl.pallas_call(
-        backward_kernel, in_specs=[VM] * 7 + [ANY, VM] + [ANY] * 13, out_specs=[VM] * 8,
+        backward_kernel, in_specs=[VM] * 7 + [ANY, VM] + [ANY] * 14, out_specs=[VM] * 9,
         out_shape=[sd((rows, D), f32), sd((BLOCK, span), f32), sd((BLOCK, span), f32), sd((BLOCK, span), f32), sd((1, D), f32), sd((2, span), f32),
-                   sd((span, BLOCK), f32), sd((S, D), f32)],
+                   sd((span, BLOCK), f32), sd((S, D), f32), sd((rows, D), bf16)],
         scratch_shapes=[like(m) for m in (w, q, k, v, qr, kr, cosine, sine, wq, wk, wv)] + [
-            vm((4, T, BLOCK), bf16), like(hidden), like(middle),
+            vm((2, T, BLOCK), bf16), like(hidden), like(middle),
             vm((8, BLOCK, 3 * HD), bf16), vm((4, BLOCK, HD), bf16), vm((8, BLOCK, HD), bf16), vm((T, HD), f32), vm((T, HD), f32),
             vm((8, span, BLOCK), bf16)] + [vm((4, span, BLOCK), bf16)] * 4 + [
             vm((S, D // 4), f32), vm((S, D // 4), f32), vm((4, S, D // 4), f32),
             vm((4, BLOCK, 3 * HD), bf16), vm((rows, 3 * span), bf16), vm((4, BLOCK, 3 * HD), bf16), vm((4, BLOCK, 3 * HD), bf16)] + [vm((half, D), bf16)] * 4 + [
             vm((rows, D), bf16), vm((2, HD), f32), vm((4, 2, HD), f32), vm((8, D // 128, 128), f32),
-            dma((17,)), dma((4,)), dma((4,)), dma((4,)), dma((4,)), dma((3, 4)), dma((3, 4)), dma((8,)), dma((8,)),
+            dma((15,)), dma((4,)), dma((4,)), dma((4,)), dma((4,)), dma((3, 4)), dma((3, 4)), dma((8,)), dma((8,)),
             dma((4,)), dma((4,)), dma((4,)), dma((4,)), dma((3, 2)), dma((3, 2)), dma((4,)), dma((4,)), dma((8,)), dma((8,)),
-        ],
-        compiler_params=pltpu.CompilerParams(collective_id=number, has_side_effects=True, vmem_limit_bytes=60 * 2**20),
-    )(ga, segc, segr, qg, kg, small, gain, w, ctx, q, k, v, qr, kr, cosine, sine, wq, wk, wv, a, hidden, middle)
+        ] + scatter_buffers(rows, D) + SCATTER_SEMS,
+        compiler_params=pltpu.CompilerParams(collective_id=number, has_side_effects=True, vmem_limit_bytes=63 * 2**20),
+    )(ga, segc, segr, qg, kg, small, gain, w, ctx, q, k, v, qr, kr, cosine, sine, wq, wk, wv, a, hidden, middle, parts)
 
 
 def on_device(
@@ -1571,12 +1622,11 @@
     )
     inverse_moe = inverse_rms(middle)
     normed_moe = middle * inverse_moe
-    total, grad_gate, grad_up, grad_down = sums_all(
-        parts.reshape(devices, rows, 2 * width + 128), everyone, grad_acts, grads_all, weighted, 2
-    )
-    output = (middle + total[:, :width].astype(f32)).astype(bf16)
+    parts = parts.reshape(devices, rows, 2 * width + 128)
+    total_a, total_b, grad_gate, grad_up, grad_down = sums_all(parts, everyone, grad_acts, grads_all, weighted, 2)
+    total = jnp.concatenate([total_a, total_b], 1)
     grad_final = cotangent.astype(f32)
-    tail = total[:, 2 * width :].astype(f32)
+    tail = total[:, width:].astype(f32)
     grad_gates = tail[:, :experts] + tail[:, experts : 2 * experts]
     logits = jnp.where(
         own_mask > 0, jnp.dot(moe_input, w_router, preferred_element_type=f32), -jnp.inf
@@ -1587,7 +1637,7 @@
         gate_weights * (grad_gates - jnp.sum(grad_gates * gate_weights, -1, keepdims=True))
     ).astype(bf16)
     grad_moe_input = jnp.dot(grad_logits, w_router.T, preferred_element_type=f32)
-    grad_moe_input = grad_moe_input + total[:, width : 2 * width].astype(f32)
+    grad_moe_input = grad_moe_input + total[:, :width].astype(f32)
     grad_middle = grad_final + norm_back(grad_moe_input * norm2_gain, normed_moe, inverse_moe)
     small = jnp.concatenate(
         [
@@ -1598,10 +1648,11 @@
         0,
     )
 
-    grad_input, grad_query, grad_key, grad_value, grad_norm1, gains, grad_w_out, small = backward_all(
+    grad_input, grad_query, grad_key, grad_value, grad_norm1, gains, grad_w_out, small, moe_out = backward_all(
         grad_middle.astype(bf16), segc, segr, query_gain[None], key_gain[None], small, norm1_gain[None], w_out, own_context,
-        queries, keys, values, q_raw, k_raw, cosine, sine, w_query, w_key, w_value, attn_all, hidden_in, grad_middle, 3,
-    )
+        queries, keys, values, q_raw, k_raw, cosine, sine, w_query, w_key, w_value, attn_all, hidden_in, grad_middle, parts, 3,
+    )
+    output = (middle + moe_out.astype(f32)).astype(bf16)
     return (
         output,
         grad_input,

time: 414 us -> 394 us (0.952)
  Pallas kernels: 365 us -> 347 us
  local copies, waits for them, and re-layouts: 23.5 us -> 19.1 us
    pallas_call x1, Pallas kernels: 101 us -> 60.9 us  [sums_all(): pl.pallas_call(sums_kernel, in_specs=[ANY] * 5, out_specs=[VM, VM, ANY, A...]
    pallas_call x1, Pallas kernels: 100 us -> 124 us  [backward_all(): pl.pallas_call(backward_kernel, in_specs=[VM] * 7 + [ANY, VM] + [ANY] * 1...]
    unnamed x38 -> x44, local copies, waits for them, and re-layouts: 17.5 us -> 15.6 us
where the time goes in v6:
time: 394 us; the launch traced here: 386 us
  Pallas kernels  347 us (88%)
  local copies, waits for them, and re-layouts  19.1 us (5%)
  other arithmetic  15.5 us (4%)
    pallas_call x1, Pallas kernels, forward_all(): pl.pallas_call(forward_kernel, in_specs=[VM] * 9 + [ANY] * 9, out_specs=[...  163 us
    pallas_call x1, Pallas kernels, backward_all(): pl.pallas_call(backward_kernel, in_specs=[VM] * 7 + [ANY, VM] + [ANY] * 1...  124 us
    pallas_call x1, Pallas kernels, sums_all(): pl.pallas_call(sums_kernel, in_specs=[ANY] * 5, out_specs=[VM, VM, ANY, A...  60.9 us
    unnamed x44, local copies, waits for them, and re-layouts  15.6 us

profile of v6, /device:TPU:0, one launch (start us, length us, event | category | flops | bytes accessed | tf_op | source)
XLA Modules:
  0.0 385.9 jit_solution(9668966709303525026)
XLA Ops:
  0.6 0.0 copy-start.14
  0.7 0.0 copy-start.11
  0.7 0.8 convert_reduce_fusion
  1.4 0.1 copy.45
  1.6 2.3 fusion.1.sent_ref
  3.9 0.0 copy-done.14
  3.9 1.3 copy.46.segc_ref
  5.2 0.0 copy-done.11
  5.2 1.0 copy.47.wr_ref
  6.2 0.2 multiply_cosine_fusion
  6.4 0.1 multiply_cosine_fusion.1
  6.6 0.3 multiply_add_fusion.1
  6.9 0.1 bitcast_negate_fusion
  7.0 1.9 pad_maximum_fusion.1
  8.9 162.7 %shard_map.263 = (bf16[256,512]{1,0:T(8,128)(2,1)}, f32[256,2048]{1,0:T(8,128)}, bf16[256,2048]{1,0:T(8,128)(2,1)}, bf16[2048,2048]{1,0:T(8,128)(2,1)}, bf16[204...) custom-call(bf16[256,2048]{1,0:T(8,128)(2,1)} %hidden_in.1, ...), custom_call_target="tpu_custom_call" | custom-call | tf_op jit(solution)/shard_map/pallas_call | solution.py:921
  171.6 1.8 multiply_reduce_fusion.2
  173.4 0.0 copy-start.6
  173.5 60.9 %shard_map.264 = (bf16[256,1024]{1,0:T(8,128)(2,1)}, bf16[256,1152]{1,0:T(8,128)(2,1)}, f32[2,2048,256]{2,1,0:T(8,128)}, f32[2,2048,256]{2,1,0:T(8,128)}, f32[2,256,2048]{2,1,0:T(8,128)}) custom-call(bf16[8,256,4224]{2,1,0:T(8,128)(2,1)} %bitcast.23, bf16[2048,2048]{1,0:T(8,128)(2,1)} %get-tuple-element.45.x_ref, ...), custom_call_target="tpu_custom_call" | custom-call | tf_op jit(solution)/shard_map/pallas_call | solution.py:622
  234.4 0.0 copy-start
  234.4 0.0 copy-start.13
  234.4 1.0 slice_convert_fusion
  235.4 0.1 copy.48
  235.5 0.0 copy-done.6
  235.5 0.5 fusion.6
  236.0 0.2 fusion.3
  236.2 0.3 multiply_reduce_fusion.3
  236.5 0.2 multiply_convert_fusion
  236.7 0.0 copy-done
  236.7 0.0 copy-done.13
  236.7 0.0 copy-start.4
  236.7 2.1 multiply_reduce_fusion
  238.8 0.0 copy-done.4
  238.8 2.3 fusion.4
  241.1 0.3 fusion.7
  241.3 0.1 pad.7.clone
  241.4 0.8 maximum_maximum_fusion.gains_small
  242.2 123.7 %shard_map.265 = (f32[256,2048]{1,0:T(8,128)}, f32[256,512]{1,0:T(8,128)}, f32[256,512]{1,0:T(8,128)}, f32[256,512]{1,0:T(8,128)}, f32[1,2048]{1,0:T(1,128)}, /*...) custom-call(bf16[256,2048]{1,0:T(8,128)(2,1)} %get-tuple-element.72.ga_ref, ...), custom_call_target="tpu_custom_call" | custom-call | tf_op jit(solution)/shard_map/pallas_call | solution.py:1301
  365.9 0.0 copy-start.16
  365.9 0.0 copy-start.12
  365.9 0.0 copy-start.5
  365.9 3.3 add_convert_fusion
  369.2 0.0 copy-done.16
  369.2 0.6 fusion.5
  369.8 0.0 copy-done.12
  369.8 0.6 slice.30
  370.4 0.7 slice_bitcast_fusion
  371.1 0.0 copy-done.5
  371.1 0.0 copy-start.8
  371.1 0.0 copy-start.7
  371.1 1.3 copy.62
  372.4 0.0 copy-done.15
  372.4 0.6 copy.63
  373.0 0.0 copy-done.10
  373.0 0.8 copy.64
  373.8 0.0 copy-done.9
  373.8 0.8 copy.65
  374.6 0.0 copy-done.8
  374.6 0.8 copy.66
  375.4 0.8 copy.67
  376.2 2.1 copy.68
  378.3 1.6 copy-done.2
  379.9 2.1 copy.69
  382.1 1.6 copy-done.1
  383.6 2.0 copy.70
  (16 shorter events, 0.1 us)
Async XLA Ops:
  0.6 3.2 copy-start.14
  0.7 4.6 %copy-start.11 = (bf16[2048,16]{0,1:T(8,128)(2,1)S(1)}, bf16[2048,16]{0,1:T(8,128)(2,1)}, u32[]{:S(2)}) copy-start(bf16[2048,16]{0,1:T(8,128)(2,1)} %param.25) | copy-start | bytes 196612
  173.4 62.1 %copy-start.6 = (bf16[256,2048]{1,0:T(8,128)(2,1)S(1)}, bf16[256,2048]{1,0:T(8,128)(2,1)}, u32[]{:S(2)}) copy-start(bf16[256,2048]{1,0:T(8,128)(2,1)} %get-tuple-element.43) | copy-start | bytes 3145732
  234.4 2.3 copy-start
  234.4 2.3 copy-start.13
  236.7 2.1 copy-start.4
  365.9 3.3 copy-start.16
  365.9 3.9 %copy-start.12 = (f32[24,2048]{1,0:T(8,128)S(1)}, f32[24,2048]{1,0:T(8,128)}, u32[]{:S(2)}) copy-start(f32[24,2048]{1,0:T(8,128)} %get-tuple-element.66) | copy-start | bytes 589828
  365.9 5.1 %copy-start.5 = (f32[256,2048]{1,0:T(8,128)S(1)}, f32[256,2048]{1,0:T(8,128)}, u32[]{:S(2)}) copy-start(f32[256,2048]{1,0:T(8,128)} %get-tuple-element.102) | copy-start | bytes 6291460
  371.1 1.4 copy-start.15
  371.1 2.0 copy-start.10
  371.1 2.8 copy-start.9
  371.1 3.5 copy-start.8
  371.1 4.3 %copy-start.7 = (f32[512,256]{1,0:T(8,128)S(1)}, f32[512,256]{1,0:T(8,128)}, u32[]{:S(2)}) copy-start(f32[512,256]{1,0:T(8,128)} %get-tuple-element.107) | copy-start | bytes 1572868
  372.4 3.8 copy-start.3
  376.2 3.7 copy-start.2
  379.9 3.7 copy-start.1

commit v7 on v6

--- a/solution.py
+++ b/solution.py
@@ -720,10 +720,6 @@
         (middle_ref, middle_out), (moe, moe_out)))]
     for copy in keeps[:5]:
         copy.start()
-    cot.hop(1)
-    cot.cross(0)
-    cot.hop_inside(2)
-
     targets = lambda r: (y if r % 2 == 0 else 1 - y)
     source_y = (y + z) % 2
 
@@ -739,6 +735,9 @@
         probs = probabilities(r, start, q_ref[pl.ds(start, BLOCK)], k_ref, segc_ref, segr_ref)
         part[r] = dot(probs.astype(bf16), v_ref[:(2 * r + 2) * BLOCK]).astype(bf16)
         pl.when(jnp.logical_not(here(r)))(lambda: to_block(r).start())
+    cot.hop(1)
+    cot.cross(0)
+    cot.hop_inside(2)
     cot.flank(0)
 
     @pl.when(z % 2 == 0)
@@ -836,18 +835,19 @@
         fetches = grads_load(i)
         for copy in fetches:
             copy.start()
-        experts.complete(i)
         slot = i % 2
         if i >= 2:
             for copy in stores(i - 2):
                 copy.wait()
+        for copy in fetches:
+            copy.wait()
+        gw = [dot_nt(p_buf[:, :D], wd[j]) for j in range(2)]
+        experts.complete(i)
 
         rows = rows_of(i)
         v = whole[rows]
-        logits = dot(v, wr_ref[...])
+        logits = dot_nt(v, wr_ref[...])
         count = logits.shape[1]
-        for copy in fetches:
-            copy.wait()
         mask = mask_all[:, :count].astype(f32) > 0
         top = jnp.max(jnp.where(mask, logits, -jnp.inf), -1, keepdims=True)
         raised = jnp.where(mask, jnp.exp(jnp.where(mask, logits - top, 0.0)), 0.0)
@@ -859,7 +859,7 @@
             gate = jnp.sum(jnp.where(mine, gates, 0.0), -1, keepdims=True)
             ga = dot(v, wg[j])
             ua = dot(v, wu[j])
-            gw_j = dot_nt(p_buf[:, :D], wd[j])
+            gw_j = gw[j]
             s = 1.0 / (1.0 + jnp.exp(-ga))
             silu = ga * s
             h = (silu * ua).astype(bf16).astype(f32)
@@ -1616,7 +1616,7 @@
     sent = jnp.concatenate([cotangent, jnp.pad(own_mask.astype(bf16), ((0, 0), (0, 128 - experts)))], 1)
     own_context, middle, moe_input, _, attn_all, queries, keys, values, q_raw, k_raw, grads_all, everyone, weighted, grad_acts, parts = (
         forward_all(
-            hidden_in, sent, norm1_gain[None], norm2_gain[None], query_gain[None], key_gain[None], segc, segr, w_router,
+            hidden_in, sent, norm1_gain[None], norm2_gain[None], query_gain[None], key_gain[None], segc, segr, w_router.T,
             w_query, w_key, w_value, cosine, sine, w_out, w_gate, w_up, w_down, 1,
         )
     )

time: 394 us -> 393 us (level)
  Pallas kernels: 347 us -> 351 us
    unnamed x44 -> x43, local copies, waits for them, and re-layouts: 15.6 us -> 14.6 us
where the time goes in v7:
time: 393 us; the launch traced here: 389 us
  Pallas kernels  351 us (89%)
  local copies, waits for them, and re-layouts  18.1 us (5%)
  other arithmetic  15.5 us (4%)
    pallas_call x1, Pallas kernels, forward_all(): pl.pallas_call(forward_kernel, in_specs=[VM] * 9 + [ANY] * 9, out_specs=[...  166 us
    pallas_call x1, Pallas kernels, backward_all(): pl.pallas_call(backward_kernel, in_specs=[VM] * 7 + [ANY, VM] + [ANY] * 1...  124 us
    pallas_call x1, Pallas kernels, sums_all(): pl.pallas_call(sums_kernel, in_specs=[ANY] * 5, out_specs=[VM, VM, ANY, A...  61.3 us
    unnamed x43, local copies, waits for them, and re-layouts  14.6 us

profile of v7, /device:TPU:0, one launch (start us, length us, event | category | flops | bytes accessed | tf_op | source)
XLA Modules:
  0.0 388.6 jit_solution(16502806537105609266)
XLA Ops:
  0.6 0.0 copy-start.14
  0.7 0.7 convert_reduce_fusion
  1.4 0.1 copy.42
  1.5 2.3 fusion.1.sent_ref
  3.8 0.0 copy-done.14
  3.8 1.3 copy.43.segc_ref
  5.2 0.2 multiply_cosine_fusion
  5.4 0.1 multiply_cosine_fusion.1
  5.5 0.3 multiply_add_fusion.1
  5.9 0.1 bitcast_negate_fusion
  5.9 1.9 pad_maximum_fusion.1
  7.9 166.2 %shard_map.263 = (bf16[256,512]{1,0:T(8,128)(2,1)}, f32[256,2048]{1,0:T(8,128)}, bf16[256,2048]{1,0:T(8,128)(2,1)}, bf16[2048,2048]{1,0:T(8,128)(2,1)}, bf16[204...) custom-call(bf16[256,2048]{1,0:T(8,128)(2,1)} %hidden_in.1, ...), custom_call_target="tpu_custom_call" | custom-call | tf_op jit(solution)/shard_map/pallas_call | solution.py:921
  174.1 1.8 multiply_reduce_fusion.2
  175.9 0.0 copy-start.6
  175.9 0.0 copy-start.11
  175.9 61.3 %shard_map.264 = (bf16[256,1024]{1,0:T(8,128)(2,1)}, bf16[256,1152]{1,0:T(8,128)(2,1)}, f32[2,2048,256]{2,1,0:T(8,128)}, f32[2,2048,256]{2,1,0:T(8,128)}, f32[2,256,2048]{2,1,0:T(8,128)}) custom-call(bf16[8,256,4224]{2,1,0:T(8,128)(2,1)} %bitcast.24, bf16[2048,2048]{1,0:T(8,128)(2,1)} %get-tuple-element.45.x_ref, ...), custom_call_target="tpu_custom_call" | custom-call | tf_op jit(solution)/shard_map/pallas_call | solution.py:622
  237.2 0.0 copy-start
  237.2 0.0 copy-start.13
  237.3 1.0 slice_convert_fusion
  238.3 0.1 copy.44
  238.4 0.0 copy-done.6
  238.4 0.0 copy-done.11
  238.4 0.5 fusion.6
  238.9 0.2 fusion.3
  239.1 0.3 multiply_reduce_fusion.3
  239.3 0.2 multiply_convert_fusion
  239.6 0.0 copy-done
  239.6 0.0 copy-done.13
  239.6 0.0 copy-start.4
  239.6 2.1 multiply_reduce_fusion
  241.7 0.0 copy-done.4
  241.7 2.3 fusion.4
  243.9 0.3 fusion.7
  244.2 0.1 pad.7.clone
  244.3 0.8 maximum_maximum_fusion.gains_small
  245.1 123.6 %shard_map.265 = (f32[256,2048]{1,0:T(8,128)}, f32[256,512]{1,0:T(8,128)}, f32[256,512]{1,0:T(8,128)}, f32[256,512]{1,0:T(8,128)}, f32[1,2048]{1,0:T(1,128)}, /*...) custom-call(bf16[256,2048]{1,0:T(8,128)(2,1)} %get-tuple-element.72.ga_ref, ...), custom_call_target="tpu_custom_call" | custom-call | tf_op jit(solution)/shard_map/pallas_call | solution.py:1301
  368.7 0.0 copy-start.16
  368.7 0.0 copy-start.12
  368.7 0.0 copy-start.5
  368.7 3.3 add_convert_fusion
  371.9 0.0 copy-done.16
  372.0 0.6 fusion.5
  372.5 0.0 copy-done.12
  372.5 0.6 slice.30
  373.1 0.7 slice_bitcast_fusion
  373.8 0.0 copy-done.5
  373.8 0.0 copy-start.8
  373.8 0.0 copy-start.7
  373.8 1.3 copy.58
  375.2 0.0 copy-done.15
  375.2 0.6 copy.59
  375.8 0.0 copy-done.10
  375.8 0.8 copy.60
  376.6 0.0 copy-done.9
  376.6 0.8 copy.61
  377.4 0.0 copy-done.8
  377.4 0.8 copy.62
  378.2 0.8 copy.63
  379.0 0.0 copy-done.3
  379.0 2.1 copy.64
  381.1 1.6 copy-done.2
  382.7 2.1 copy.65
  384.8 1.6 copy-done.1
  386.4 2.0 copy.66
  (15 shorter events, 0.1 us)
Async XLA Ops:
  0.6 3.2 copy-start.14
  175.9 62.5 %copy-start.6 = (bf16[256,2048]{1,0:T(8,128)(2,1)S(1)}, bf16[256,2048]{1,0:T(8,128)(2,1)}, u32[]{:S(2)}) copy-start(bf16[256,2048]{1,0:T(8,128)(2,1)} %get-tuple-element.43) | copy-start | bytes 3145732
  175.9 62.5 %copy-start.11 = (bf16[2048,16]{0,1:T(8,128)(2,1)S(1)}, bf16[2048,16]{0,1:T(8,128)(2,1)}, u32[]{:S(2)}) copy-start(bf16[2048,16]{0,1:T(8,128)(2,1)} %param.25) | copy-start | bytes 196612
  237.2 2.3 copy-start
  237.2 2.3 copy-start.13
  239.6 2.1 copy-start.4
  368.7 3.3 copy-start.16
  368.7 3.9 copy-start.12
  368.7 5.1 %copy-start.5 = (f32[256,2048]{1,0:T(8,128)S(1)}, f32[256,2048]{1,0:T(8,128)}, u32[]{:S(2)}) copy-start(f32[256,2048]{1,0:T(8,128)} %get-tuple-element.102) | copy-start | bytes 6291460
  373.8 1.4 copy-start.15
  373.8 2.0 copy-start.10
  373.8 2.8 copy-start.9
  373.8 3.5 copy-start.8
  373.8 4.3 %copy-start.7 = (f32[512,256]{1,0:T(8,128)S(1)}, f32[512,256]{1,0:T(8,128)}, u32[]{:S(2)}) copy-start(f32[512,256]{1,0:T(8,128)} %get-tuple-element.107) | copy-start | bytes 1572868
  375.2 3.8 copy-start.3
  379.0 3.7 copy-start.2
  382.7 3.7 copy-start.1
